TPU v7x, 32 devices: a whole 2x2x4 slice. The times are simulated.
32 devices in a mesh: dp: 16 (over z, y, x), head: 2 (over core).
Axes of the slice: x: 2, y: 2, z: 4, core: 2. Of those that a mesh axis runs over, the one named last changes fastest.
Arguments:
- query_stream: bfloat16 [32768, 512], P('dp'), may hold values from -6 to 6
- kv_stream: bfloat16 [32768, 512], P('dp'), may hold values from -6 to 6
- memory: bfloat16 [32768, 512], P('dp'), may hold values from -6 to 6
- out_grad: bfloat16 [32768, 512], P('dp'), may hold values from -6 to 6
- lengths: int32 [16, 32], P('dp'), may hold values from 1 to 1024, 2048 in all within a row
- obs_rank: int32 [32768], P('dp'), may hold values from 0 to 2047
- obs_count: int32 [32768], P('dp'), may hold values from 0 to 2047
- unit_owner: int32 [256], replicated, may hold values from 0 to 15, as said below
- master: float32 [512, 2, 16, 512], P('dp', 'head'), may hold values from -2 to 2, as said below
- first_moment: float32 [512, 2, 16, 512], P('dp', 'head'), may hold values from -506.85414 to 506.85414
- second_moment: float32 [512, 2, 16, 512], P('dp', 'head'), may hold values from 1310.72 to 64225.28
- norm_master: float32 [4096], P('dp'), may hold values from -0.8 to 1.4
- norm_first: float32 [4096], P('dp'), may hold values from -768 to 768
- norm_second: float32 [4096], P('dp'), may hold values from 65536 to 262144
Outputs:
- output: bfloat16 [32768, 512], P('dp')
- grad_query: bfloat16 [32768, 512], P('dp')
- grad_kv: bfloat16 [32768, 512], P('dp')
- grad_memory: bfloat16 [32768, 512], P('dp')
- weight_grad: float32 [512, 2, 16, 512], P('dp', 'head')
- weight_first: float32 [512, 2, 16, 512], P('dp', 'head')
- weight_second: float32 [512, 2, 16, 512], P('dp', 'head')
- weight_new: float32 [512, 2, 16, 512], P('dp', 'head')
- norm_grad: float32 [4096], P('dp')
- norm_first_new: float32 [4096], P('dp')
- norm_second_new: float32 [4096], P('dp')
- norm_new: float32 [4096], P('dp')
Inputs may be any that keep to these rules, and one draw needn't show every extreme that they name: `unit_owner`: every dp index owns at most 32 units and some own exactly 32. `master`: slots that no unit names hold values that are never read.
All inputs are finite; a program needn't handle non-finite values.
Results may differ from a plain program's by a relative error of at most 0.025.
Values may be sent and summed in bfloat16 or wider, within the bound.
A program may use at most 192 MiB of HBM per device.

v0:
```python
from functools import partial

import jax
import jax.numpy as jnp
from jax import lax
from jax.sharding import PartitionSpec as P

HEAD_DIM = 64
ROW = 2048
DOCS = 32
STEP = 10


EPS_NORM = 1e-05
ADAM_EPS = 1e-08
BETA_ONE = 0.5
BETA_TWO = 0.5
RATE_MATRIX = 0.1
RATE_NORM = 0.3
WEIGHT_DECAY = 0.01
MASKED_SCORE = -1000000000.0


def layer_norm(vector, norm_gain, norm_shift):
    row_mean = jnp.mean(vector, -1, keepdims=True)
    centred = vector - row_mean
    row_var = jnp.mean(centred * centred, -1, keepdims=True)
    return centred * lax.rsqrt(row_var + EPS_NORM) * norm_gain + norm_shift


def norm_pullback(vector, norm_gain, norm_shift, cotangent):
    unused_value, pullback = jax.vjp(layer_norm, vector, norm_gain, norm_shift)
    return pullback(cotangent)


def product(left_side, right_side):
    return jnp.dot(left_side, right_side, preferred_element_type=jnp.float32)


def inner_rows(left_side, right_side):
    return jnp.einsum("tk,tn->kn", left_side, right_side, preferred_element_type=jnp.float32)


def product_back(left_side, right_side):
    return jnp.einsum("tn,kn->tk", left_side, right_side, preferred_element_type=jnp.float32)


def slot_places(unit_owner, dev_count, slot_count):
    onehot_table = (unit_owner[:, None] == jnp.arange(dev_count, dtype=jnp.int32)[None, :]).astype(
        jnp.int32
    )
    before = jnp.cumsum(onehot_table, 0) - onehot_table
    return unit_owner * slot_count + jnp.sum(before * onehot_table, 1)


def unpack(gathered, places, features, head_shards):
    flat_rows = gathered[places].reshape(-1, features)
    head_cols = features // head_shards
    ffn_cols = (flat_rows.shape[0] - 8 * head_cols) // 2
    pieces = [
        flat_rows[number * head_cols : (number + 1) * head_cols].reshape(features, head_cols)
        for number in range(6)
    ]
    pieces.append(flat_rows[6 * head_cols : 7 * head_cols])
    pieces.append(flat_rows[7 * head_cols : 8 * head_cols])
    pieces.append(flat_rows[8 * head_cols : 8 * head_cols + ffn_cols].reshape(features, ffn_cols))
    pieces.append(flat_rows[8 * head_cols + ffn_cols :])
    return pieces


def row_layout(lengths):
    doc_ends = jnp.cumsum(lengths, 1)
    local_pos = jnp.arange(ROW, dtype=jnp.int32)
    doc_ids = jnp.sum((local_pos[None, :, None] >= doc_ends[:, None, :]).astype(jnp.int32), 2)
    doc_match = doc_ids[:, :, None] == jnp.arange(DOCS, dtype=jnp.int32)[None, None, :]
    first_pos = jnp.sum(jnp.where(doc_match, (doc_ends - lengths)[:, None, :], 0), 2)
    return (doc_ids.reshape(-1), first_pos.reshape(-1))


def allowed_pairs(layout, query_at, key_at, block_rows, with_seen):
    doc_ids, first_pos, obs_rank, obs_count = layout
    query_doc = lax.dynamic_slice_in_dim(doc_ids, query_at, block_rows)
    allowed = query_doc[:, None] == doc_ids[None, :]
    if with_seen:
        key_pos = jnp.arange(ROW, dtype=jnp.int32)
        query_pos = query_at - key_at + jnp.arange(block_rows, dtype=jnp.int32)
        query_first = lax.dynamic_slice_in_dim(first_pos, query_at, block_rows)
        query_count = lax.dynamic_slice_in_dim(obs_count, query_at, block_rows)
        observed = (key_pos[None, :] == query_first[:, None]) | (
            key_pos[None, :] != query_pos[:, None]
        ) & (obs_rank[None, :] < query_count[:, None])
        allowed = allowed & observed
    return allowed


def attend_forward(queries, keys, values, layout, with_seen):
    tokens, head_cols = queries.shape
    head_count = head_cols // HEAD_DIM
    block_rows = min(512, ROW)
    scaling = HEAD_DIM ** (-0.5)

    def one_block(number):
        query_at = number * block_rows
        key_at = query_at // ROW * ROW
        query_heads = lax.dynamic_slice_in_dim(queries, query_at, block_rows).reshape(
            block_rows, head_count, HEAD_DIM
        )
        key_heads = keys.reshape(ROW, head_count, HEAD_DIM)
        value_heads = values.reshape(ROW, head_count, HEAD_DIM)
        allowed = allowed_pairs(layout, query_at, key_at, block_rows, with_seen)
        raw_scores = jnp.einsum(
            "qhe,khe->hqk", query_heads, key_heads, preferred_element_type=jnp.float32
        )
        scores = jnp.where(allowed[None], raw_scores * scaling, MASKED_SCORE)
        largest = jnp.max(scores, -1, keepdims=True)
        exponent = jnp.exp(scores - largest)
        summed = jnp.sum(exponent, -1, keepdims=True)
        attention = (exponent / summed).astype(jnp.bfloat16)
        mixed_block = jnp.einsum(
            "hqk,khe->qhe", attention, value_heads, preferred_element_type=jnp.float32
        )
        return (mixed_block.reshape(block_rows, head_cols), (largest + jnp.log(summed))[:, :, 0])

    mixed_blocks, log_totals = lax.map(one_block, jnp.arange(tokens // block_rows, dtype=jnp.int32))
    return (mixed_blocks.reshape(tokens, head_cols).astype(jnp.bfloat16), log_totals)


def attend_backward(queries, keys, values, grad_mixed, log_totals, layout, with_seen):
    tokens, head_cols = queries.shape
    head_count = head_cols // HEAD_DIM
    block_rows = min(512, ROW)
    scaling = HEAD_DIM ** (-0.5)

    def one_block(running, number):
        key_grad, value_grad = running
        query_at = number * block_rows
        key_at = query_at // ROW * ROW
        query_heads = lax.dynamic_slice_in_dim(queries, query_at, block_rows).reshape(
            block_rows, head_count, HEAD_DIM
        )
        key_heads = keys.reshape(ROW, head_count, HEAD_DIM)
        value_heads = values.reshape(ROW, head_count, HEAD_DIM)
        grad_heads = lax.dynamic_slice_in_dim(grad_mixed, query_at, block_rows).reshape(
            block_rows, head_count, HEAD_DIM
        )
        allowed = allowed_pairs(layout, query_at, key_at, block_rows, with_seen)
        raw_scores = jnp.einsum(
            "qhe,khe->hqk", query_heads, key_heads, preferred_element_type=jnp.float32
        )
        scores = jnp.where(allowed[None], raw_scores * scaling, MASKED_SCORE)
        attention = jnp.exp(scores - log_totals[number][:, :, None])
        grad_attention = jnp.einsum(
            "qhe,khe->hqk", grad_heads, value_heads, preferred_element_type=jnp.float32
        )
        delta_rows = jnp.sum(attention * grad_attention, -1, keepdims=True)
        grad_scores = (attention * (grad_attention - delta_rows) * scaling).astype(jnp.bfloat16)
        query_part = jnp.einsum(
            "hqk,khe->qhe", grad_scores, key_heads, preferred_element_type=jnp.float32
        ).reshape(block_rows, head_cols)
        key_part = jnp.einsum(
            "hqk,qhe->khe", grad_scores, query_heads, preferred_element_type=jnp.float32
        ).reshape(ROW, head_cols)
        value_part = jnp.einsum(
            "hqk,qhe->khe",
            attention.astype(jnp.bfloat16),
            grad_heads,
            preferred_element_type=jnp.float32,
        ).reshape(ROW, head_cols)
        key_grad = key_grad + key_part
        value_grad = value_grad + value_part
        return ((key_grad, value_grad), query_part)

    zero_rows = jnp.zeros((tokens, head_cols), jnp.float32)
    finals, query_parts = lax.scan(
        one_block, (zero_rows, zero_rows), jnp.arange(tokens // block_rows, dtype=jnp.int32)
    )
    key_grad, value_grad = finals
    return (
        query_parts.reshape(tokens, head_cols).astype(jnp.bfloat16),
        key_grad.astype(jnp.bfloat16),
        value_grad.astype(jnp.bfloat16),
    )


def adamw_step(gradient, first, second, weight, rate, decay):
    first_new = BETA_ONE * first + (1.0 - BETA_ONE) * gradient
    second_new = BETA_TWO * second + (1.0 - BETA_TWO) * gradient * gradient
    corr_one = 1.0 - BETA_ONE**STEP
    corr_two = 1.0 - BETA_TWO**STEP
    direction = first_new / corr_one / (jnp.sqrt(second_new / corr_two) + ADAM_EPS)
    return (first_new, second_new, weight - rate * (direction + decay * weight))


def local(
    query_stream,
    kv_stream,
    memory,
    out_grad,
    lengths,
    obs_rank,
    obs_count,
    unit_owner,
    master,
    first_moment,
    second_moment,
    norm_master,
    norm_first,
    norm_second,
):
    dev_count = lax.axis_size("dp")
    head_shards = lax.axis_size("head")
    my_index = lax.axis_index("dp")
    slot_count = master.shape[0]
    unit_rows = master.shape[2]
    features = query_stream.shape[1]
    unit_total = unit_owner.shape[0]
    places = slot_places(unit_owner, dev_count, slot_count)
    low_master = master.astype(jnp.bfloat16)
    gathered, norm_all = (
        lax.all_gather(low_master, "dp", axis=0, tiled=True),
        lax.all_gather(norm_master.astype(jnp.bfloat16), "dp", axis=0, tiled=True),
    )
    matrices = unpack(gathered, places, features, head_shards)
    norm_params = norm_all.astype(jnp.float32).reshape(8, features)
    doc_ids, first_pos = row_layout(lengths)
    layout = (doc_ids, first_pos, obs_rank, obs_count)
    stream_q = query_stream.astype(jnp.float32)
    stream_kv = kv_stream.astype(jnp.float32)
    normed_q = layer_norm(stream_q, norm_params[0], norm_params[1]).astype(jnp.bfloat16)
    normed_kv = layer_norm(stream_kv, norm_params[2], norm_params[3]).astype(jnp.bfloat16)
    queries_self = product(normed_q, matrices[0]).astype(jnp.bfloat16)
    keys_self = product(normed_kv, matrices[1]).astype(jnp.bfloat16)
    values_self = product(normed_kv, matrices[2]).astype(jnp.bfloat16)
    mixed_self, totals_self = attend_forward(queries_self, keys_self, values_self, layout, True)
    self_sum = lax.psum(product(mixed_self, matrices[6]).astype(jnp.bfloat16), "head").astype(
        jnp.float32
    )
    residual = stream_q + self_sum
    normed_c = layer_norm(residual, norm_params[4], norm_params[5]).astype(jnp.bfloat16)
    queries_cross = product(normed_c, matrices[3]).astype(jnp.bfloat16)
    keys_cross = product(memory, matrices[4]).astype(jnp.bfloat16)
    values_cross = product(memory, matrices[5]).astype(jnp.bfloat16)
    mixed_cross, totals_cross = attend_forward(
        queries_cross, keys_cross, values_cross, layout, False
    )
    cross_sum = lax.psum(product(mixed_cross, matrices[7]).astype(jnp.bfloat16), "head").astype(
        jnp.float32
    )
    cross_res = residual + cross_sum
    normed_f = layer_norm(cross_res, norm_params[6], norm_params[7]).astype(jnp.bfloat16)
    pre_act = product(normed_f, matrices[8])
    hidden = jax.nn.gelu(pre_act, approximate=False).astype(jnp.bfloat16)
    ffn_sum = lax.psum(product(hidden, matrices[9]).astype(jnp.bfloat16), "head").astype(
        jnp.float32
    )
    output = (cross_res + ffn_sum).astype(jnp.bfloat16)
    grad_w2 = inner_rows(hidden, out_grad)
    grad_hidden = product_back(out_grad, matrices[9])
    unused_value, gelu_pull = jax.vjp(partial(jax.nn.gelu, approximate=False), pre_act)
    grad_pre = gelu_pull(grad_hidden)[0].astype(jnp.bfloat16)
    grad_w1 = inner_rows(normed_f, grad_pre)
    normed_f_grad = lax.psum(
        product_back(grad_pre, matrices[8]).astype(jnp.bfloat16), "head"
    ).astype(jnp.float32)
    grad_cross_res, gain_f, shift_f = norm_pullback(
        cross_res, norm_params[6], norm_params[7], normed_f_grad
    )
    grad_cross_res = grad_cross_res + out_grad.astype(jnp.float32)
    cross_low = grad_cross_res.astype(jnp.bfloat16)
    grad_wo_cross = inner_rows(mixed_cross, cross_low)
    grad_mixed_cross = product_back(cross_low, matrices[7]).astype(jnp.bfloat16)
    grad_q_cross, grad_k_cross, grad_v_cross = attend_backward(
        queries_cross, keys_cross, values_cross, grad_mixed_cross, totals_cross, layout, False
    )
    grad_wq_cross = inner_rows(normed_c, grad_q_cross)
    grad_wk_cross = inner_rows(memory, grad_k_cross)
    grad_wv_cross = inner_rows(memory, grad_v_cross)
    normed_c_grad, memory_sum = (
        lax.psum(product_back(grad_q_cross, matrices[3]).astype(jnp.bfloat16), "head").astype(
            jnp.float32
        ),
        lax.psum(
            (
                product_back(grad_k_cross, matrices[4]) + product_back(grad_v_cross, matrices[5])
            ).astype(jnp.bfloat16),
            "head",
        ).astype(jnp.float32),
    )
    grad_residual, gain_c, shift_c = norm_pullback(
        residual, norm_params[4], norm_params[5], normed_c_grad
    )
    grad_residual = grad_residual + grad_cross_res
    self_low = grad_residual.astype(jnp.bfloat16)
    grad_wo_self = inner_rows(mixed_self, self_low)
    grad_mixed_self = product_back(self_low, matrices[6]).astype(jnp.bfloat16)
    grad_q_self, grad_k_self, grad_v_self = attend_backward(
        queries_self, keys_self, values_self, grad_mixed_self, totals_self, layout, True
    )
    grad_wq_self = inner_rows(normed_q, grad_q_self)
    grad_wk_self = inner_rows(normed_kv, grad_k_self)
    grad_wv_self = inner_rows(normed_kv, grad_v_self)
    normed_q_grad, normed_kv_grad = (
        lax.psum(product_back(grad_q_self, matrices[0]).astype(jnp.bfloat16), "head").astype(
            jnp.float32
        ),
        lax.psum(
            (
                product_back(grad_k_self, matrices[1]) + product_back(grad_v_self, matrices[2])
            ).astype(jnp.bfloat16),
            "head",
        ).astype(jnp.float32),
    )
    grad_stream_q, gain_q, shift_q = norm_pullback(
        stream_q, norm_params[0], norm_params[1], normed_q_grad
    )
    grad_stream_kv, gain_kv, shift_kv = norm_pullback(
        stream_kv, norm_params[2], norm_params[3], normed_kv_grad
    )
    grad_query = (grad_stream_q + grad_residual).astype(jnp.bfloat16)
    grad_kv = grad_stream_kv.astype(jnp.bfloat16)
    grad_memory = memory_sum.astype(jnp.bfloat16)
    grad_list = [
        grad_wq_self,
        grad_wk_self,
        grad_wv_self,
        grad_wq_cross,
        grad_wk_cross,
        grad_wv_cross,
        grad_wo_self,
        grad_wo_cross,
        grad_w1,
        grad_w2,
    ]
    flat_grads = jnp.concatenate([piece.reshape(-1, features) for piece in grad_list], 0)
    unit_grads = flat_grads.reshape(unit_total, 1, unit_rows, features)
    norm_grads = jnp.stack(
        [gain_q, shift_q, gain_kv, shift_kv, gain_c, shift_c, gain_f, shift_f]
    ).reshape(-1)
    outgoing = (
        jnp.zeros((dev_count * slot_count, 1, unit_rows, features), jnp.float32)
        .at[places]
        .set(unit_grads)
    )
    slot_grads, norm_share = (
        lax.psum_scatter(outgoing, "dp", scatter_dimension=0, tiled=True),
        lax.psum_scatter(norm_grads, "dp", scatter_dimension=0, tiled=True),
    )
    owned_count = jnp.sum((unit_owner == my_index).astype(jnp.int32))
    slot_live = (jnp.arange(slot_count, dtype=jnp.int32) < owned_count)[:, None, None, None]
    slot_grads = jnp.where(slot_live, slot_grads, 0.0)
    first_new, second_new, weight_updated = adamw_step(
        slot_grads, first_moment, second_moment, master, RATE_MATRIX, WEIGHT_DECAY
    )
    weight_first = jnp.where(slot_live, first_new, 0.0)
    weight_second = jnp.where(slot_live, second_new, 0.0)
    weight_new = jnp.where(slot_live, weight_updated, 0.0)
    norm_first_new, norm_second_new, norm_new = adamw_step(
        norm_share, norm_first, norm_second, norm_master, RATE_NORM, 0.0
    )
    return (
        output,
        grad_query,
        grad_kv,
        grad_memory,
        slot_grads,
        weight_first,
        weight_second,
        weight_new,
        norm_share,
        norm_first_new,
        norm_second_new,
        norm_new,
    )


def solution(mesh):
    in_specs = (
        P("dp", None),
        P("dp", None),
        P("dp", None),
        P("dp", None),
        P("dp", None),
        P("dp"),
        P("dp"),
        P(),
        P("dp", "head", None, None),
        P("dp", "head", None, None),
        P("dp", "head", None, None),
        P("dp"),
        P("dp"),
        P("dp"),
    )
    out_specs = (
        P("dp", None),
        P("dp", None),
        P("dp", None),
        P("dp", None),
        P("dp", "head", None, None),
        P("dp", "head", None, None),
        P("dp", "head", None, None),
        P("dp", "head", None, None),
        P("dp"),
        P("dp"),
        P("dp"),
        P("dp"),
    )
    return jax.shard_map(local, mesh=mesh, in_specs=in_specs, out_specs=out_specs, check_vma=False)
```

profile of v0, /device:TPU:0, one launch (start us, length us, event | category | flops | bytes accessed | tf_op | source)
XLA Modules:
  0.0 1876.0 jit_solution(15453931517627124649)
XLA Ops:
  12.6 42.8 %all-gather = bf16[16,1,256]{2,1,0:T(2,128)(2,1)S(1)} all-gather(bf16[1,1,256]{2,1,0:T(2,128)(2,1)S(1)} %reshape.868), channel_id=1, replica_groups=mesh['dp'=16,'head'=2] {'dp'}, dimensions={0}, use_global_device_ids=true | all-gather | bytes 8704 | tf_op jit(solution)/shard_map/all_gather | solution.py:221
  69.7 57.6 %all-gather.3.cloned.1.call-done = bf16[512,1,16,512]{3,2,1,0:T(8,128)(2,1)} async-done(((bf16[32,1,16,512]{3,2,1,0:T(8,128)(2,1)}), bf16[512,1,16,512]{3,2,1,0:T(8,128)(2,1)}) %all-gather.3.cloned.1.call-update) | async-done | bytes 8388624 | tf_op jit(solution)/shard_map/all_gather | solution.py:220
  156.8 81.5 %while.58 = (s32[]{:T(128)}, bf16[4,512,256]{2,1,0:T(8,128)(2,1)}, f32[4,4,512]{2,1,0:T(4,128)S(1)}, s32[4]{0:T(128)S(1)}, s32[2048]{0:T(1024)S(1)}, /*index=5*/...) while((s32[]{:T(128)}, bf16[4,512,256]{2,1,0:T(8,128)(2,1)}, ...), condition=%wide.region_13.14_spmd, body=%wide.region_10.13_spmd.sunk | while | flops 1131411968 | bytes 63019968 | solution.py:124
  250.7 11.0 all-reduce.8.cloned.1.call-done
  274.3 75.4 %while.59 = (s32[]{:T(128)}, bf16[4,512,256]{2,1,0:T(8,128)(2,1)}, f32[4,4,512]{2,1,0:T(4,128)}, s32[4]{0:T(128)S(1)}, s32[2048]{0:T(1024)S(1)}, /*index=5*/s32[...) while((s32[]{:T(128)}, bf16[4,512,256]{2,1,0:T(8,128)(2,1)}, ...), condition=%wide.region_20.21_spmd, body=%wide.region_17.20_spmd.sunk | while | flops 1125120000 | bytes 62995672 | solution.py:124
  358.5 17.1 all-reduce.10.cloned.1.call-done
  381.4 22.2 %multiply_convert_fusion.2 = (bf16[2048,1024]{1,0:T(8,128)(2,1)}, f32[2048,1024]{1,0:T(8,128)S(1)}, f32[2048,1024]{1,0:T(8,128)}) fusion(bf16[512,1024]{1,0:T(8,128)(2,1)S(1)} %copy-done.62, f32[2048,512]{1,0:T(8,128)S(1)} %get-tuple-element.878, f32[512]{0:T(512)S(1)} %bitcast.397, f32[512]{0:T(512)S(1)} %bitcast.381, f32[2048]{0:T(1024)S(1)} %fusion.172, ...), kind=kOutput, calls=%fused_computation.113 | convolution fusion | flops 2289041408 | bytes 26234880 | tf_op jit(solution)/shard_map/dot_general | solution.py:37
  416.5 22.5 %all-reduce.12.cloned.1.call-done = bf16[2048,512]{1,0:T(8,128)(2,1)} async-done(((bf16[2048,512]{1,0:T(8,128)(2,1)}), bf16[2048,512]{1,0:T(8,128)(2,1)}) %all-reduce.12.cloned.1.call-update) | async-done | bytes 2097168 | tf_op jit(solution)/shard_map/psum | solution.py:262
  450.5 448.1 %while.60 = (s32[]{:T(128)}, f32[2048,256]{0,1:T(8,128)}, f32[2048,256]{0,1:T(8,128)}, bf16[4,512,256]{2,1,0:T(8,128)(2,1)}, s32[4]{0:T(128)S(1)}, /*index=5*/bf...) while((s32[]{:T(128)}, f32[2048,256]{0,1:T(8,128)}, ...), condition=%wide.region_30.31_spmd.clone, body=%wide.region_28.30_spmd.clone.sunk | while | flops 2796560384 | bytes 145546000 | solution.py:174
  453.1 8.1 fusion.326
  464.7 9.4 fusion.328
  478.5 33.1 %fusion.329 = f32[4,64,2048]{2,1,0:T(8,128)} fusion(bf16[512,4,64]{0,2,1:T(8,128)(2,1)S(1)} %bitcast.324, f32[4,512,2048]{2,1,0:T(8,128)} %fusion.328, f32[4,512,2048]{2,1,0:T(8,128)} %fusion.326, f32[4,512]{1,0:T(4,128)S(1)} %dynamic-slice_bitcast_fusion.4, pred[512,2048]{1,0:T(8,128)(4,1)} %broadcast_compare_fusion.5), kind=kOutput, calls=%fused_computation.38.clone.1 | convolution fusion | flops 583012352 | bytes 36970496 | tf_op jit(solution)/shard_map/while/body/eval_jaxpr/hqk,qhe->khe/dot_general | solution.py:160
  511.6 11.8 fusion.327
  528.8 31.2 %fusion.330 = bf16[4,512,64]{1,2,0:T(8,128)(2,1)} fusion(bf16[2048,4,64]{0,2,1:T(8,128)(2,1)S(1)} %bitcast.315, f32[4,512,2048]{2,1,0:T(8,128)} %fusion.328, f32[4,512,2048]{2,1,0:T(8,128)} %fusion.326, f32[4,512]{1,0:T(4,128)S(1)} %dynamic-slice_bitcast_fusion.4, pred[512,2048]{1,0:T(8,128)(4,1)} %broadcast_compare_fusion.5), kind=kOutput, calls=%fused_computation.37.clone.1 | convolution fusion | flops 583012352 | bytes 35921920 | tf_op jit(solution)/shard_map/while/body/eval_jaxpr/hqk,khe->qhe/dot_general | solution.py:157
  575.7 9.4 fusion.328
  589.5 33.1 %fusion.329 = f32[4,64,2048]{2,1,0:T(8,128)} fusion(bf16[512,4,64]{0,2,1:T(8,128)(2,1)S(1)} %bitcast.324, f32[4,512,2048]{2,1,0:T(8,128)} %fusion.328, f32[4,512,2048]{2,1,0:T(8,128)} %fusion.326, f32[4,512]{1,0:T(4,128)S(1)} %dynamic-slice_bitcast_fusion.4, pred[512,2048]{1,0:T(8,128)(4,1)} %broadcast_compare_fusion.5), kind=kOutput, calls=%fused_computation.38.clone.1 | convolution fusion | flops 583012352 | bytes 36970496 | tf_op jit(solution)/shard_map/while/body/eval_jaxpr/hqk,qhe->khe/dot_general | solution.py:160
  622.6 11.8 fusion.327
  641.0 31.2 %fusion.330 = bf16[4,512,64]{1,2,0:T(8,128)(2,1)} fusion(bf16[2048,4,64]{0,2,1:T(8,128)(2,1)S(1)} %bitcast.315, f32[4,512,2048]{2,1,0:T(8,128)} %fusion.328, f32[4,512,2048]{2,1,0:T(8,128)} %fusion.326, f32[4,512]{1,0:T(4,128)S(1)} %dynamic-slice_bitcast_fusion.4, pred[512,2048]{1,0:T(8,128)(4,1)} %broadcast_compare_fusion.5), kind=kOutput, calls=%fused_computation.37.clone.1 | convolution fusion | flops 583012352 | bytes 35921920 | tf_op jit(solution)/shard_map/while/body/eval_jaxpr/hqk,khe->qhe/dot_general | solution.py:157
  676.3 8.1 fusion.326
  687.9 9.4 fusion.328
  701.7 33.1 %fusion.329 = f32[4,64,2048]{2,1,0:T(8,128)} fusion(bf16[512,4,64]{0,2,1:T(8,128)(2,1)S(1)} %bitcast.324, f32[4,512,2048]{2,1,0:T(8,128)} %fusion.328, f32[4,512,2048]{2,1,0:T(8,128)} %fusion.326, f32[4,512]{1,0:T(4,128)S(1)} %dynamic-slice_bitcast_fusion.4, pred[512,2048]{1,0:T(8,128)(4,1)} %broadcast_compare_fusion.5), kind=kOutput, calls=%fused_computation.38.clone.1 | convolution fusion | flops 583012352 | bytes 36970496 | tf_op jit(solution)/shard_map/while/body/eval_jaxpr/hqk,qhe->khe/dot_general | solution.py:160
  734.8 11.8 fusion.327
  753.2 31.2 %fusion.330 = bf16[4,512,64]{1,2,0:T(8,128)(2,1)} fusion(bf16[2048,4,64]{0,2,1:T(8,128)(2,1)S(1)} %bitcast.315, f32[4,512,2048]{2,1,0:T(8,128)} %fusion.328, f32[4,512,2048]{2,1,0:T(8,128)} %fusion.326, f32[4,512]{1,0:T(4,128)S(1)} %dynamic-slice_bitcast_fusion.4, pred[512,2048]{1,0:T(8,128)(4,1)} %broadcast_compare_fusion.5), kind=kOutput, calls=%fused_computation.37.clone.1 | convolution fusion | flops 583012352 | bytes 35921920 | tf_op jit(solution)/shard_map/while/body/eval_jaxpr/hqk,khe->qhe/dot_general | solution.py:157
  800.1 9.4 fusion.328
  813.9 33.1 %fusion.329 = f32[4,64,2048]{2,1,0:T(8,128)} fusion(bf16[512,4,64]{0,2,1:T(8,128)(2,1)S(1)} %bitcast.324, f32[4,512,2048]{2,1,0:T(8,128)} %fusion.328, f32[4,512,2048]{2,1,0:T(8,128)} %fusion.326, f32[4,512]{1,0:T(4,128)S(1)} %dynamic-slice_bitcast_fusion.4, pred[512,2048]{1,0:T(8,128)(4,1)} %broadcast_compare_fusion.5), kind=kOutput, calls=%fused_computation.38.clone.1 | convolution fusion | flops 583012352 | bytes 36970496 | tf_op jit(solution)/shard_map/while/body/eval_jaxpr/hqk,qhe->khe/dot_general | solution.py:160
  847.0 11.8 fusion.327
  865.4 31.2 %fusion.330 = bf16[4,512,64]{1,2,0:T(8,128)(2,1)} fusion(bf16[2048,4,64]{0,2,1:T(8,128)(2,1)S(1)} %bitcast.315, f32[4,512,2048]{2,1,0:T(8,128)} %fusion.328, f32[4,512,2048]{2,1,0:T(8,128)} %fusion.326, f32[4,512]{1,0:T(4,128)S(1)} %dynamic-slice_bitcast_fusion.4, pred[512,2048]{1,0:T(8,128)(4,1)} %broadcast_compare_fusion.5), kind=kOutput, calls=%fused_computation.37.clone.1 | convolution fusion | flops 583012352 | bytes 35921920 | tf_op jit(solution)/shard_map/while/body/eval_jaxpr/hqk,khe->qhe/dot_general | solution.py:157
  912.5 12.2 all-reduce.14.cloned.1.call-done
  940.2 455.6 %while.61 = (s32[]{:T(128)}, f32[2048,256]{0,1:T(8,128)}, f32[2048,256]{0,1:T(8,128)}, bf16[4,512,256]{2,1,0:T(8,128)(2,1)}, s32[4]{0:T(128)S(1)}, /*index=5*/bf...) while((s32[]{:T(128)}, f32[2048,256]{0,1:T(8,128)}, ...), condition=%wide.region_36.37_spmd.clone, body=%wide.region_34.36_spmd.clone.sunk | while | flops 2802852352 | bytes 145570800 | solution.py:174
  958.6 9.4 fusion.344
  970.7 32.8 %fusion.345 = f32[4,64,2048]{2,1,0:T(8,128)} fusion(bf16[512,4,64]{0,2,1:T(8,128)(2,1)S(1)} %bitcast.326, f32[4,512,2048]{2,1,0:T(8,128)} %fusion.344, f32[4,512,2048]{2,1,0:T(8,128)} %fusion.341, f32[4,512]{1,0:T(4,128)S(1)} %dynamic-slice_bitcast_fusion.5, pred[512,2048]{1,0:T(8,128)(4,1)} %fusion.342), kind=kOutput, calls=%fused_computation.71.clone.1 | convolution fusion | flops 583012352 | bytes 36970496 | tf_op jit(solution)/shard_map/while/body/eval_jaxpr/hqk,qhe->khe/dot_general | solution.py:160
  1003.5 11.8 fusion.343
  1020.7 30.9 %fusion.346 = bf16[4,512,64]{1,2,0:T(8,128)(2,1)} fusion(bf16[2048,4,64]{0,2,1:T(8,128)(2,1)S(1)} %bitcast.312, f32[4,512,2048]{2,1,0:T(8,128)} %fusion.344, f32[4,512,2048]{2,1,0:T(8,128)} %fusion.341, f32[4,512]{1,0:T(4,128)S(1)} %dynamic-slice_bitcast_fusion.5, pred[512,2048]{1,0:T(8,128)(4,1)} %fusion.342), kind=kOutput, calls=%fused_computation.70.clone.1 | convolution fusion | flops 583012352 | bytes 35921920 | tf_op jit(solution)/shard_map/while/body/eval_jaxpr/hqk,khe->qhe/dot_general | solution.py:157
  1071.4 9.4 fusion.344
  1083.5 32.8 %fusion.345 = f32[4,64,2048]{2,1,0:T(8,128)} fusion(bf16[512,4,64]{0,2,1:T(8,128)(2,1)S(1)} %bitcast.326, f32[4,512,2048]{2,1,0:T(8,128)} %fusion.344, f32[4,512,2048]{2,1,0:T(8,128)} %fusion.341, f32[4,512]{1,0:T(4,128)S(1)} %dynamic-slice_bitcast_fusion.5, pred[512,2048]{1,0:T(8,128)(4,1)} %fusion.342), kind=kOutput, calls=%fused_computation.71.clone.1 | convolution fusion | flops 583012352 | bytes 36970496 | tf_op jit(solution)/shard_map/while/body/eval_jaxpr/hqk,qhe->khe/dot_general | solution.py:160
  1116.3 11.8 fusion.343
  1134.7 30.9 %fusion.346 = bf16[4,512,64]{1,2,0:T(8,128)(2,1)} fusion(bf16[2048,4,64]{0,2,1:T(8,128)(2,1)S(1)} %bitcast.312, f32[4,512,2048]{2,1,0:T(8,128)} %fusion.344, f32[4,512,2048]{2,1,0:T(8,128)} %fusion.341, f32[4,512]{1,0:T(4,128)S(1)} %dynamic-slice_bitcast_fusion.5, pred[512,2048]{1,0:T(8,128)(4,1)} %fusion.342), kind=kOutput, calls=%fused_computation.70.clone.1 | convolution fusion | flops 583012352 | bytes 35921920 | tf_op jit(solution)/shard_map/while/body/eval_jaxpr/hqk,khe->qhe/dot_general | solution.py:157
  1185.5 9.4 fusion.344
  1197.6 32.8 %fusion.345 = f32[4,64,2048]{2,1,0:T(8,128)} fusion(bf16[512,4,64]{0,2,1:T(8,128)(2,1)S(1)} %bitcast.326, f32[4,512,2048]{2,1,0:T(8,128)} %fusion.344, f32[4,512,2048]{2,1,0:T(8,128)} %fusion.341, f32[4,512]{1,0:T(4,128)S(1)} %dynamic-slice_bitcast_fusion.5, pred[512,2048]{1,0:T(8,128)(4,1)} %fusion.342), kind=kOutput, calls=%fused_computation.71.clone.1 | convolution fusion | flops 583012352 | bytes 36970496 | tf_op jit(solution)/shard_map/while/body/eval_jaxpr/hqk,qhe->khe/dot_general | solution.py:160
  1230.3 11.8 fusion.343
  1248.8 30.9 %fusion.346 = bf16[4,512,64]{1,2,0:T(8,128)(2,1)} fusion(bf16[2048,4,64]{0,2,1:T(8,128)(2,1)S(1)} %bitcast.312, f32[4,512,2048]{2,1,0:T(8,128)} %fusion.344, f32[4,512,2048]{2,1,0:T(8,128)} %fusion.341, f32[4,512]{1,0:T(4,128)S(1)} %dynamic-slice_bitcast_fusion.5, pred[512,2048]{1,0:T(8,128)(4,1)} %fusion.342), kind=kOutput, calls=%fused_computation.70.clone.1 | convolution fusion | flops 583012352 | bytes 35921920 | tf_op jit(solution)/shard_map/while/body/eval_jaxpr/hqk,khe->qhe/dot_general | solution.py:157
  1299.6 9.4 fusion.344
  1311.6 32.8 %fusion.345 = f32[4,64,2048]{2,1,0:T(8,128)} fusion(bf16[512,4,64]{0,2,1:T(8,128)(2,1)S(1)} %bitcast.326, f32[4,512,2048]{2,1,0:T(8,128)} %fusion.344, f32[4,512,2048]{2,1,0:T(8,128)} %fusion.341, f32[4,512]{1,0:T(4,128)S(1)} %dynamic-slice_bitcast_fusion.5, pred[512,2048]{1,0:T(8,128)(4,1)} %fusion.342), kind=kOutput, calls=%fused_computation.71.clone.1 | convolution fusion | flops 583012352 | bytes 36970496 | tf_op jit(solution)/shard_map/while/body/eval_jaxpr/hqk,qhe->khe/dot_general | solution.py:160
  1344.4 11.8 fusion.343
  1362.9 30.9 %fusion.346 = bf16[4,512,64]{1,2,0:T(8,128)(2,1)} fusion(bf16[2048,4,64]{0,2,1:T(8,128)(2,1)S(1)} %bitcast.312, f32[4,512,2048]{2,1,0:T(8,128)} %fusion.344, f32[4,512,2048]{2,1,0:T(8,128)} %fusion.341, f32[4,512]{1,0:T(4,128)S(1)} %dynamic-slice_bitcast_fusion.5, pred[512,2048]{1,0:T(8,128)(4,1)} %fusion.342), kind=kOutput, calls=%fused_computation.70.clone.1 | convolution fusion | flops 583012352 | bytes 35921920 | tf_op jit(solution)/shard_map/while/body/eval_jaxpr/hqk,khe->qhe/dot_general | solution.py:157
  1473.2 37.2 %scatter_fusion = f32[512,16,512]{2,1,0:T(8,128)} fusion(f32[512,16,512]{2,1,0:T(8,128)} %broadcast.636, s32[256]{0:T(256)S(1)} %copy-done.104, f32[256,16,512]{2,1,0:T(8,128)} %bitcast.331), kind=kCustom, calls=%fused_computation.1 | custom fusion | bytes 25166848 | tf_op jit(solution)/shard_map/scatter | solution.py:342
  1524.3 80.4 %all-reduce = f32[4096]{0:T(1024)S(1)} all-reduce(f32[4096]{0:T(1024)S(1)} %bitcast.368), channel_id=3, replica_groups=mesh['dp'=16,'head'=2] {'dp'}, use_global_device_ids=true, to_apply=%region_55.56.clone | all-reduce | flops 4096 | bytes 32768
  1616.9 244.0 %reduce-scatter.2.cloned.1.call-done = f32[32,1,16,512]{3,2,1,0:T(8,128)} async-done(((f32[512,1,16,512]{3,2,1,0:T(8,128)}), f32[32,1,16,512]{3,2,1,0:T(8,128)}) %reduce-scatter.2.cloned.1.call-update) | async-done | bytes 1048592 | tf_op jit(solution)/shard_map/reduce_scatter | solution.py:345
  (588 shorter events, 586.8 us)
Async XLA Ops:
  7.2 238.9 %copy-start = (bf16[2048,512]{1,0:T(8,128)(2,1)S(1)}, bf16[2048,512]{1,0:T(8,128)(2,1)}, u32[]{:S(2)}) copy-start(bf16[2048,512]{1,0:T(8,128)(2,1)} %param.24) | copy-start | bytes 6291460
  7.2 120.1 %all-gather.3.cloned.1.call-start = ((), (), s32[]{:S(2)}) async-start(), calls=%async_computation.1 | async-start | bytes 8912896 | tf_op jit(solution)/shard_map/all_gather | solution.py:220
  9.5 252.1 %all-reduce.8.cloned.1.call-start = ((), (), s32[]{:S(2)}) async-start(), calls=%async_computation.2 | async-start | bytes 4194304 | tf_op jit(solution)/shard_map/psum | solution.py:235
  12.6 49.7 %copy-start.17 = (bf16[2048,512]{1,0:T(8,128)(2,1)S(1)}, bf16[2048,512]{1,0:T(8,128)(2,1)}, u32[]{:S(2)}) copy-start(bf16[2048,512]{1,0:T(8,128)(2,1)} %param.23) | copy-start | bytes 6291460
  12.6 51.4 %copy-start.1 = (bf16[2048,512]{1,0:T(8,128)(2,1)S(1)}, bf16[2048,512]{1,0:T(8,128)(2,1)}, u32[]{:S(2)}) copy-start(bf16[2048,512]{1,0:T(8,128)(2,1)} %param.22) | copy-start | bytes 6291460
  62.3 5.4 copy-start.69
  142.8 7.4 copy-start.59
  150.2 6.6 copy-start.67
  238.3 10.6 copy-start.6
  238.3 10.6 copy-start.75
  238.3 10.6 copy-start.84
  238.3 5.9 copy-start.61
  242.0 133.6 %all-reduce.10.cloned.1.call-start = ((), (), s32[]{:S(2)}) async-start(), calls=%async_computation.3 | async-start | bytes 4194304 | tf_op jit(solution)/shard_map/psum | solution.py:246
  246.1 18.5 copy-start.50
  250.6 15.5 copy-start.99
  250.6 15.5 copy-start.109
  268.7 5.6 copy-start.8
  353.1 85.9 %all-reduce.12.cloned.1.call-start = ((), (), s32[]{:S(2)}) async-start(), calls=%async_computation.4 | async-start | bytes 4194304 | tf_op jit(solution)/shard_map/psum | solution.py:262
  379.4 24.2 %copy-start.9 = (f32[2048,512]{1,0:T(8,128)}, f32[2048,512]{1,0:T(8,128)S(1)}, u32[]{:S(2)}) copy-start(f32[2048,512]{1,0:T(8,128)S(1)} %get-tuple-element.878) | copy-start | bytes 12582916
  379.4 64.5 %copy-start.82 = (f32[2048]{0:T(1024)}, f32[2048]{0:T(1024)S(1)}, u32[]{:S(2)}) copy-start(f32[2048]{0:T(1024)S(1)} %broadcast_multiply_fusion) | copy-start | bytes 24580
  380.3 63.6 %copy-start.93 = (f32[2048]{0:T(1024)}, f32[2048]{0:T(1024)S(1)}, u32[]{:S(2)}) copy-start(f32[2048]{0:T(1024)S(1)} %fusion.172) | copy-start | bytes 24580
  381.4 22.2 %copy-start.29 = (bf16[2048,512]{1,0:T(8,128)(2,1)S(1)}, bf16[2048,512]{1,0:T(8,128)(2,1)}, u32[]{:S(2)}) copy-start(bf16[2048,512]{1,0:T(8,128)(2,1)} %param.25) | copy-start | bytes 6291460
  381.4 22.2 %copy-start.63 = (bf16[64,16,512]{2,1,0:T(8,128)(2,1)S(1)}, bf16[64,16,512]{2,1,0:T(8,128)(2,1)}, u32[]{:S(2)}) copy-start(bf16[64,16,512]{2,1,0:T(8,128)(2,1)} %get-tuple-element.887) | copy-start | bytes 3145732
  416.4 508.2 %all-reduce.14.cloned.1.call-start = ((), (), s32[]{:S(2)}) async-start(), calls=%async_computation.5 | async-start | bytes 4194304 | tf_op jit(solution)/shard_map/psum | solution.py:279
  902.1 610.9 %all-reduce.16.cloned.1.call-start = ((), (), s32[]{:S(2)}) async-start(), calls=%async_computation.7 | async-start | bytes 16777216 | tf_op jit(solution)/shard_map/psum | solution.py:253
  902.2 6.0 copy-start.12
  902.2 6.0 copy-start.52
  910.4 14.3 copy-start.72
  910.4 14.3 copy-start.100
  912.5 17.2 copy-start.92
  912.5 17.2 copy-start.79
  1402.6 458.3 %reduce-scatter.2.cloned.1.call-start = ((), (), s32[]{:S(2)}) async-start(), calls=%async_computation.6 | async-start | bytes 17825792 | tf_op jit(solution)/shard_map/reduce_scatter | solution.py:345
  1422.5 11.4 copy-start.37
  1447.6 8.2 copy-start.38
  1449.7 6.1 copy-start.56
  1449.7 6.1 copy-start.20
  1465.3 7.9 copy-start.104
  1513.0 5.9 copy-start.88
  1513.1 6.0 copy-start.90
  1513.1 6.0 copy-start.18
  1513.1 6.0 copy-start.28
  1513.1 6.0 copy-start.77
  1519.1 5.1 copy-start.105
  1519.1 5.1 copy-start.106
  1519.1 85.6 %copy-start.112 = (f32[256]{0:T(256)S(1)}, f32[256]{0:T(256)}, u32[]{:S(2)}) copy-start(f32[256]{0:T(256)} %param.33) | copy-start | bytes 3076
  1519.1 85.6 %copy-start.113 = (f32[256]{0:T(256)S(1)}, f32[256]{0:T(256)}, u32[]{:S(2)}) copy-start(f32[256]{0:T(256)} %param.35) | copy-start | bytes 3076
  1519.1 85.6 %copy-start.114 = (f32[256]{0:T(256)S(1)}, f32[256]{0:T(256)}, u32[]{:S(2)}) copy-start(f32[256]{0:T(256)} %param.34) | copy-start | bytes 3076
  1613.9 247.0 %copy-start.44 = (f32[32,1,16,512]{3,2,1,0:T(8,128)S(1)}, f32[32,1,16,512]{3,2,1,0:T(8,128)}, u32[]{:S(2)}) copy-start(f32[32,1,16,512]{3,2,1,0:T(8,128)} %param.30) | copy-start | bytes 3145732
  (82 other events, 249.2 us)
Sparse Core Ops, SparseCore 0:
  11.4 115.8 all-gather.2
  242.2 19.4 all-reduce.7
  353.2 22.3 all-reduce.9
  416.6 22.3 all-reduce.11
  902.2 22.3 all-reduce.13
  1402.7 40.3 all-reduce.15
  1510.6 350.2 reduce-scatter.1
where the time goes:
time: 1890 us; the launch traced here: 1880 us
  matrix products  930 us (49%)
  waiting for transfers between devices  364 us (19%)
  local copies, waits for them, and re-layouts  225 us (12%)
  other arithmetic  188 us (10%)
  blocking collectives  123 us (7%)
  loops' own time  27.9 us (1%)
    dot_general x8, matrix products, one_block(): jnp.einsum('hqk,qhe->khe', grad_scores, query_heads, preferred_element_ty...  263 us
    dot_general x8, matrix products, one_block(): jnp.einsum('hqk,khe->qhe', grad_scores, key_heads, preferred_element_type...  249 us
    reduce_scatter x1, waiting for transfers between devices, local(): lax.psum_scatter(outgoing, 'dp', scatter_dimension=0, tiled=True)  244 us
    dot_general x8, matrix products, one_block(): jnp.einsum('hqk,qhe->khe', attention.astype(jnp.bfloat16), grad_heads, pr...  94.3 us
    dot_general x16, matrix products, one_block(): jnp.einsum('qhe,khe->hqk', query_heads, key_heads, preferred_element_type...  90.5 us
    unnamed x1, blocking collectives  80.4 us
    dot_general x8, matrix products, one_block(): jnp.einsum('qhe,khe->hqk', grad_heads, value_heads, preferred_element_typ...  75.3 us
    all_gather x1, waiting for transfers between devices, local(): lax.all_gather(low_master, 'dp', axis=0, tiled=True)  57.6 us
  transfers between devices with their start and end apart: 7, of which 6 were waited for; matrix products, arithmetic and copies ran while one was open for 9% of the time, Pallas kernels for 0%

commit v1 on v0

--- a/solution.py
+++ b/solution.py
@@ -3,6 +3,8 @@
 import jax
 import jax.numpy as jnp
 from jax import lax
+from jax.experimental import pallas as pl
+from jax.experimental.pallas import tpu as pltpu
 from jax.sharding import PartitionSpec as P
 
 HEAD_DIM = 64
@@ -68,118 +70,288 @@
     return pieces
 
 
-def row_layout(lengths):
-    doc_ends = jnp.cumsum(lengths, 1)
-    local_pos = jnp.arange(ROW, dtype=jnp.int32)
-    doc_ids = jnp.sum((local_pos[None, :, None] >= doc_ends[:, None, :]).astype(jnp.int32), 2)
-    doc_match = doc_ids[:, :, None] == jnp.arange(DOCS, dtype=jnp.int32)[None, None, :]
-    first_pos = jnp.sum(jnp.where(doc_match, (doc_ends - lengths)[:, None, :], 0), 2)
-    return (doc_ids.reshape(-1), first_pos.reshape(-1))
-
-
-def allowed_pairs(layout, query_at, key_at, block_rows, with_seen):
-    doc_ids, first_pos, obs_rank, obs_count = layout
-    query_doc = lax.dynamic_slice_in_dim(doc_ids, query_at, block_rows)
-    allowed = query_doc[:, None] == doc_ids[None, :]
+TQ = 256
+TK = 256
+FAR = 32768.0
+F32 = jnp.float32
+BF = jnp.bfloat16
+
+def nt(a, b):
+    return lax.dot_general(a, b, (((1,), (1,)), ((), ())), preferred_element_type=F32)
+
+def nn(a, b):
+    return lax.dot_general(a, b, (((1,), (0,)), ((), ())), preferred_element_type=F32)
+
+def doc_bounds(len_ref):
+    starts = []
+    ends = []
+    at = jnp.int32(0)
+    for d in range(DOCS):
+        starts.append(at)
+        at = at + len_ref[0, d]
+        ends.append(at)
+    return starts, ends
+
+def lane_vector(scalars):
+    lanes = lax.broadcasted_iota(jnp.int32, (1, 128), 1)
+    out = jnp.full((1, 128), -1, jnp.int32)
+    for d, value in enumerate(scalars):
+        out = jnp.where(lanes == d, value, out)
+    return out
+
+def doc_hot_rows(starts, ends, q0):
+    pos = lax.broadcasted_iota(jnp.int32, (1, TQ), 1) + q0
+    rows = [jnp.where((pos >= starts[d]) & (pos < ends[d]), FAR, 0.0) for d in range(DOCS)]
+    return jnp.concatenate(rows, 0)
+
+def key_range(starts, ends, q0):
+    low = jnp.int32(0)
+    high = jnp.int32(0)
+    for d in range(DOCS):
+        low = jnp.where(starts[d] <= q0, starts[d], low)
+        high = jnp.where(starts[d] <= q0 + TQ - 1, ends[d], high)
+    first = lax.div(low, 128) * 128
+    steps = lax.div(high - first + TK - 1, TK)
+    return first, steps
+
+def head_lanes(pair_rows, h):
+    lanes = lax.broadcasted_iota(jnp.int32, pair_rows.shape, 1)
+    keep = (lanes < HEAD_DIM) if h % 2 == 0 else (lanes >= HEAD_DIM)
+    return jnp.where(keep, pair_rows, jnp.zeros_like(pair_rows))
+
+def doc_hot(start_lane, end_lane, at, rows):
+    pos = lax.broadcasted_iota(jnp.int32, (rows, 128), 0) + at
+    return (pos >= start_lane) & (pos < end_lane)
+
+def fill_keys(kaug, k_ref, start_lane, end_lane, heads, with_stats):
+    lanes = lax.broadcasted_iota(jnp.int32, (TK, 128), 1)
+    def one(t, c):
+        at = pl.multiple_of(t * TK, TK)
+        hot = doc_hot(start_lane, end_lane, at, TK)
+        base = jnp.where(hot | (lanes >= DOCS), 0.0, -FAR)
+        for h in range(heads):
+            pair = k_ref[pl.ds(at, TK), pl.ds(h // 2 * 128, 128)]
+            kaug[h, pl.ds(at, TK), 0:128] = (head_lanes(pair, h).astype(F32) * HEAD_DIM ** -0.5).astype(BF)
+            aug = base
+            if with_stats:
+                aug = jnp.where((lanes == 64 + h) | (lanes == 72 + h) | (lanes == 80 + h), -1.0, base)
+            kaug[h, pl.ds(at, TK), 128:256] = aug.astype(BF)
+        return c
+    lax.fori_loop(0, ROW // TK, one, 0)
+    for h in range(heads):
+        kaug[h, ROW:, 0:128] = jnp.zeros((TK, 128), BF)
+        kaug[h, ROW:, 128:256] = jnp.where(lanes < DOCS, -FAR, 0.0).astype(BF)
+
+def fill_ranks(rank_cols, rank_ref, starts):
+    pos = lax.broadcasted_iota(jnp.int32, (1, ROW), 1)
+    first = jnp.zeros((1, ROW), jnp.bool_)
+    for d in range(DOCS):
+        first = first | (pos == starts[d])
+    rank = jnp.where(first, -1.0, rank_ref[...].astype(F32))
+    for t in range(ROW // 128):
+        block = jnp.broadcast_to(rank[:, t * 128:(t + 1) * 128], (128, 128))
+        rank_cols[t * 128:(t + 1) * 128, :] = block.T
+    rank_cols[ROW:, :] = jnp.zeros((TK, 128), F32)
+
+def seen_bias(rank_cols, count_row, k0, q0):
+    rank = rank_cols[pl.ds(k0, TK), :]
+    rank = jnp.concatenate([rank] * (TQ // 128), 1)
+    kpos = lax.broadcasted_iota(jnp.int32, (TK, TQ), 0)
+    qpos = lax.broadcasted_iota(jnp.int32, (TK, TQ), 1)
+    off_diag = (kpos - qpos) != (q0 - k0)
+    allowed = (rank < count_row) & (off_diag | (rank < 0.0))
+    return jnp.where(allowed, 0.0, -FAR * FAR)
+
+def attn_fwd_kernel(with_seen, heads, len_ref, q_ref, k_ref, v_ref, rank_ref, count_ref, o_ref, lse_ref,
+                    kaug, vt, rank_cols, acc, top, qt):
+    starts, ends = doc_bounds(len_ref)
+    start_lane, end_lane = lane_vector(starts), lane_vector(ends)
+    fill_keys(kaug, k_ref, start_lane, end_lane, heads, False)
+    for t in range(ROW // TK):
+        vt[:, :HEAD_DIM, t * TK:(t + 1) * TK] = v_ref[t * TK:(t + 1) * TK, :].T.reshape(heads, HEAD_DIM, TK)
+    vt[:, :HEAD_DIM, ROW:] = jnp.zeros((heads, HEAD_DIM, TK), BF)
+    vt[:, HEAD_DIM:, :] = jnp.ones((heads, 16, ROW + TK), BF)
     if with_seen:
-        key_pos = jnp.arange(ROW, dtype=jnp.int32)
-        query_pos = query_at - key_at + jnp.arange(block_rows, dtype=jnp.int32)
-        query_first = lax.dynamic_slice_in_dim(first_pos, query_at, block_rows)
-        query_count = lax.dynamic_slice_in_dim(obs_count, query_at, block_rows)
-        observed = (key_pos[None, :] == query_first[:, None]) | (
-            key_pos[None, :] != query_pos[:, None]
-        ) & (obs_rank[None, :] < query_count[:, None])
-        allowed = allowed & observed
-    return allowed
-
-
-def attend_forward(queries, keys, values, layout, with_seen):
-    tokens, head_cols = queries.shape
-    head_count = head_cols // HEAD_DIM
-    block_rows = min(512, ROW)
-    scaling = HEAD_DIM ** (-0.5)
-
-    def one_block(number):
-        query_at = number * block_rows
-        key_at = query_at // ROW * ROW
-        query_heads = lax.dynamic_slice_in_dim(queries, query_at, block_rows).reshape(
-            block_rows, head_count, HEAD_DIM
-        )
-        key_heads = keys.reshape(ROW, head_count, HEAD_DIM)
-        value_heads = values.reshape(ROW, head_count, HEAD_DIM)
-        allowed = allowed_pairs(layout, query_at, key_at, block_rows, with_seen)
-        raw_scores = jnp.einsum(
-            "qhe,khe->hqk", query_heads, key_heads, preferred_element_type=jnp.float32
-        )
-        scores = jnp.where(allowed[None], raw_scores * scaling, MASKED_SCORE)
-        largest = jnp.max(scores, -1, keepdims=True)
-        exponent = jnp.exp(scores - largest)
-        summed = jnp.sum(exponent, -1, keepdims=True)
-        attention = (exponent / summed).astype(jnp.bfloat16)
-        mixed_block = jnp.einsum(
-            "hqk,khe->qhe", attention, value_heads, preferred_element_type=jnp.float32
-        )
-        return (mixed_block.reshape(block_rows, head_cols), (largest + jnp.log(summed))[:, :, 0])
-
-    mixed_blocks, log_totals = lax.map(one_block, jnp.arange(tokens // block_rows, dtype=jnp.int32))
-    return (mixed_blocks.reshape(tokens, head_cols).astype(jnp.bfloat16), log_totals)
-
-
-def attend_backward(queries, keys, values, grad_mixed, log_totals, layout, with_seen):
-    tokens, head_cols = queries.shape
-    head_count = head_cols // HEAD_DIM
-    block_rows = min(512, ROW)
-    scaling = HEAD_DIM ** (-0.5)
-
-    def one_block(running, number):
-        key_grad, value_grad = running
-        query_at = number * block_rows
-        key_at = query_at // ROW * ROW
-        query_heads = lax.dynamic_slice_in_dim(queries, query_at, block_rows).reshape(
-            block_rows, head_count, HEAD_DIM
-        )
-        key_heads = keys.reshape(ROW, head_count, HEAD_DIM)
-        value_heads = values.reshape(ROW, head_count, HEAD_DIM)
-        grad_heads = lax.dynamic_slice_in_dim(grad_mixed, query_at, block_rows).reshape(
-            block_rows, head_count, HEAD_DIM
-        )
-        allowed = allowed_pairs(layout, query_at, key_at, block_rows, with_seen)
-        raw_scores = jnp.einsum(
-            "qhe,khe->hqk", query_heads, key_heads, preferred_element_type=jnp.float32
-        )
-        scores = jnp.where(allowed[None], raw_scores * scaling, MASKED_SCORE)
-        attention = jnp.exp(scores - log_totals[number][:, :, None])
-        grad_attention = jnp.einsum(
-            "qhe,khe->hqk", grad_heads, value_heads, preferred_element_type=jnp.float32
-        )
-        delta_rows = jnp.sum(attention * grad_attention, -1, keepdims=True)
-        grad_scores = (attention * (grad_attention - delta_rows) * scaling).astype(jnp.bfloat16)
-        query_part = jnp.einsum(
-            "hqk,khe->qhe", grad_scores, key_heads, preferred_element_type=jnp.float32
-        ).reshape(block_rows, head_cols)
-        key_part = jnp.einsum(
-            "hqk,qhe->khe", grad_scores, query_heads, preferred_element_type=jnp.float32
-        ).reshape(ROW, head_cols)
-        value_part = jnp.einsum(
-            "hqk,qhe->khe",
-            attention.astype(jnp.bfloat16),
-            grad_heads,
-            preferred_element_type=jnp.float32,
-        ).reshape(ROW, head_cols)
-        key_grad = key_grad + key_part
-        value_grad = value_grad + value_part
-        return ((key_grad, value_grad), query_part)
-
-    zero_rows = jnp.zeros((tokens, head_cols), jnp.float32)
-    finals, query_parts = lax.scan(
-        one_block, (zero_rows, zero_rows), jnp.arange(tokens // block_rows, dtype=jnp.int32)
-    )
-    key_grad, value_grad = finals
-    return (
-        query_parts.reshape(tokens, head_cols).astype(jnp.bfloat16),
-        key_grad.astype(jnp.bfloat16),
-        value_grad.astype(jnp.bfloat16),
-    )
+        fill_ranks(rank_cols, rank_ref, starts)
+
+    def one_q(t, c):
+        q0 = pl.multiple_of(t * TQ, TQ)
+        first, steps = key_range(starts, ends, q0)
+        hot = jnp.concatenate([doc_hot_rows(starts, ends, q0), jnp.zeros((128 - DOCS, TQ), F32)], 0).astype(BF)
+        for p in range(heads // 2):
+            qt[p, 0:128, :] = q_ref[pl.ds(q0, TQ), p * 128:(p + 1) * 128].T
+            qt[p, 128:256, :] = hot
+        count_row = count_ref[:, pl.ds(q0, TQ)].astype(F32)
+        acc[...] = jnp.zeros_like(acc)
+        top[...] = jnp.full_like(top, -jnp.inf)
+
+        def one_k(s, c):
+            k0 = pl.multiple_of(first + s * TK, 128)
+            bias = seen_bias(rank_cols, count_row, k0, q0) if with_seen else None
+            old = top[...]
+            scores = [nn(kaug[h, pl.ds(k0, TK), :], qt[h // 2]) for h in range(heads)]
+            if with_seen:
+                scores = [score + bias for score in scores]
+            vts = [vt[h, :, pl.ds(k0, TK)] for h in range(heads)]
+            accs = [acc[h] for h in range(heads)]
+            news, sums = [], []
+            for h in range(heads):
+                score = scores[h]
+                new = jnp.maximum(old[h:h + 1, :], jnp.max(score, 0, keepdims=True))
+                p = jnp.exp(score - new).astype(BF)
+                news.append(new)
+                sums.append(accs[h] * jnp.exp(old[h:h + 1, :] - new) + nn(vts[h], p))
+            for h in range(heads):
+                acc[h] = sums[h]
+            top[...] = jnp.concatenate(news + [old[heads:, :]], 0)
+            return c
+        lax.fori_loop(0, steps, one_k, 0)
+        outs = []
+        for h in range(heads):
+            a = acc[h]
+            total = a[HEAD_DIM:HEAD_DIM + 1, :]
+            outs.append(a[:HEAD_DIM, :] / total)
+            lse_ref[h:h + 1, pl.ds(q0, TQ)] = top[h:h + 1, :] + jnp.log(total)
+        o_ref[pl.ds(q0, TQ), :] = jnp.concatenate(outs, 0).T.astype(BF)
+        return c
+    lax.fori_loop(0, ROW // TQ, one_q, 0)
+
+def attend_forward(lengths, q, k, v, rank, count, with_seen):
+    rows, cols = q.shape
+    heads = cols // HEAD_DIM
+    V = pl.BlockSpec(memory_space=pltpu.VMEM)
+    return pl.pallas_call(
+        partial(attn_fwd_kernel, with_seen, heads),
+        out_shape=(jax.ShapeDtypeStruct((rows, cols), BF), jax.ShapeDtypeStruct((8, rows), F32)),
+        in_specs=[pl.BlockSpec(memory_space=pltpu.SMEM)] + [V] * 5,
+        out_specs=(V, V),
+        scratch_shapes=[
+            pltpu.VMEM((heads, ROW + TK, 256), BF),
+            pltpu.VMEM((heads, HEAD_DIM + 16, ROW + TK), BF),
+            pltpu.VMEM((ROW + TK, 128), F32),
+            pltpu.VMEM((heads, HEAD_DIM + 16, TQ), F32),
+            pltpu.VMEM((8, TQ), F32),
+            pltpu.VMEM((heads // 2, 256, TQ), BF),
+        ],
+        compiler_params=pltpu.CompilerParams(vmem_limit_bytes=56 * 2**20),
+        name="attend_self_forward" if with_seen else "attend_cross_forward",
+    )(lengths, q, k, v, rank, count)
+
+def three_way(value):
+    hi = value.astype(BF).astype(F32)
+    mid = (value - hi).astype(BF).astype(F32)
+    return hi, mid, value - hi - mid
+
+def attn_bwd_kernel(with_seen, heads, len_ref, q_ref, k_ref, v_ref, g_ref, o_ref, lse_ref, rank_ref, count_ref,
+                    dq_ref, dk_ref, dv_ref, kaug, vaug, kt, rank_cols, dk_sum, dv_sum, dq_sum, q_diag, g_diag, qt, gt):
+    cols = heads * HEAD_DIM
+    starts, ends = doc_bounds(len_ref)
+    start_lane, end_lane = lane_vector(starts), lane_vector(ends)
+    fill_keys(kaug, k_ref, start_lane, end_lane, heads, True)
+    lanes = lax.broadcasted_iota(jnp.int32, (TK, 128), 1)
+    for h in range(heads):
+        picks = (lanes == h) | (lanes == 8 + h) | (lanes == 16 + h)
+        side = jnp.where(picks, -1.0, 0.0).astype(BF)
+        for t in range(ROW // TK):
+            pair = v_ref[t * TK:(t + 1) * TK, h // 2 * 128:h // 2 * 128 + 128]
+            vaug[h, t * TK:(t + 1) * TK, 0:128] = head_lanes(pair, h)
+            vaug[h, t * TK:(t + 1) * TK, 128:256] = side
+        vaug[h, ROW:, :] = jnp.zeros((TK, 256), BF)
+    for t in range(ROW // TK):
+        kt[:, t * TK:(t + 1) * TK] = k_ref[t * TK:(t + 1) * TK, :].T
+    kt[:, ROW:] = jnp.zeros((cols, TK), BF)
+    if with_seen:
+        fill_ranks(rank_cols, rank_ref, starts)
+    dk_sum[...] = jnp.zeros_like(dk_sum)
+    dv_sum[...] = jnp.zeros_like(dv_sum)
+    sel_row = lax.broadcasted_iota(jnp.int32, (8, cols), 0)
+    sel_lane = lax.div(lax.broadcasted_iota(jnp.int32, (8, cols), 1), HEAD_DIM)
+    selector = jnp.where(sel_lane == sel_row, 1.0, 0.0).astype(BF)
+
+    def one_q(t, c):
+        q0 = pl.multiple_of(t * TQ, TQ)
+        first, steps = key_range(starts, ends, q0)
+        g = g_ref[pl.ds(q0, TQ), :]
+        q = q_ref[pl.ds(q0, TQ), :]
+        spread = g.astype(F32) * o_ref[pl.ds(q0, TQ), :].astype(F32)
+        spread_hi = spread.astype(BF)
+        delta = nt(selector, spread_hi) + nt(selector, (spread - spread_hi.astype(F32)).astype(BF))
+        daug = jnp.concatenate(list(three_way(delta)) + [jnp.zeros((104, TQ), F32)], 0).astype(BF)
+        lse = lse_ref[:, pl.ds(q0, TQ)]
+        hi, mid, lo = three_way(lse)
+        side = jnp.concatenate([doc_hot_rows(starts, ends, q0), jnp.zeros((32, TQ), F32), hi, mid, lo, jnp.zeros((40, TQ), F32)], 0).astype(BF)
+        for p in range(heads // 2):
+            qt[p, 0:128, :] = q[:, p * 128:(p + 1) * 128].T
+            qt[p, 128:256, :] = side
+            gt[p, 0:128, :] = g[:, p * 128:(p + 1) * 128].T
+            gt[p, 128:256, :] = daug
+        wide = lax.div(lax.broadcasted_iota(jnp.int32, (TQ, cols), 1), HEAD_DIM)
+        for h in range(heads):
+            q_diag[h * TQ:(h + 1) * TQ, :] = jnp.where(wide == h, q, jnp.zeros_like(q))
+            g_diag[h * TQ:(h + 1) * TQ, :] = jnp.where(wide == h, g, jnp.zeros_like(g))
+        count_row = count_ref[:, pl.ds(q0, TQ)].astype(F32)
+        dq_sum[...] = jnp.zeros_like(dq_sum)
+
+        def one_k(s, c):
+            k0 = pl.multiple_of(first + s * TK, 128)
+            bias = seen_bias(rank_cols, count_row, k0, q0) if with_seen else None
+            all_ds, all_p, all_dq = [], [], []
+            kaugs = [kaug[h, pl.ds(k0, TK), :] for h in range(heads)]
+            vaugs = [vaug[h, pl.ds(k0, TK), :] for h in range(heads)]
+            keys_t = kt[:, pl.ds(k0, TK)]
+            qts = [qt[p] for p in range(heads // 2)]
+            gts = [gt[p] for p in range(heads // 2)]
+            qd, gd = q_diag[...], g_diag[...]
+            scores = [nn(kaugs[h], qts[h // 2]) for h in range(heads)]
+            dps = [nn(vaugs[h], gts[h // 2]) for h in range(heads)]
+            if with_seen:
+                scores = [score + bias for score in scores]
+            for h in range(heads):
+                p = jnp.exp(scores[h])
+                ds = (p * dps[h]).astype(BF)
+                all_ds.append(ds)
+                all_p.append(p.astype(BF))
+                all_dq.append(nn(keys_t[h * HEAD_DIM:(h + 1) * HEAD_DIM, :], ds))
+            dk = dk_sum[pl.ds(k0, TK), :] + nn(jnp.concatenate(all_ds, 1), qd)
+            dv = dv_sum[pl.ds(k0, TK), :] + nn(jnp.concatenate(all_p, 1), gd)
+            dq = dq_sum[...] + jnp.concatenate(all_dq, 0)
+            dk_sum[pl.ds(k0, TK), :] = dk
+            dv_sum[pl.ds(k0, TK), :] = dv
+            dq_sum[...] = dq
+            return c
+        lax.fori_loop(0, steps, one_k, 0)
+        dq_ref[pl.ds(q0, TQ), :] = (dq_sum[...] * HEAD_DIM ** -0.5).T.astype(BF)
+        return c
+    lax.fori_loop(0, ROW // TQ, one_q, 0)
+    dk_ref[...] = (dk_sum[:ROW, :] * HEAD_DIM ** -0.5).astype(BF)
+    dv_ref[...] = dv_sum[:ROW, :].astype(BF)
+
+def attend_backward(lengths, q, k, v, g, o, lse, rank, count, with_seen):
+    rows, cols = q.shape
+    heads = cols // HEAD_DIM
+    V = pl.BlockSpec(memory_space=pltpu.VMEM)
+    like = jax.ShapeDtypeStruct((rows, cols), BF)
+    return pl.pallas_call(
+        partial(attn_bwd_kernel, with_seen, heads),
+        out_shape=(like, like, like),
+        in_specs=[pl.BlockSpec(memory_space=pltpu.SMEM)] + [V] * 8,
+        out_specs=(V, V, V),
+        scratch_shapes=[
+            pltpu.VMEM((heads, ROW + TK, 256), BF),
+            pltpu.VMEM((heads, ROW + TK, 256), BF),
+            pltpu.VMEM((cols, ROW + TK), BF),
+            pltpu.VMEM((ROW + TK, 128), F32),
+            pltpu.VMEM((ROW + TK, cols), F32),
+            pltpu.VMEM((ROW + TK, cols), F32),
+            pltpu.VMEM((cols, TQ), F32),
+            pltpu.VMEM((heads * TQ, cols), BF),
+            pltpu.VMEM((heads * TQ, cols), BF),
+            pltpu.VMEM((heads // 2, 256, TQ), BF),
+            pltpu.VMEM((heads // 2, 256, TQ), BF),
+        ],
+        compiler_params=pltpu.CompilerParams(vmem_limit_bytes=56 * 2**20),
+        name="attend_self_backward" if with_seen else "attend_cross_backward",
+    )(lengths, q, k, v, g, o, lse, rank, count)
 
 
 def adamw_step(gradient, first, second, weight, rate, decay):
@@ -222,8 +394,7 @@
     )
     matrices = unpack(gathered, places, features, head_shards)
     norm_params = norm_all.astype(jnp.float32).reshape(8, features)
-    doc_ids, first_pos = row_layout(lengths)
-    layout = (doc_ids, first_pos, obs_rank, obs_count)
+    rank_row, count_row = obs_rank.reshape(1, ROW), obs_count.reshape(1, ROW)
     stream_q = query_stream.astype(jnp.float32)
     stream_kv = kv_stream.astype(jnp.float32)
     normed_q = layer_norm(stream_q, norm_params[0], norm_params[1]).astype(jnp.bfloat16)
@@ -231,7 +402,7 @@
     queries_self = product(normed_q, matrices[0]).astype(jnp.bfloat16)
     keys_self = product(normed_kv, matrices[1]).astype(jnp.bfloat16)
     values_self = product(normed_kv, matrices[2]).astype(jnp.bfloat16)
-    mixed_self, totals_self = attend_forward(queries_self, keys_self, values_self, layout, True)
+    mixed_self, totals_self = attend_forward(lengths, queries_self, keys_self, values_self, rank_row, count_row, True)
     self_sum = lax.psum(product(mixed_self, matrices[6]).astype(jnp.bfloat16), "head").astype(
         jnp.float32
     )
@@ -241,7 +412,7 @@
     keys_cross = product(memory, matrices[4]).astype(jnp.bfloat16)
     values_cross = product(memory, matrices[5]).astype(jnp.bfloat16)
     mixed_cross, totals_cross = attend_forward(
-        queries_cross, keys_cross, values_cross, layout, False
+        lengths, queries_cross, keys_cross, values_cross, rank_row, count_row, False
     )
     cross_sum = lax.psum(product(mixed_cross, matrices[7]).astype(jnp.bfloat16), "head").astype(
         jnp.float32
@@ -270,7 +441,7 @@
     grad_wo_cross = inner_rows(mixed_cross, cross_low)
     grad_mixed_cross = product_back(cross_low, matrices[7]).astype(jnp.bfloat16)
     grad_q_cross, grad_k_cross, grad_v_cross = attend_backward(
-        queries_cross, keys_cross, values_cross, grad_mixed_cross, totals_cross, layout, False
+        lengths, queries_cross, keys_cross, values_cross, grad_mixed_cross, mixed_cross, totals_cross, rank_row, count_row, False
     )
     grad_wq_cross = inner_rows(normed_c, grad_q_cross)
     grad_wk_cross = inner_rows(memory, grad_k_cross)
@@ -294,7 +465,7 @@
     grad_wo_self = inner_rows(mixed_self, self_low)
     grad_mixed_self = product_back(self_low, matrices[6]).astype(jnp.bfloat16)
     grad_q_self, grad_k_self, grad_v_self = attend_backward(
-        queries_self, keys_self, values_self, grad_mixed_self, totals_self, layout, True
+        lengths, queries_self, keys_self, values_self, grad_mixed_self, mixed_self, totals_self, rank_row, count_row, True
     )
     grad_wq_self = inner_rows(normed_q, grad_q_self)
     grad_wk_self = inner_rows(normed_kv, grad_k_self)

time: 1890 us -> 939 us (0.50)
  matrix products: 930 us -> 105 us
  Pallas kernels: 0 us -> 128 us
  local copies, waits for them, and re-layouts: 225 us -> 106 us
  other arithmetic: 188 us -> 69.6 us
  loops' own time: 27.9 us -> 0 us
    dot_general x56 -> x0, matrix products: 820 us -> none  [the longest x8 263 us: one_block(): jnp.einsum('hqk,qhe->khe', grad_scores, query_heads, preferred_element_ty...]
    pallas_call x0 -> x4, Pallas kernels: none -> 128 us  [the longest x2 77.2 us: attend_backward(): pl.pallas_call(partial(attn_bwd_kernel, with_seen, heads), out_shape=(lik...]
    dynamic_slice x80 -> x0, local copies, waits for them, and re-layouts: 63.1 us -> none  [the longest x16 27.7 us: one_block(): lax.dynamic_slice_in_dim(grad_mixed, query_at, block_rows)]
    add x16 -> x0, other arithmetic: 51 us -> none  [the longest x8 50.9 us: one_block(): value_grad = value_grad + value_part]
    reduce_sum x10 -> x0, other arithmetic: 34.9 us -> none  [the longest x8 34.6 us: one_block(): summed = jnp.sum(exponent, -1, keepdims=True)]
    dynamic_update_slice x32 -> x0, local copies, waits for them, and re-layouts: 28.9 us -> none  [attend_forward(): lax.map(one_block, jnp.arange(tokens // block_rows, dtype=jnp.int32))]
    another operation x4 -> x0, loops' own time: 27.9 us -> none  [the longest x2 22.2 us: attend_backward(): lax.scan(one_block, (zero_rows, zero_rows), jnp.arange(tokens // block_ro...]
  transfers between devices with their start and end apart: 7 -> 7, of which waited for: 6 -> 6; matrix products, arithmetic and copies ran while one was open for 9% -> 16% of each run, Pallas kernels for 0% -> 0%
where the time goes in v1:
time: 939 us; the launch traced here: 925 us
  waiting for transfers between devices  375 us (40%)
  Pallas kernels  128 us (14%)
  blocking collectives  124 us (13%)
  local copies, waits for them, and re-layouts  106 us (11%)
  matrix products  105 us (11%)
  other arithmetic  69.6 us (7%)
  between operations  16.3 us (2%)
    reduce_scatter x1, waiting for transfers between devices, local(): lax.psum_scatter(outgoing, 'dp', scatter_dimension=0, tiled=True)  244 us
    unnamed x1, blocking collectives  81 us
    pallas_call x2, Pallas kernels, attend_backward(): pl.pallas_call(partial(attn_bwd_kernel, with_seen, heads), out_shape=(lik...  77.2 us
    all_gather x1, waiting for transfers between devices, local(): lax.all_gather(low_master, 'dp', axis=0, tiled=True)  60 us
    pallas_call x2, Pallas kernels, attend_forward(): pl.pallas_call(partial(attn_fwd_kernel, with_seen, heads), out_shape=(jax...  50.8 us
    dot_general x10, matrix products, product(): return jnp.dot(left_side, right_side, preferred_element_type=jnp.float32)  48.1 us
    all_gather x1, blocking collectives, local(): lax.all_gather(norm_master.astype(jnp.bfloat16), 'dp', axis=0, tiled=True)  42.8 us
    scatter x1, local copies, waits for them, and re-layouts, local(): outgoing = jnp.zeros((dev_count * slot_count, 1, unit_rows, features), jn...  37.3 us
  transfers between devices with their start and end apart: 7, of which 6 were waited for; matrix products, arithmetic and copies ran while one was open for 16% of the time, Pallas kernels for 0%

profile of v1, /device:TPU:0, one launch (start us, length us, event | category | flops | bytes accessed | tf_op | source)
XLA Modules:
  0.0 925.1 jit_solution(5276205879439723479)
XLA Ops:
  7.2 2.2 convert_element_type.140
  11.7 42.8 %all-gather = bf16[16,1,256]{2,1,0:T(2,128)(2,1)S(1)} all-gather(bf16[1,1,256]{2,1,0:T(2,128)(2,1)S(1)} %reshape.341), channel_id=1, replica_groups=mesh['dp'=16,'head'=2] {'dp'}, dimensions={0}, use_global_device_ids=true | all-gather | bytes 8704 | tf_op jit(solution)/shard_map/all_gather | solution.py:393
  67.2 60.0 %all-gather.3.cloned.1.call-done = bf16[512,1,16,512]{3,2,1,0:T(8,128)(2,1)} async-done(((bf16[32,1,16,512]{3,2,1,0:T(8,128)(2,1)}), bf16[512,1,16,512]{3,2,1,0:T(8,128)(2,1)}) %all-gather.3.cloned.1.call-update) | async-done | bytes 8388624 | tf_op jit(solution)/shard_map/all_gather | solution.py:392
  127.2 6.2 gather_fusion
  133.4 2.5 fusion.71
  137.8 3.4 convolution_convert_fusion.11.v_ref
  143.9 3.4 convolution_convert_fusion.13.q_ref
  147.3 26.0 %attend_self_forward.1 = (bf16[2048,256]{1,0:T(8,128)(2,1)}, f32[8,2048]{1,0:T(8,128)}) custom-call(s32[1,32]{1,0:T(1,128)} %len_ref.7, bf16[2048,256]{1,0:T(8,128)(2,1)} %convolution_convert_fusion.13.q_ref, bf16[2048,256]{1,0:T(8,128)(2,1)} %convolution_convert_fusion.12.k_ref, bf16[2048,256]{1,0:T(8,128)(2,1)} %convolution_convert_fusion.11.v_ref, ...), custom_call_target="tpu_custom_call" | custom-call | tf_op jit(solution)/shard_map/attend_self_forward/pallas_call | solution.py:223
  173.3 3.2 convolution_convert_fusion.5
  181.3 15.5 %all-reduce.8.cloned.1.call-done = bf16[2048,512]{1,0:T(8,128)(2,1)} async-done(((bf16[2048,512]{1,0:T(8,128)(2,1)}), bf16[2048,512]{1,0:T(8,128)(2,1)}) %all-reduce.8.cloned.1.call-update) | async-done | bytes 2097168 | tf_op jit(solution)/shard_map/psum | solution.py:406
  196.8 3.0 fusion.44
  205.5 24.8 %attend_cross_forward.1 = (bf16[2048,256]{1,0:T(8,128)(2,1)}, f32[8,2048]{1,0:T(8,128)}) custom-call(s32[1,32]{1,0:T(1,128)} %len_ref.7, bf16[2048,256]{1,0:T(8,128)(2,1)} %convolution_convert_fusion.10.q_ref, bf16[2048,256]{1,0:T(8,128)(2,1)} %fusion.48.k_ref, bf16[2048,256]{1,0:T(8,128)(2,1)} %fusion.49.v_ref, s32[1,2048]{1,0:T(1,128)} %bitcast.140, ...), custom_call_target="tpu_custom_call" | custom-call | tf_op jit(solution)/shard_map/attend_cross_forward/pallas_call | solution.py:223
  230.3 3.2 convolution_convert_fusion.4
  233.9 2.7 fusion.70
  237.7 19.0 %all-reduce.10.cloned.1.call-done = bf16[2048,512]{1,0:T(8,128)(2,1)} async-done(((bf16[2048,512]{1,0:T(8,128)(2,1)}), bf16[2048,512]{1,0:T(8,128)(2,1)}) %all-reduce.10.cloned.1.call-update) | async-done | bytes 2097168 | tf_op jit(solution)/shard_map/psum | solution.py:417
  256.7 3.7 fusion.69
  262.4 22.1 %multiply_convert_fusion = (bf16[2048,1024]{1,0:T(8,128)(2,1)}, f32[2048,1024]{1,0:T(8,128)S(1)}, f32[2048,1024]{1,0:T(8,128)}) fusion(bf16[512,1024]{1,0:T(8,128)(2,1)S(1)} %copy-done.55, f32[2048,512]{1,0:T(8,128)S(1)} %get-tuple-element.62, f32[512]{0:T(512)S(1)} %bitcast.177, f32[512]{0:T(512)S(1)} %bitcast.161, f32[2048]{0:T(1024)S(1)} %fusion.60, ...), kind=kOutput, calls=%fused_computation.13 | convolution fusion | flops 2289041408 | bytes 26234880 | tf_op jit(solution)/shard_map/dot_general | solution.py:39
  284.6 7.2 fusion.6
  293.7 3.7 convolution_convert_fusion.2
  297.9 22.0 %all-reduce.12.cloned.1.call-done = bf16[2048,512]{1,0:T(8,128)(2,1)} async-done(((bf16[2048,512]{1,0:T(8,128)(2,1)}), bf16[2048,512]{1,0:T(8,128)(2,1)}) %all-reduce.12.cloned.1.call-update) | async-done | bytes 2097168 | tf_op jit(solution)/shard_map/psum | solution.py:433
  320.0 4.6 fusion.39
  330.2 37.7 %attend_cross_backward.1 = (bf16[2048,256]{1,0:T(8,128)(2,1)}, bf16[2048,256]{1,0:T(8,128)(2,1)}, bf16[2048,256]{1,0:T(8,128)(2,1)}) custom-call(s32[1,32]{1,0:T(1,128)} %len_ref.7, bf16[2048,256]{1,0:T(8,128)(2,1)} %convolution_convert_fusion.10.q_ref, bf16[2048,256]{1,0:T(8,128)(2,1)} %fusion.48.k_ref, bf16[2048,256]{1,0:T(8,128)(2,1)} %fusion.49.v_ref, ...), custom_call_target="tpu_custom_call" | custom-call | tf_op jit(solution)/shard_map/attend_cross_backward/pallas_call | solution.py:334
  367.9 3.3 convolution_convert_fusion.1
  371.3 6.0 convolution_convert_fusion.3
  380.6 14.0 %all-reduce.14.cloned.1.call-done = bf16[2048,512]{1,0:T(8,128)(2,1)} async-done(((bf16[2048,512]{1,0:T(8,128)(2,1)}), bf16[2048,512]{1,0:T(8,128)(2,1)}) %all-reduce.14.cloned.1.call-update) | async-done | bytes 2097168 | tf_op jit(solution)/shard_map/psum | solution.py:450
  394.6 4.6 convert_reduce_fusion.2
  399.4 2.5 fusion.40
  402.1 2.5 add_add_fusion.4
  408.2 39.5 %attend_self_backward.1 = (bf16[2048,256]{1,0:T(8,128)(2,1)}, bf16[2048,256]{1,0:T(8,128)(2,1)}, bf16[2048,256]{1,0:T(8,128)(2,1)}) custom-call(s32[1,32]{1,0:T(1,128)} %len_ref.7, bf16[2048,256]{1,0:T(8,128)(2,1)} %convolution_convert_fusion.13.q_ref, bf16[2048,256]{1,0:T(8,128)(2,1)} %convolution_convert_fusion.12.k_ref, ...), custom_call_target="tpu_custom_call" | custom-call | tf_op jit(solution)/shard_map/attend_self_backward/pallas_call | solution.py:334
  454.1 7.3 fusion.64
  461.4 3.8 reshape.287
  465.2 3.6 fusion.78
  474.1 2.7 convolution_bitcast_fusion
  481.0 3.8 fusion.75
  486.9 3.3 fusion.76
  492.3 3.7 fusion.77
  508.0 2.4 convolution_dynamic-update-slice_fusion
  510.4 3.2 copy-done.27
  513.6 7.9 broadcast.318
  521.5 37.3 %scatter_fusion = f32[512,16,512]{2,1,0:T(8,128)} fusion(f32[512,16,512]{2,1,0:T(8,128)} %broadcast.318, s32[256]{0:T(256)S(1)} %copy-done.82, f32[256,16,512]{2,1,0:T(8,128)} %bitcast.131), kind=kCustom, calls=%fused_computation.1 | custom fusion | bytes 25166848 | tf_op jit(solution)/shard_map/scatter | solution.py:513
  561.4 6.1 convert_reduce_fusion
  567.7 2.4 fusion.42
  570.1 2.4 fusion.41
  572.6 81.0 %all-reduce = f32[4096]{0:T(1024)S(1)} all-reduce(f32[4096]{0:T(1024)S(1)} %bitcast.148), channel_id=3, replica_groups=mesh['dp'=16,'head'=2] {'dp'}, use_global_device_ids=true, to_apply=%region_38.39.clone | all-reduce | flops 4096 | bytes 32768
  654.3 4.3 add_convert_fusion.1
  662.8 3.0 add_convert_fusion.3
  665.8 244.0 %reduce-scatter.2.cloned.1.call-done = f32[32,1,16,512]{3,2,1,0:T(8,128)} async-done(((f32[512,1,16,512]{3,2,1,0:T(8,128)}), f32[32,1,16,512]{3,2,1,0:T(8,128)}) %reduce-scatter.2.cloned.1.call-update) | async-done | bytes 1048592 | tf_op jit(solution)/shard_map/reduce_scatter | solution.py:516
  909.8 3.9 subtract_select_fusion.1
  (272 shorter events, 91.2 us)
Async XLA Ops:
  7.2 170.8 %copy-start = (bf16[2048,512]{1,0:T(8,128)(2,1)S(1)}, bf16[2048,512]{1,0:T(8,128)(2,1)}, u32[]{:S(2)}) copy-start(bf16[2048,512]{1,0:T(8,128)(2,1)} %param.16) | copy-start | bytes 6291460
  7.2 120.0 %all-gather.3.cloned.1.call-start = ((), (), s32[]{:S(2)}) async-start(), calls=%async_computation.1 | async-start | bytes 8912896 | tf_op jit(solution)/shard_map/all_gather | solution.py:392
  9.5 187.3 %all-reduce.8.cloned.1.call-start = ((), (), s32[]{:S(2)}) async-start(), calls=%async_computation.2 | async-start | bytes 4194304 | tf_op jit(solution)/shard_map/psum | solution.py:406
  11.7 48.8 %copy-start.11 = (bf16[2048,512]{1,0:T(8,128)(2,1)S(1)}, bf16[2048,512]{1,0:T(8,128)(2,1)}, u32[]{:S(2)}) copy-start(bf16[2048,512]{1,0:T(8,128)(2,1)} %param.15) | copy-start | bytes 6291460
  11.7 50.5 %copy-start.1 = (bf16[2048,512]{1,0:T(8,128)(2,1)S(1)}, bf16[2048,512]{1,0:T(8,128)(2,1)}, u32[]{:S(2)}) copy-start(bf16[2048,512]{1,0:T(8,128)(2,1)} %param.14) | copy-start | bytes 6291460
  60.5 4.7 copy-start.65
  135.9 37.4 %copy-start.45 = (bf16[16,16,512]{2,1,0:T(8,128)(2,1)}, bf16[16,16,512]{2,1,0:T(8,128)(2,1)S(1)}, u32[]{:S(2)}) copy-start(bf16[16,16,512]{2,1,0:T(8,128)(2,1)S(1)} %get-tuple-element.69) | copy-start | bytes 786436
  137.8 5.1 copy-start.50
  147.3 29.6 %copy-start.54 = (bf16[16,16,512]{2,1,0:T(8,128)(2,1)S(1)}, bf16[16,16,512]{2,1,0:T(8,128)(2,1)}, u32[]{:S(2)}) copy-start(bf16[16,16,512]{2,1,0:T(8,128)(2,1)} %get-tuple-element.68) | copy-start | bytes 786436
  176.6 80.1 %all-reduce.10.cloned.1.call-start = ((), (), s32[]{:S(2)}) async-start(), calls=%async_computation.3 | async-start | bytes 4194304 | tf_op jit(solution)/shard_map/psum | solution.py:417
  233.6 86.4 %all-reduce.12.cloned.1.call-start = ((), (), s32[]{:S(2)}) async-start(), calls=%async_computation.4 | async-start | bytes 4194304 | tf_op jit(solution)/shard_map/psum | solution.py:433
  260.4 24.1 %copy-start.6 = (f32[2048,512]{1,0:T(8,128)}, f32[2048,512]{1,0:T(8,128)S(1)}, u32[]{:S(2)}) copy-start(f32[2048,512]{1,0:T(8,128)S(1)} %get-tuple-element.62) | copy-start | bytes 12582916
  262.4 22.1 %copy-start.22 = (bf16[2048,512]{1,0:T(8,128)(2,1)S(1)}, bf16[2048,512]{1,0:T(8,128)(2,1)}, u32[]{:S(2)}) copy-start(bf16[2048,512]{1,0:T(8,128)(2,1)} %param.17) | copy-start | bytes 6291460
  262.4 22.1 %copy-start.56 = (bf16[64,16,512]{2,1,0:T(8,128)(2,1)S(1)}, bf16[64,16,512]{2,1,0:T(8,128)(2,1)}, u32[]{:S(2)}) copy-start(bf16[64,16,512]{2,1,0:T(8,128)(2,1)} %get-tuple-element.63) | copy-start | bytes 3145732
  297.4 97.2 %all-reduce.14.cloned.1.call-start = ((), (), s32[]{:S(2)}) async-start(), calls=%async_computation.5 | async-start | bytes 4194304 | tf_op jit(solution)/shard_map/psum | solution.py:450
  320.0 4.6 copy-start.7
  320.0 4.7 copy-start.33
  328.5 39.4 %copy-start.60 = (bf16[512,256]{1,0:T(8,128)(2,1)S(1)}, bf16[512,256]{1,0:T(8,128)(2,1)}, u32[]{:S(2)}) copy-start(bf16[512,256]{1,0:T(8,128)(2,1)} %reshape.277) | copy-start | bytes 786436
  371.2 190.1 %all-reduce.16.cloned.1.call-start = ((), (), s32[]{:S(2)}) async-start(), calls=%async_computation.7 | async-start | bytes 16777216 | tf_op jit(solution)/shard_map/psum | solution.py:424
  371.3 6.0 copy-start.44
  371.3 6.0 copy-start.53
  394.6 4.6 copy-start.3
  394.6 4.6 copy-start.10
  394.6 4.7 copy-start.26
  402.1 4.4 copy-start.46
  406.5 41.2 %copy-start.51 = (bf16[512,256]{1,0:T(8,128)(2,1)S(1)}, bf16[512,256]{1,0:T(8,128)(2,1)}, u32[]{:S(2)}) copy-start(bf16[512,256]{1,0:T(8,128)(2,1)} %copy-done.50) | copy-start | bytes 786436
  447.8 4.2 copy-start.43
  447.8 4.2 copy-start.62
  454.1 455.7 %reduce-scatter.2.cloned.1.call-start = ((), (), s32[]{:S(2)}) async-start(), calls=%async_computation.6 | async-start | bytes 17825792 | tf_op jit(solution)/shard_map/reduce_scatter | solution.py:516
  476.9 10.1 %copy-start.34 = (bf16[2048,256]{1,0:T(8,128)(2,1)S(1)}, bf16[2048,256]{1,0:T(8,128)(2,1)}, u32[]{:S(2)}) copy-start(bf16[2048,256]{1,0:T(8,128)(2,1)} %get-tuple-element.28) | copy-start | bytes 3145732
  496.0 8.2 copy-start.28
  498.0 6.1 copy-start.48
  498.0 6.1 copy-start.14
  513.6 7.9 copy-start.82
  561.4 6.2 copy-start.74
  561.4 6.2 copy-start.76
  561.4 6.2 copy-start.12
  561.4 6.2 copy-start.21
  561.4 6.2 copy-start.70
  567.7 85.9 %copy-start.83 = (f32[256]{0:T(256)S(1)}, f32[256]{0:T(256)}, u32[]{:S(2)}) copy-start(f32[256]{0:T(256)} %param.25) | copy-start | bytes 3076
  567.7 85.9 %copy-start.84 = (f32[256]{0:T(256)S(1)}, f32[256]{0:T(256)}, u32[]{:S(2)}) copy-start(f32[256]{0:T(256)} %param.27) | copy-start | bytes 3076
  567.7 85.9 %copy-start.85 = (f32[256]{0:T(256)S(1)}, f32[256]{0:T(256)}, u32[]{:S(2)}) copy-start(f32[256]{0:T(256)} %param.26) | copy-start | bytes 3076
  653.6 5.0 copy-start.8
  653.6 5.0 copy-start.49
  658.6 4.2 copy-start.20
  662.8 247.0 %copy-start.35 = (f32[32,1,16,512]{3,2,1,0:T(8,128)S(1)}, f32[32,1,16,512]{3,2,1,0:T(8,128)}, u32[]{:S(2)}) copy-start(f32[32,1,16,512]{3,2,1,0:T(8,128)} %param.22) | copy-start | bytes 3145732
  909.8 4.0 copy-start.40
  913.8 4.0 copy-start.41
  (47 other events, 115.1 us)
Sparse Core Ops, SparseCore 0:
  11.4 115.7 all-gather.2
  176.7 20.0 all-reduce.7
  233.7 22.9 all-reduce.9
  297.5 22.3 all-reduce.11
  371.3 23.2 all-reduce.13
  454.2 41.2 all-reduce.15
  558.9 350.8 reduce-scatter.1

commit v2 on v1

--- a/solution.py
+++ b/solution.py
@@ -11,7 +11,7 @@
 ROW = 2048
 DOCS = 32
 STEP = 10
-
+UNIT = 16
 
 EPS_NORM = 1e-05
 ADAM_EPS = 1e-08
@@ -20,61 +20,12 @@
 RATE_MATRIX = 0.1
 RATE_NORM = 0.3
 WEIGHT_DECAY = 0.01
-MASKED_SCORE = -1000000000.0
-
-
-def layer_norm(vector, norm_gain, norm_shift):
-    row_mean = jnp.mean(vector, -1, keepdims=True)
-    centred = vector - row_mean
-    row_var = jnp.mean(centred * centred, -1, keepdims=True)
-    return centred * lax.rsqrt(row_var + EPS_NORM) * norm_gain + norm_shift
-
-
-def norm_pullback(vector, norm_gain, norm_shift, cotangent):
-    unused_value, pullback = jax.vjp(layer_norm, vector, norm_gain, norm_shift)
-    return pullback(cotangent)
-
-
-def product(left_side, right_side):
-    return jnp.dot(left_side, right_side, preferred_element_type=jnp.float32)
-
-
-def inner_rows(left_side, right_side):
-    return jnp.einsum("tk,tn->kn", left_side, right_side, preferred_element_type=jnp.float32)
-
-
-def product_back(left_side, right_side):
-    return jnp.einsum("tn,kn->tk", left_side, right_side, preferred_element_type=jnp.float32)
-
-
-def slot_places(unit_owner, dev_count, slot_count):
-    onehot_table = (unit_owner[:, None] == jnp.arange(dev_count, dtype=jnp.int32)[None, :]).astype(
-        jnp.int32
-    )
-    before = jnp.cumsum(onehot_table, 0) - onehot_table
-    return unit_owner * slot_count + jnp.sum(before * onehot_table, 1)
-
-
-def unpack(gathered, places, features, head_shards):
-    flat_rows = gathered[places].reshape(-1, features)
-    head_cols = features // head_shards
-    ffn_cols = (flat_rows.shape[0] - 8 * head_cols) // 2
-    pieces = [
-        flat_rows[number * head_cols : (number + 1) * head_cols].reshape(features, head_cols)
-        for number in range(6)
-    ]
-    pieces.append(flat_rows[6 * head_cols : 7 * head_cols])
-    pieces.append(flat_rows[7 * head_cols : 8 * head_cols])
-    pieces.append(flat_rows[8 * head_cols : 8 * head_cols + ffn_cols].reshape(features, ffn_cols))
-    pieces.append(flat_rows[8 * head_cols + ffn_cols :])
-    return pieces
-
-
+
+F32 = jnp.float32
+BF = jnp.bfloat16
 TQ = 256
 TK = 256
 FAR = 32768.0
-F32 = jnp.float32
-BF = jnp.bfloat16
 
 def nt(a, b):
     return lax.dot_general(a, b, (((1,), (1,)), ((), ())), preferred_element_type=F32)
@@ -354,6 +305,553 @@
     )(lengths, q, k, v, g, o, lse, rank, count)
 
 
+def send(src, dst, send_sem, recv_sem, **where):
+    copy = pltpu.make_async_remote_copy(src_ref=src, dst_ref=dst, send_sem=send_sem, recv_sem=recv_sem,
+                                        device_id=where, device_id_type=pl.DeviceIdType.MESH)
+    copy.start()
+    return copy
+
+def greet(peers):
+    barrier = pltpu.get_barrier_semaphore()
+    for where in peers:
+        pl.semaphore_signal(barrier, inc=1, device_id=where, device_id_type=pl.DeviceIdType.MESH)
+    pl.semaphore_wait(barrier, len(peers))
+
+def places_of(count):
+    me = lax.axis_index("dp")
+    across = count // 4
+    x, y, z = lax.rem(me, 2), lax.rem(lax.div(me, 2), 2), lax.div(me, 4)
+    xpeer, ypeer = me + 1 - 2 * x, me + 2 - 4 * y
+    order = sorted(range(1, across), key=lambda d: min(d, across - d))
+    ahead = lambda d: lax.rem(z + d, across) * 4 + y * 2 + x
+    behind = lambda d: lax.rem(z + across - d, across) * 4 + y * 2 + x
+    return me, x, y, z, xpeer, ypeer, order, ahead, behind
+
+def spread_blocks(count, out, rows, places, zs, xs, ys, gx, gy):
+    me, x, y, z, xpeer, ypeer, order, ahead, behind = places
+    half = rows // 32 * 16
+    whole = pl.ds(0, rows)
+    sent, recv = [], {}
+    def go(src_block, at, sem, d, to):
+        copy = send(out.at[src_block, at], out.at[src_block, at], sem.at[0, d], sem.at[1, d], dp=to)
+        sent.append(copy)
+        return copy
+    near = go(me, whole, xs, 0, xpeer), go(me, whole, ys, 0, ypeer)
+    recv[0] = near
+    zcopies = {}
+    for d in order:
+        zcopies[d] = go(me, whole, zs, d, ahead(d))
+    steps = [0] + order
+    diag = []
+    for k, d in enumerate(steps):
+        if d:
+            zcopies[d].wait_recv()
+            recv[d] = go(behind(d), whole, xs, d, xpeer), go(behind(d), whole, ys, d, ypeer)
+        if k:
+            forward(go, diag, recv, steps[k - 1], behind, places, half, rows, gx, gy)
+    forward(go, diag, recv, steps[-1], behind, places, half, rows, gx, gy)
+    for copy in diag:
+        copy.wait_recv()
+    for copy in sent:
+        copy.wait_send()
+
+def forward(go, diag, recv, d, behind, places, half, rows, gx, gy):
+    me, x, y, z, xpeer, ypeer, order, ahead, _ = places
+    base = behind(d) if d else me
+    recv[d][0].wait_recv()
+    diag.append(go(base + 1 - 2 * x, pl.ds(0, half), gy, d, ypeer))
+    recv[d][1].wait_recv()
+    diag.append(go(base + 2 - 4 * y, pl.ds(half, rows - half), gx, d, xpeer))
+
+def gather_kernel(count, in_ref, out_ref, local_sem, zs, xs, ys, gx, gy):
+    places = places_of(count)
+    me, x, y, z, xpeer, ypeer, order, ahead, behind = places
+    rows = in_ref.shape[0]
+    own = pltpu.make_async_copy(in_ref, out_ref.at[me], local_sem)
+    own.start()
+    greet([{"dp": xpeer}, {"dp": ypeer}] + [{"dp": ahead(d)} for d in order])
+    own.wait()
+    spread_blocks(count, out_ref, rows, places, zs, xs, ys, gx, gy)
+
+def gather_blocks(block, count, number=0):
+    rows, cols = block.shape
+    across = count // 4
+    sems = pltpu.SemaphoreType.DMA((2, across))
+    return pl.pallas_call(
+        partial(gather_kernel, count),
+        out_shape=jax.ShapeDtypeStruct((count, rows, cols), block.dtype),
+        in_specs=[pl.BlockSpec(memory_space=pltpu.VMEM)],
+        out_specs=pl.BlockSpec(memory_space=pltpu.VMEM),
+        scratch_shapes=[pltpu.SemaphoreType.DMA] + [sems] * 5,
+        compiler_params=pltpu.CompilerParams(collective_id=number, has_side_effects=True, vmem_limit_bytes=56 * 2**20),
+        name="gather_units",
+    )(block)
+
+def reduce_kernel(count, in_ref, out_ref, keep, r1, r2, r3, s1, s2, s3, zs, xs, ys, gx, gy):
+    places = places_of(count)
+    me, x, y, z, xpeer, ypeer, order, ahead, behind = places
+    across = count // 4
+    rows = in_ref.shape[1]
+    half = rows // 2
+    greet([{"dp": xpeer}, {"dp": ypeer}] + [{"dp": ahead(d)} for d in order])
+    steps = order + [0]
+    base = lambda d: lax.rem(z + d, across) * 4
+    part_rows = [pl.ds(0, half), pl.ds(half, half)]
+    def at(d, first, second, part):
+        return base(d) + (first + 2 * second if part == 0 else 2 * first + second)
+    mine = [(x, y), (y, x)]
+    peers = [(xpeer, ypeer), (ypeer, xpeer)]
+    first_copies = {}
+    for d in steps:
+        for part in (0, 1):
+            f, s = mine[part]
+            for t in (0, 1):
+                second = s if t else 1 - s
+                first_copies[d, part, t] = send(in_ref.at[at(d, 1 - f, second, part), part_rows[part]], r1.at[part, d, t],
+                                                s1.at[0, part, d, t], s1.at[1, part, d, t], dp=peers[part][0])
+    second_copies, third_copies = {}, {}
+    def second_stage(d):
+        for part in (0, 1):
+            f, s = mine[part]
+            for t in (0, 1):
+                second = s if t else 1 - s
+                first_copies[d, part, t].wait_recv()
+                total = (in_ref[at(d, f, second, part), part_rows[part], :].astype(F32) + r1[part, d, t].astype(F32)).astype(BF)
+                keep[part, d, t] = total
+                if t == 0:
+                    second_copies[d, part] = send(keep.at[part, d, 0], r2.at[part, d], s2.at[0, part, d], s2.at[1, part, d],
+                                                  dp=peers[part][1])
+    def third_stage(d):
+        for part in (0, 1):
+            second_copies[d, part].wait_recv()
+            total = (keep[part, d, 1].astype(F32) + r2[part, d].astype(F32)).astype(BF)
+            keep[part, d, 1] = total
+            if d:
+                third_copies[d, part] = send(keep.at[part, d, 1], r3.at[part, d], s3.at[0, part, d], s3.at[1, part, d], dp=ahead(d))
+    for k, d in enumerate(steps):
+        second_stage(d)
+        if k:
+            third_stage(steps[k - 1])
+    third_stage(0)
+    for part in (0, 1):
+        total = keep[part, 0, 1].astype(F32)
+        for d in order:
+            third_copies[d, part].wait_recv()
+            total = total + r3[part, d].astype(F32)
+        out_ref[me, part_rows[part], :] = total.astype(BF)
+    spread_blocks(count, out_ref, rows, places, zs, xs, ys, gx, gy)
+    for copies in (first_copies, second_copies, third_copies):
+        for copy in copies.values():
+            copy.wait_send()
+
+def reduce_blocks(flat, count, number=1):
+    total_rows, cols = flat.shape
+    rows = total_rows // count
+    half = rows // 2
+    across = count // 4
+    sems = pltpu.SemaphoreType.DMA((2, across))
+    D = pltpu.SemaphoreType.DMA
+    return pl.pallas_call(
+        partial(reduce_kernel, count),
+        out_shape=jax.ShapeDtypeStruct((count, rows, cols), BF),
+        in_specs=[pl.BlockSpec(memory_space=pltpu.VMEM)],
+        out_specs=pl.BlockSpec(memory_space=pltpu.VMEM),
+        scratch_shapes=[
+            pltpu.VMEM((2, across, 2, half, cols), BF),
+            pltpu.VMEM((2, across, 2, half, cols), BF),
+            pltpu.VMEM((2, across, half, cols), BF),
+            pltpu.VMEM((2, across, half, cols), BF),
+            D((2, 2, across, 2)), D((2, 2, across)), D((2, 2, across)),
+        ] + [sems] * 5,
+        compiler_params=pltpu.CompilerParams(collective_id=number, has_side_effects=True, vmem_limit_bytes=56 * 2**20),
+        name="reduce_gradients",
+    )(flat.reshape(count, rows, cols)).reshape(total_rows, cols)
+
+
+CHUNK = 256
+
+
+def tn(a, b):
+    return lax.dot_general(a, b, (((0,), (0,)), ((), ())), preferred_element_type=F32)
+
+
+def normalise(value):
+    centred = value - jnp.mean(value, -1, keepdims=True)
+    scale = lax.rsqrt(jnp.mean(centred * centred, -1, keepdims=True) + EPS_NORM)
+    return centred * scale, scale
+
+
+def norm_back(unit, scale, gain, grad):
+    inner = grad * gain
+    return scale * (inner - jnp.mean(inner, -1, keepdims=True) - unit * jnp.mean(inner * unit, -1, keepdims=True))
+
+
+def fold_rows(value):
+    return jnp.sum(value.reshape(value.shape[0] // 8, 8, value.shape[1]), 0)
+
+
+def interleave(size):
+    row = lax.broadcasted_iota(jnp.int32, (size, size), 0)
+    col = lax.broadcasted_iota(jnp.int32, (size, size), 1)
+    source = jnp.where((row & 1) == 0, row >> 1, (row >> 1) + size // 2)
+    return jnp.where(col == source, 1.0, 0.0).astype(BF)
+
+
+def part_rows(matrix, order):
+    return lax.dot_general(order, matrix, (((0,), (0,)), ((), ())), preferred_element_type=F32).astype(BF)
+
+
+def as_units(gradient, order):
+    parted = part_rows(gradient.astype(BF), order)
+    half = parted.shape[0] // 2
+    return jnp.concatenate([parted[:half], parted[half:]], 1)
+
+
+def other_core(mine, theirs, sems, step):
+    rows = pl.ds(step * CHUNK, CHUNK)
+    return pltpu.make_async_remote_copy(
+        src_ref=mine.at[rows], dst_ref=theirs.at[rows], send_sem=sems.at[0, step], recv_sem=sems.at[1, step],
+        device_id={"head": 1 - lax.axis_index("head")}, device_id_type=pl.DeviceIdType.MESH)
+
+
+def greet_core():
+    greet([{"head": 1 - lax.axis_index("head")}])
+
+
+def chunks(total, body):
+    def one(step, carry):
+        body(step, pl.ds(pl.multiple_of(step * CHUNK, CHUNK), CHUNK))
+        return carry
+    lax.fori_loop(0, total // CHUNK, one, 0)
+
+
+def drain(total, mine, theirs, sems):
+    def body(step, rows):
+        other_core(mine, theirs, sems, step).wait_send()
+    chunks(total, body)
+
+
+def project_kernel(owner_ref, gathered, norms, query_ref, kv_ref, memory_ref,
+                   nq_ref, nkv_ref, q_ref, k_ref, v_ref, kc_ref, vc_ref, ws_ref, wc_ref, wos_ref, woc_ref, w1_ref, w2_ref,
+                   flat, used):
+    tokens, features = query_ref.shape
+    devices = gathered.shape[0]
+    units = owner_ref.shape[0]
+    for d in range(devices):
+        used[d] = 0
+
+    def one_unit(u, carry):
+        owner = owner_ref[u]
+        slot = used[owner]
+        used[owner] = slot + 1
+        flat[pl.ds(pl.multiple_of(u * UNIT, UNIT), UNIT), :] = gathered[owner, pl.ds(pl.multiple_of(slot * UNIT, UNIT), UNIT), :]
+        return carry
+    lax.fori_loop(0, units, one_unit, 0, unroll=4)
+    order = interleave(features)
+    cols = q_ref.shape[1]
+    for number in range(6):
+        rows = flat[number * cols:(number + 1) * cols, :]
+        stacked = jnp.concatenate([rows[:, :cols], rows[:, cols:]], 0)
+        matrix = nn(order, stacked).astype(BF)
+        if number < 3:
+            ws_ref[number] = matrix
+        else:
+            wc_ref[number - 3] = matrix
+    wos_ref[...] = flat[6 * cols:7 * cols, :]
+    woc_ref[...] = flat[7 * cols:8 * cols, :]
+    hidden = w2_ref.shape[0]
+    for block in range(hidden // features):
+        at = 8 * cols + block * features
+        parted = part_rows(flat[at:at + features, :], order)
+        half = features // 2
+        w1_ref[block * half:(block + 1) * half, :] = jnp.concatenate([parted[:half], parted[half:]], 1)
+    w2_ref[...] = flat[8 * cols + hidden:, :]
+
+    def body(step, rows):
+        nq = (normalise(query_ref[rows, :].astype(F32))[0] * norms[0:1, :] + norms[1:2, :]).astype(BF)
+        nkv = (normalise(kv_ref[rows, :].astype(F32))[0] * norms[2:3, :] + norms[3:4, :]).astype(BF)
+        source = memory_ref[rows, :]
+        nq_ref[rows, :] = nq
+        nkv_ref[rows, :] = nkv
+        q_ref[rows, :] = nn(nq, ws_ref[0]).astype(BF)
+        k_ref[rows, :] = nn(nkv, ws_ref[1]).astype(BF)
+        v_ref[rows, :] = nn(nkv, ws_ref[2]).astype(BF)
+        kc_ref[rows, :] = nn(source, wc_ref[1]).astype(BF)
+        vc_ref[rows, :] = nn(source, wc_ref[2]).astype(BF)
+    chunks(tokens, body)
+
+
+def call(kernel, name, args, smem, outs, scratch, number=None):
+    V = pl.BlockSpec(memory_space=pltpu.VMEM)
+    S = pl.BlockSpec(memory_space=pltpu.SMEM)
+    extra = {} if number is None else dict(collective_id=number, has_side_effects=True)
+    return pl.pallas_call(
+        kernel,
+        out_shape=tuple(jax.ShapeDtypeStruct(shape, dtype) for shape, dtype in outs),
+        in_specs=[S] * smem + [V] * (len(args) - smem),
+        out_specs=tuple(V for _ in outs),
+        scratch_shapes=scratch,
+        compiler_params=pltpu.CompilerParams(vmem_limit_bytes=60 * 2**20, **extra),
+        name=name,
+    )(*args)
+
+
+def pair_sems(tokens):
+    return pltpu.SemaphoreType.DMA((2, tokens // CHUNK))
+
+
+def project(unit_owner, gathered, norms, query_stream, kv_stream, memory, cols, hidden):
+    tokens, features = query_stream.shape
+    wide, narrow = ((tokens, features), BF), ((tokens, cols), BF)
+    outs = [wide, wide] + [narrow] * 5 + [
+        ((3, features, cols), BF), ((3, features, cols), BF), ((cols, features), BF), ((cols, features), BF),
+        ((features, hidden), BF), ((hidden, features), BF)]
+    return call(project_kernel, "project", [unit_owner, gathered, norms, query_stream, kv_stream, memory], 1, outs,
+                [pltpu.VMEM((8 * cols + 2 * hidden, features), BF), pltpu.SMEM((gathered.shape[0],), jnp.int32)])
+
+
+def self_out_kernel(mixed, wo, query, wc, norms, res_ref, nc_ref, q_ref, mine, theirs, sems):
+    tokens = query.shape[0]
+    greet_core()
+
+    def give(step, rows):
+        mine[rows, :] = nn(mixed[rows, :], wo[...]).astype(BF)
+        other_core(mine, theirs, sems, step).start()
+    chunks(tokens, give)
+
+    def take(step, rows):
+        other_core(mine, theirs, sems, step).wait_recv()
+        res = query[rows, :].astype(F32) + (mine[rows, :].astype(F32) + theirs[rows, :].astype(F32))
+        res_ref[rows, :] = res
+        nc = (normalise(res)[0] * norms[4:5, :] + norms[5:6, :]).astype(BF)
+        nc_ref[rows, :] = nc
+        q_ref[rows, :] = nn(nc, wc[0]).astype(BF)
+    chunks(tokens, take)
+    drain(tokens, mine, theirs, sems)
+
+
+def self_out(mixed, wo, query, wc, norms):
+    tokens, features = query.shape
+    outs = [((tokens, features), F32), ((tokens, features), BF), (mixed.shape, BF)]
+    wide = pltpu.VMEM((tokens, features), BF)
+    return call(self_out_kernel, "self_out", [mixed, wo, query, wc, norms], 0, outs, [wide, wide, pair_sems(tokens)], 2)
+
+
+def gelu_parts(value):
+    size = jnp.abs(value)
+    bell = jnp.exp(-0.5 * value * value)
+    t = 1.0 / (1.0 + (0.3275911 * 0.7071067811865476) * size)
+    poly = ((((1.061405429 * t - 1.453152027) * t + 1.421413741) * t - 0.284496736) * t + 0.254829592) * t
+    tail = 0.5 * poly * bell
+    below = jnp.where(value < 0.0, tail, 1.0 - tail)
+    return value * below, below + value * (bell * 0.3989422804014327)
+
+
+def feed_forward_kernel(mixed, wo, res, w1, w2, out_grad, norms,
+                        out_ref, gres_ref, gmix_ref, gw1_ref, gw2_ref, gwo_ref, sums_ref,
+                        mine, theirs, nf_all, hid_all, pre_all, low_all, mine_o, theirs_o, mine_g, theirs_g,
+                        sems, sems_o, sems_g):
+    tokens, features = out_grad.shape
+    hidden = w2.shape[0]
+    greet_core()
+
+    def give(step, rows):
+        mine[rows, :] = nn(mixed[rows, :], wo[...]).astype(BF)
+        other_core(mine, theirs, sems, step).start()
+    chunks(tokens, give)
+
+    def middle(step, rows):
+        other_core(mine, theirs, sems, step).wait_recv()
+        value = res[rows, :] + (mine[rows, :].astype(F32) + theirs[rows, :].astype(F32))
+        gres_ref[rows, :] = value
+        nf = (normalise(value)[0] * norms[6:7, :] + norms[7:8, :]).astype(BF)
+        nf_all[rows, :] = nf
+        grad = out_grad[rows, :]
+        out_part = jnp.zeros((CHUNK, features), F32)
+        grad_part = jnp.zeros((CHUNK, features), F32)
+        for block in range(hidden // 256):
+            at = slice(block * 256, (block + 1) * 256)
+            act, slope = gelu_parts(nn(nf, w1[:, at]))
+            act = act.astype(BF)
+            hid_all[rows, at] = act
+            pre = (slope * nt(grad, w2[at, :])).astype(BF)
+            pre_all[rows, at] = pre
+            out_part = out_part + nn(act, w2[at, :])
+            grad_part = grad_part + nt(pre, w1[:, at])
+        mine_o[rows, :] = out_part.astype(BF)
+        other_core(mine_o, theirs_o, sems_o, step).start()
+        mine_g[rows, :] = grad_part.astype(BF)
+        other_core(mine_g, theirs_g, sems_g, step).start()
+    chunks(tokens, middle)
+
+    order = interleave(features)
+    half = features // 2
+    for block in range(hidden // 256):
+        at = slice(block * 256, (block + 1) * 256)
+        gw2_ref[at, :] = tn(hid_all[:, at], out_grad[...]).astype(BF)
+    for block in range(hidden // features):
+        gradient = tn(nf_all[:, block * half:(block + 1) * half], pre_all[...]).astype(BF)
+        stacked = jnp.concatenate([gradient[:, :features], gradient[:, features:]], 0)
+        gw1_ref[block * features:(block + 1) * features, :] = nn(order, stacked).astype(BF)
+    sums_ref[...] = jnp.zeros_like(sums_ref)
+
+    def close(step, rows):
+        other_core(mine_o, theirs_o, sems_o, step).wait_recv()
+        other_core(mine_g, theirs_g, sems_g, step).wait_recv()
+        value = gres_ref[rows, :]
+        out_ref[rows, :] = (value + (mine_o[rows, :].astype(F32) + theirs_o[rows, :].astype(F32))).astype(BF)
+        grad = mine_g[rows, :].astype(F32) + theirs_g[rows, :].astype(F32)
+        unit, scale = normalise(value)
+        gres = norm_back(unit, scale, norms[6:7, :], grad) + out_grad[rows, :].astype(F32)
+        gres_ref[rows, :] = gres
+        sums_ref[0:8, :] += fold_rows(grad * unit)
+        sums_ref[8:16, :] += fold_rows(grad)
+        low = gres.astype(BF)
+        low_all[rows, :] = low
+        gmix_ref[rows, :] = nt(low, wo[...]).astype(BF)
+    chunks(tokens, close)
+    gwo_ref[...] = tn(mixed[...], low_all[...]).astype(BF)
+    drain(tokens, mine, theirs, sems)
+    drain(tokens, mine_o, theirs_o, sems_o)
+    drain(tokens, mine_g, theirs_g, sems_g)
+
+
+def feed_forward(mixed, wo, res, w1, w2, out_grad, norms):
+    tokens, features = out_grad.shape
+    hidden = w2.shape[0]
+    outs = [((tokens, features), BF), ((tokens, features), F32), (mixed.shape, BF), ((hidden, features), BF),
+            ((hidden, features), BF), (wo.shape, BF), ((16, features), F32)]
+    wide = pltpu.VMEM((tokens, features), BF)
+    deep = pltpu.VMEM((tokens, hidden), BF)
+    return call(feed_forward_kernel, "feed_forward", [mixed, wo, res, w1, w2, out_grad, norms], 0, outs,
+                [wide, wide, wide, deep, deep, wide, wide, wide, wide, wide] + [pair_sems(tokens)] * 3, 3)
+
+
+def branch_back(first_in, second_in, dq, dk, dv, weights, gw_ref, mine_a, theirs_a, mine_b, theirs_b, sems_a, sems_b):
+    tokens, features = first_in.shape
+    cols = dq.shape[1]
+    greet_core()
+
+    def give(step, rows):
+        mine_a[rows, :] = nt(dq[rows, :], weights[0]).astype(BF)
+        other_core(mine_a, theirs_a, sems_a, step).start()
+        mine_b[rows, :] = (nt(dk[rows, :], weights[1]) + nt(dv[rows, :], weights[2])).astype(BF)
+        other_core(mine_b, theirs_b, sems_b, step).start()
+    chunks(tokens, give)
+    order = interleave(features)
+    for number, (entering, grad) in enumerate(((first_in, dq), (second_in, dk), (second_in, dv))):
+        gw_ref[number * cols:(number + 1) * cols, :] = as_units(tn(entering[...], grad[...]), order)
+
+
+def cross_back_kernel(dq, dk, dv, wc, nc, memory, res, gres, mixed, wo, norms,
+                      gmem_ref, gnew_ref, gmix_ref, gw_ref, gwo_ref, sums_ref,
+                      mine_a, theirs_a, mine_b, theirs_b, low_all, sems_a, sems_b):
+    tokens, features = nc.shape
+    branch_back(nc, memory, dq, dk, dv, wc, gw_ref, mine_a, theirs_a, mine_b, theirs_b, sems_a, sems_b)
+    sums_ref[...] = jnp.zeros_like(sums_ref)
+
+    def close(step, rows):
+        other_core(mine_a, theirs_a, sems_a, step).wait_recv()
+        grad = mine_a[rows, :].astype(F32) + theirs_a[rows, :].astype(F32)
+        unit, scale = normalise(res[rows, :])
+        gnew = norm_back(unit, scale, norms[4:5, :], grad) + gres[rows, :]
+        gnew_ref[rows, :] = gnew
+        sums_ref[0:8, :] += fold_rows(grad * unit)
+        sums_ref[8:16, :] += fold_rows(grad)
+        low = gnew.astype(BF)
+        low_all[rows, :] = low
+        gmix_ref[rows, :] = nt(low, wo[...]).astype(BF)
+        other_core(mine_b, theirs_b, sems_b, step).wait_recv()
+        gmem_ref[rows, :] = (mine_b[rows, :].astype(F32) + theirs_b[rows, :].astype(F32)).astype(BF)
+    chunks(tokens, close)
+    gwo_ref[...] = tn(mixed[...], low_all[...]).astype(BF)
+    drain(tokens, mine_a, theirs_a, sems_a)
+    drain(tokens, mine_b, theirs_b, sems_b)
+
+
+def cross_back(dq, dk, dv, wc, nc, memory, res, gres, mixed, wo, norms):
+    tokens, features = nc.shape
+    cols = dq.shape[1]
+    outs = [((tokens, features), BF), ((tokens, features), F32), (dq.shape, BF), ((3 * cols, features), BF),
+            (wo.shape, BF), ((16, features), F32)]
+    wide = pltpu.VMEM((tokens, features), BF)
+    return call(cross_back_kernel, "cross_back", [dq, dk, dv, wc, nc, memory, res, gres, mixed, wo, norms], 0, outs,
+                [wide] * 5 + [pair_sems(tokens)] * 2, 4)
+
+
+def self_back_kernel(dq, dk, dv, ws, nq, nkv, query, kv, gres, norms, sums_c, sums_f,
+                     gquery_ref, gkv_ref, gw_ref, gnorm_ref,
+                     mine_a, theirs_a, mine_b, theirs_b, sums, sems_a, sems_b):
+    tokens, features = nq.shape
+    branch_back(nq, nkv, dq, dk, dv, ws, gw_ref, mine_a, theirs_a, mine_b, theirs_b, sems_a, sems_b)
+    sums[...] = jnp.zeros_like(sums)
+
+    def close(step, rows):
+        other_core(mine_a, theirs_a, sems_a, step).wait_recv()
+        grad = mine_a[rows, :].astype(F32) + theirs_a[rows, :].astype(F32)
+        unit, scale = normalise(query[rows, :].astype(F32))
+        gquery_ref[rows, :] = (norm_back(unit, scale, norms[0:1, :], grad) + gres[rows, :]).astype(BF)
+        sums[0:8, :] += fold_rows(grad * unit)
+        sums[8:16, :] += fold_rows(grad)
+        other_core(mine_b, theirs_b, sems_b, step).wait_recv()
+        grad = mine_b[rows, :].astype(F32) + theirs_b[rows, :].astype(F32)
+        unit, scale = normalise(kv[rows, :].astype(F32))
+        gkv_ref[rows, :] = norm_back(unit, scale, norms[2:3, :], grad).astype(BF)
+        sums[16:24, :] += fold_rows(grad * unit)
+        sums[24:32, :] += fold_rows(grad)
+    chunks(tokens, close)
+    parts = [sums[8 * i:8 * i + 8, :] for i in range(4)]
+    parts += [sums_c[0:8, :], sums_c[8:16, :], sums_f[0:8, :], sums_f[8:16, :]]
+    vectors = [jnp.sum(part, 0, keepdims=True) for part in parts]
+    gnorm_ref[...] = jnp.concatenate(vectors + [jnp.zeros((8, features), F32)], 0).astype(BF)
+    drain(tokens, mine_a, theirs_a, sems_a)
+    drain(tokens, mine_b, theirs_b, sems_b)
+
+
+def self_back(dq, dk, dv, ws, nq, nkv, query, kv, gres, norms, sums_c, sums_f):
+    tokens, features = nq.shape
+    cols = dq.shape[1]
+    outs = [((tokens, features), BF), ((tokens, features), BF), ((3 * cols, features), BF), ((16, features), BF)]
+    wide = pltpu.VMEM((tokens, features), BF)
+    return call(self_back_kernel, "self_back", [dq, dk, dv, ws, nq, nkv, query, kv, gres, norms, sums_c, sums_f], 0, outs,
+                [wide] * 4 + [pltpu.VMEM((32, features), F32)] + [pair_sems(tokens)] * 2, 5)
+
+
+def update_kernel(owner_ref, me_ref, summed, master, first, second, grad_ref, first_ref, second_ref, new_ref, held):
+    units = owner_ref.shape[0]
+    slots = master.shape[0]
+    me = me_ref[0]
+
+    def find(u, count):
+        held[count] = u
+        return count + (owner_ref[u] == me).astype(jnp.int32)
+    count = lax.fori_loop(0, units, find, jnp.int32(0), unroll=4)
+
+    def one(slot, carry):
+        @pl.when(slot < count)
+        def _():
+            unit = held[slot]
+            gradient = summed[pl.ds(pl.multiple_of(unit * UNIT, UNIT), UNIT), :].astype(F32)
+            first_new, second_new, weight = adamw_step(gradient, first[slot], second[slot], master[slot], RATE_MATRIX, WEIGHT_DECAY)
+            grad_ref[slot] = gradient
+            first_ref[slot] = first_new
+            second_ref[slot] = second_new
+            new_ref[slot] = weight
+
+        @pl.when(slot >= count)
+        def _():
+            for ref in (grad_ref, first_ref, second_ref, new_ref):
+                ref[slot] = jnp.zeros(ref.shape[1:], F32)
+        return carry
+    lax.fori_loop(0, slots, one, 0)
+
+
+def update(unit_owner, me, summed, master, first, second):
+    outs = [(master.shape, F32)] * 4
+    return call(update_kernel, "update", [unit_owner, me, summed, master, first, second], 2, outs,
+                [pltpu.SMEM((unit_owner.shape[0] + 8,), jnp.int32)])
+
+
 def adamw_step(gradient, first, second, weight, rate, decay):
     first_new = BETA_ONE * first + (1.0 - BETA_ONE) * gradient
     second_new = BETA_TWO * second + (1.0 - BETA_TWO) * gradient * gradient
@@ -364,183 +862,55 @@
 
 
 def local(
-    query_stream,
-    kv_stream,
-    memory,
-    out_grad,
-    lengths,
-    obs_rank,
-    obs_count,
-    unit_owner,
-    master,
-    first_moment,
-    second_moment,
-    norm_master,
-    norm_first,
-    norm_second,
+    query_stream, kv_stream, memory, out_grad, lengths, obs_rank, obs_count, unit_owner,
+    master, first_moment, second_moment, norm_master, norm_first, norm_second,
 ):
-    dev_count = lax.axis_size("dp")
-    head_shards = lax.axis_size("head")
-    my_index = lax.axis_index("dp")
-    slot_count = master.shape[0]
-    unit_rows = master.shape[2]
-    features = query_stream.shape[1]
-    unit_total = unit_owner.shape[0]
-    places = slot_places(unit_owner, dev_count, slot_count)
-    low_master = master.astype(jnp.bfloat16)
-    gathered, norm_all = (
-        lax.all_gather(low_master, "dp", axis=0, tiled=True),
-        lax.all_gather(norm_master.astype(jnp.bfloat16), "dp", axis=0, tiled=True),
-    )
-    matrices = unpack(gathered, places, features, head_shards)
-    norm_params = norm_all.astype(jnp.float32).reshape(8, features)
+    devices = lax.axis_size("dp")
+    shards = lax.axis_size("head")
+    me = lax.axis_index("dp")
+    slots, unit_rows, features = master.shape[0], master.shape[2], master.shape[3]
+    units = unit_owner.shape[0]
+    norm_share = norm_master.shape[0]
+    cols = features // shards
+    hidden = (units * unit_rows - 8 * cols) // 2
+
+    own = master.astype(BF).reshape(slots * unit_rows, features)
+    norm_row = jnp.pad(norm_master.astype(BF).reshape(1, norm_share), ((0, UNIT - 1), (0, features - norm_share)))
+    gathered = gather_blocks(jnp.concatenate([own, norm_row], 0), devices)
+    norms = gathered[:, slots * unit_rows, :norm_share].reshape(8, features).astype(F32)
+
     rank_row, count_row = obs_rank.reshape(1, ROW), obs_count.reshape(1, ROW)
-    stream_q = query_stream.astype(jnp.float32)
-    stream_kv = kv_stream.astype(jnp.float32)
-    normed_q = layer_norm(stream_q, norm_params[0], norm_params[1]).astype(jnp.bfloat16)
-    normed_kv = layer_norm(stream_kv, norm_params[2], norm_params[3]).astype(jnp.bfloat16)
-    queries_self = product(normed_q, matrices[0]).astype(jnp.bfloat16)
-    keys_self = product(normed_kv, matrices[1]).astype(jnp.bfloat16)
-    values_self = product(normed_kv, matrices[2]).astype(jnp.bfloat16)
-    mixed_self, totals_self = attend_forward(lengths, queries_self, keys_self, values_self, rank_row, count_row, True)
-    self_sum = lax.psum(product(mixed_self, matrices[6]).astype(jnp.bfloat16), "head").astype(
-        jnp.float32
-    )
-    residual = stream_q + self_sum
-    normed_c = layer_norm(residual, norm_params[4], norm_params[5]).astype(jnp.bfloat16)
-    queries_cross = product(normed_c, matrices[3]).astype(jnp.bfloat16)
-    keys_cross = product(memory, matrices[4]).astype(jnp.bfloat16)
-    values_cross = product(memory, matrices[5]).astype(jnp.bfloat16)
-    mixed_cross, totals_cross = attend_forward(
-        lengths, queries_cross, keys_cross, values_cross, rank_row, count_row, False
-    )
-    cross_sum = lax.psum(product(mixed_cross, matrices[7]).astype(jnp.bfloat16), "head").astype(
-        jnp.float32
-    )
-    cross_res = residual + cross_sum
-    normed_f = layer_norm(cross_res, norm_params[6], norm_params[7]).astype(jnp.bfloat16)
-    pre_act = product(normed_f, matrices[8])
-    hidden = jax.nn.gelu(pre_act, approximate=False).astype(jnp.bfloat16)
-    ffn_sum = lax.psum(product(hidden, matrices[9]).astype(jnp.bfloat16), "head").astype(
-        jnp.float32
-    )
-    output = (cross_res + ffn_sum).astype(jnp.bfloat16)
-    grad_w2 = inner_rows(hidden, out_grad)
-    grad_hidden = product_back(out_grad, matrices[9])
-    unused_value, gelu_pull = jax.vjp(partial(jax.nn.gelu, approximate=False), pre_act)
-    grad_pre = gelu_pull(grad_hidden)[0].astype(jnp.bfloat16)
-    grad_w1 = inner_rows(normed_f, grad_pre)
-    normed_f_grad = lax.psum(
-        product_back(grad_pre, matrices[8]).astype(jnp.bfloat16), "head"
-    ).astype(jnp.float32)
-    grad_cross_res, gain_f, shift_f = norm_pullback(
-        cross_res, norm_params[6], norm_params[7], normed_f_grad
-    )
-    grad_cross_res = grad_cross_res + out_grad.astype(jnp.float32)
-    cross_low = grad_cross_res.astype(jnp.bfloat16)
-    grad_wo_cross = inner_rows(mixed_cross, cross_low)
-    grad_mixed_cross = product_back(cross_low, matrices[7]).astype(jnp.bfloat16)
-    grad_q_cross, grad_k_cross, grad_v_cross = attend_backward(
-        lengths, queries_cross, keys_cross, values_cross, grad_mixed_cross, mixed_cross, totals_cross, rank_row, count_row, False
-    )
-    grad_wq_cross = inner_rows(normed_c, grad_q_cross)
-    grad_wk_cross = inner_rows(memory, grad_k_cross)
-    grad_wv_cross = inner_rows(memory, grad_v_cross)
-    normed_c_grad, memory_sum = (
-        lax.psum(product_back(grad_q_cross, matrices[3]).astype(jnp.bfloat16), "head").astype(
-            jnp.float32
-        ),
-        lax.psum(
-            (
-                product_back(grad_k_cross, matrices[4]) + product_back(grad_v_cross, matrices[5])
-            ).astype(jnp.bfloat16),
-            "head",
-        ).astype(jnp.float32),
-    )
-    grad_residual, gain_c, shift_c = norm_pullback(
-        residual, norm_params[4], norm_params[5], normed_c_grad
-    )
-    grad_residual = grad_residual + grad_cross_res
-    self_low = grad_residual.astype(jnp.bfloat16)
-    grad_wo_self = inner_rows(mixed_self, self_low)
-    grad_mixed_self = product_back(self_low, matrices[6]).astype(jnp.bfloat16)
-    grad_q_self, grad_k_self, grad_v_self = attend_backward(
-        lengths, queries_self, keys_self, values_self, grad_mixed_self, mixed_self, totals_self, rank_row, count_row, True
-    )
-    grad_wq_self = inner_rows(normed_q, grad_q_self)
-    grad_wk_self = inner_rows(normed_kv, grad_k_self)
-    grad_wv_self = inner_rows(normed_kv, grad_v_self)
-    normed_q_grad, normed_kv_grad = (
-        lax.psum(product_back(grad_q_self, matrices[0]).astype(jnp.bfloat16), "head").astype(
-            jnp.float32
-        ),
-        lax.psum(
-            (
-                product_back(grad_k_self, matrices[1]) + product_back(grad_v_self, matrices[2])
-            ).astype(jnp.bfloat16),
-            "head",
-        ).astype(jnp.float32),
-    )
-    grad_stream_q, gain_q, shift_q = norm_pullback(
-        stream_q, norm_params[0], norm_params[1], normed_q_grad
-    )
-    grad_stream_kv, gain_kv, shift_kv = norm_pullback(
-        stream_kv, norm_params[2], norm_params[3], normed_kv_grad
-    )
-    grad_query = (grad_stream_q + grad_residual).astype(jnp.bfloat16)
-    grad_kv = grad_stream_kv.astype(jnp.bfloat16)
-    grad_memory = memory_sum.astype(jnp.bfloat16)
-    grad_list = [
-        grad_wq_self,
-        grad_wk_self,
-        grad_wv_self,
-        grad_wq_cross,
-        grad_wk_cross,
-        grad_wv_cross,
-        grad_wo_self,
-        grad_wo_cross,
-        grad_w1,
-        grad_w2,
-    ]
-    flat_grads = jnp.concatenate([piece.reshape(-1, features) for piece in grad_list], 0)
-    unit_grads = flat_grads.reshape(unit_total, 1, unit_rows, features)
-    norm_grads = jnp.stack(
-        [gain_q, shift_q, gain_kv, shift_kv, gain_c, shift_c, gain_f, shift_f]
-    ).reshape(-1)
-    outgoing = (
-        jnp.zeros((dev_count * slot_count, 1, unit_rows, features), jnp.float32)
-        .at[places]
-        .set(unit_grads)
-    )
-    slot_grads, norm_share = (
-        lax.psum_scatter(outgoing, "dp", scatter_dimension=0, tiled=True),
-        lax.psum_scatter(norm_grads, "dp", scatter_dimension=0, tiled=True),
-    )
-    owned_count = jnp.sum((unit_owner == my_index).astype(jnp.int32))
-    slot_live = (jnp.arange(slot_count, dtype=jnp.int32) < owned_count)[:, None, None, None]
-    slot_grads = jnp.where(slot_live, slot_grads, 0.0)
-    first_new, second_new, weight_updated = adamw_step(
-        slot_grads, first_moment, second_moment, master, RATE_MATRIX, WEIGHT_DECAY
-    )
-    weight_first = jnp.where(slot_live, first_new, 0.0)
-    weight_second = jnp.where(slot_live, second_new, 0.0)
-    weight_new = jnp.where(slot_live, weight_updated, 0.0)
+    nq, nkv, q, k, v, kc, vc, ws, wc, wo_self, wo_cross, w1, w2 = project(
+        unit_owner, gathered, norms, query_stream, kv_stream, memory, cols, hidden)
+    mixed_self, total_self = attend_forward(lengths, q, k, v, rank_row, count_row, True)
+    residual, nc, qc = self_out(mixed_self, wo_self, query_stream, wc, norms)
+    mixed_cross, total_cross = attend_forward(lengths, qc, kc, vc, rank_row, count_row, False)
+    output, grad_cross_res, grad_mixed, gw1, gw2, gwo_cross, sums_f = feed_forward(
+        mixed_cross, wo_cross, residual, w1, w2, out_grad, norms)
+    dq, dk, dv = attend_backward(lengths, qc, kc, vc, grad_mixed, mixed_cross, total_cross, rank_row, count_row, False)
+    grad_memory, grad_residual, grad_mixed, gw_cross, gwo_self, sums_c = cross_back(
+        dq, dk, dv, wc, nc, memory, residual, grad_cross_res, mixed_self, wo_self, norms)
+    dq, dk, dv = attend_backward(lengths, q, k, v, grad_mixed, mixed_self, total_self, rank_row, count_row, True)
+    grad_query, grad_kv, gw_self, gnorm = self_back(
+        dq, dk, dv, ws, nq, nkv, query_stream, kv_stream, grad_residual, norms, sums_c, sums_f)
+
+    pieces = [gw_self, gw_cross, gwo_self, gwo_cross, gw1, gw2, gnorm]
+    used = units * unit_rows + UNIT
+    whole = -(-used // (devices * 2 * UNIT)) * (devices * 2 * UNIT)
+    flat = jnp.concatenate(pieces + [jnp.zeros((whole - used, features), BF)], 0)
+    summed = reduce_blocks(flat, devices)
+    shape = (slots, unit_rows, features)
+    weight_grad, weight_first, weight_second, weight_new = [
+        part.reshape(master.shape)
+        for part in update(unit_owner, me.reshape(1), summed, master.reshape(shape), first_moment.reshape(shape),
+                           second_moment.reshape(shape))]
+    norm_grads = summed[units * unit_rows:units * unit_rows + 8].reshape(-1).astype(F32)
+    norm_grad = lax.dynamic_slice_in_dim(norm_grads, me * norm_share, norm_share)
     norm_first_new, norm_second_new, norm_new = adamw_step(
-        norm_share, norm_first, norm_second, norm_master, RATE_NORM, 0.0
-    )
+        norm_grad, norm_first, norm_second, norm_master, RATE_NORM, 0.0)
     return (
-        output,
-        grad_query,
-        grad_kv,
-        grad_memory,
-        slot_grads,
-        weight_first,
-        weight_second,
-        weight_new,
-        norm_share,
-        norm_first_new,
-        norm_second_new,
-        norm_new,
+        output, grad_query, grad_kv, grad_memory, weight_grad, weight_first, weight_second, weight_new,
+        norm_grad, norm_first_new, norm_second_new, norm_new,
     )
 
 

time: 939 us -> 466 us (0.50); the launches traced: 925 us -> 466 us
  waiting for transfers between devices: 375 us -> 0 us
  Pallas kernels: 128 us -> 450 us
  blocking collectives: 124 us -> 0 us
  matrix products: 105 us -> 0 us
  local copies, waits for them, and re-layouts: 106 us -> 9.88 us
  other arithmetic: 69.6 us -> 5.07 us
  between operations: 16.3 us -> 0.91 us
    pallas_call x0 -> x8, Pallas kernels: none -> 322 us  [the longest x6 126 us: call(): pl.pallas_call(kernel, out_shape=tuple((jax.ShapeDtypeStruct(shape, dtype...]
    reduce_scatter x1 -> x0, waiting for transfers between devices: 244 us -> none  [local(): lax.psum_scatter(outgoing, 'dp', scatter_dimension=0, tiled=True)]
    dot_general x30 -> x0, matrix products: 105 us -> none  [the longest x10 48.1 us: product(): return jnp.dot(left_side, right_side, preferred_element_type=jnp.float32)]
    unnamed x1 -> x0, blocking collectives: 81 us -> none
    psum x5 -> x0, waiting for transfers between devices: 70.5 us -> none  [the longest x1 22 us: local(): lax.psum(product_back(grad_pre, matrices[8]).astype(jnp.bfloat16), 'head')]
    all_gather x1 -> x0, waiting for transfers between devices: 60 us -> none  [local(): lax.all_gather(low_master, 'dp', axis=0, tiled=True)]
    all_gather x1 -> x0, blocking collectives: 42.8 us -> none  [local(): lax.all_gather(norm_master.astype(jnp.bfloat16), 'dp', axis=0, tiled=True)]
    reduce_sum x17 -> x0, other arithmetic: 41 us -> none  [the longest x6 22.6 us: layer_norm(): return centred * lax.rsqrt(row_var + EPS_NORM) * norm_gain + norm_shift]
  transfers between devices with their start and end apart: 7 -> 0, of which waited for: 6 -> 0; matrix products, arithmetic and copies ran while one was open for 16% -> 0% of each run, Pallas kernels for 0% -> 0%
where the time goes in v2:
time: 466 us
  Pallas kernels  450 us (97%)
  local copies, waits for them, and re-layouts  9.88 us (2%)
  other arithmetic  5.07 us (1%)
    pallas_call x6, Pallas kernels, call(): pl.pallas_call(kernel, out_shape=tuple((jax.ShapeDtypeStruct(shape, dtype...  126 us
    pallas_call x1, Pallas kernels, reduce_blocks(): pl.pallas_call(partial(reduce_kernel, count), out_shape=jax.ShapeDtypeStr...  113 us
    pallas_call x1, Pallas kernels, gather_blocks(): pl.pallas_call(partial(gather_kernel, count), out_shape=jax.ShapeDtypeStr...  83.4 us
    pallas_call x2, Pallas kernels, attend_backward(): pl.pallas_call(partial(attn_bwd_kernel, with_seen, heads), out_shape=(lik...  77.2 us
    pallas_call x2, Pallas kernels, attend_forward(): pl.pallas_call(partial(attn_fwd_kernel, with_seen, heads), out_shape=(jax...  50.7 us

profile of v2, /device:TPU:0, one launch (start us, length us, event | category | flops | bytes accessed | tf_op | source)
XLA Modules:
  0.0 466.1 jit_solution(14403926556060582747)
XLA Ops:
  0.6 1.3 convert_element_type.19
  2.0 0.7 convert_element_type.20
  2.6 0.8 fusion.1.in_ref
  3.5 83.4 %gather_units.1.gathered = bf16[16,528,512]{2,1,0:T(8,128)(2,1)} custom-call(bf16[528,512]{1,0:T(8,128)(2,1)} %fusion.1.in_ref), custom_call_target="tpu_custom_call" | custom-call | tf_op jit(solution)/shard_map/gather_units/pallas_call | solution.py:380
  86.9 0.9 convert_reduce_fusion
  87.8 0.6 reshape.85.norms
  88.4 19.2 %project.1 = (bf16[2048,512]{1,0:T(8,128)(2,1)}, bf16[2048,512]{1,0:T(8,128)(2,1)}, bf16[2048,256]{1,0:T(8,128)(2,1)}, bf16[2048,256]{1,0:T(8,128)(2,1)}, bf16[2...) custom-call(s32[256]{0:T(256)} %owner_ref.3, ...), custom_call_target="tpu_custom_call" | custom-call | tf_op jit(solution)/shard_map/project/pallas_call | solution.py:588
  107.7 26.0 %attend_self_forward.1 = (bf16[2048,256]{1,0:T(8,128)(2,1)}, f32[8,2048]{1,0:T(8,128)}) custom-call(s32[1,32]{1,0:T(1,128)} %len_ref.7, bf16[2048,256]{1,0:T(8,128)(2,1)} %get-tuple-element.59.q_ref, bf16[2048,256]{1,0:T(8,128)(2,1)} %get-tuple-element.60.k_ref, bf16[2048,256]{1,0:T(8,128)(2,1)} %get-tuple-element.61.v_ref, s32[1,2048]{1,0:T(1,128)} %bitcast.31, ...), custom_call_target="tpu_custom_call" | custom-call | tf_op jit(solution)/shard_map/attend_self_forward/pallas_call | solution.py:174
  133.7 10.6 %self_out.1 = (f32[2048,512]{1,0:T(8,128)}, bf16[2048,512]{1,0:T(8,128)(2,1)}, bf16[2048,256]{1,0:T(8,128)(2,1)}) custom-call(bf16[2048,256]{1,0:T(8,128)(2,1)} %get-tuple-element.62.mixed.o_ref, bf16[256,512]{1,0:T(8,128)(2,1)} %get-tuple-element.63.wo, bf16[2048,512]{1,0:T(8,128)(2,1)} %query.3, bf16[3,512,256]{2,1,0:T(8,128)(2,1)} %get-tuple-element.64.wc, ...), custom_call_target="tpu_custom_call" | custom-call | tf_op jit(solution)/shard_map/self_out/pallas_call | solution.py:588
  144.3 24.7 %attend_cross_forward.1 = (bf16[2048,256]{1,0:T(8,128)(2,1)}, f32[8,2048]{1,0:T(8,128)}) custom-call(s32[1,32]{1,0:T(1,128)} %len_ref.7, bf16[2048,256]{1,0:T(8,128)(2,1)} %get-tuple-element.65.q_ref, bf16[2048,256]{1,0:T(8,128)(2,1)} %get-tuple-element.66.k_ref, bf16[2048,256]{1,0:T(8,128)(2,1)} %get-tuple-element.67.v_ref, s32[1,2048]{1,0:T(1,128)} %bitcast.32, ...), custom_call_target="tpu_custom_call" | custom-call | tf_op jit(solution)/shard_map/attend_cross_forward/pallas_call | solution.py:174
  169.0 39.8 %feed_forward.1 = (bf16[2048,512]{1,0:T(8,128)(2,1)}, f32[2048,512]{1,0:T(8,128)}, bf16[2048,256]{1,0:T(8,128)(2,1)}, bf16[1024,512]{1,0:T(8,128)(2,1)}, bf16[10...) custom-call(bf16[2048,256]{1,0:T(8,128)(2,1)} %get-tuple-element.68.mixed.o_ref, ...), custom_call_target="tpu_custom_call" | custom-call | tf_op jit(solution)/shard_map/feed_forward/pallas_call | solution.py:588
  208.8 37.7 %attend_cross_backward.1 = (bf16[2048,256]{1,0:T(8,128)(2,1)}, bf16[2048,256]{1,0:T(8,128)(2,1)}, bf16[2048,256]{1,0:T(8,128)(2,1)}) custom-call(s32[1,32]{1,0:T(1,128)} %len_ref.7, bf16[2048,256]{1,0:T(8,128)(2,1)} %get-tuple-element.65.q_ref, bf16[2048,256]{1,0:T(8,128)(2,1)} %get-tuple-element.66.k_ref, bf16[2048,256]{1,0:T(8,128)(2,1)} %get-tuple-element.67.v_ref, ...), custom_call_target="tpu_custom_call" | custom-call | tf_op jit(solution)/shard_map/attend_cross_backward/pallas_call | solution.py:285
  246.5 24.4 %cross_back.1 = (bf16[2048,512]{1,0:T(8,128)(2,1)}, f32[2048,512]{1,0:T(8,128)}, bf16[2048,256]{1,0:T(8,128)(2,1)}, bf16[768,512]{1,0:T(8,128)(2,1)}, bf16[256,512]{1,0:T(8,128)(2,1)}, /*index=5*/f32[16,512]{1,0:T(8,128)}) custom-call(bf16[2048,256]{1,0:T(8,128)(2,1)} %get-tuple-element.76.dq, bf16[2048,256]{1,0:T(8,128)(2,1)} %get-tuple-element.77.dk, ...), custom_call_target="tpu_custom_call" | custom-call | tf_op jit(solution)/shard_map/cross_back/pallas_call | solution.py:588
  270.9 39.5 %attend_self_backward.1 = (bf16[2048,256]{1,0:T(8,128)(2,1)}, bf16[2048,256]{1,0:T(8,128)(2,1)}, bf16[2048,256]{1,0:T(8,128)(2,1)}) custom-call(s32[1,32]{1,0:T(1,128)} %len_ref.7, bf16[2048,256]{1,0:T(8,128)(2,1)} %get-tuple-element.59.q_ref, bf16[2048,256]{1,0:T(8,128)(2,1)} %get-tuple-element.60.k_ref, bf16[2048,256]{1,0:T(8,128)(2,1)} %get-tuple-element.61.v_ref, ...), custom_call_target="tpu_custom_call" | custom-call | tf_op jit(solution)/shard_map/attend_self_backward/pallas_call | solution.py:285
  310.4 24.5 %self_back.1 = (bf16[2048,512]{1,0:T(8,128)(2,1)}, bf16[2048,512]{1,0:T(8,128)(2,1)}, bf16[768,512]{1,0:T(8,128)(2,1)}, bf16[16,512]{1,0:T(8,128)(2,1)}) custom-call(bf16[2048,256]{1,0:T(8,128)(2,1)} %get-tuple-element.83.dq, bf16[2048,256]{1,0:T(8,128)(2,1)} %get-tuple-element.84.dk, bf16[2048,256]{1,0:T(8,128)(2,1)} %get-tuple-element.85.dv, ...), custom_call_target="tpu_custom_call" | custom-call | tf_op jit(solution)/shard_map/self_back/pallas_call | solution.py:588
  334.9 0.0 copy-start.6
  335.0 0.0 copy-start.5
  335.0 0.0 copy-start.10
  335.0 1.3 constant_dynamic-update-slice_fusion.6
  336.3 0.0 copy-done.7
  336.3 0.1 constant_dynamic-update-slice_fusion.5
  336.4 0.0 copy-done.9
  336.4 0.0 copy-done.8
  336.5 0.0 copy-done.6
  336.5 0.1 constant_dynamic-update-slice_fusion.2
  336.5 0.2 copy-done.5
  336.7 0.1 constant_dynamic-update-slice_fusion.1
  336.8 0.0 copy-done.10
  336.9 0.0 copy-start
  336.9 2.1 copy-done
  339.0 113.3 %reduce_gradients.1 = bf16[16,288,512]{2,1,0:T(8,128)(2,1)} custom-call(bf16[16,288,512]{2,1,0:T(8,128)(2,1)} %bitcast.26), custom_call_target="tpu_custom_call" | custom-call | tf_op jit(solution)/shard_map/reduce_gradients/pallas_call | solution.py:454
  452.3 0.0 copy-start.11
  452.3 0.0 copy-start.12
  452.3 0.0 copy-start.13
  452.4 0.0 copy-start.1
  452.4 7.0 %update.1 = (f32[32,16,512]{2,1,0:T(8,128)}, f32[32,16,512]{2,1,0:T(8,128)}, f32[32,16,512]{2,1,0:T(8,128)}, f32[32,16,512]{2,1,0:T(8,128)}) custom-call(s32[256]{0:T(256)} %owner_ref.3, s32[1]{0:T(128)} %bitcast.3.me_ref, bf16[4608,512]{1,0:T(8,128)(2,1)} %bitcast.24, f32[32,16,512]{2,1,0:T(8,128)} %bitcast.27, f32[32,16,512]{2,1,0:T(8,128)} %bitcast.29, ...), custom_call_target="tpu_custom_call" | custom-call | tf_op jit(solution)/shard_map/update/pallas_call | solution.py:588
  459.4 0.7 convert_bitcast_fusion
  460.1 0.0 copy-done.11
  460.1 0.0 copy-done.13
  460.1 0.0 copy-start.4
  460.1 0.0 copy-start.3
  460.1 0.7 multiply_subtract_fusion
  460.8 1.3 copy.42
  462.1 1.3 copy.43
  463.4 0.0 copy-done.3
  463.4 1.3 copy.44
  464.7 0.0 copy-done.2
  464.8 1.3 copy.45
  (13 shorter events, 0.1 us)
Async XLA Ops:
  310.4 25.9 %copy-start.7 = (bf16[768,512]{1,0:T(8,128)(2,1)S(1)}, bf16[768,512]{1,0:T(8,128)(2,1)}, u32[]{:S(2)}) copy-start(bf16[768,512]{1,0:T(8,128)(2,1)} %get-tuple-element.96) | copy-start | bytes 2359300
  310.4 26.0 %copy-start.9 = (bf16[256,512]{1,0:T(8,128)(2,1)S(1)}, bf16[256,512]{1,0:T(8,128)(2,1)}, u32[]{:S(2)}) copy-start(bf16[256,512]{1,0:T(8,128)(2,1)} %get-tuple-element.97) | copy-start | bytes 786436
  310.4 26.0 %copy-start.8 = (bf16[256,512]{1,0:T(8,128)(2,1)S(1)}, bf16[256,512]{1,0:T(8,128)(2,1)}, u32[]{:S(2)}) copy-start(bf16[256,512]{1,0:T(8,128)(2,1)} %get-tuple-element.98) | copy-start | bytes 786436
  334.9 1.5 copy-start.6
  335.0 1.8 copy-start.5
  335.0 1.8 copy-start.10
  336.9 2.1 copy-start
  452.3 7.8 %copy-start.11 = (f32[256]{0:T(256)S(1)}, f32[256]{0:T(256)}, u32[]{:S(2)}) copy-start(f32[256]{0:T(256)} %param.25) | copy-start | bytes 3076
  452.3 7.7 %copy-start.12 = (f32[256]{0:T(256)S(1)}, f32[256]{0:T(256)}, u32[]{:S(2)}) copy-start(f32[256]{0:T(256)} %param.27) | copy-start | bytes 3076
  452.3 7.7 %copy-start.13 = (f32[256]{0:T(256)S(1)}, f32[256]{0:T(256)}, u32[]{:S(2)}) copy-start(f32[256]{0:T(256)} %param.26) | copy-start | bytes 3076
  452.4 8.4 %copy-start.1 = (bf16[2048,512]{1,0:T(8,128)(2,1)S(1)}, bf16[2048,512]{1,0:T(8,128)(2,1)}, u32[]{:S(2)}) copy-start(bf16[2048,512]{1,0:T(8,128)(2,1)} %get-tuple-element.134) | copy-start | bytes 6291460
  460.1 2.0 copy-start.4
  460.1 3.3 copy-start.3
  462.1 2.7 copy-start.2

commit v3 on v2

--- a/solution.py
+++ b/solution.py
@@ -185,6 +185,7 @@
             pltpu.VMEM((heads // 2, 256, TQ), BF),
         ],
         compiler_params=pltpu.CompilerParams(vmem_limit_bytes=56 * 2**20),
+        cost_estimate=pl.CostEstimate(flops=4 * 10**10, bytes_accessed=16 * 2**20, transcendentals=0),
         name="attend_self_forward" if with_seen else "attend_cross_forward",
     )(lengths, q, k, v, rank, count)
 
@@ -193,8 +194,11 @@
     mid = (value - hi).astype(BF).astype(F32)
     return hi, mid, value - hi - mid
 
-def attn_bwd_kernel(with_seen, heads, len_ref, q_ref, k_ref, v_ref, g_ref, o_ref, lse_ref, rank_ref, count_ref,
-                    dq_ref, dk_ref, dv_ref, kaug, vaug, kt, rank_cols, dk_sum, dv_sum, dq_sum, q_diag, g_diag, qt, gt):
+def attn_bwd_kernel(with_seen, heads, len_ref, q_ref, k_ref, v_ref, g_ref, o_ref, lse_ref, rank_ref, count_ref, pass_in,
+                    dq_ref, dk_ref, dv_ref, pass_out,
+                    kaug, vaug, kt, rank_cols, dk_sum, dv_sum, dq_sum, q_diag, g_diag, qt, gt, held, pass_sem):
+    entering = pltpu.make_async_copy(pass_in, held, pass_sem.at[0])
+    entering.start()
     cols = heads * HEAD_DIM
     starts, ends = doc_bounds(len_ref)
     start_lane, end_lane = lane_vector(starts), lane_vector(ends)
@@ -213,6 +217,9 @@
     kt[:, ROW:] = jnp.zeros((cols, TK), BF)
     if with_seen:
         fill_ranks(rank_cols, rank_ref, starts)
+    entering.wait()
+    leaving = pltpu.make_async_copy(held, pass_out, pass_sem.at[1])
+    leaving.start()
     dk_sum[...] = jnp.zeros_like(dk_sum)
     dv_sum[...] = jnp.zeros_like(dv_sum)
     sel_row = lax.broadcasted_iota(jnp.int32, (8, cols), 0)
@@ -276,17 +283,18 @@
     lax.fori_loop(0, ROW // TQ, one_q, 0)
     dk_ref[...] = (dk_sum[:ROW, :] * HEAD_DIM ** -0.5).astype(BF)
     dv_ref[...] = dv_sum[:ROW, :].astype(BF)
-
-def attend_backward(lengths, q, k, v, g, o, lse, rank, count, with_seen):
+    leaving.wait()
+
+def attend_backward(lengths, q, k, v, g, o, lse, rank, count, passed, with_seen):
     rows, cols = q.shape
     heads = cols // HEAD_DIM
     V = pl.BlockSpec(memory_space=pltpu.VMEM)
     like = jax.ShapeDtypeStruct((rows, cols), BF)
     return pl.pallas_call(
         partial(attn_bwd_kernel, with_seen, heads),
-        out_shape=(like, like, like),
-        in_specs=[pl.BlockSpec(memory_space=pltpu.SMEM)] + [V] * 8,
-        out_specs=(V, V, V),
+        out_shape=(like, like, like, jax.ShapeDtypeStruct(passed.shape, passed.dtype)),
+        in_specs=[pl.BlockSpec(memory_space=pltpu.SMEM)] + [V] * 8 + [pl.BlockSpec(memory_space=pl.ANY)],
+        out_specs=(V, V, V, pl.BlockSpec(memory_space=pl.ANY)),
         scratch_shapes=[
             pltpu.VMEM((heads, ROW + TK, 256), BF),
             pltpu.VMEM((heads, ROW + TK, 256), BF),
@@ -299,10 +307,13 @@
             pltpu.VMEM((heads * TQ, cols), BF),
             pltpu.VMEM((heads // 2, 256, TQ), BF),
             pltpu.VMEM((heads // 2, 256, TQ), BF),
+            pltpu.VMEM(passed.shape, passed.dtype),
+            pltpu.SemaphoreType.DMA((2,)),
         ],
         compiler_params=pltpu.CompilerParams(vmem_limit_bytes=56 * 2**20),
+        cost_estimate=pl.CostEstimate(flops=4 * 10**10, bytes_accessed=16 * 2**20, transcendentals=0),
         name="attend_self_backward" if with_seen else "attend_cross_backward",
-    )(lengths, q, k, v, g, o, lse, rank, count)
+    )(lengths, q, k, v, g, o, lse, rank, count, passed)
 
 
 def send(src, dst, send_sem, recv_sem, **where):
@@ -363,109 +374,130 @@
     recv[d][1].wait_recv()
     diag.append(go(base + 2 - 4 * y, pl.ds(half, rows - half), gx, d, xpeer))
 
-def gather_kernel(count, in_ref, out_ref, local_sem, zs, xs, ys, gx, gy):
+def gather_kernel(count, master, norm, out_ref, zs, xs, ys, gx, gy):
     places = places_of(count)
     me, x, y, z, xpeer, ypeer, order, ahead, behind = places
-    rows = in_ref.shape[0]
-    own = pltpu.make_async_copy(in_ref, out_ref.at[me], local_sem)
-    own.start()
+    rows = master.shape[0]
+    out_ref[me, 0:rows, :] = master[...].astype(BF)
+    out_ref[me, rows:rows + UNIT, :] = jnp.broadcast_to(norm[...], (UNIT, norm.shape[1])).astype(BF)
     greet([{"dp": xpeer}, {"dp": ypeer}] + [{"dp": ahead(d)} for d in order])
-    own.wait()
-    spread_blocks(count, out_ref, rows, places, zs, xs, ys, gx, gy)
-
-def gather_blocks(block, count, number=0):
-    rows, cols = block.shape
-    across = count // 4
-    sems = pltpu.SemaphoreType.DMA((2, across))
-    return pl.pallas_call(
-        partial(gather_kernel, count),
-        out_shape=jax.ShapeDtypeStruct((count, rows, cols), block.dtype),
-        in_specs=[pl.BlockSpec(memory_space=pltpu.VMEM)],
-        out_specs=pl.BlockSpec(memory_space=pltpu.VMEM),
-        scratch_shapes=[pltpu.SemaphoreType.DMA] + [sems] * 5,
-        compiler_params=pltpu.CompilerParams(collective_id=number, has_side_effects=True, vmem_limit_bytes=56 * 2**20),
-        name="gather_units",
-    )(block)
-
-def reduce_kernel(count, in_ref, out_ref, keep, r1, r2, r3, s1, s2, s3, zs, xs, ys, gx, gy):
-    places = places_of(count)
-    me, x, y, z, xpeer, ypeer, order, ahead, behind = places
-    across = count // 4
-    rows = in_ref.shape[1]
-    half = rows // 2
-    greet([{"dp": xpeer}, {"dp": ypeer}] + [{"dp": ahead(d)} for d in order])
-    steps = order + [0]
-    base = lambda d: lax.rem(z + d, across) * 4
-    part_rows = [pl.ds(0, half), pl.ds(half, half)]
-    def at(d, first, second, part):
-        return base(d) + (first + 2 * second if part == 0 else 2 * first + second)
-    mine = [(x, y), (y, x)]
-    peers = [(xpeer, ypeer), (ypeer, xpeer)]
-    first_copies = {}
-    for d in steps:
-        for part in (0, 1):
-            f, s = mine[part]
+    spread_blocks(count, out_ref, rows + UNIT, places, zs, xs, ys, gx, gy)
+
+
+def gather_blocks(master, norm, count):
+    rows, cols = master.shape
+    sems = pltpu.SemaphoreType.DMA((2, count // 4))
+    return call(partial(gather_kernel, count), "gather_units", [master, norm], "VV",
+                [((count, rows + UNIT, cols), BF, "V")], [sems] * 5, 0)[0]
+
+
+def part_sizes(rows):
+    first = rows // 2 // UNIT * UNIT
+    return [(part, pl.ds(start, size), size) for part, start, size in ((0, 0, first), (1, first, rows - first)) if size]
+
+
+class BlockSum:
+    def __init__(self, count, places, source, out, keep, r1, r2, r3, s1, s2, s3):
+        self.count, self.places, self.source, self.out = count, places, source, out
+        self.keep, self.r1, self.r2, self.r3, self.s1, self.s2, self.s3 = keep, r1, r2, r3, s1, s2, s3
+        self.parts = part_sizes(source.shape[1])
+        self.first, self.second, self.third = {}, {}, {}
+
+    def at(self, d, first, second, part):
+        z, across = self.places[3], self.count // 4
+        return lax.rem(z + d, across) * 4 + (first + 2 * second if part == 0 else 2 * first + second)
+
+    def start(self):
+        me, x, y, z, xpeer, ypeer, order, ahead, behind = self.places
+        self.steps = order + [0]
+        self.mine = [(x, y), (y, x)]
+        self.peers = [(xpeer, ypeer), (ypeer, xpeer)]
+        for d in self.steps:
+            for part, rows, size in self.parts:
+                f, s = self.mine[part]
+                for t in (0, 1):
+                    second = s if t else 1 - s
+                    self.first[d, part, t] = send(
+                        self.source.at[self.at(d, 1 - f, second, part), rows], self.r1.at[part, d, t, pl.ds(0, size)],
+                        self.s1.at[0, part, d, t], self.s1.at[1, part, d, t], dp=self.peers[part][0])
+
+    def second_stage(self, d):
+        for part, rows, size in self.parts:
+            f, s = self.mine[part]
+            into = pl.ds(0, size)
             for t in (0, 1):
                 second = s if t else 1 - s
-                first_copies[d, part, t] = send(in_ref.at[at(d, 1 - f, second, part), part_rows[part]], r1.at[part, d, t],
-                                                s1.at[0, part, d, t], s1.at[1, part, d, t], dp=peers[part][0])
-    second_copies, third_copies = {}, {}
-    def second_stage(d):
-        for part in (0, 1):
-            f, s = mine[part]
-            for t in (0, 1):
-                second = s if t else 1 - s
-                first_copies[d, part, t].wait_recv()
-                total = (in_ref[at(d, f, second, part), part_rows[part], :].astype(F32) + r1[part, d, t].astype(F32)).astype(BF)
-                keep[part, d, t] = total
+                self.first[d, part, t].wait_recv()
+                self.keep[part, d, t, into, :] = (self.source[self.at(d, f, second, part), rows, :].astype(F32)
+                                                  + self.r1[part, d, t, into, :].astype(F32)).astype(BF)
                 if t == 0:
-                    second_copies[d, part] = send(keep.at[part, d, 0], r2.at[part, d], s2.at[0, part, d], s2.at[1, part, d],
-                                                  dp=peers[part][1])
-    def third_stage(d):
-        for part in (0, 1):
-            second_copies[d, part].wait_recv()
-            total = (keep[part, d, 1].astype(F32) + r2[part, d].astype(F32)).astype(BF)
-            keep[part, d, 1] = total
+                    self.second[d, part] = send(self.keep.at[part, d, 0, into], self.r2.at[part, d, into],
+                                                self.s2.at[0, part, d], self.s2.at[1, part, d], dp=self.peers[part][1])
+
+    def third_stage(self, d):
+        ahead = self.places[7]
+        for part, rows, size in self.parts:
+            into = pl.ds(0, size)
+            self.second[d, part].wait_recv()
+            self.keep[part, d, 1, into, :] = (self.keep[part, d, 1, into, :].astype(F32)
+                                              + self.r2[part, d, into, :].astype(F32)).astype(BF)
             if d:
-                third_copies[d, part] = send(keep.at[part, d, 1], r3.at[part, d], s3.at[0, part, d], s3.at[1, part, d], dp=ahead(d))
-    for k, d in enumerate(steps):
-        second_stage(d)
-        if k:
-            third_stage(steps[k - 1])
-    third_stage(0)
-    for part in (0, 1):
-        total = keep[part, 0, 1].astype(F32)
-        for d in order:
-            third_copies[d, part].wait_recv()
-            total = total + r3[part, d].astype(F32)
-        out_ref[me, part_rows[part], :] = total.astype(BF)
-    spread_blocks(count, out_ref, rows, places, zs, xs, ys, gx, gy)
-    for copies in (first_copies, second_copies, third_copies):
-        for copy in copies.values():
-            copy.wait_send()
-
-def reduce_blocks(flat, count, number=1):
-    total_rows, cols = flat.shape
-    rows = total_rows // count
-    half = rows // 2
+                self.third[d, part] = send(self.keep.at[part, d, 1, into], self.r3.at[part, d, into],
+                                           self.s3.at[0, part, d], self.s3.at[1, part, d], dp=ahead(d))
+
+    def finish(self):
+        me, order = self.places[0], self.places[6]
+        for k, d in enumerate(self.steps):
+            self.second_stage(d)
+            if k:
+                self.third_stage(self.steps[k - 1])
+        self.third_stage(0)
+        for part, rows, size in self.parts:
+            into = pl.ds(0, size)
+            total = self.keep[part, 0, 1, into, :].astype(F32)
+            for d in order:
+                self.third[d, part].wait_recv()
+                total = total + self.r3[part, d, into, :].astype(F32)
+            self.out[me, rows, :] = total.astype(BF)
+
+    def drain(self):
+        for copies in (self.first, self.second, self.third):
+            for copy in copies.values():
+                copy.wait_send()
+
+
+def block_sum_scratch(count, rows, cols):
     across = count // 4
-    sems = pltpu.SemaphoreType.DMA((2, across))
+    size = max(size for _, _, size in part_sizes(rows))
     D = pltpu.SemaphoreType.DMA
+    return [
+        pltpu.VMEM((2, across, 2, size, cols), BF), pltpu.VMEM((2, across, 2, size, cols), BF),
+        pltpu.VMEM((2, across, size, cols), BF), pltpu.VMEM((2, across, size, cols), BF),
+        D((2, 2, across, 2)), D((2, 2, across)), D((2, 2, across))]
+
+
+def plane_swap(value, count, f):
+    return lax.ppermute(value, "dp", [(i, i // 4 * 4 + (i % 4 ^ f)) for i in range(count)])
+
+
+def plane_offset(places, f):
+    x, y = places[1], places[2]
+    return lax.rem(x + f % 2, 2) + 2 * lax.rem(y + f // 2, 2)
+
+
+def call(kernel, name, args, kinds, outs, scratch, number=None):
+    space = {"V": pltpu.VMEM, "S": pltpu.SMEM, "A": pl.ANY}
+    extra = {} if number is None else dict(collective_id=number, has_side_effects=True)
     return pl.pallas_call(
-        partial(reduce_kernel, count),
-        out_shape=jax.ShapeDtypeStruct((count, rows, cols), BF),
-        in_specs=[pl.BlockSpec(memory_space=pltpu.VMEM)],
-        out_specs=pl.BlockSpec(memory_space=pltpu.VMEM),
-        scratch_shapes=[
-            pltpu.VMEM((2, across, 2, half, cols), BF),
-            pltpu.VMEM((2, across, 2, half, cols), BF),
-            pltpu.VMEM((2, across, half, cols), BF),
-            pltpu.VMEM((2, across, half, cols), BF),
-            D((2, 2, across, 2)), D((2, 2, across)), D((2, 2, across)),
-        ] + [sems] * 5,
-        compiler_params=pltpu.CompilerParams(collective_id=number, has_side_effects=True, vmem_limit_bytes=56 * 2**20),
-        name="reduce_gradients",
-    )(flat.reshape(count, rows, cols)).reshape(total_rows, cols)
+        kernel,
+        out_shape=tuple(jax.ShapeDtypeStruct(shape, dtype) for shape, dtype, _ in outs),
+        in_specs=[pl.BlockSpec(memory_space=space[kind]) for kind in kinds],
+        out_specs=tuple(pl.BlockSpec(memory_space=space[kind]) for _, _, kind in outs),
+        scratch_shapes=scratch,
+        compiler_params=pltpu.CompilerParams(vmem_limit_bytes=60 * 2**20, **extra),
+        cost_estimate=pl.CostEstimate(flops=4 * 10**10, bytes_accessed=16 * 2**20, transcendentals=0),
+        name=name,
+    )(*args)
 
 
 CHUNK = 256
@@ -531,12 +563,46 @@
     chunks(total, body)
 
 
-def project_kernel(owner_ref, gathered, norms, query_ref, kv_ref, memory_ref,
-                   nq_ref, nkv_ref, q_ref, k_ref, v_ref, kc_ref, vc_ref, ws_ref, wc_ref, wos_ref, woc_ref, w1_ref, w2_ref,
-                   flat, used):
+class Late:
+    def __init__(self, pairs, sems):
+        self.copies = [pltpu.make_async_copy(source, held, sems.at[i]) for i, (source, held) in enumerate(pairs)]
+        for copy in self.copies:
+            copy.start()
+
+    def wait(self, *which):
+        for i in which:
+            self.copies[i].wait()
+
+
+class Out:
+    def __init__(self, pairs, sems):
+        self.pairs, self.sems = pairs, sems
+
+    def copy(self, i, step):
+        held, out = self.pairs[i]
+        rows = pl.ds(pl.multiple_of(step * CHUNK, CHUNK), CHUNK)
+        return pltpu.make_async_copy(held.at[rows], out.at[rows], self.sems.at[i, step])
+
+    def start(self, i, step):
+        self.copy(i, step).start()
+
+    def drain(self, tokens):
+        def body(step, rows):
+            for i in range(len(self.pairs)):
+                self.copy(i, step).wait()
+        chunks(tokens, body)
+
+
+def project_kernel(owner_ref, gathered, norms, query_hbm, kv_hbm, memory_hbm,
+                   nq_out, nkv_out, q_out, k_out, v_out, kc_out, vc_out, ws_ref, wc_ref, wos_ref, woc_ref, w1_ref, w2_ref,
+                   flat, used, query_ref, kv_ref, memory_ref, nq_ref, nkv_ref, q_ref, k_ref, v_ref, kc_ref, vc_ref,
+                   late_sems, out_sems):
     tokens, features = query_ref.shape
     devices = gathered.shape[0]
     units = owner_ref.shape[0]
+    late = Late([(query_hbm, query_ref), (kv_hbm, kv_ref), (memory_hbm, memory_ref)], late_sems)
+    out = Out([(nq_ref, nq_out), (nkv_ref, nkv_out), (q_ref, q_out), (k_ref, k_out), (v_ref, v_out), (kc_ref, kc_out),
+               (vc_ref, vc_out)], out_sems)
     for d in range(devices):
         used[d] = 0
 
@@ -566,75 +632,76 @@
         half = features // 2
         w1_ref[block * half:(block + 1) * half, :] = jnp.concatenate([parted[:half], parted[half:]], 1)
     w2_ref[...] = flat[8 * cols + hidden:, :]
+    late.wait(0, 1, 2)
 
     def body(step, rows):
         nq = (normalise(query_ref[rows, :].astype(F32))[0] * norms[0:1, :] + norms[1:2, :]).astype(BF)
         nkv = (normalise(kv_ref[rows, :].astype(F32))[0] * norms[2:3, :] + norms[3:4, :]).astype(BF)
         source = memory_ref[rows, :]
-        nq_ref[rows, :] = nq
-        nkv_ref[rows, :] = nkv
-        q_ref[rows, :] = nn(nq, ws_ref[0]).astype(BF)
-        k_ref[rows, :] = nn(nkv, ws_ref[1]).astype(BF)
-        v_ref[rows, :] = nn(nkv, ws_ref[2]).astype(BF)
-        kc_ref[rows, :] = nn(source, wc_ref[1]).astype(BF)
-        vc_ref[rows, :] = nn(source, wc_ref[2]).astype(BF)
+        results = [nq, nkv, nn(nq, ws_ref[0]), nn(nkv, ws_ref[1]), nn(nkv, ws_ref[2]), nn(source, wc_ref[1]), nn(source, wc_ref[2])]
+        for i, (ref, result) in enumerate(zip((nq_ref, nkv_ref, q_ref, k_ref, v_ref, kc_ref, vc_ref), results)):
+            ref[rows, :] = result.astype(BF)
+            out.start(i, step)
     chunks(tokens, body)
-
-
-def call(kernel, name, args, smem, outs, scratch, number=None):
-    V = pl.BlockSpec(memory_space=pltpu.VMEM)
-    S = pl.BlockSpec(memory_space=pltpu.SMEM)
-    extra = {} if number is None else dict(collective_id=number, has_side_effects=True)
-    return pl.pallas_call(
-        kernel,
-        out_shape=tuple(jax.ShapeDtypeStruct(shape, dtype) for shape, dtype in outs),
-        in_specs=[S] * smem + [V] * (len(args) - smem),
-        out_specs=tuple(V for _ in outs),
-        scratch_shapes=scratch,
-        compiler_params=pltpu.CompilerParams(vmem_limit_bytes=60 * 2**20, **extra),
-        name=name,
-    )(*args)
+    out.drain(tokens)
 
 
 def pair_sems(tokens):
     return pltpu.SemaphoreType.DMA((2, tokens // CHUNK))
 
 
+def out_semaphores(count, tokens):
+    return pltpu.SemaphoreType.DMA((count, tokens // CHUNK))
+
+
 def project(unit_owner, gathered, norms, query_stream, kv_stream, memory, cols, hidden):
     tokens, features = query_stream.shape
-    wide, narrow = ((tokens, features), BF), ((tokens, cols), BF)
-    outs = [wide, wide] + [narrow] * 5 + [
-        ((3, features, cols), BF), ((3, features, cols), BF), ((cols, features), BF), ((cols, features), BF),
-        ((features, hidden), BF), ((hidden, features), BF)]
-    return call(project_kernel, "project", [unit_owner, gathered, norms, query_stream, kv_stream, memory], 1, outs,
-                [pltpu.VMEM((8 * cols + 2 * hidden, features), BF), pltpu.SMEM((gathered.shape[0],), jnp.int32)])
-
-
-def self_out_kernel(mixed, wo, query, wc, norms, res_ref, nc_ref, q_ref, mine, theirs, sems):
+    wide, narrow = (tokens, features), (tokens, cols)
+    outs = [(wide, BF, "A")] * 2 + [(narrow, BF, "A")] * 5 + [
+        ((3, features, cols), BF, "V"), ((3, features, cols), BF, "V"), ((cols, features), BF, "V"), ((cols, features), BF, "V"),
+        ((features, hidden), BF, "V"), ((hidden, features), BF, "V")]
+    scratch = [pltpu.VMEM((8 * cols + 2 * hidden, features), BF), pltpu.SMEM((gathered.shape[0],), jnp.int32)]
+    scratch += [pltpu.VMEM(wide, BF)] * 5 + [pltpu.VMEM(narrow, BF)] * 5
+    scratch += [pltpu.SemaphoreType.DMA((3,)), out_semaphores(7, tokens)]
+    return call(project_kernel, "project", [unit_owner, gathered, norms, query_stream, kv_stream, memory], "SVVAAA", outs, scratch)
+
+
+def self_out_kernel(mixed, wo, query_hbm, wc, norms, res_out, nc_out, q_out,
+                    query, res_ref, nc_ref, q_ref, mine, theirs, sems, late_sems, out_sems):
     tokens = query.shape[0]
+    late = Late([(query_hbm, query)], late_sems)
+    out = Out([(res_ref, res_out), (nc_ref, nc_out), (q_ref, q_out)], out_sems)
     greet_core()
 
     def give(step, rows):
         mine[rows, :] = nn(mixed[rows, :], wo[...]).astype(BF)
         other_core(mine, theirs, sems, step).start()
     chunks(tokens, give)
+    late.wait(0)
 
     def take(step, rows):
         other_core(mine, theirs, sems, step).wait_recv()
         res = query[rows, :].astype(F32) + (mine[rows, :].astype(F32) + theirs[rows, :].astype(F32))
         res_ref[rows, :] = res
+        out.start(0, step)
         nc = (normalise(res)[0] * norms[4:5, :] + norms[5:6, :]).astype(BF)
         nc_ref[rows, :] = nc
+        out.start(1, step)
         q_ref[rows, :] = nn(nc, wc[0]).astype(BF)
+        out.start(2, step)
     chunks(tokens, take)
     drain(tokens, mine, theirs, sems)
+    out.drain(tokens)
 
 
 def self_out(mixed, wo, query, wc, norms):
     tokens, features = query.shape
-    outs = [((tokens, features), F32), ((tokens, features), BF), (mixed.shape, BF)]
-    wide = pltpu.VMEM((tokens, features), BF)
-    return call(self_out_kernel, "self_out", [mixed, wo, query, wc, norms], 0, outs, [wide, wide, pair_sems(tokens)], 2)
+    wide = (tokens, features)
+    outs = [(wide, F32, "A"), (wide, BF, "A"), (mixed.shape, BF, "A")]
+    scratch = [pltpu.VMEM(wide, BF), pltpu.VMEM(wide, F32), pltpu.VMEM(wide, BF), pltpu.VMEM(mixed.shape, BF),
+               pltpu.VMEM(wide, BF), pltpu.VMEM(wide, BF), pair_sems(tokens), pltpu.SemaphoreType.DMA((1,)),
+               out_semaphores(3, tokens)]
+    return call(self_out_kernel, "self_out", [mixed, wo, query, wc, norms], "VVAVV", outs, scratch, 2)
 
 
 def gelu_parts(value):
@@ -647,18 +714,31 @@
     return value * below, below + value * (bell * 0.3989422804014327)
 
 
-def feed_forward_kernel(mixed, wo, res, w1, w2, out_grad, norms,
-                        out_ref, gres_ref, gmix_ref, gw1_ref, gw2_ref, gwo_ref, sums_ref,
+def spread_flat(devices, places, flat, refs):
+    rows = flat.shape[0] // devices
+    for f, ref in enumerate(refs):
+        place = plane_offset(places, f)
+        for level in range(devices // 4):
+            ref[level, ref.shape[1] - rows:, :] = flat[pl.ds(pl.multiple_of((level * 4 + place) * rows, UNIT), rows), :]
+
+
+def feed_forward_kernel(devices, mixed, wo, res_hbm, w1, w2, out_grad_hbm, norms,
+                        out_out, gres_out, gmix_out, part0, part1, part2, part3, gwo_ref, sums_ref,
+                        res, out_grad, out_ref, gres_ref, gmix_ref, flat,
                         mine, theirs, nf_all, hid_all, pre_all, low_all, mine_o, theirs_o, mine_g, theirs_g,
-                        sems, sems_o, sems_g):
+                        sems, sems_o, sems_g, late_sems, out_sems):
     tokens, features = out_grad.shape
     hidden = w2.shape[0]
+    places = places_of(devices)
+    late = Late([(res_hbm, res), (out_grad_hbm, out_grad)], late_sems)
+    out = Out([(out_ref, out_out), (gres_ref, gres_out), (gmix_ref, gmix_out)], out_sems)
     greet_core()
 
     def give(step, rows):
         mine[rows, :] = nn(mixed[rows, :], wo[...]).astype(BF)
         other_core(mine, theirs, sems, step).start()
     chunks(tokens, give)
+    late.wait(0, 1)
 
     def middle(step, rows):
         other_core(mine, theirs, sems, step).wait_recv()
@@ -688,11 +768,12 @@
     half = features // 2
     for block in range(hidden // 256):
         at = slice(block * 256, (block + 1) * 256)
-        gw2_ref[at, :] = tn(hid_all[:, at], out_grad[...]).astype(BF)
+        flat[hidden + block * 256:hidden + (block + 1) * 256, :] = tn(hid_all[:, at], out_grad[...]).astype(BF)
     for block in range(hidden // features):
         gradient = tn(nf_all[:, block * half:(block + 1) * half], pre_all[...]).astype(BF)
         stacked = jnp.concatenate([gradient[:, :features], gradient[:, features:]], 0)
-        gw1_ref[block * features:(block + 1) * features, :] = nn(order, stacked).astype(BF)
+        flat[block * features:(block + 1) * features, :] = nn(order, stacked).astype(BF)
+    spread_flat(devices, places, flat, (part0, part1, part2, part3))
     sums_ref[...] = jnp.zeros_like(sums_ref)
 
     def close(step, rows):
@@ -700,55 +781,98 @@
         other_core(mine_g, theirs_g, sems_g, step).wait_recv()
         value = gres_ref[rows, :]
         out_ref[rows, :] = (value + (mine_o[rows, :].astype(F32) + theirs_o[rows, :].astype(F32))).astype(BF)
+        out.start(0, step)
         grad = mine_g[rows, :].astype(F32) + theirs_g[rows, :].astype(F32)
         unit, scale = normalise(value)
         gres = norm_back(unit, scale, norms[6:7, :], grad) + out_grad[rows, :].astype(F32)
         gres_ref[rows, :] = gres
+        out.start(1, step)
         sums_ref[0:8, :] += fold_rows(grad * unit)
         sums_ref[8:16, :] += fold_rows(grad)
         low = gres.astype(BF)
         low_all[rows, :] = low
         gmix_ref[rows, :] = nt(low, wo[...]).astype(BF)
+        out.start(2, step)
     chunks(tokens, close)
     gwo_ref[...] = tn(mixed[...], low_all[...]).astype(BF)
+    out.drain(tokens)
     drain(tokens, mine, theirs, sems)
     drain(tokens, mine_o, theirs_o, sems_o)
     drain(tokens, mine_g, theirs_g, sems_g)
 
 
-def feed_forward(mixed, wo, res, w1, w2, out_grad, norms):
+def feed_forward(devices, mixed, wo, res, w1, w2, out_grad, norms):
     tokens, features = out_grad.shape
     hidden = w2.shape[0]
-    outs = [((tokens, features), BF), ((tokens, features), F32), (mixed.shape, BF), ((hidden, features), BF),
-            ((hidden, features), BF), (wo.shape, BF), ((16, features), F32)]
-    wide = pltpu.VMEM((tokens, features), BF)
-    deep = pltpu.VMEM((tokens, hidden), BF)
-    return call(feed_forward_kernel, "feed_forward", [mixed, wo, res, w1, w2, out_grad, norms], 0, outs,
-                [wide, wide, wide, deep, deep, wide, wide, wide, wide, wide] + [pair_sems(tokens)] * 3, 3)
-
-
-def branch_back(first_in, second_in, dq, dk, dv, weights, gw_ref, mine_a, theirs_a, mine_b, theirs_b, sems_a, sems_b):
-    tokens, features = first_in.shape
-    cols = dq.shape[1]
-    greet_core()
-
+    part = ((devices // 4, 2 * hidden // devices, features), BF, "V")
+    wide = (tokens, features)
+    outs = [(wide, BF, "A"), (wide, F32, "A"), (mixed.shape, BF, "A")] + [part] * 4 + [
+        (wo.shape, BF, "V"), ((16, features), F32, "V")]
+    deep, narrow = pltpu.VMEM((tokens, hidden), BF), pltpu.VMEM(wide, BF)
+    scratch = [pltpu.VMEM(wide, F32), narrow, narrow, pltpu.VMEM(wide, F32), pltpu.VMEM(mixed.shape, BF),
+               pltpu.VMEM((2 * hidden, features), BF), narrow, narrow, narrow, deep, deep, narrow] + [narrow] * 4
+    scratch += [pair_sems(tokens)] * 3 + [pltpu.SemaphoreType.DMA((2,)), out_semaphores(3, tokens)]
+    return call(partial(feed_forward_kernel, devices), "feed_forward", [mixed, wo, res, w1, w2, out_grad, norms], "VVAVVAV",
+                outs, scratch, 3)
+
+
+def branch_give(dq, dk, dv, weights, mine_a, theirs_a, mine_b, theirs_b, sems_a, sems_b):
     def give(step, rows):
         mine_a[rows, :] = nt(dq[rows, :], weights[0]).astype(BF)
         other_core(mine_a, theirs_a, sems_a, step).start()
         mine_b[rows, :] = (nt(dk[rows, :], weights[1]) + nt(dv[rows, :], weights[2])).astype(BF)
         other_core(mine_b, theirs_b, sems_b, step).start()
-    chunks(tokens, give)
-    order = interleave(features)
+    chunks(dq.shape[0], give)
+
+
+def branch_weights(first_in, second_in, dq, dk, dv, flat):
+    cols = dq.shape[1]
+    order = interleave(first_in.shape[1])
     for number, (entering, grad) in enumerate(((first_in, dq), (second_in, dk), (second_in, dv))):
-        gw_ref[number * cols:(number + 1) * cols, :] = as_units(tn(entering[...], grad[...]), order)
-
-
-def cross_back_kernel(dq, dk, dv, wc, nc, memory, res, gres, mixed, wo, norms,
-                      gmem_ref, gnew_ref, gmix_ref, gw_ref, gwo_ref, sums_ref,
-                      mine_a, theirs_a, mine_b, theirs_b, low_all, sems_a, sems_b):
+        flat[number * cols:(number + 1) * cols, :] = as_units(tn(entering[...], grad[...]), order)
+
+
+def z_sum_start(devices, places, pieces, landed, sems):
+    me, x, y, z, xpeer, ypeer, order, ahead, behind = places
+    return [send(pieces.at[lax.rem(z + d, devices // 4)], landed.at[d], sems.at[0, d], sems.at[1, d], dp=ahead(d)) for d in order]
+
+
+def z_sum_end(places, pieces, landed, copies):
+    z, order = places[3], places[6]
+    total = pieces[z].astype(F32)
+    for copy, d in zip(copies, order):
+        copy.wait_recv()
+        total = total + landed[d].astype(F32)
+    return total.astype(BF)
+
+
+def four_sum(parts, at):
+    return (parts[0][at].astype(F32) + parts[1][at].astype(F32) + parts[2][at].astype(F32) + parts[3][at].astype(F32)).astype(BF)
+
+
+def cross_back_kernel(devices, dq, dk, dv, wc, nc_hbm, memory_hbm, res_hbm, gres_hbm, mixed, wo, norms, gwo_cross,
+                      part0, part1, part2, part3,
+                      gmem_out, gnew_out, gmix_out, give0, give1, give2, give3, sums_ref,
+                      nc, memory, res, gres, gmem_ref, gnew_ref, gmix_ref, flat, pieces, landed, blocks,
+                      mine_a, theirs_a, mine_b, theirs_b, low_all, sems_a, sems_b, late_sems, out_sems, z_sems, zz_sems):
     tokens, features = nc.shape
-    branch_back(nc, memory, dq, dk, dv, wc, gw_ref, mine_a, theirs_a, mine_b, theirs_b, sems_a, sems_b)
+    cols = dq.shape[1]
+    across = devices // 4
+    places = places_of(devices)
+    me, x, y, z, xpeer, ypeer, order, ahead, behind = places
+    late = Late([(nc_hbm, nc), (memory_hbm, memory), (res_hbm, res), (gres_hbm, gres)], late_sems)
+    out = Out([(gmem_ref, gmem_out), (gnew_ref, gnew_out), (gmix_ref, gmix_out)], out_sems)
+    for level in range(across):
+        pieces[level] = four_sum((part0, part1, part2, part3), level)
+    greet([{"head": 1 - lax.axis_index("head")}] + [{"dp": ahead(d)} for d in order])
+    z_copies = z_sum_start(devices, places, pieces, landed, z_sems)
+    branch_give(dq, dk, dv, wc, mine_a, theirs_a, mine_b, theirs_b, sems_a, sems_b)
+    late.wait(0, 1)
+    branch_weights(nc, memory, dq, dk, dv, flat)
+    blocks[0] = z_sum_end(places, pieces, landed, z_copies)
+    zz_copies = [send(blocks.at[0], blocks.at[d], zz_sems.at[0, d], zz_sems.at[1, d], dp=ahead(d)) for d in order]
     sums_ref[...] = jnp.zeros_like(sums_ref)
+    late.wait(2, 3)
 
     def close(step, rows):
         other_core(mine_a, theirs_a, sems_a, step).wait_recv()
@@ -756,82 +880,186 @@
         unit, scale = normalise(res[rows, :])
         gnew = norm_back(unit, scale, norms[4:5, :], grad) + gres[rows, :]
         gnew_ref[rows, :] = gnew
+        out.start(1, step)
         sums_ref[0:8, :] += fold_rows(grad * unit)
         sums_ref[8:16, :] += fold_rows(grad)
         low = gnew.astype(BF)
         low_all[rows, :] = low
         gmix_ref[rows, :] = nt(low, wo[...]).astype(BF)
+        out.start(2, step)
         other_core(mine_b, theirs_b, sems_b, step).wait_recv()
         gmem_ref[rows, :] = (mine_b[rows, :].astype(F32) + theirs_b[rows, :].astype(F32)).astype(BF)
+        out.start(0, step)
     chunks(tokens, close)
-    gwo_ref[...] = tn(mixed[...], low_all[...]).astype(BF)
+    flat[3 * cols:4 * cols, :] = tn(mixed[...], low_all[...]).astype(BF)
+    flat[4 * cols:5 * cols, :] = gwo_cross[...]
+    if flat.shape[0] > 5 * cols:
+        flat[5 * cols:, :] = jnp.zeros((flat.shape[0] - 5 * cols, features), BF)
+    gives = (give0, give1, give2, give3)
+    spread_flat(devices, places, flat, gives)
+    for copy in zz_copies:
+        copy.wait_recv()
+    ready_rows = blocks.shape[1]
+    for ref in gives:
+        for d in range(across):
+            ref[d, 0:ready_rows, :] = blocks[d]
+    for copy in z_copies + zz_copies:
+        copy.wait_send()
+    out.drain(tokens)
     drain(tokens, mine_a, theirs_a, sems_a)
     drain(tokens, mine_b, theirs_b, sems_b)
 
 
-def cross_back(dq, dk, dv, wc, nc, memory, res, gres, mixed, wo, norms):
+def cross_back(devices, dq, dk, dv, wc, nc, memory, res, gres, mixed, wo, norms, gwo_cross, parts):
     tokens, features = nc.shape
     cols = dq.shape[1]
-    outs = [((tokens, features), BF), ((tokens, features), F32), (dq.shape, BF), ((3 * cols, features), BF),
-            (wo.shape, BF), ((16, features), F32)]
-    wide = pltpu.VMEM((tokens, features), BF)
-    return call(cross_back_kernel, "cross_back", [dq, dk, dv, wc, nc, memory, res, gres, mixed, wo, norms], 0, outs,
-                [wide] * 5 + [pair_sems(tokens)] * 2, 4)
-
-
-def self_back_kernel(dq, dk, dv, ws, nq, nkv, query, kv, gres, norms, sums_c, sums_f,
-                     gquery_ref, gkv_ref, gw_ref, gnorm_ref,
-                     mine_a, theirs_a, mine_b, theirs_b, sums, sems_a, sems_b):
+    across, ready_rows = devices // 4, parts[0].shape[1]
+    flat_rows = -(-5 * cols // (devices * UNIT)) * devices * UNIT
+    give = ((across, ready_rows + flat_rows // devices, features), BF, "V")
+    wide = (tokens, features)
+    outs = [(wide, BF, "A"), (wide, F32, "A"), (dq.shape, BF, "A")] + [give] * 4 + [((16, features), F32, "V")]
+    low, high = pltpu.VMEM(wide, BF), pltpu.VMEM(wide, F32)
+    small = pltpu.VMEM((across, ready_rows, features), BF)
+    z_sems = pltpu.SemaphoreType.DMA((2, across))
+    scratch = [low, low, high, high, low, high, pltpu.VMEM(dq.shape, BF), pltpu.VMEM((flat_rows, features), BF), small, small, small]
+    scratch += [low] * 5 + [pair_sems(tokens)] * 2 + [pltpu.SemaphoreType.DMA((4,)), out_semaphores(3, tokens), z_sems, z_sems]
+    return call(partial(cross_back_kernel, devices), "cross_back",
+                [dq, dk, dv, wc, nc, memory, res, gres, mixed, wo, norms, gwo_cross] + parts, "VVVVAAAAVVVVVVVV", outs, scratch, 4)
+
+
+def self_back_kernel(devices, ready_rows, dq, dk, dv, ws, nq_hbm, nkv_hbm, query_hbm, kv_hbm, gres_hbm, norms, sums_c, sums_f,
+                     part0, part1, part2, part3,
+                     gquery_out, gkv_out, summed, gnorm_ref,
+                     nq, nkv, query, kv, gres, gquery_ref, gkv_ref, flat, source, pieces, landed, norm_mine, norm_all,
+                     mine_a, theirs_a, mine_b, theirs_b, sums, sems_a, sems_b, late_sems, out_sems, z_sems, n_sems, *block_refs):
     tokens, features = nq.shape
-    branch_back(nq, nkv, dq, dk, dv, ws, gw_ref, mine_a, theirs_a, mine_b, theirs_b, sems_a, sems_b)
+    across = devices // 4
+    places = places_of(devices)
+    me, x, y, z, xpeer, ypeer, order, ahead, behind = places
+    late = Late([(nq_hbm, nq), (nkv_hbm, nkv), (query_hbm, query), (kv_hbm, kv), (gres_hbm, gres)], late_sems)
+    out = Out([(gquery_ref, gquery_out), (gkv_ref, gkv_out)], out_sems)
+    more_rows = part0.shape[1] - ready_rows
+    for level in range(across):
+        pieces[level] = four_sum((part0, part1, part2, part3), (level, pl.ds(ready_rows, more_rows)))
+    others = [lax.rem(me + d, devices) for d in range(1, devices)]
+    greet([{"head": 1 - lax.axis_index("head")}] + [{"dp": other} for other in others])
+    z_copies = z_sum_start(devices, places, pieces, landed, z_sems)
+    branch_give(dq, dk, dv, ws, mine_a, theirs_a, mine_b, theirs_b, sems_a, sems_b)
+    late.wait(0, 1)
+    branch_weights(nq, nkv, dq, dk, dv, flat)
+    rows = source.shape[1]
+    if flat.shape[0] > 3 * dq.shape[1]:
+        flat[3 * dq.shape[1]:, :] = jnp.zeros((flat.shape[0] - 3 * dq.shape[1], features), BF)
+    for block in range(devices):
+        source[block] = flat[block * rows:(block + 1) * rows, :]
+    block_sum = BlockSum(devices, places, source, summed, *block_refs[:7])
+    block_sum.start()
+    summed[me, pl.ds(rows, more_rows), :] = z_sum_end(places, pieces, landed, z_copies)
     sums[...] = jnp.zeros_like(sums)
+    late.wait(2, 3, 4)
 
     def close(step, rows):
         other_core(mine_a, theirs_a, sems_a, step).wait_recv()
         grad = mine_a[rows, :].astype(F32) + theirs_a[rows, :].astype(F32)
         unit, scale = normalise(query[rows, :].astype(F32))
         gquery_ref[rows, :] = (norm_back(unit, scale, norms[0:1, :], grad) + gres[rows, :]).astype(BF)
+        out.start(0, step)
         sums[0:8, :] += fold_rows(grad * unit)
         sums[8:16, :] += fold_rows(grad)
         other_core(mine_b, theirs_b, sems_b, step).wait_recv()
         grad = mine_b[rows, :].astype(F32) + theirs_b[rows, :].astype(F32)
         unit, scale = normalise(kv[rows, :].astype(F32))
         gkv_ref[rows, :] = norm_back(unit, scale, norms[2:3, :], grad).astype(BF)
+        out.start(1, step)
         sums[16:24, :] += fold_rows(grad * unit)
         sums[24:32, :] += fold_rows(grad)
     chunks(tokens, close)
     parts = [sums[8 * i:8 * i + 8, :] for i in range(4)]
     parts += [sums_c[0:8, :], sums_c[8:16, :], sums_f[0:8, :], sums_f[8:16, :]]
-    vectors = [jnp.sum(part, 0, keepdims=True) for part in parts]
-    gnorm_ref[...] = jnp.concatenate(vectors + [jnp.zeros((8, features), F32)], 0).astype(BF)
+    norm_mine[...] = jnp.concatenate([jnp.sum(part, 0, keepdims=True) for part in parts], 0)
+    n_copies = [send(norm_mine, norm_all.at[d], n_sems.at[0, d], n_sems.at[1, d], dp=other)
+                for d, other in zip(range(1, devices), others)]
+    block_sum.finish()
+    spread_blocks(devices, summed, summed.shape[1], places, *block_refs[7:])
+    total = norm_mine[...]
+    for d, copy in zip(range(1, devices), n_copies):
+        copy.wait_recv()
+        total = total + norm_all[d]
+    gnorm_ref[...] = total
+    block_sum.drain()
+    for copy in z_copies + n_copies:
+        copy.wait_send()
+    out.drain(tokens)
     drain(tokens, mine_a, theirs_a, sems_a)
     drain(tokens, mine_b, theirs_b, sems_b)
 
 
-def self_back(dq, dk, dv, ws, nq, nkv, query, kv, gres, norms, sums_c, sums_f):
+def self_back(devices, ready_rows, dq, dk, dv, ws, nq, nkv, query, kv, gres, norms, sums_c, sums_f, parts):
     tokens, features = nq.shape
     cols = dq.shape[1]
-    outs = [((tokens, features), BF), ((tokens, features), BF), ((3 * cols, features), BF), ((16, features), BF)]
-    wide = pltpu.VMEM((tokens, features), BF)
-    return call(self_back_kernel, "self_back", [dq, dk, dv, ws, nq, nkv, query, kv, gres, norms, sums_c, sums_f], 0, outs,
-                [wide] * 4 + [pltpu.VMEM((32, features), F32)] + [pair_sems(tokens)] * 2, 5)
-
-
-def update_kernel(owner_ref, me_ref, summed, master, first, second, grad_ref, first_ref, second_ref, new_ref, held):
+    across, more_rows = devices // 4, parts[0].shape[1] - ready_rows
+    flat_rows = -(-3 * cols // (devices * UNIT)) * devices * UNIT
+    rows = flat_rows // devices
+    wide = (tokens, features)
+    outs = [(wide, BF, "A"), (wide, BF, "A"), ((devices, rows + more_rows, features), BF, "V"), ((8, features), F32, "V")]
+    low, high = pltpu.VMEM(wide, BF), pltpu.VMEM(wide, F32)
+    small = pltpu.VMEM((across, more_rows, features), BF)
+    D = pltpu.SemaphoreType.DMA
+    scratch = [low, low, low, low, high, low, low, pltpu.VMEM((flat_rows, features), BF), pltpu.VMEM((devices, rows, features), BF),
+               small, small, pltpu.VMEM((8, features), F32), pltpu.VMEM((devices, 8, features), F32)]
+    scratch += [low] * 4 + [pltpu.VMEM((32, features), F32)] + [pair_sems(tokens)] * 2
+    scratch += [D((5,)), out_semaphores(2, tokens), D((2, across)), D((2, devices))]
+    scratch += block_sum_scratch(devices, rows, features) + [D((2, across))] * 5
+    return call(partial(self_back_kernel, devices, ready_rows), "self_back",
+                [dq, dk, dv, ws, nq, nkv, query, kv, gres, norms, sums_c, sums_f] + parts, "VVVVAAAAAVVVVVVV", outs, scratch, 5)
+
+
+def update_kernel(devices, early_unit, late_unit, own_rows, last_rows, owner_ref, me_ref, summed, part0, part1, part2, part3,
+                  master, first, second, gquery_in, gkv_in, grad_ref, first_ref, second_ref, new_ref, gquery_out, gkv_out,
+                  held, taken, held_q, held_kv, sems):
     units = owner_ref.shape[0]
     slots = master.shape[0]
+    across = devices // 4
+    more_rows = summed.shape[1] - own_rows
     me = me_ref[0]
+    entering = Late([(gquery_in, held_q), (gkv_in, held_kv)], sems.at[0])
+    here, level = lax.rem(me, 4), lax.div(me, 4)
 
     def find(u, count):
         held[count] = u
         return count + (owner_ref[u] == me).astype(jnp.int32)
     count = lax.fori_loop(0, units, find, jnp.int32(0), unroll=4)
+    entering.wait(0, 1)
+    leaving = Late([(held_q, gquery_out), (held_kv, gkv_out)], sems.at[1])
+
+    def rows_of(row, size, start):
+        return pl.ds(pl.multiple_of(lax.rem(row, size) + start, UNIT), UNIT)
 
     def one(slot, carry):
         @pl.when(slot < count)
         def _():
             unit = held[slot]
-            gradient = summed[pl.ds(pl.multiple_of(unit * UNIT, UNIT), UNIT), :].astype(F32)
+
+            @pl.when(unit < early_unit)
+            def _():
+                row = unit * UNIT
+                taken[...] = summed[lax.div(row, own_rows), rows_of(row, own_rows, 0), :]
+
+            @pl.when((unit >= early_unit) & (unit < late_unit))
+            def _():
+                row = (unit - early_unit) * UNIT
+                taken[...] = summed[lax.div(row, more_rows), rows_of(row, more_rows, own_rows), :]
+
+            @pl.when(unit >= late_unit)
+            def _():
+                row = (unit - late_unit) * UNIT
+                block = lax.div(row, last_rows)
+                behind = lax.rem(level - lax.div(block, 4) + across, across)
+                for f, part in enumerate((part0, part1, part2, part3)):
+                    @pl.when(lax.rem(block, 4) == here ^ f)
+                    def _():
+                        taken[...] = part[behind, rows_of(row, last_rows, 0), :]
+            gradient = taken[...].astype(F32)
             first_new, second_new, weight = adamw_step(gradient, first[slot], second[slot], master[slot], RATE_MATRIX, WEIGHT_DECAY)
             grad_ref[slot] = gradient
             first_ref[slot] = first_new
@@ -844,12 +1072,15 @@
                 ref[slot] = jnp.zeros(ref.shape[1:], F32)
         return carry
     lax.fori_loop(0, slots, one, 0)
-
-
-def update(unit_owner, me, summed, master, first, second):
-    outs = [(master.shape, F32)] * 4
-    return call(update_kernel, "update", [unit_owner, me, summed, master, first, second], 2, outs,
-                [pltpu.SMEM((unit_owner.shape[0] + 8,), jnp.int32)])
+    leaving.wait(0, 1)
+
+
+def update(devices, early_unit, late_unit, own_rows, last_rows, unit_owner, me, summed, parts, master, first, second, gquery, gkv):
+    outs = [(master.shape, F32, "V")] * 4 + [(gquery.shape, BF, "A")] * 2
+    kernel = partial(update_kernel, devices, early_unit, late_unit, own_rows, last_rows)
+    return call(kernel, "update", [unit_owner, me, summed] + parts + [master, first, second, gquery, gkv], "SSVVVVVVVVAA", outs,
+                [pltpu.SMEM((unit_owner.shape[0] + 8,), jnp.int32), pltpu.VMEM((UNIT, master.shape[2]), BF),
+                 pltpu.VMEM(gquery.shape, BF), pltpu.VMEM(gkv.shape, BF), pltpu.SemaphoreType.DMA((2, 2))])
 
 
 def adamw_step(gradient, first, second, weight, rate, decay):
@@ -874,9 +1105,9 @@
     cols = features // shards
     hidden = (units * unit_rows - 8 * cols) // 2
 
-    own = master.astype(BF).reshape(slots * unit_rows, features)
-    norm_row = jnp.pad(norm_master.astype(BF).reshape(1, norm_share), ((0, UNIT - 1), (0, features - norm_share)))
-    gathered = gather_blocks(jnp.concatenate([own, norm_row], 0), devices)
+    shape = (slots, unit_rows, features)
+    norm_row = jnp.pad(norm_master.reshape(1, norm_share), ((0, 0), (0, features - norm_share)))
+    gathered = gather_blocks(master.reshape(slots * unit_rows, features), norm_row, devices)
     norms = gathered[:, slots * unit_rows, :norm_share].reshape(8, features).astype(F32)
 
     rank_row, count_row = obs_rank.reshape(1, ROW), obs_count.reshape(1, ROW)
@@ -885,27 +1116,31 @@
     mixed_self, total_self = attend_forward(lengths, q, k, v, rank_row, count_row, True)
     residual, nc, qc = self_out(mixed_self, wo_self, query_stream, wc, norms)
     mixed_cross, total_cross = attend_forward(lengths, qc, kc, vc, rank_row, count_row, False)
-    output, grad_cross_res, grad_mixed, gw1, gw2, gwo_cross, sums_f = feed_forward(
-        mixed_cross, wo_cross, residual, w1, w2, out_grad, norms)
-    dq, dk, dv = attend_backward(lengths, qc, kc, vc, grad_mixed, mixed_cross, total_cross, rank_row, count_row, False)
-    grad_memory, grad_residual, grad_mixed, gw_cross, gwo_self, sums_c = cross_back(
-        dq, dk, dv, wc, nc, memory, residual, grad_cross_res, mixed_self, wo_self, norms)
-    dq, dk, dv = attend_backward(lengths, q, k, v, grad_mixed, mixed_self, total_self, rank_row, count_row, True)
-    grad_query, grad_kv, gw_self, gnorm = self_back(
-        dq, dk, dv, ws, nq, nkv, query_stream, kv_stream, grad_residual, norms, sums_c, sums_f)
-
-    pieces = [gw_self, gw_cross, gwo_self, gwo_cross, gw1, gw2, gnorm]
-    used = units * unit_rows + UNIT
-    whole = -(-used // (devices * 2 * UNIT)) * (devices * 2 * UNIT)
-    flat = jnp.concatenate(pieces + [jnp.zeros((whole - used, features), BF)], 0)
-    summed = reduce_blocks(flat, devices)
-    shape = (slots, unit_rows, features)
+    output, grad_cross_res, grad_mixed, *parts, gwo_cross, sums_f = feed_forward(
+        devices, mixed_cross, wo_cross, residual, w1, w2, out_grad, norms)
+    tie = lax.optimization_barrier
+    ready_rows = parts[0].shape[1]
+    parts = [parts[0]] + [plane_swap(parts[f], devices, f) for f in (1, 2, 3)]
+    dq, dk, dv, output = attend_backward(
+        lengths, qc, kc, vc, grad_mixed, mixed_cross, total_cross, rank_row, count_row, output, False)
+    parts, dq = tie((parts, dq))
+    grad_memory, grad_residual, grad_mixed, *parts, sums_c = cross_back(
+        devices, dq, dk, dv, wc, nc, memory, residual, grad_cross_res, mixed_self, wo_self, norms, gwo_cross, parts)
+    parts = [parts[0]] + [plane_swap(parts[f], devices, f) for f in (1, 2, 3)]
+    dq, dk, dv, grad_memory = attend_backward(
+        lengths, q, k, v, grad_mixed, mixed_self, total_self, rank_row, count_row, grad_memory, True)
+    parts, dq = tie((parts, dq))
+    grad_query, grad_kv, summed, norm_grads = self_back(
+        devices, ready_rows, dq, dk, dv, ws, nq, nkv, query_stream, kv_stream, grad_residual, norms, sums_c, sums_f, parts)
+
+    early, late = 3 * cols // unit_rows, 8 * cols // unit_rows
+    own_rows = -(-3 * cols // (devices * UNIT)) * UNIT
+    weight_grad, weight_first, weight_second, weight_new, grad_query, grad_kv = update(
+        devices, early, late, own_rows, ready_rows, unit_owner, me.reshape(1), summed, parts, master.reshape(shape),
+        first_moment.reshape(shape), second_moment.reshape(shape), grad_query, grad_kv)
     weight_grad, weight_first, weight_second, weight_new = [
-        part.reshape(master.shape)
-        for part in update(unit_owner, me.reshape(1), summed, master.reshape(shape), first_moment.reshape(shape),
-                           second_moment.reshape(shape))]
-    norm_grads = summed[units * unit_rows:units * unit_rows + 8].reshape(-1).astype(F32)
-    norm_grad = lax.dynamic_slice_in_dim(norm_grads, me * norm_share, norm_share)
+        part.reshape(master.shape) for part in (weight_grad, weight_first, weight_second, weight_new)]
+    norm_grad = lax.dynamic_slice_in_dim(norm_grads.reshape(-1), me * norm_share, norm_share)
     norm_first_new, norm_second_new, norm_new = adamw_step(
         norm_grad, norm_first, norm_second, norm_master, RATE_NORM, 0.0)
     return (

time: 466 us -> 395 us (0.85)
  Pallas kernels: 450 us -> 379 us
  starting transfers between devices: 0 us -> 8.03 us
  local copies, waits for them, and re-layouts: 9.88 us -> 5.12 us
    pallas_call x2 -> x0, Pallas kernels: 197 us -> none  [the longest x1 113 us: reduce_blocks(): pl.pallas_call(partial(reduce_kernel, count), out_shape=jax.ShapeDtypeStr...]
    pallas_call x6 -> x7, Pallas kernels: 126 us -> 248 us  [call(): pl.pallas_call(kernel, out_shape=tuple((jax.ShapeDtypeStruct(shape, dtype...]
    ppermute x0 -> x6, starting transfers between devices: none -> 8.03 us  [plane_swap(): lax.ppermute(value, 'dp', [(i, i // 4 * 4 + (i % 4 ^ f)) for i in range(c...]
    unnamed x40 -> x19, local copies, waits for them, and re-layouts: 9.24 us -> 3.25 us
  transfers between devices with their start and end apart: 0 -> 6, of which waited for: 0 -> 0; matrix products, arithmetic and copies ran while one was open for 0% -> 0% of each run, Pallas kernels for 0% -> 20%
where the time goes in v3:
time: 395 us
  Pallas kernels  379 us (96%)
  starting transfers between devices  8.03 us (2%)
  local copies, waits for them, and re-layouts  5.12 us (1%)
    pallas_call x7, Pallas kernels, call(): pl.pallas_call(kernel, out_shape=tuple((jax.ShapeDtypeStruct(shape, dtype...  248 us
    pallas_call x2, Pallas kernels, attend_backward(): pl.pallas_call(partial(attn_bwd_kernel, with_seen, heads), out_shape=(lik...  79.5 us
    pallas_call x2, Pallas kernels, attend_forward(): pl.pallas_call(partial(attn_fwd_kernel, with_seen, heads), out_shape=(jax...  52 us
    ppermute x6, starting transfers between devices, plane_swap(): lax.ppermute(value, 'dp', [(i, i // 4 * 4 + (i % 4 ^ f)) for i in range(c...  8.03 us
  transfers between devices with their start and end apart: 6, of which 0 were waited for; matrix products, arithmetic and copies ran while one was open for 0% of the time, Pallas kernels for 20%

profile of v3, /device:TPU:0, one launch (start us, length us, event | category | flops | bytes accessed | tf_op | source)
XLA Modules:
  0.0 394.8 jit_solution(6118411623045869303)
XLA Ops:
  0.6 1.3 pad.4.norm
  1.9 83.6 %gather_units.1.gathered = bf16[16,528,512]{2,1,0:T(8,128)(2,1)} custom-call(f32[512,512]{1,0:T(8,128)} %bitcast.25, f32[1,512]{1,0:T(1,128)} %pad.4.norm), custom_call_target="tpu_custom_call" | custom-call | flops 40000000000 | bytes 16777216 | tf_op jit(solution)/shard_map/gather_units/pallas_call | solution.py:491
  85.5 0.9 convert_reduce_fusion
  86.4 0.6 reshape.78.norms
  87.0 15.9 %project.1 = (bf16[2048,512]{1,0:T(8,128)(2,1)}, bf16[2048,512]{1,0:T(8,128)(2,1)}, bf16[2048,256]{1,0:T(8,128)(2,1)}, bf16[2048,256]{1,0:T(8,128)(2,1)}, bf16[2...) custom-call(s32[256]{0:T(256)} %owner_ref.3, ...), custom_call_target="tpu_custom_call" | custom-call | flops 40000000000 | bytes 16777216 | tf_op jit(solution)/shard_map/project/pallas_call | solution.py:491
  103.0 26.7 %attend_self_forward.1 = (bf16[2048,256]{1,0:T(8,128)(2,1)}, f32[8,2048]{1,0:T(8,128)}) custom-call(s32[1,32]{1,0:T(1,128)} %len_ref.7, bf16[2048,256]{1,0:T(8,128)(2,1)} %get-tuple-element.77.q_ref, bf16[2048,256]{1,0:T(8,128)(2,1)} %get-tuple-element.78.k_ref, bf16[2048,256]{1,0:T(8,128)(2,1)} %get-tuple-element.79.v_ref, s32[1,2048]{1,0:T(1,128)} %bitcast.29, ...), custom_call_target="tpu_custom_call" | custom-call | flops 40000000000 | bytes 16777216 | tf_op jit(solution)/shard_map/attend_self_forward/pallas_call | solution.py:174
  129.6 7.9 %self_out.1 = (f32[2048,512]{1,0:T(8,128)}, bf16[2048,512]{1,0:T(8,128)(2,1)}, bf16[2048,256]{1,0:T(8,128)(2,1)}) custom-call(bf16[2048,256]{1,0:T(8,128)(2,1)} %get-tuple-element.80.mixed.o_ref, bf16[256,512]{1,0:T(8,128)(2,1)} %get-tuple-element.81.wo, bf16[2048,512]{1,0:T(8,128)(2,1)} %query_hbm.5, bf16[3,512,256]{2,1,0:T(8,128)(2,1)} %get-tuple-element.82.wc, ...), custom_call_target="tpu_custom_call" | custom-call | flops 40000000000 | bytes 16777216 | tf_op jit(solution)/shard_map/self_out/pallas_call | solution.py:491
  137.5 25.4 %attend_cross_forward.1 = (bf16[2048,256]{1,0:T(8,128)(2,1)}, f32[8,2048]{1,0:T(8,128)}) custom-call(s32[1,32]{1,0:T(1,128)} %len_ref.7, bf16[2048,256]{1,0:T(8,128)(2,1)} %get-tuple-element.83.q_ref, bf16[2048,256]{1,0:T(8,128)(2,1)} %get-tuple-element.84.k_ref, bf16[2048,256]{1,0:T(8,128)(2,1)} %get-tuple-element.85.v_ref, s32[1,2048]{1,0:T(1,128)} %bitcast.30, ...), custom_call_target="tpu_custom_call" | custom-call | flops 40000000000 | bytes 16777216 | tf_op jit(solution)/shard_map/attend_cross_forward/pallas_call | solution.py:174
  162.9 36.8 %feed_forward.1 = (bf16[2048,512]{1,0:T(8,128)(2,1)}, f32[2048,512]{1,0:T(8,128)}, bf16[2048,256]{1,0:T(8,128)(2,1)}, bf16[4,128,512]{2,1,0:T(8,128)(2,1)}, bf16...) custom-call(bf16[2048,256]{1,0:T(8,128)(2,1)} %get-tuple-element.86., ...), custom_call_target="tpu_custom_call" | custom-call | flops 40000000000 | bytes 16777216 | tf_op jit(solution)/shard_map/feed_forward/pallas_call | solution.py:491
  199.6 0.6 collective-permute-start
  200.2 2.8 collective-permute-start.1
  203.1 0.1 collective-permute-start.2
  203.2 38.7 %attend_cross_backward.1 = (bf16[2048,256]{1,0:T(8,128)(2,1)}, bf16[2048,256]{1,0:T(8,128)(2,1)}, bf16[2048,256]{1,0:T(8,128)(2,1)}, bf16[2048,512]{1,0:T(8,128)(2,1)}) custom-call(s32[1,32]{1,0:T(1,128)} %len_ref.7, bf16[2048,256]{1,0:T(8,128)(2,1)} %get-tuple-element.83.q_ref, bf16[2048,256]{1,0:T(8,128)(2,1)} %get-tuple-element.84.k_ref, ...), custom_call_target="tpu_custom_call" | custom-call | flops 40000000000 | bytes 16777216 | tf_op jit(solution)/shard_map/attend_cross_backward/pallas_call | solution.py:293
  241.9 0.0 collective-permute-done.part1
  241.9 0.0 copy-start.6
  242.0 0.0 collective-permute-done.1.part2
  242.0 0.0 copy-start.7
  242.0 0.0 collective-permute-done.2.part3
  242.0 0.0 copy-start.8
  242.0 0.7 copy-done.6
  242.7 0.2 copy-done.7
  242.9 0.2 copy-done.8
  243.1 35.5 %cross_back.1 = (bf16[2048,512]{1,0:T(8,128)(2,1)}, f32[2048,512]{1,0:T(8,128)}, bf16[2048,256]{1,0:T(8,128)(2,1)}, bf16[4,208,512]{2,1,0:T(8,128)(2,1)}, bf16[4...) custom-call(bf16[2048,256]{1,0:T(8,128)(2,1)} %get-tuple-element.100.dq, ...), custom_call_target="tpu_custom_call" | custom-call | flops 40000000000 | bytes 16777216 | tf_op jit(solution)/shard_map/cross_back/pallas_call | solution.py:491
  278.6 0.7 collective-permute-start.3
  279.3 3.0 collective-permute-start.4
  282.3 0.8 collective-permute-start.5
  283.1 40.8 %attend_self_backward.1 = (bf16[2048,256]{1,0:T(8,128)(2,1)}, bf16[2048,256]{1,0:T(8,128)(2,1)}, bf16[2048,256]{1,0:T(8,128)(2,1)}, bf16[2048,512]{1,0:T(8,128)(2,1)}) custom-call(s32[1,32]{1,0:T(1,128)} %len_ref.7, bf16[2048,256]{1,0:T(8,128)(2,1)} %get-tuple-element.77.q_ref, bf16[2048,256]{1,0:T(8,128)(2,1)} %get-tuple-element.78.k_ref, ...), custom_call_target="tpu_custom_call" | custom-call | flops 40000000000 | bytes 16777216 | tf_op jit(solution)/shard_map/attend_self_backward/pallas_call | solution.py:293
  323.9 0.0 collective-permute-done.3.part1
  323.9 0.0 copy-start.3
  323.9 0.0 collective-permute-done.4.part2
  323.9 0.0 copy-start.4
  323.9 0.0 collective-permute-done.5.part3
  323.9 0.0 copy-start.5
  324.0 0.9 copy-done.3
  324.8 0.3 copy-done.4
  325.1 0.2 copy-done.5
  325.4 0.0 copy-start
  325.4 0.0 copy-start.1
  325.4 0.0 copy-start.2
  325.4 58.0 %self_back.1 = (bf16[2048,512]{1,0:T(8,128)(2,1)}, bf16[2048,512]{1,0:T(8,128)(2,1)}, bf16[16,128,512]{2,1,0:T(8,128)(2,1)}, f32[8,512]{1,0:T(8,128)}) custom-call(bf16[2048,256]{1,0:T(8,128)(2,1)} %get-tuple-element.118.dq, bf16[2048,256]{1,0:T(8,128)(2,1)} %get-tuple-element.119.dk, bf16[2048,256]{1,0:T(8,128)(2,1)} %get-tuple-element.120.dv, ...), custom_call_target="tpu_custom_call" | custom-call | flops 40000000000 | bytes 16777216 | tf_op jit(solution)/shard_map/self_back/pallas_call | solution.py:491
  383.4 0.7 copy.30
  384.1 0.0 copy-done
  384.1 0.0 copy-done.1
  384.1 0.0 copy-done.2
  384.1 0.7 multiply_subtract_fusion
  384.8 9.8 %update.1 = (f32[32,16,512]{2,1,0:T(8,128)}, f32[32,16,512]{2,1,0:T(8,128)}, f32[32,16,512]{2,1,0:T(8,128)}, f32[32,16,512]{2,1,0:T(8,128)}, bf16[2048,512]{1,0:T(8,128)(2,1)}, /*index=5*/bf16[2048,512]{1,0:T(8,128)(2,1)}) custom-call(s32[256]{0:T(256)} %owner_ref.3, s32[1]{0:T(128)} %bitcast.4.me_ref, bf16[16,128,512]{2,1,0:T(8,128)(2,1)} %get-tuple-element.131.summed, ...), custom_call_target="tpu_custom_call" | custom-call | flops 40000000000 | bytes 16777216 | tf_op jit(solution)/shard_map/update/pallas_call | solution.py:491
Async XLA Ops:
  199.6 42.3 %collective-permute-start = (bf16[4,128,512]{2,1,0:T(8,128)(2,1)}, bf16[4,128,512]{2,1,0:T(8,128)(2,1)S(1)}, u32[]{:S(2)}, u32[]{:S(2)}) collective-permute-start(bf16[4,128,512]{2,1,0:T(8,128)(2,1)} %get-tuple-element.96), channel_id=1, source_target_pairs={{0,2},{2,0},{4,6},{6,4},{8,10},{10,8},{12,14},{14,12},{16,18},{18,... | collective-permute-start | bytes 1572872 | tf_op jit(solution)/shard_map/ppermute | solution.py:480
  200.2 41.7 %collective-permute-start.1 = (bf16[4,128,512]{2,1,0:T(8,128)(2,1)}, bf16[4,128,512]{2,1,0:T(8,128)(2,1)S(1)}, u32[]{:S(2)}, u32[]{:S(2)}) collective-permute-start(bf16[4,128,512]{2,1,0:T(8,128)(2,1)} %get-tuple-element.97), channel_id=1, source_target_pairs={{0,4},{2,6},{4,0},{6,2},{8,12},{10,14},{12,8},{14,10},{16,20},{18,... | collective-permute-start | bytes 1572872 | tf_op jit(solution)/shard_map/ppermute | solution.py:480
  203.1 38.9 %collective-permute-start.2 = (bf16[4,128,512]{2,1,0:T(8,128)(2,1)}, bf16[4,128,512]{2,1,0:T(8,128)(2,1)S(1)}, u32[]{:S(2)}, u32[]{:S(2)}) collective-permute-start(bf16[4,128,512]{2,1,0:T(8,128)(2,1)} %get-tuple-element.98), channel_id=1, source_target_pairs={{0,6},{2,4},{4,2},{6,0},{8,14},{10,12},{12,10},{14,8},{16,22},{18,... | collective-permute-start | bytes 1572872 | tf_op jit(solution)/shard_map/ppermute | solution.py:480
  241.9 0.8 copy-start.6
  242.0 0.9 copy-start.7
  242.0 1.1 copy-start.8
  278.6 45.3 %collective-permute-start.3 = (bf16[4,208,512]{2,1,0:T(8,128)(2,1)}, bf16[4,208,512]{2,1,0:T(8,128)(2,1)S(1)}, u32[]{:S(2)}, u32[]{:S(2)}) collective-permute-start(bf16[4,208,512]{2,1,0:T(8,128)(2,1)} %get-tuple-element.111), channel_id=1, source_target_pairs={{0,2},{2,0},{4,6},{6,4},{8,10},{10,8},{12,14},{14,12},{16,18},{18,... | collective-permute-start | bytes 2555912 | tf_op jit(solution)/shard_map/ppermute | solution.py:480
  279.3 44.6 %collective-permute-start.4 = (bf16[4,208,512]{2,1,0:T(8,128)(2,1)}, bf16[4,208,512]{2,1,0:T(8,128)(2,1)S(1)}, u32[]{:S(2)}, u32[]{:S(2)}) collective-permute-start(bf16[4,208,512]{2,1,0:T(8,128)(2,1)} %get-tuple-element.112), channel_id=1, source_target_pairs={{0,4},{2,6},{4,0},{6,2},{8,12},{10,14},{12,8},{14,10},{16,20},{18,... | collective-permute-start | bytes 2555912 | tf_op jit(solution)/shard_map/ppermute | solution.py:480
  282.3 41.6 %collective-permute-start.5 = (bf16[4,208,512]{2,1,0:T(8,128)(2,1)}, bf16[4,208,512]{2,1,0:T(8,128)(2,1)S(1)}, u32[]{:S(2)}, u32[]{:S(2)}) collective-permute-start(bf16[4,208,512]{2,1,0:T(8,128)(2,1)} %get-tuple-element.113), channel_id=1, source_target_pairs={{0,6},{2,4},{4,2},{6,0},{8,14},{10,12},{12,10},{14,8},{16,22},{18,... | collective-permute-start | bytes 2555912 | tf_op jit(solution)/shard_map/ppermute | solution.py:480
  323.9 0.9 copy-start.3
  323.9 1.2 copy-start.4
  323.9 1.4 copy-start.5
  325.4 58.8 %copy-start = (f32[256]{0:T(256)S(1)}, f32[256]{0:T(256)}, u32[]{:S(2)}) copy-start(f32[256]{0:T(256)} %param.25) | copy-start | bytes 3076
  325.4 58.8 %copy-start.1 = (f32[256]{0:T(256)S(1)}, f32[256]{0:T(256)}, u32[]{:S(2)}) copy-start(f32[256]{0:T(256)} %param.27) | copy-start | bytes 3076
  325.4 58.8 %copy-start.2 = (f32[256]{0:T(256)S(1)}, f32[256]{0:T(256)}, u32[]{:S(2)}) copy-start(f32[256]{0:T(256)} %param.26) | copy-start | bytes 3076

commit v4 on v3

--- a/solution.py
+++ b/solution.py
@@ -26,16 +26,19 @@
 TQ = 256
 TK = 256
 FAR = 32768.0
+LANES = (64, 72, 80)
+
 
 def nt(a, b):
     return lax.dot_general(a, b, (((1,), (1,)), ((), ())), preferred_element_type=F32)
 
+
 def nn(a, b):
     return lax.dot_general(a, b, (((1,), (0,)), ((), ())), preferred_element_type=F32)
 
+
 def doc_bounds(len_ref):
-    starts = []
-    ends = []
+    starts, ends = [], []
     at = jnp.int32(0)
     for d in range(DOCS):
         starts.append(at)
@@ -43,17 +46,6 @@
         ends.append(at)
     return starts, ends
 
-def lane_vector(scalars):
-    lanes = lax.broadcasted_iota(jnp.int32, (1, 128), 1)
-    out = jnp.full((1, 128), -1, jnp.int32)
-    for d, value in enumerate(scalars):
-        out = jnp.where(lanes == d, value, out)
-    return out
-
-def doc_hot_rows(starts, ends, q0):
-    pos = lax.broadcasted_iota(jnp.int32, (1, TQ), 1) + q0
-    rows = [jnp.where((pos >= starts[d]) & (pos < ends[d]), FAR, 0.0) for d in range(DOCS)]
-    return jnp.concatenate(rows, 0)
 
 def key_range(starts, ends, q0):
     low = jnp.int32(0)
@@ -63,257 +55,264 @@
         high = jnp.where(starts[d] <= q0 + TQ - 1, ends[d], high)
     first = lax.div(low, 128) * 128
     steps = lax.div(high - first + TK - 1, TK)
-    return first, steps
-
-def head_lanes(pair_rows, h):
-    lanes = lax.broadcasted_iota(jnp.int32, pair_rows.shape, 1)
-    keep = (lanes < HEAD_DIM) if h % 2 == 0 else (lanes >= HEAD_DIM)
-    return jnp.where(keep, pair_rows, jnp.zeros_like(pair_rows))
-
-def doc_hot(start_lane, end_lane, at, rows):
-    pos = lax.broadcasted_iota(jnp.int32, (rows, 128), 0) + at
-    return (pos >= start_lane) & (pos < end_lane)
-
-def fill_keys(kaug, k_ref, start_lane, end_lane, heads, with_stats):
-    lanes = lax.broadcasted_iota(jnp.int32, (TK, 128), 1)
-    def one(t, c):
-        at = pl.multiple_of(t * TK, TK)
-        hot = doc_hot(start_lane, end_lane, at, TK)
-        base = jnp.where(hot | (lanes >= DOCS), 0.0, -FAR)
-        for h in range(heads):
-            pair = k_ref[pl.ds(at, TK), pl.ds(h // 2 * 128, 128)]
-            kaug[h, pl.ds(at, TK), 0:128] = (head_lanes(pair, h).astype(F32) * HEAD_DIM ** -0.5).astype(BF)
-            aug = base
-            if with_stats:
-                aug = jnp.where((lanes == 64 + h) | (lanes == 72 + h) | (lanes == 80 + h), -1.0, base)
-            kaug[h, pl.ds(at, TK), 128:256] = aug.astype(BF)
-        return c
-    lax.fori_loop(0, ROW // TK, one, 0)
-    for h in range(heads):
-        kaug[h, ROW:, 0:128] = jnp.zeros((TK, 128), BF)
-        kaug[h, ROW:, 128:256] = jnp.where(lanes < DOCS, -FAR, 0.0).astype(BF)
-
-def fill_ranks(rank_cols, rank_ref, starts):
+    return jnp.minimum(first, ROW - steps * TK), steps
+
+
+def mask_tables(len_ref, rank_ref, side_ref, hot_ref, rank_cols):
+    starts, ends = doc_bounds(len_ref)
+    lanes = lax.broadcasted_iota(jnp.int32, (1, 128), 1)
+    start_lane = jnp.full((1, 128), -1, jnp.int32)
+    end_lane = jnp.full((1, 128), -1, jnp.int32)
+    for d in range(DOCS):
+        start_lane = jnp.where(lanes == d, starts[d], start_lane)
+        end_lane = jnp.where(lanes == d, ends[d], end_lane)
+    one = (lanes == LANES[0]) | (lanes == LANES[1]) | (lanes == LANES[2])
+    for t in range(ROW // 256):
+        pos = lax.broadcasted_iota(jnp.int32, (256, 128), 0) + t * 256
+        hot = (pos >= start_lane) & (pos < end_lane)
+        side = jnp.where(hot | (lanes >= DOCS), jnp.where(one, -1.0, 0.0), -FAR)
+        side_ref[t * 256:(t + 1) * 256, :] = side.astype(BF)
     pos = lax.broadcasted_iota(jnp.int32, (1, ROW), 1)
     first = jnp.zeros((1, ROW), jnp.bool_)
+    rows = []
     for d in range(DOCS):
         first = first | (pos == starts[d])
+        rows.append(jnp.where((pos >= starts[d]) & (pos < ends[d]), FAR, 0.0))
+    hot_ref[...] = jnp.concatenate(rows + [jnp.zeros((128 - DOCS, ROW), F32)], 0).astype(BF)
     rank = jnp.where(first, -1.0, rank_ref[...].astype(F32))
     for t in range(ROW // 128):
-        block = jnp.broadcast_to(rank[:, t * 128:(t + 1) * 128], (128, 128))
-        rank_cols[t * 128:(t + 1) * 128, :] = block.T
-    rank_cols[ROW:, :] = jnp.zeros((TK, 128), F32)
-
-def seen_bias(rank_cols, count_row, k0, q0):
+        rank_cols[t * 128:(t + 1) * 128, :] = jnp.broadcast_to(rank[:, t * 128:(t + 1) * 128], (128, 128)).T
+
+
+STEPS = (ROW // TQ) * (ROW // TK) + 8
+
+
+def step_table(len_ref, table):
+    starts, ends = doc_bounds(len_ref)
+    idle = ROW // TQ
+
+    def put(at, tile, first):
+        table[0, at] = tile
+        table[1, at] = first
+    put(0, idle, ROW)
+    put(1, idle, ROW)
+    at = jnp.int32(2)
+    for tile in range(idle):
+        first, steps = key_range(starts, ends, tile * TQ)
+
+        def fill(s, at):
+            put(at, tile, first + s * TK)
+            return at + 1
+        at = lax.fori_loop(0, steps, fill, at)
+    put(at, idle, ROW)
+    put(at + 1, idle, ROW)
+    table[0, STEPS - 1] = at
+
+
+def step_of(table, i):
+    return table[0, i], pl.multiple_of(table[1, i], 128)
+
+
+def real_step(table, i):
+    return jnp.minimum(table[0, i], ROW // TQ - 1), pl.multiple_of(jnp.minimum(table[1, i], ROW - TK), 128)
+
+
+def seen_bias(rank_cols, counts, tile, k0):
     rank = rank_cols[pl.ds(k0, TK), :]
     rank = jnp.concatenate([rank] * (TQ // 128), 1)
     kpos = lax.broadcasted_iota(jnp.int32, (TK, TQ), 0)
     qpos = lax.broadcasted_iota(jnp.int32, (TK, TQ), 1)
-    off_diag = (kpos - qpos) != (q0 - k0)
-    allowed = (rank < count_row) & (off_diag | (rank < 0.0))
+    off_diag = (kpos - qpos) != (tile * TQ - k0)
+    allowed = (rank < counts[tile, 0:1, :]) & (off_diag | (rank < 0.0))
     return jnp.where(allowed, 0.0, -FAR * FAR)
 
-def attn_fwd_kernel(with_seen, heads, len_ref, q_ref, k_ref, v_ref, rank_ref, count_ref, o_ref, lse_ref,
-                    kaug, vt, rank_cols, acc, top, qt):
-    starts, ends = doc_bounds(len_ref)
-    start_lane, end_lane = lane_vector(starts), lane_vector(ends)
-    fill_keys(kaug, k_ref, start_lane, end_lane, heads, False)
-    for t in range(ROW // TK):
-        vt[:, :HEAD_DIM, t * TK:(t + 1) * TK] = v_ref[t * TK:(t + 1) * TK, :].T.reshape(heads, HEAD_DIM, TK)
-    vt[:, :HEAD_DIM, ROW:] = jnp.zeros((heads, HEAD_DIM, TK), BF)
-    vt[:, HEAD_DIM:, :] = jnp.ones((heads, 16, ROW + TK), BF)
+
+def count_tiles(counts, count_ref):
+    for tile in range(ROW // TQ):
+        counts[tile] = jnp.broadcast_to(count_ref[:, tile * TQ:(tile + 1) * TQ].astype(F32), (8, TQ))
+
+
+def query_columns(qt, qt_ref, side, tile, h, q0):
+    rows = qt_ref[h * HEAD_DIM:(h + 1) * HEAD_DIM, pl.ds(q0, TQ)].astype(F32) * HEAD_DIM ** -0.5
+    own, other = h % 2 * HEAD_DIM, (1 - h % 2) * HEAD_DIM
+    qt[tile, h, own:own + HEAD_DIM, :] = rows.astype(BF)
+    qt[tile, h, other:other + HEAD_DIM, :] = jnp.zeros((HEAD_DIM, TQ), BF)
+    qt[tile, h, 128:256, :] = side
+
+
+def pair_rows(ref, side_ref, h, k0):
+    return jnp.concatenate([ref[pl.ds(k0, TK), h // 2 * 128:(h // 2 + 1) * 128], side_ref[pl.ds(k0, TK), :]], 1)
+
+
+def attn_fwd_kernel(with_seen, heads, table, qt_ref, k_ref, vt_ref, side_ref, hot_ref, *refs):
     if with_seen:
-        fill_ranks(rank_cols, rank_ref, starts)
-
-    def one_q(t, c):
-        q0 = pl.multiple_of(t * TQ, TQ)
-        first, steps = key_range(starts, ends, q0)
-        hot = jnp.concatenate([doc_hot_rows(starts, ends, q0), jnp.zeros((128 - DOCS, TQ), F32)], 0).astype(BF)
-        for p in range(heads // 2):
-            qt[p, 0:128, :] = q_ref[pl.ds(q0, TQ), p * 128:(p + 1) * 128].T
-            qt[p, 128:256, :] = hot
-        count_row = count_ref[:, pl.ds(q0, TQ)].astype(F32)
-        acc[...] = jnp.zeros_like(acc)
-        top[...] = jnp.full_like(top, -jnp.inf)
-
-        def one_k(s, c):
-            k0 = pl.multiple_of(first + s * TK, 128)
-            bias = seen_bias(rank_cols, count_row, k0, q0) if with_seen else None
-            old = top[...]
-            scores = [nn(kaug[h, pl.ds(k0, TK), :], qt[h // 2]) for h in range(heads)]
-            if with_seen:
-                scores = [score + bias for score in scores]
-            vts = [vt[h, :, pl.ds(k0, TK)] for h in range(heads)]
-            accs = [acc[h] for h in range(heads)]
-            news, sums = [], []
-            for h in range(heads):
-                score = scores[h]
-                new = jnp.maximum(old[h:h + 1, :], jnp.max(score, 0, keepdims=True))
-                p = jnp.exp(score - new).astype(BF)
-                news.append(new)
-                sums.append(accs[h] * jnp.exp(old[h:h + 1, :] - new) + nn(vts[h], p))
-            for h in range(heads):
-                acc[h] = sums[h]
-            top[...] = jnp.concatenate(news + [old[heads:, :]], 0)
-            return c
-        lax.fori_loop(0, steps, one_k, 0)
+        rank_cols, count_ref, *refs = refs
+    o_ref, ot_ref, lse_ref, qt, acc, top, sc, probs, fade, counts = refs
+    tiles = ROW // TQ
+    lse_ref[...] = jnp.zeros_like(lse_ref)
+    acc[...] = jnp.zeros_like(acc)
+    top[...] = jnp.full_like(top, -jnp.inf)
+    if with_seen:
+        count_tiles(counts, count_ref)
+
+    def prepare(tile, c):
+        q0 = pl.multiple_of(tile * TQ, TQ)
+        for h in range(heads):
+            query_columns(qt, qt_ref, hot_ref[:, pl.ds(q0, TQ)], tile, h, q0)
+        return c
+    lax.fori_loop(0, tiles, prepare, 0)
+    ones = jnp.ones((16, TK), BF)
+
+    def one_step(s, c):
+        out_tile, _ = step_of(table, s)
+        _, out_k = real_step(table, s)
+        mid_tile, _ = step_of(table, s + 1)
+        in_tile, in_k = real_step(table, s + 2)
+        sums = []
+        for h in range(heads):
+            values = jnp.concatenate([vt_ref[h * HEAD_DIM:(h + 1) * HEAD_DIM, pl.ds(out_k, TK)], ones], 0)
+            sums.append(acc[out_tile, h] * fade[h:h + 1, :] + nn(values, probs[h]))
+        old = top[mid_tile]
+        news = []
+        for h in range(heads):
+            score = sc[h]
+            new = jnp.maximum(old[h:h + 1, :], jnp.max(score, 0, keepdims=True))
+            probs[h] = jnp.exp(score - new).astype(BF)
+            news.append(new)
+        new = jnp.concatenate(news + [old[heads:, :]], 0)
+        fade[...] = jnp.exp(old - new)
+        bias = seen_bias(rank_cols, counts, in_tile, in_k) if with_seen else None
+        for h in range(heads):
+            score = nn(pair_rows(k_ref, side_ref, h, in_k), qt[in_tile, h])
+            sc[h] = score + bias if with_seen else score
+        top[mid_tile] = new
+        for h in range(heads):
+            acc[out_tile, h] = sums[h]
+        return c
+    lax.fori_loop(0, table[0, STEPS - 1], one_step, 0)
+
+    def finish(tile, c):
+        q0 = pl.multiple_of(tile * TQ, TQ)
         outs = []
+        peak = top[tile]
         for h in range(heads):
-            a = acc[h]
+            a = acc[tile, h]
             total = a[HEAD_DIM:HEAD_DIM + 1, :]
-            outs.append(a[:HEAD_DIM, :] / total)
-            lse_ref[h:h + 1, pl.ds(q0, TQ)] = top[h:h + 1, :] + jnp.log(total)
-        o_ref[pl.ds(q0, TQ), :] = jnp.concatenate(outs, 0).T.astype(BF)
+            outs.append(a[:HEAD_DIM, :] * (1.0 / total))
+            lse_ref[h:h + 1, pl.ds(q0, TQ)] = peak[h:h + 1, :] + jnp.log(total)
+        out = jnp.concatenate(outs, 0)
+        ot_ref[:, pl.ds(q0, TQ)] = out.astype(BF)
+        o_ref[pl.ds(q0, TQ), :] = out.T.astype(BF)
         return c
-    lax.fori_loop(0, ROW // TQ, one_q, 0)
-
-def attend_forward(lengths, q, k, v, rank, count, with_seen):
-    rows, cols = q.shape
+    lax.fori_loop(0, tiles, finish, 0)
+
+
+def attend_forward(steps, qt, k, vt, tables, count, with_seen):
+    cols, rows = qt.shape
     heads = cols // HEAD_DIM
-    V = pl.BlockSpec(memory_space=pltpu.VMEM)
-    return pl.pallas_call(
-        partial(attn_fwd_kernel, with_seen, heads),
-        out_shape=(jax.ShapeDtypeStruct((rows, cols), BF), jax.ShapeDtypeStruct((8, rows), F32)),
-        in_specs=[pl.BlockSpec(memory_space=pltpu.SMEM)] + [V] * 5,
-        out_specs=(V, V),
-        scratch_shapes=[
-            pltpu.VMEM((heads, ROW + TK, 256), BF),
-            pltpu.VMEM((heads, HEAD_DIM + 16, ROW + TK), BF),
-            pltpu.VMEM((ROW + TK, 128), F32),
-            pltpu.VMEM((heads, HEAD_DIM + 16, TQ), F32),
-            pltpu.VMEM((8, TQ), F32),
-            pltpu.VMEM((heads // 2, 256, TQ), BF),
-        ],
-        compiler_params=pltpu.CompilerParams(vmem_limit_bytes=56 * 2**20),
-        cost_estimate=pl.CostEstimate(flops=4 * 10**10, bytes_accessed=16 * 2**20, transcendentals=0),
-        name="attend_self_forward" if with_seen else "attend_cross_forward",
-    )(lengths, q, k, v, rank, count)
-
-def three_way(value):
-    hi = value.astype(BF).astype(F32)
-    mid = (value - hi).astype(BF).astype(F32)
-    return hi, mid, value - hi - mid
-
-def attn_bwd_kernel(with_seen, heads, len_ref, q_ref, k_ref, v_ref, g_ref, o_ref, lse_ref, rank_ref, count_ref, pass_in,
-                    dq_ref, dk_ref, dv_ref, pass_out,
-                    kaug, vaug, kt, rank_cols, dk_sum, dv_sum, dq_sum, q_diag, g_diag, qt, gt, held, pass_sem):
+    side, hot, rank_cols = tables
+    args = [steps, qt, k, vt, side, hot] + ([rank_cols, count] if with_seen else [])
+    return call(partial(attn_fwd_kernel, with_seen, heads), "attend_self_forward" if with_seen else "attend_cross_forward",
+                args, "S" + "V" * (len(args) - 1), [((rows, cols), BF, "V"), ((cols, rows), BF, "V"), ((8, rows), F32, "V")],
+                [pltpu.VMEM((ROW // TQ, heads, 256, TQ), BF), pltpu.VMEM((ROW // TQ + 1, heads, HEAD_DIM + 16, TQ), F32),
+                 pltpu.VMEM((ROW // TQ + 1, 8, TQ), F32), pltpu.VMEM((heads, TK, TQ), F32), pltpu.VMEM((heads, TK, TQ), BF),
+                 pltpu.VMEM((8, TQ), F32)] + [pltpu.VMEM((ROW // TQ, 8, TQ), F32)])
+
+
+def three_rows(value):
+    high = value.astype(BF).astype(F32)
+    middle = (value - high).astype(BF).astype(F32)
+    row = lax.broadcasted_iota(jnp.int32, (128, value.shape[1]), 0)
+    return jnp.where(row == LANES[0], high, jnp.where(row == LANES[1], middle, jnp.where(row == LANES[2], value - high - middle, 0.0)))
+
+
+def attn_bwd_kernel(with_seen, heads, table, qt_ref, k_ref, kt_ref, v_ref, gt_ref, ot_ref, lse_ref,
+                    side_ref, hot_ref, *refs):
+    if with_seen:
+        rank_cols, count_ref, *refs = refs
+    (pass_in, dq_ref, dk_ref, dv_ref, pass_out, dk_sum, dv_sum, dq_sum, qt, gt, sc, dps, all_ds, all_p,
+     held, pass_sem, counts) = refs
     entering = pltpu.make_async_copy(pass_in, held, pass_sem.at[0])
     entering.start()
-    cols = heads * HEAD_DIM
-    starts, ends = doc_bounds(len_ref)
-    start_lane, end_lane = lane_vector(starts), lane_vector(ends)
-    fill_keys(kaug, k_ref, start_lane, end_lane, heads, True)
-    lanes = lax.broadcasted_iota(jnp.int32, (TK, 128), 1)
-    for h in range(heads):
-        picks = (lanes == h) | (lanes == 8 + h) | (lanes == 16 + h)
-        side = jnp.where(picks, -1.0, 0.0).astype(BF)
-        for t in range(ROW // TK):
-            pair = v_ref[t * TK:(t + 1) * TK, h // 2 * 128:h // 2 * 128 + 128]
-            vaug[h, t * TK:(t + 1) * TK, 0:128] = head_lanes(pair, h)
-            vaug[h, t * TK:(t + 1) * TK, 128:256] = side
-        vaug[h, ROW:, :] = jnp.zeros((TK, 256), BF)
-    for t in range(ROW // TK):
-        kt[:, t * TK:(t + 1) * TK] = k_ref[t * TK:(t + 1) * TK, :].T
-    kt[:, ROW:] = jnp.zeros((cols, TK), BF)
+    tiles = ROW // TQ
+    dk_sum[...] = jnp.zeros_like(dk_sum)
+    dv_sum[...] = jnp.zeros_like(dv_sum)
+    dq_sum[...] = jnp.zeros_like(dq_sum)
     if with_seen:
-        fill_ranks(rank_cols, rank_ref, starts)
+        count_tiles(counts, count_ref)
     entering.wait()
     leaving = pltpu.make_async_copy(held, pass_out, pass_sem.at[1])
     leaving.start()
-    dk_sum[...] = jnp.zeros_like(dk_sum)
-    dv_sum[...] = jnp.zeros_like(dv_sum)
-    sel_row = lax.broadcasted_iota(jnp.int32, (8, cols), 0)
-    sel_lane = lax.div(lax.broadcasted_iota(jnp.int32, (8, cols), 1), HEAD_DIM)
-    selector = jnp.where(sel_lane == sel_row, 1.0, 0.0).astype(BF)
-
-    def one_q(t, c):
-        q0 = pl.multiple_of(t * TQ, TQ)
-        first, steps = key_range(starts, ends, q0)
-        g = g_ref[pl.ds(q0, TQ), :]
-        q = q_ref[pl.ds(q0, TQ), :]
-        spread = g.astype(F32) * o_ref[pl.ds(q0, TQ), :].astype(F32)
-        spread_hi = spread.astype(BF)
-        delta = nt(selector, spread_hi) + nt(selector, (spread - spread_hi.astype(F32)).astype(BF))
-        daug = jnp.concatenate(list(three_way(delta)) + [jnp.zeros((104, TQ), F32)], 0).astype(BF)
-        lse = lse_ref[:, pl.ds(q0, TQ)]
-        hi, mid, lo = three_way(lse)
-        side = jnp.concatenate([doc_hot_rows(starts, ends, q0), jnp.zeros((32, TQ), F32), hi, mid, lo, jnp.zeros((40, TQ), F32)], 0).astype(BF)
-        for p in range(heads // 2):
-            qt[p, 0:128, :] = q[:, p * 128:(p + 1) * 128].T
-            qt[p, 128:256, :] = side
-            gt[p, 0:128, :] = g[:, p * 128:(p + 1) * 128].T
-            gt[p, 128:256, :] = daug
-        wide = lax.div(lax.broadcasted_iota(jnp.int32, (TQ, cols), 1), HEAD_DIM)
+
+    def prepare(tile, c):
+        q0 = pl.multiple_of(tile * TQ, TQ)
+        hot = hot_ref[:, pl.ds(q0, TQ)].astype(F32)
         for h in range(heads):
-            q_diag[h * TQ:(h + 1) * TQ, :] = jnp.where(wide == h, q, jnp.zeros_like(q))
-            g_diag[h * TQ:(h + 1) * TQ, :] = jnp.where(wide == h, g, jnp.zeros_like(g))
-        count_row = count_ref[:, pl.ds(q0, TQ)].astype(F32)
-        dq_sum[...] = jnp.zeros_like(dq_sum)
-
-        def one_k(s, c):
-            k0 = pl.multiple_of(first + s * TK, 128)
-            bias = seen_bias(rank_cols, count_row, k0, q0) if with_seen else None
-            all_ds, all_p, all_dq = [], [], []
-            kaugs = [kaug[h, pl.ds(k0, TK), :] for h in range(heads)]
-            vaugs = [vaug[h, pl.ds(k0, TK), :] for h in range(heads)]
-            keys_t = kt[:, pl.ds(k0, TK)]
-            qts = [qt[p] for p in range(heads // 2)]
-            gts = [gt[p] for p in range(heads // 2)]
-            qd, gd = q_diag[...], g_diag[...]
-            scores = [nn(kaugs[h], qts[h // 2]) for h in range(heads)]
-            dps = [nn(vaugs[h], gts[h // 2]) for h in range(heads)]
-            if with_seen:
-                scores = [score + bias for score in scores]
-            for h in range(heads):
-                p = jnp.exp(scores[h])
-                ds = (p * dps[h]).astype(BF)
-                all_ds.append(ds)
-                all_p.append(p.astype(BF))
-                all_dq.append(nn(keys_t[h * HEAD_DIM:(h + 1) * HEAD_DIM, :], ds))
-            dk = dk_sum[pl.ds(k0, TK), :] + nn(jnp.concatenate(all_ds, 1), qd)
-            dv = dv_sum[pl.ds(k0, TK), :] + nn(jnp.concatenate(all_p, 1), gd)
-            dq = dq_sum[...] + jnp.concatenate(all_dq, 0)
-            dk_sum[pl.ds(k0, TK), :] = dk
-            dv_sum[pl.ds(k0, TK), :] = dv
-            dq_sum[...] = dq
-            return c
-        lax.fori_loop(0, steps, one_k, 0)
-        dq_ref[pl.ds(q0, TQ), :] = (dq_sum[...] * HEAD_DIM ** -0.5).T.astype(BF)
+            rows = slice(h * HEAD_DIM, (h + 1) * HEAD_DIM)
+            side = hot + three_rows(lse_ref[h:h + 1, pl.ds(q0, TQ)])
+            query_columns(qt, qt_ref, side.astype(BF), tile, h, q0)
+            grads = gt_ref[rows, pl.ds(q0, TQ)]
+            delta = jnp.sum(grads.astype(F32) * ot_ref[rows, pl.ds(q0, TQ)].astype(F32), 0, keepdims=True)
+            other = (1 - h % 2) * HEAD_DIM
+            gt[tile, h, h % 2 * HEAD_DIM:(h % 2 + 1) * HEAD_DIM, :] = grads
+            gt[tile, h, other:other + HEAD_DIM, :] = jnp.zeros((HEAD_DIM, TQ), BF)
+            gt[tile, h, 128:256, :] = three_rows(delta).astype(BF)
         return c
-    lax.fori_loop(0, ROW // TQ, one_q, 0)
-    dk_ref[...] = (dk_sum[:ROW, :] * HEAD_DIM ** -0.5).astype(BF)
-    dv_ref[...] = dv_sum[:ROW, :].astype(BF)
+    lax.fori_loop(0, tiles, prepare, 0)
+
+    def one_step(s, c):
+        out_tile, out_k = step_of(table, s)
+        read_tile, read_k = real_step(table, s)
+        in_tile, in_k = real_step(table, s + 2)
+        keys = pl.ds(out_k, TK)
+        queries = pl.ds(pl.multiple_of(read_tile * TQ, TQ), TQ)
+        own = [slice(h * HEAD_DIM, (h + 1) * HEAD_DIM) for h in range(heads)]
+        dk = [dk_sum[h, :, keys] + nt(qt_ref[own[h], queries], all_ds[h]) for h in range(heads)]
+        dv = [dv_sum[h, :, keys] + nt(gt_ref[own[h], queries], all_p[h]) for h in range(heads)]
+        dq = [dq_sum[out_tile, h] + nn(kt_ref[own[h], pl.ds(read_k, TK)], all_ds[h]) for h in range(heads)]
+        for h in range(heads):
+            p = jnp.exp(sc[h])
+            all_ds[h] = (p * dps[h]).astype(BF)
+            all_p[h] = p.astype(BF)
+        bias = seen_bias(rank_cols, counts, in_tile, in_k) if with_seen else None
+        for h in range(heads):
+            score = nn(pair_rows(k_ref, side_ref, h, in_k), qt[in_tile, h])
+            sc[h] = score + bias if with_seen else score
+            dps[h] = nn(pair_rows(v_ref, side_ref, h, in_k), gt[in_tile, h])
+        for h in range(heads):
+            dk_sum[h, :, keys] = dk[h]
+            dv_sum[h, :, keys] = dv[h]
+            dq_sum[out_tile, h] = dq[h]
+        return c
+    lax.fori_loop(0, table[0, STEPS - 1], one_step, 0)
+
+    def finish(tile, c):
+        q0 = pl.multiple_of(tile * TQ, TQ)
+        rows = pl.ds(q0, TQ)
+        dq = jnp.concatenate([dq_sum[tile, h] for h in range(heads)], 0) * HEAD_DIM ** -0.5
+        dk = jnp.concatenate([dk_sum[h, :, rows] for h in range(heads)], 0) * HEAD_DIM ** -0.5
+        dv = jnp.concatenate([dv_sum[h, :, rows] for h in range(heads)], 0)
+        for ref, value in ((dq_ref, dq), (dk_ref, dk), (dv_ref, dv)):
+            ref[rows, :] = value.astype(BF).T
+        return c
+    lax.fori_loop(0, tiles, finish, 0)
     leaving.wait()
 
-def attend_backward(lengths, q, k, v, g, o, lse, rank, count, passed, with_seen):
-    rows, cols = q.shape
+
+def attend_backward(steps, qt, k, kt, v, gt, ot, lse, tables, count, passed, with_seen):
+    rows, cols = v.shape
     heads = cols // HEAD_DIM
-    V = pl.BlockSpec(memory_space=pltpu.VMEM)
-    like = jax.ShapeDtypeStruct((rows, cols), BF)
-    return pl.pallas_call(
-        partial(attn_bwd_kernel, with_seen, heads),
-        out_shape=(like, like, like, jax.ShapeDtypeStruct(passed.shape, passed.dtype)),
-        in_specs=[pl.BlockSpec(memory_space=pltpu.SMEM)] + [V] * 8 + [pl.BlockSpec(memory_space=pl.ANY)],
-        out_specs=(V, V, V, pl.BlockSpec(memory_space=pl.ANY)),
-        scratch_shapes=[
-            pltpu.VMEM((heads, ROW + TK, 256), BF),
-            pltpu.VMEM((heads, ROW + TK, 256), BF),
-            pltpu.VMEM((cols, ROW + TK), BF),
-            pltpu.VMEM((ROW + TK, 128), F32),
-            pltpu.VMEM((ROW + TK, cols), F32),
-            pltpu.VMEM((ROW + TK, cols), F32),
-            pltpu.VMEM((cols, TQ), F32),
-            pltpu.VMEM((heads * TQ, cols), BF),
-            pltpu.VMEM((heads * TQ, cols), BF),
-            pltpu.VMEM((heads // 2, 256, TQ), BF),
-            pltpu.VMEM((heads // 2, 256, TQ), BF),
-            pltpu.VMEM(passed.shape, passed.dtype),
-            pltpu.SemaphoreType.DMA((2,)),
-        ],
-        compiler_params=pltpu.CompilerParams(vmem_limit_bytes=56 * 2**20),
-        cost_estimate=pl.CostEstimate(flops=4 * 10**10, bytes_accessed=16 * 2**20, transcendentals=0),
-        name="attend_self_backward" if with_seen else "attend_cross_backward",
-    )(lengths, q, k, v, g, o, lse, rank, count, passed)
+    side, hot, rank_cols = tables
+    args = [steps, qt, k, kt, v, gt, ot, lse, side, hot] + ([rank_cols, count] if with_seen else []) + [passed]
+    like = ((rows, cols), BF, "V")
+    tiles = ROW // TQ
+    summed = pltpu.VMEM((heads, HEAD_DIM, rows + TK), F32)
+    columns, square = pltpu.VMEM((tiles, heads, 256, TQ), BF), pltpu.VMEM((heads, TK, TQ), F32)
+    small = pltpu.VMEM((heads, TK, TQ), BF)
+    return call(partial(attn_bwd_kernel, with_seen, heads), "attend_self_backward" if with_seen else "attend_cross_backward",
+                args, "S" + "V" * (len(args) - 2) + "A", [like, like, like, (passed.shape, passed.dtype, "A")],
+                [summed, summed, pltpu.VMEM((tiles + 1, heads, HEAD_DIM, TQ), F32), columns, columns, square, square,
+                 small, small, pltpu.VMEM(passed.shape, passed.dtype), pltpu.SemaphoreType.DMA((2,))] + [pltpu.VMEM((ROW // TQ, 8, TQ), F32)])
 
 
 def send(src, dst, send_sem, recv_sem, **where):
@@ -338,13 +337,12 @@
     behind = lambda d: lax.rem(z + across - d, across) * 4 + y * 2 + x
     return me, x, y, z, xpeer, ypeer, order, ahead, behind
 
-def spread_blocks(count, out, rows, places, zs, xs, ys, gx, gy):
+def spread_blocks(count, piece, rows, half, places, zs, xs, ys, gx, gy, meanwhile=None):
     me, x, y, z, xpeer, ypeer, order, ahead, behind = places
-    half = rows // 32 * 16
-    whole = pl.ds(0, rows)
+    whole = (0, rows)
     sent, recv = [], {}
     def go(src_block, at, sem, d, to):
-        copy = send(out.at[src_block, at], out.at[src_block, at], sem.at[0, d], sem.at[1, d], dp=to)
+        copy = send(piece(src_block, *at), piece(src_block, *at), sem.at[0, d], sem.at[1, d], dp=to)
         sent.append(copy)
         return copy
     near = go(me, whole, xs, 0, xpeer), go(me, whole, ys, 0, ypeer)
@@ -352,6 +350,8 @@
     zcopies = {}
     for d in order:
         zcopies[d] = go(me, whole, zs, d, ahead(d))
+    if meanwhile is not None:
+        meanwhile()
     steps = [0] + order
     diag = []
     for k, d in enumerate(steps):
@@ -370,26 +370,9 @@
     me, x, y, z, xpeer, ypeer, order, ahead, _ = places
     base = behind(d) if d else me
     recv[d][0].wait_recv()
-    diag.append(go(base + 1 - 2 * x, pl.ds(0, half), gy, d, ypeer))
+    diag.append(go(base + 1 - 2 * x, (0, half), gy, d, ypeer))
     recv[d][1].wait_recv()
-    diag.append(go(base + 2 - 4 * y, pl.ds(half, rows - half), gx, d, xpeer))
-
-def gather_kernel(count, master, norm, out_ref, zs, xs, ys, gx, gy):
-    places = places_of(count)
-    me, x, y, z, xpeer, ypeer, order, ahead, behind = places
-    rows = master.shape[0]
-    out_ref[me, 0:rows, :] = master[...].astype(BF)
-    out_ref[me, rows:rows + UNIT, :] = jnp.broadcast_to(norm[...], (UNIT, norm.shape[1])).astype(BF)
-    greet([{"dp": xpeer}, {"dp": ypeer}] + [{"dp": ahead(d)} for d in order])
-    spread_blocks(count, out_ref, rows + UNIT, places, zs, xs, ys, gx, gy)
-
-
-def gather_blocks(master, norm, count):
-    rows, cols = master.shape
-    sems = pltpu.SemaphoreType.DMA((2, count // 4))
-    return call(partial(gather_kernel, count), "gather_units", [master, norm], "VV",
-                [((count, rows + UNIT, cols), BF, "V")], [sems] * 5, 0)[0]
-
+    diag.append(go(base + 2 - 4 * y, (half, rows - half), gx, d, xpeer))
 
 def part_sizes(rows):
     first = rows // 2 // UNIT * UNIT
@@ -580,8 +563,12 @@
 
     def copy(self, i, step):
         held, out = self.pairs[i]
-        rows = pl.ds(pl.multiple_of(step * CHUNK, CHUNK), CHUNK)
-        return pltpu.make_async_copy(held.at[rows], out.at[rows], self.sems.at[i, step])
+        part = pl.ds(pl.multiple_of(step * CHUNK, CHUNK), CHUNK)
+        if held.shape[0] < held.shape[1]:
+            held, out = held.at[:, part], out.at[:, part]
+        else:
+            held, out = held.at[part], out.at[part]
+        return pltpu.make_async_copy(held, out, self.sems.at[i, step])
 
     def start(self, i, step):
         self.copy(i, step).start()
@@ -593,28 +580,71 @@
         chunks(tokens, body)
 
 
-def project_kernel(owner_ref, gathered, norms, query_hbm, kv_hbm, memory_hbm,
-                   nq_out, nkv_out, q_out, k_out, v_out, kc_out, vc_out, ws_ref, wc_ref, wos_ref, woc_ref, w1_ref, w2_ref,
-                   flat, used, query_ref, kv_ref, memory_ref, nq_ref, nkv_ref, q_ref, k_ref, v_ref, kc_ref, vc_ref,
-                   late_sems, out_sems):
-    tokens, features = query_ref.shape
-    devices = gathered.shape[0]
-    units = owner_ref.shape[0]
-    late = Late([(query_hbm, query_ref), (kv_hbm, kv_ref), (memory_hbm, memory_ref)], late_sems)
-    out = Out([(nq_ref, nq_out), (nkv_ref, nkv_out), (q_ref, q_out), (k_ref, k_out), (v_ref, v_out), (kc_ref, kc_out),
-               (vc_ref, vc_out)], out_sems)
-    for d in range(devices):
+def plan_kernel(block, owner_ref, len_ref, place_ref, table, used):
+    for d in range(used.shape[0]):
         used[d] = 0
 
     def one_unit(u, carry):
         owner = owner_ref[u]
         slot = used[owner]
+        place_ref[u] = owner * block + slot
         used[owner] = slot + 1
-        flat[pl.ds(pl.multiple_of(u * UNIT, UNIT), UNIT), :] = gathered[owner, pl.ds(pl.multiple_of(slot * UNIT, UNIT), UNIT), :]
+        return carry
+    lax.fori_loop(0, owner_ref.shape[0], one_unit, 0, unroll=4)
+    step_table(len_ref, table)
+
+
+def plan(unit_owner, lengths, devices, block):
+    return call(partial(plan_kernel, block), "plan", [unit_owner, lengths], "SS",
+                [(unit_owner.shape, jnp.int32, "S"), ((2, STEPS), jnp.int32, "S")], [pltpu.SMEM((devices,), jnp.int32)])
+
+
+def project_kernel(devices, place_ref, len_ref, master, norm_row, rank_ref, query_hbm, kv_hbm, memory_hbm,
+                   nq_out, nkv_out, qt_out, k_out, kt_out, v_out, vt_out, kc_out, kct_out, vc_out, vct_out,
+                   ws_ref, wc_ref, wos_ref, woc_ref, w1_ref, w2_ref, norms, side_ref, hot_ref, rank_cols,
+                   gathered, flat, query_ref, kv_ref, memory_ref, unit_q, unit_kv,
+                   nq_ref, nkv_ref, qt_ref, k_ref, kt_ref, v_ref, vt_ref, kc_ref, kct_ref, vc_ref, vct_ref,
+                   late_sems, out_sems, zs, xs, ys, gx, gy):
+    tokens, features = query_ref.shape
+    units = place_ref.shape[0]
+    late = Late([(query_hbm, query_ref), (kv_hbm, kv_ref), (memory_hbm, memory_ref)], late_sems)
+    held = (nq_ref, nkv_ref, qt_ref, k_ref, kt_ref, v_ref, vt_ref, kc_ref, kct_ref, vc_ref, vct_ref)
+    out = Out(list(zip(held, (nq_out, nkv_out, qt_out, k_out, kt_out, v_out, vt_out, kc_out, kct_out, vc_out, vct_out))), out_sems)
+    places = places_of(devices)
+    me, x, y, z, xpeer, ypeer, order, ahead, behind = places
+    slots = master.shape[0]
+    block = slots + 1
+    gathered[pl.ds(me * block, slots)] = master[...].astype(BF)
+    gathered[me * block + slots] = jnp.broadcast_to(norm_row[...], (UNIT, features)).astype(BF)
+    greet([{"dp": xpeer}, {"dp": ypeer}] + [{"dp": ahead(d)} for d in order])
+
+    def meanwhile():
+        mask_tables(len_ref, rank_ref, side_ref, hot_ref, rank_cols)
+        late.wait(0, 1, 2)
+
+        def units_of(step, rows):
+            unit_q[rows, :] = normalise(query_ref[rows, :].astype(F32))[0]
+            unit_kv[rows, :] = normalise(kv_ref[rows, :].astype(F32))[0]
+        chunks(tokens, units_of)
+    spread_blocks(devices, lambda number, start, size: gathered.at[pl.ds(number * block + start, size)], block, block // 2,
+                  places, zs, xs, ys, gx, gy, meanwhile)
+
+    share = devices // 8
+    vectors = []
+    for number in range(8):
+        pieces = [gathered[(number * share + i) * block + slots].astype(F32) for i in range(share)]
+        total = pieces[0]
+        for piece in pieces[1:]:
+            total = total + piece
+        vectors.append(total[0:1, :])
+    norms[...] = jnp.concatenate(vectors, 0)
+
+    def one_unit(u, carry):
+        flat[pl.ds(pl.multiple_of(u * UNIT, UNIT), UNIT), :] = gathered[place_ref[u]]
         return carry
     lax.fori_loop(0, units, one_unit, 0, unroll=4)
     order = interleave(features)
-    cols = q_ref.shape[1]
+    cols = v_ref.shape[1]
     for number in range(6):
         rows = flat[number * cols:(number + 1) * cols, :]
         stacked = jnp.concatenate([rows[:, :cols], rows[:, cols:]], 0)
@@ -632,15 +662,19 @@
         half = features // 2
         w1_ref[block * half:(block + 1) * half, :] = jnp.concatenate([parted[:half], parted[half:]], 1)
     w2_ref[...] = flat[8 * cols + hidden:, :]
-    late.wait(0, 1, 2)
 
     def body(step, rows):
-        nq = (normalise(query_ref[rows, :].astype(F32))[0] * norms[0:1, :] + norms[1:2, :]).astype(BF)
-        nkv = (normalise(kv_ref[rows, :].astype(F32))[0] * norms[2:3, :] + norms[3:4, :]).astype(BF)
+        nq = (unit_q[rows, :] * norms[0:1, :] + norms[1:2, :]).astype(BF)
+        nkv = (unit_kv[rows, :] * norms[2:3, :] + norms[3:4, :]).astype(BF)
         source = memory_ref[rows, :]
-        results = [nq, nkv, nn(nq, ws_ref[0]), nn(nkv, ws_ref[1]), nn(nkv, ws_ref[2]), nn(source, wc_ref[1]), nn(source, wc_ref[2])]
-        for i, (ref, result) in enumerate(zip((nq_ref, nkv_ref, q_ref, k_ref, v_ref, kc_ref, vc_ref), results)):
-            ref[rows, :] = result.astype(BF)
+        low = lambda left, right: nn(left, right).astype(BF)
+        k, v, kc, vc = low(nkv, ws_ref[1]), low(nkv, ws_ref[2]), low(source, wc_ref[1]), low(source, wc_ref[2])
+        results = [nq, nkv, low(nq, ws_ref[0]).T, k, k.T, v, v.T, kc, kc.T, vc, vc.T]
+        for i, (ref, result) in enumerate(zip(held, results)):
+            if ref.shape[0] < ref.shape[1]:
+                ref[:, rows] = result
+            else:
+                ref[rows, :] = result
             out.start(i, step)
     chunks(tokens, body)
     out.drain(tokens)
@@ -654,16 +688,21 @@
     return pltpu.SemaphoreType.DMA((count, tokens // CHUNK))
 
 
-def project(unit_owner, gathered, norms, query_stream, kv_stream, memory, cols, hidden):
+def project(devices, place_of, lengths, master, norm_row, rank_row, query_stream, kv_stream, memory, cols, hidden):
     tokens, features = query_stream.shape
-    wide, narrow = (tokens, features), (tokens, cols)
-    outs = [(wide, BF, "A")] * 2 + [(narrow, BF, "A")] * 5 + [
+    wide, narrow, across = (tokens, features), (tokens, cols), (cols, tokens)
+    shapes = [wide, wide, across] + [narrow, across] * 4
+    outs = [(shape, BF, "A") for shape in shapes] + [
         ((3, features, cols), BF, "V"), ((3, features, cols), BF, "V"), ((cols, features), BF, "V"), ((cols, features), BF, "V"),
-        ((features, hidden), BF, "V"), ((hidden, features), BF, "V")]
-    scratch = [pltpu.VMEM((8 * cols + 2 * hidden, features), BF), pltpu.SMEM((gathered.shape[0],), jnp.int32)]
-    scratch += [pltpu.VMEM(wide, BF)] * 5 + [pltpu.VMEM(narrow, BF)] * 5
-    scratch += [pltpu.SemaphoreType.DMA((3,)), out_semaphores(7, tokens)]
-    return call(project_kernel, "project", [unit_owner, gathered, norms, query_stream, kv_stream, memory], "SVVAAA", outs, scratch)
+        ((features, hidden), BF, "V"), ((hidden, features), BF, "V"), ((8, features), F32, "V"),
+        ((ROW, 128), BF, "V"), ((128, ROW), BF, "V"), ((ROW, 128), F32, "V")]
+    D = pltpu.SemaphoreType.DMA
+    scratch = [pltpu.VMEM((devices * (master.shape[0] + 1), UNIT, features), BF), pltpu.VMEM((8 * cols + 2 * hidden, features), BF)]
+    scratch += [pltpu.VMEM(wide, BF)] * 3 + [pltpu.VMEM(wide, F32)] * 2 + [pltpu.VMEM(shape, BF) for shape in shapes]
+    scratch += [D((3,)), out_semaphores(len(shapes), tokens)] + [D((2, devices // 4))] * 5
+    return call(partial(project_kernel, devices), "project",
+                [place_of, lengths, master, norm_row, rank_row, query_stream, kv_stream, memory], "SSVVVAAA",
+                outs, scratch, 0)
 
 
 def self_out_kernel(mixed, wo, query_hbm, wc, norms, res_out, nc_out, q_out,
@@ -687,7 +726,7 @@
         nc = (normalise(res)[0] * norms[4:5, :] + norms[5:6, :]).astype(BF)
         nc_ref[rows, :] = nc
         out.start(1, step)
-        q_ref[rows, :] = nn(nc, wc[0]).astype(BF)
+        q_ref[:, rows] = nn(nc, wc[0]).astype(BF).T
         out.start(2, step)
     chunks(tokens, take)
     drain(tokens, mine, theirs, sems)
@@ -697,8 +736,9 @@
 def self_out(mixed, wo, query, wc, norms):
     tokens, features = query.shape
     wide = (tokens, features)
-    outs = [(wide, F32, "A"), (wide, BF, "A"), (mixed.shape, BF, "A")]
-    scratch = [pltpu.VMEM(wide, BF), pltpu.VMEM(wide, F32), pltpu.VMEM(wide, BF), pltpu.VMEM(mixed.shape, BF),
+    across = (mixed.shape[1], tokens)
+    outs = [(wide, F32, "A"), (wide, BF, "A"), (across, BF, "A")]
+    scratch = [pltpu.VMEM(wide, BF), pltpu.VMEM(wide, F32), pltpu.VMEM(wide, BF), pltpu.VMEM(across, BF),
                pltpu.VMEM(wide, BF), pltpu.VMEM(wide, BF), pair_sems(tokens), pltpu.SemaphoreType.DMA((1,)),
                out_semaphores(3, tokens)]
     return call(self_out_kernel, "self_out", [mixed, wo, query, wc, norms], "VVAVV", outs, scratch, 2)
@@ -791,7 +831,7 @@
         sums_ref[8:16, :] += fold_rows(grad)
         low = gres.astype(BF)
         low_all[rows, :] = low
-        gmix_ref[rows, :] = nt(low, wo[...]).astype(BF)
+        gmix_ref[:, rows] = nt(low, wo[...]).astype(BF).T
         out.start(2, step)
     chunks(tokens, close)
     gwo_ref[...] = tn(mixed[...], low_all[...]).astype(BF)
@@ -806,10 +846,11 @@
     hidden = w2.shape[0]
     part = ((devices // 4, 2 * hidden // devices, features), BF, "V")
     wide = (tokens, features)
-    outs = [(wide, BF, "A"), (wide, F32, "A"), (mixed.shape, BF, "A")] + [part] * 4 + [
+    across = (mixed.shape[1], tokens)
+    outs = [(wide, BF, "A"), (wide, F32, "A"), (across, BF, "A")] + [part] * 4 + [
         (wo.shape, BF, "V"), ((16, features), F32, "V")]
     deep, narrow = pltpu.VMEM((tokens, hidden), BF), pltpu.VMEM(wide, BF)
-    scratch = [pltpu.VMEM(wide, F32), narrow, narrow, pltpu.VMEM(wide, F32), pltpu.VMEM(mixed.shape, BF),
+    scratch = [pltpu.VMEM(wide, F32), narrow, narrow, pltpu.VMEM(wide, F32), pltpu.VMEM(across, BF),
                pltpu.VMEM((2 * hidden, features), BF), narrow, narrow, narrow, deep, deep, narrow] + [narrow] * 4
     scratch += [pair_sems(tokens)] * 3 + [pltpu.SemaphoreType.DMA((2,)), out_semaphores(3, tokens)]
     return call(partial(feed_forward_kernel, devices), "feed_forward", [mixed, wo, res, w1, w2, out_grad, norms], "VVAVVAV",
@@ -885,7 +926,7 @@
         sums_ref[8:16, :] += fold_rows(grad)
         low = gnew.astype(BF)
         low_all[rows, :] = low
-        gmix_ref[rows, :] = nt(low, wo[...]).astype(BF)
+        gmix_ref[:, rows] = nt(low, wo[...]).astype(BF).T
         out.start(2, step)
         other_core(mine_b, theirs_b, sems_b, step).wait_recv()
         gmem_ref[rows, :] = (mine_b[rows, :].astype(F32) + theirs_b[rows, :].astype(F32)).astype(BF)
@@ -917,11 +958,11 @@
     flat_rows = -(-5 * cols // (devices * UNIT)) * devices * UNIT
     give = ((across, ready_rows + flat_rows // devices, features), BF, "V")
     wide = (tokens, features)
-    outs = [(wide, BF, "A"), (wide, F32, "A"), (dq.shape, BF, "A")] + [give] * 4 + [((16, features), F32, "V")]
+    outs = [(wide, BF, "A"), (wide, F32, "A"), ((cols, tokens), BF, "A")] + [give] * 4 + [((16, features), F32, "V")]
     low, high = pltpu.VMEM(wide, BF), pltpu.VMEM(wide, F32)
     small = pltpu.VMEM((across, ready_rows, features), BF)
     z_sems = pltpu.SemaphoreType.DMA((2, across))
-    scratch = [low, low, high, high, low, high, pltpu.VMEM(dq.shape, BF), pltpu.VMEM((flat_rows, features), BF), small, small, small]
+    scratch = [low, low, high, high, low, high, pltpu.VMEM((cols, tokens), BF), pltpu.VMEM((flat_rows, features), BF), small, small, small]
     scratch += [low] * 5 + [pair_sems(tokens)] * 2 + [pltpu.SemaphoreType.DMA((4,)), out_semaphores(3, tokens), z_sems, z_sems]
     return call(partial(cross_back_kernel, devices), "cross_back",
                 [dq, dk, dv, wc, nc, memory, res, gres, mixed, wo, norms, gwo_cross] + parts, "VVVVAAAAVVVVVVVV", outs, scratch, 4)
@@ -980,7 +1021,9 @@
     n_copies = [send(norm_mine, norm_all.at[d], n_sems.at[0, d], n_sems.at[1, d], dp=other)
                 for d, other in zip(range(1, devices), others)]
     block_sum.finish()
-    spread_blocks(devices, summed, summed.shape[1], places, *block_refs[7:])
+    out_rows = summed.shape[1]
+    spread_blocks(devices, lambda block, start, size: summed.at[block, pl.ds(start, size)], out_rows, out_rows // 2 // UNIT * UNIT,
+                  places, *block_refs[7:])
     total = norm_mine[...]
     for d, copy in zip(range(1, devices), n_copies):
         copy.wait_recv()
@@ -1106,29 +1149,29 @@
     hidden = (units * unit_rows - 8 * cols) // 2
 
     shape = (slots, unit_rows, features)
-    norm_row = jnp.pad(norm_master.reshape(1, norm_share), ((0, 0), (0, features - norm_share)))
-    gathered = gather_blocks(master.reshape(slots * unit_rows, features), norm_row, devices)
-    norms = gathered[:, slots * unit_rows, :norm_share].reshape(8, features).astype(F32)
-
+    norm_row = lax.dynamic_update_slice(
+        jnp.zeros((1, features), F32), norm_master.reshape(1, norm_share), (0, lax.rem(me * norm_share, features)))
     rank_row, count_row = obs_rank.reshape(1, ROW), obs_count.reshape(1, ROW)
-    nq, nkv, q, k, v, kc, vc, ws, wc, wo_self, wo_cross, w1, w2 = project(
-        unit_owner, gathered, norms, query_stream, kv_stream, memory, cols, hidden)
-    mixed_self, total_self = attend_forward(lengths, q, k, v, rank_row, count_row, True)
-    residual, nc, qc = self_out(mixed_self, wo_self, query_stream, wc, norms)
-    mixed_cross, total_cross = attend_forward(lengths, qc, kc, vc, rank_row, count_row, False)
+    place_of, steps = plan(unit_owner, lengths, devices, slots + 1)
+    nq, nkv, qt, k, kt, v, vt, kc, kct, vc, vct, ws, wc, wo_self, wo_cross, w1, w2, norms, *tables = project(
+        devices, place_of, lengths, master.reshape(shape), norm_row, rank_row,
+        query_stream, kv_stream, memory, cols, hidden)
+    mixed_self, mixed_self_t, total_self = attend_forward(steps, qt, k, vt, tables, count_row, True)
+    residual, nc, qct = self_out(mixed_self, wo_self, query_stream, wc, norms)
+    mixed_cross, mixed_cross_t, total_cross = attend_forward(steps, qct, kc, vct, tables, count_row, False)
     output, grad_cross_res, grad_mixed, *parts, gwo_cross, sums_f = feed_forward(
         devices, mixed_cross, wo_cross, residual, w1, w2, out_grad, norms)
     tie = lax.optimization_barrier
     ready_rows = parts[0].shape[1]
     parts = [parts[0]] + [plane_swap(parts[f], devices, f) for f in (1, 2, 3)]
     dq, dk, dv, output = attend_backward(
-        lengths, qc, kc, vc, grad_mixed, mixed_cross, total_cross, rank_row, count_row, output, False)
+        steps, qct, kc, kct, vc, grad_mixed, mixed_cross_t, total_cross, tables, count_row, output, False)
     parts, dq = tie((parts, dq))
     grad_memory, grad_residual, grad_mixed, *parts, sums_c = cross_back(
         devices, dq, dk, dv, wc, nc, memory, residual, grad_cross_res, mixed_self, wo_self, norms, gwo_cross, parts)
     parts = [parts[0]] + [plane_swap(parts[f], devices, f) for f in (1, 2, 3)]
     dq, dk, dv, grad_memory = attend_backward(
-        lengths, q, k, v, grad_mixed, mixed_self, total_self, rank_row, count_row, grad_memory, True)
+        steps, qt, k, kt, v, grad_mixed, mixed_self_t, total_self, tables, count_row, grad_memory, True)
     parts, dq = tie((parts, dq))
     grad_query, grad_kv, summed, norm_grads = self_back(
         devices, ready_rows, dq, dk, dv, ws, nq, nkv, query_stream, kv_stream, grad_residual, norms, sums_c, sums_f, parts)

time: 395 us -> 377 us (0.954)
  Pallas kernels: 379 us -> 363 us
    pallas_call x4 -> x0, Pallas kernels: 132 us -> none  [the longest x2 79.5 us: attend_backward(): pl.pallas_call(partial(attn_bwd_kernel, with_seen, heads), out_shape=(lik...]
    pallas_call x7 -> x11, Pallas kernels: 248 us -> 363 us  [call(): pl.pallas_call(kernel, out_shape=tuple((jax.ShapeDtypeStruct(shape, dtype...]
  transfers between devices with their start and end apart: 6 -> 6, of which waited for: 0 -> 0; matrix products, arithmetic and copies ran while one was open for 0% -> 0% of each run, Pallas kernels for 20% -> 21%
where the time goes in v4:
time: 377 us; the launch traced here: 375 us
  Pallas kernels  363 us (96%)
  starting transfers between devices  7.1 us (2%)
  local copies, waits for them, and re-layouts  3.94 us (1%)
    pallas_call x11, Pallas kernels, call(): pl.pallas_call(kernel, out_shape=tuple((jax.ShapeDtypeStruct(shape, dtype...  363 us
  transfers between devices with their start and end apart: 6, of which 0 were waited for; matrix products, arithmetic and copies ran while one was open for 0% of the time, Pallas kernels for 21%

profile of v4, /device:TPU:0, one launch (start us, length us, event | category | flops | bytes accessed | tf_op | source)
XLA Modules:
  0.0 375.5 jit_solution(17845250438595327164)
XLA Ops:
  0.7 0.0 copy-start
  0.7 3.6 plan.1
  4.2 0.0 copy-done
  4.3 0.0 copy-start.2
  4.3 0.6 copy-done.2
  4.9 92.2 %project.1 = (bf16[2048,512]{1,0:T(8,128)(2,1)}, bf16[2048,512]{1,0:T(8,128)(2,1)}, bf16[256,2048]{1,0:T(8,128)(2,1)}, bf16[2048,256]{1,0:T(8,128)(2,1)}, bf16[2...) custom-call(s32[256]{0:T(256)} %get-tuple-element.90.place_ref, ...), custom_call_target="tpu_custom_call" | custom-call | flops 40000000000 | bytes 16777216 | tf_op jit(solution)/shard_map/project/pallas_call | solution.py:474
  97.1 21.2 %attend_self_forward.1 = (bf16[2048,256]{1,0:T(8,128)(2,1)}, bf16[256,2048]{1,0:T(8,128)(2,1)}, f32[8,2048]{1,0:T(8,128)}) custom-call(s32[2,72]{1,0:T(2,128)} %get-tuple-element.89.table, bf16[256,2048]{1,0:T(8,128)(2,1)} %get-tuple-element.91.qt_ref, bf16[2048,256]{1,0:T(8,128)(2,1)} %get-tuple-element.92.k_ref, ...), custom_call_target="tpu_custom_call" | custom-call | flops 40000000000 | bytes 16777216 | tf_op jit(solution)/shard_map/attend_self_forward/pallas_call | solution.py:474
  118.2 8.4 %self_out.1 = (f32[2048,512]{1,0:T(8,128)}, bf16[2048,512]{1,0:T(8,128)(2,1)}, bf16[256,2048]{1,0:T(8,128)(2,1)}) custom-call(bf16[2048,256]{1,0:T(8,128)(2,1)} %get-tuple-element.97.mixed, bf16[256,512]{1,0:T(8,128)(2,1)} %get-tuple-element.98.wo, bf16[2048,512]{1,0:T(8,128)(2,1)} %query_hbm.5, bf16[3,512,256]{2,1,0:T(8,128)(2,1)} %get-tuple-element.99.wc, ...), custom_call_target="tpu_custom_call" | custom-call | flops 40000000000 | bytes 16777216 | tf_op jit(solution)/shard_map/self_out/pallas_call | solution.py:474
  126.6 20.4 %attend_cross_forward.1 = (bf16[2048,256]{1,0:T(8,128)(2,1)}, bf16[256,2048]{1,0:T(8,128)(2,1)}, f32[8,2048]{1,0:T(8,128)}) custom-call(s32[2,72]{1,0:T(2,128)} %get-tuple-element.89.table, bf16[256,2048]{1,0:T(8,128)(2,1)} %get-tuple-element.101.qt_ref, bf16[2048,256]{1,0:T(8,128)(2,1)} %get-tuple-element.102.k_ref, ...), custom_call_target="tpu_custom_call" | custom-call | flops 40000000000 | bytes 16777216 | tf_op jit(solution)/shard_map/attend_cross_forward/pallas_call | solution.py:474
  147.0 37.0 %feed_forward.1 = (bf16[2048,512]{1,0:T(8,128)(2,1)}, f32[2048,512]{1,0:T(8,128)}, bf16[256,2048]{1,0:T(8,128)(2,1)}, bf16[4,128,512]{2,1,0:T(8,128)(2,1)}, bf16...) custom-call(bf16[2048,256]{1,0:T(8,128)(2,1)} %get-tuple-element.106, ...), custom_call_target="tpu_custom_call" | custom-call | flops 40000000000 | bytes 16777216 | tf_op jit(solution)/shard_map/feed_forward/pallas_call | solution.py:474
  184.0 1.6 collective-permute-start
  185.6 0.7 collective-permute-start.1
  186.3 1.3 collective-permute-start.2
  187.6 38.0 %attend_cross_backward.1 = (bf16[2048,256]{1,0:T(8,128)(2,1)}, bf16[2048,256]{1,0:T(8,128)(2,1)}, bf16[2048,256]{1,0:T(8,128)(2,1)}, bf16[2048,512]{1,0:T(8,128)(2,1)}) custom-call(s32[2,72]{1,0:T(2,128)} %get-tuple-element.89.table, bf16[256,2048]{1,0:T(8,128)(2,1)} %get-tuple-element.101.qt_ref, bf16[2048,256]{1,0:T(8,128)(2,1)} %get-tuple-element.102.k_ref, ...), custom_call_target="tpu_custom_call" | custom-call | flops 40000000000 | bytes 16777216 | tf_op jit(solution)/shard_map/attend_cross_backward/pallas_call | solution.py:474
  225.6 0.0 collective-permute-done.part1
  225.6 0.0 copy-start.8
  225.6 0.0 collective-permute-done.1.part2
  225.6 0.0 copy-start.9
  225.6 0.0 collective-permute-done.2.part3
  225.6 0.0 copy-start.10
  225.6 0.7 copy-done.8
  226.4 0.2 copy-done.9
  226.5 0.2 copy-done.10
  226.7 37.0 %cross_back.1 = (bf16[2048,512]{1,0:T(8,128)(2,1)}, f32[2048,512]{1,0:T(8,128)}, bf16[256,2048]{1,0:T(8,128)(2,1)}, bf16[4,208,512]{2,1,0:T(8,128)(2,1)}, bf16[4...) custom-call(bf16[2048,256]{1,0:T(8,128)(2,1)} %get-tuple-element.121.dq, ...), custom_call_target="tpu_custom_call" | custom-call | flops 40000000000 | bytes 16777216 | tf_op jit(solution)/shard_map/cross_back/pallas_call | solution.py:474
  263.8 0.1 collective-permute-start.3
  263.8 1.8 collective-permute-start.4
  265.6 1.7 collective-permute-start.5
  267.3 39.1 %attend_self_backward.1 = (bf16[2048,256]{1,0:T(8,128)(2,1)}, bf16[2048,256]{1,0:T(8,128)(2,1)}, bf16[2048,256]{1,0:T(8,128)(2,1)}, bf16[2048,512]{1,0:T(8,128)(2,1)}) custom-call(s32[2,72]{1,0:T(2,128)} %get-tuple-element.89.table, bf16[256,2048]{1,0:T(8,128)(2,1)} %get-tuple-element.91.qt_ref, bf16[2048,256]{1,0:T(8,128)(2,1)} %get-tuple-element.92.k_ref, ...), custom_call_target="tpu_custom_call" | custom-call | flops 40000000000 | bytes 16777216 | tf_op jit(solution)/shard_map/attend_self_backward/pallas_call | solution.py:474
  306.4 0.0 collective-permute-done.3.part1
  306.4 0.0 copy-start.5
  306.4 0.0 collective-permute-done.4.part2
  306.4 0.0 copy-start.6
  306.4 0.0 collective-permute-done.5.part3
  306.4 0.0 copy-start.7
  306.5 0.9 copy-done.5
  307.3 0.3 copy-done.6
  307.6 0.3 copy-done.7
  307.9 0.0 copy-start.1
  307.9 0.0 copy-start.3
  307.9 0.0 copy-start.4
  307.9 56.2 %self_back.1 = (bf16[2048,512]{1,0:T(8,128)(2,1)}, bf16[2048,512]{1,0:T(8,128)(2,1)}, bf16[16,128,512]{2,1,0:T(8,128)(2,1)}, f32[8,512]{1,0:T(8,128)}) custom-call(bf16[2048,256]{1,0:T(8,128)(2,1)} %get-tuple-element.142.dq, bf16[2048,256]{1,0:T(8,128)(2,1)} %get-tuple-element.143.dk, bf16[2048,256]{1,0:T(8,128)(2,1)} %get-tuple-element.144.dv, ...), custom_call_target="tpu_custom_call" | custom-call | flops 40000000000 | bytes 16777216 | tf_op jit(solution)/shard_map/self_back/pallas_call | solution.py:474
  364.1 0.7 copy.30
  364.8 0.0 copy-done.1
  364.8 0.0 copy-done.3
  364.8 0.0 copy-done.4
  364.8 0.7 multiply_subtract_fusion
  365.5 9.8 %update.1 = (f32[32,16,512]{2,1,0:T(8,128)}, f32[32,16,512]{2,1,0:T(8,128)}, f32[32,16,512]{2,1,0:T(8,128)}, f32[32,16,512]{2,1,0:T(8,128)}, bf16[2048,512]{1,0:T(8,128)(2,1)}, /*index=5*/bf16[2048,512]{1,0:T(8,128)(2,1)}) custom-call(s32[256]{0:T(256)} %owner_ref.3, s32[1]{0:T(128)} %bitcast.4.me_ref, bf16[16,128,512]{2,1,0:T(8,128)(2,1)} %get-tuple-element.155.summed, ...), custom_call_target="tpu_custom_call" | custom-call | flops 40000000000 | bytes 16777216 | tf_op jit(solution)/shard_map/update/pallas_call | solution.py:474
  (2 shorter events, 0.0 us)
Async XLA Ops:
  0.7 3.6 copy-start
  4.3 0.6 copy-start.2
  184.0 41.5 %collective-permute-start = (bf16[4,128,512]{2,1,0:T(8,128)(2,1)}, bf16[4,128,512]{2,1,0:T(8,128)(2,1)S(1)}, u32[]{:S(2)}, u32[]{:S(2)}) collective-permute-start(bf16[4,128,512]{2,1,0:T(8,128)(2,1)} %get-tuple-element.117), channel_id=1, source_target_pairs={{0,2},{2,0},{4,6},{6,4},{8,10},{10,8},{12,14},{14,12},{16,18},{18,... | collective-permute-start | bytes 1572872 | tf_op jit(solution)/shard_map/ppermute | solution.py:463
  185.6 40.0 %collective-permute-start.1 = (bf16[4,128,512]{2,1,0:T(8,128)(2,1)}, bf16[4,128,512]{2,1,0:T(8,128)(2,1)S(1)}, u32[]{:S(2)}, u32[]{:S(2)}) collective-permute-start(bf16[4,128,512]{2,1,0:T(8,128)(2,1)} %get-tuple-element.118), channel_id=1, source_target_pairs={{0,4},{2,6},{4,0},{6,2},{8,12},{10,14},{12,8},{14,10},{16,20},{18,... | collective-permute-start | bytes 1572872 | tf_op jit(solution)/shard_map/ppermute | solution.py:463
  186.3 39.3 %collective-permute-start.2 = (bf16[4,128,512]{2,1,0:T(8,128)(2,1)}, bf16[4,128,512]{2,1,0:T(8,128)(2,1)S(1)}, u32[]{:S(2)}, u32[]{:S(2)}) collective-permute-start(bf16[4,128,512]{2,1,0:T(8,128)(2,1)} %get-tuple-element.119), channel_id=1, source_target_pairs={{0,6},{2,4},{4,2},{6,0},{8,14},{10,12},{12,10},{14,8},{16,22},{18,... | collective-permute-start | bytes 1572872 | tf_op jit(solution)/shard_map/ppermute | solution.py:463
  225.6 0.8 copy-start.8
  225.6 0.9 copy-start.9
  225.6 1.1 copy-start.10
  263.8 42.6 %collective-permute-start.3 = (bf16[4,208,512]{2,1,0:T(8,128)(2,1)}, bf16[4,208,512]{2,1,0:T(8,128)(2,1)S(1)}, u32[]{:S(2)}, u32[]{:S(2)}) collective-permute-start(bf16[4,208,512]{2,1,0:T(8,128)(2,1)} %get-tuple-element.132), channel_id=1, source_target_pairs={{0,2},{2,0},{4,6},{6,4},{8,10},{10,8},{12,14},{14,12},{16,18},{18,... | collective-permute-start | bytes 2555912 | tf_op jit(solution)/shard_map/ppermute | solution.py:463
  263.8 42.6 %collective-permute-start.4 = (bf16[4,208,512]{2,1,0:T(8,128)(2,1)}, bf16[4,208,512]{2,1,0:T(8,128)(2,1)S(1)}, u32[]{:S(2)}, u32[]{:S(2)}) collective-permute-start(bf16[4,208,512]{2,1,0:T(8,128)(2,1)} %get-tuple-element.133), channel_id=1, source_target_pairs={{0,4},{2,6},{4,0},{6,2},{8,12},{10,14},{12,8},{14,10},{16,20},{18,... | collective-permute-start | bytes 2555912 | tf_op jit(solution)/shard_map/ppermute | solution.py:463
  265.6 40.8 %collective-permute-start.5 = (bf16[4,208,512]{2,1,0:T(8,128)(2,1)}, bf16[4,208,512]{2,1,0:T(8,128)(2,1)S(1)}, u32[]{:S(2)}, u32[]{:S(2)}) collective-permute-start(bf16[4,208,512]{2,1,0:T(8,128)(2,1)} %get-tuple-element.134), channel_id=1, source_target_pairs={{0,6},{2,4},{4,2},{6,0},{8,14},{10,12},{12,10},{14,8},{16,22},{18,... | collective-permute-start | bytes 2555912 | tf_op jit(solution)/shard_map/ppermute | solution.py:463
  306.4 0.9 copy-start.5
  306.4 1.2 copy-start.6
  306.4 1.5 copy-start.7
  307.9 56.9 %copy-start.1 = (f32[256]{0:T(256)S(1)}, f32[256]{0:T(256)}, u32[]{:S(2)}) copy-start(f32[256]{0:T(256)} %param.25) | copy-start | bytes 3076
  307.9 56.9 %copy-start.3 = (f32[256]{0:T(256)S(1)}, f32[256]{0:T(256)}, u32[]{:S(2)}) copy-start(f32[256]{0:T(256)} %param.27) | copy-start | bytes 3076
  307.9 56.9 %copy-start.4 = (f32[256]{0:T(256)S(1)}, f32[256]{0:T(256)}, u32[]{:S(2)}) copy-start(f32[256]{0:T(256)} %param.26) | copy-start | bytes 3076

commit v5 on v4

--- a/solution.py
+++ b/solution.py
@@ -24,7 +24,7 @@
 F32 = jnp.float32
 BF = jnp.bfloat16
 TQ = 256
-TK = 256
+TK = 384
 FAR = 32768.0
 LANES = (64, 72, 80)
 
@@ -55,7 +55,7 @@
         high = jnp.where(starts[d] <= q0 + TQ - 1, ends[d], high)
     first = lax.div(low, 128) * 128
     steps = lax.div(high - first + TK - 1, TK)
-    return jnp.minimum(first, ROW - steps * TK), steps
+    return first, steps
 
 
 def mask_tables(len_ref, rank_ref, side_ref, hot_ref, rank_cols):
@@ -84,7 +84,7 @@
         rank_cols[t * 128:(t + 1) * 128, :] = jnp.broadcast_to(rank[:, t * 128:(t + 1) * 128], (128, 128)).T
 
 
-STEPS = (ROW // TQ) * (ROW // TK) + 8
+STEPS = (ROW // TQ) * -(-ROW // TK) + 8
 
 
 def step_table(len_ref, table):
@@ -114,7 +114,21 @@
 
 
 def real_step(table, i):
-    return jnp.minimum(table[0, i], ROW // TQ - 1), pl.multiple_of(jnp.minimum(table[1, i], ROW - TK), 128)
+    return jnp.minimum(table[0, i], ROW // TQ - 1), pl.multiple_of(table[1, i], 128)
+
+
+def padded(ref):
+    return ref.at[pl.ds(0, ROW)] if ref.shape[0] > ref.shape[1] else ref.at[:, pl.ds(0, ROW)]
+
+
+def fill_padding(refs, side_ref):
+    for ref in refs:
+        if ref.shape[0] > ref.shape[1]:
+            ref[ROW:, :] = jnp.zeros((TK, ref.shape[1]), ref.dtype)
+        else:
+            ref[:, ROW:] = jnp.zeros((ref.shape[0], TK), ref.dtype)
+    lanes = lax.broadcasted_iota(jnp.int32, (TK, 128), 1)
+    side_ref[ROW:, :] = jnp.where(lanes < DOCS, -FAR, 0.0).astype(BF)
 
 
 def seen_bias(rank_cols, counts, tile, k0):
@@ -144,16 +158,21 @@
     return jnp.concatenate([ref[pl.ds(k0, TK), h // 2 * 128:(h // 2 + 1) * 128], side_ref[pl.ds(k0, TK), :]], 1)
 
 
-def attn_fwd_kernel(with_seen, heads, table, qt_ref, k_ref, vt_ref, side_ref, hot_ref, *refs):
-    if with_seen:
-        rank_cols, count_ref, *refs = refs
-    o_ref, ot_ref, lse_ref, qt, acc, top, sc, probs, fade, counts = refs
+def attn_fwd_kernel(with_seen, heads, table, count_ref, qt_hbm, hot_hbm, k_hbm, vt_hbm, side_hbm, rank_hbm,
+                    o_out, ot_out, lse_ref, qt, acc, top, sc, probs, fade, counts,
+                    qt_ref, hot_ref, k_ref, vt_ref, side_ref, rank_cols, o_ref, ot_ref, late_sems, out_sems):
+    pairs = [(qt_hbm, qt_ref), (hot_hbm, hot_ref), (k_hbm, padded(k_ref)), (vt_hbm, padded(vt_ref)),
+             (side_hbm, padded(side_ref))]
+    late = Late(pairs + ([(rank_hbm, padded(rank_cols))] if with_seen else []), late_sems)
+    fill_padding((k_ref, vt_ref, rank_cols), side_ref)
+    out = Out([(o_ref, o_out), (ot_ref, ot_out)], out_sems)
     tiles = ROW // TQ
     lse_ref[...] = jnp.zeros_like(lse_ref)
     acc[...] = jnp.zeros_like(acc)
     top[...] = jnp.full_like(top, -jnp.inf)
     if with_seen:
         count_tiles(counts, count_ref)
+    late.wait(0, 1)
 
     def prepare(tile, c):
         q0 = pl.multiple_of(tile * TQ, TQ)
@@ -161,6 +180,7 @@
             query_columns(qt, qt_ref, hot_ref[:, pl.ds(q0, TQ)], tile, h, q0)
         return c
     lax.fori_loop(0, tiles, prepare, 0)
+    late.wait(*range(2, 6 if with_seen else 5))
     ones = jnp.ones((16, TK), BF)
 
     def one_step(s, c):
@@ -200,23 +220,31 @@
             total = a[HEAD_DIM:HEAD_DIM + 1, :]
             outs.append(a[:HEAD_DIM, :] * (1.0 / total))
             lse_ref[h:h + 1, pl.ds(q0, TQ)] = peak[h:h + 1, :] + jnp.log(total)
-        out = jnp.concatenate(outs, 0)
-        ot_ref[:, pl.ds(q0, TQ)] = out.astype(BF)
-        o_ref[pl.ds(q0, TQ), :] = out.T.astype(BF)
+        mixed = jnp.concatenate(outs, 0).astype(BF)
+        ot_ref[:, pl.ds(q0, TQ)] = mixed
+        out.start(1, tile)
+        o_ref[pl.ds(q0, TQ), :] = mixed.T
+        out.start(0, tile)
         return c
     lax.fori_loop(0, tiles, finish, 0)
+    out.drain(ROW)
 
 
 def attend_forward(steps, qt, k, vt, tables, count, with_seen):
     cols, rows = qt.shape
     heads = cols // HEAD_DIM
     side, hot, rank_cols = tables
-    args = [steps, qt, k, vt, side, hot] + ([rank_cols, count] if with_seen else [])
+    args = [steps, count, qt, hot, k, vt, side, rank_cols]
+    across, down = (cols, rows), (rows, cols)
+    held = [pltpu.VMEM(arg.shape, BF) for arg in (qt, hot)] + [
+        pltpu.VMEM((rows + TK, cols), BF), pltpu.VMEM((cols, rows + TK), BF), pltpu.VMEM((rows + TK, 128), BF),
+        pltpu.VMEM((rows + TK, 128), F32)]
     return call(partial(attn_fwd_kernel, with_seen, heads), "attend_self_forward" if with_seen else "attend_cross_forward",
-                args, "S" + "V" * (len(args) - 1), [((rows, cols), BF, "V"), ((cols, rows), BF, "V"), ((8, rows), F32, "V")],
+                args, "SV" + "A" * 6, [(down, BF, "A"), (across, BF, "A"), ((8, rows), F32, "V")],
                 [pltpu.VMEM((ROW // TQ, heads, 256, TQ), BF), pltpu.VMEM((ROW // TQ + 1, heads, HEAD_DIM + 16, TQ), F32),
                  pltpu.VMEM((ROW // TQ + 1, 8, TQ), F32), pltpu.VMEM((heads, TK, TQ), F32), pltpu.VMEM((heads, TK, TQ), BF),
-                 pltpu.VMEM((8, TQ), F32)] + [pltpu.VMEM((ROW // TQ, 8, TQ), F32)])
+                 pltpu.VMEM((8, TQ), F32), pltpu.VMEM((ROW // TQ, 8, TQ), F32)] + held
+                + [pltpu.VMEM(down, BF), pltpu.VMEM(across, BF), pltpu.SemaphoreType.DMA((6,)), out_semaphores(2, rows)])
 
 
 def three_rows(value):
@@ -226,23 +254,25 @@
     return jnp.where(row == LANES[0], high, jnp.where(row == LANES[1], middle, jnp.where(row == LANES[2], value - high - middle, 0.0)))
 
 
-def attn_bwd_kernel(with_seen, heads, table, qt_ref, k_ref, kt_ref, v_ref, gt_ref, ot_ref, lse_ref,
-                    side_ref, hot_ref, *refs):
-    if with_seen:
-        rank_cols, count_ref, *refs = refs
-    (pass_in, dq_ref, dk_ref, dv_ref, pass_out, dk_sum, dv_sum, dq_sum, qt, gt, sc, dps, all_ds, all_p,
-     held, pass_sem, counts) = refs
+def attn_bwd_kernel(with_seen, heads, table, count_ref, lse_ref, qt_hbm, hot_hbm, gt_hbm, ot_hbm, k_hbm, kt_hbm, v_hbm, side_hbm,
+                    rank_hbm, pass_in,
+                    dq_out, dk_out, dv_out, pass_out, dk_sum, dv_sum, dq_sum, qt, gt, q_own, g_own, sc, dps, all_ds, all_p, counts,
+                    qt_ref, hot_ref, gt_ref, ot_ref, k_ref, kt_ref, v_ref, side_ref, rank_cols, held, dq_ref, dk_ref, dv_ref,
+                    late_sems, out_sems, pass_sem):
+    pairs = [(qt_hbm, qt_ref), (hot_hbm, hot_ref), (gt_hbm, gt_ref), (ot_hbm, ot_ref), (k_hbm, padded(k_ref)),
+             (kt_hbm, padded(kt_ref)), (v_hbm, padded(v_ref)), (side_hbm, padded(side_ref))]
+    late = Late(pairs + ([(rank_hbm, padded(rank_cols))] if with_seen else []), late_sems)
+    fill_padding((k_ref, kt_ref, v_ref, rank_cols), side_ref)
     entering = pltpu.make_async_copy(pass_in, held, pass_sem.at[0])
     entering.start()
+    out = Out([(dq_ref, dq_out), (dk_ref, dk_out), (dv_ref, dv_out)], out_sems)
     tiles = ROW // TQ
     dk_sum[...] = jnp.zeros_like(dk_sum)
     dv_sum[...] = jnp.zeros_like(dv_sum)
     dq_sum[...] = jnp.zeros_like(dq_sum)
     if with_seen:
         count_tiles(counts, count_ref)
-    entering.wait()
-    leaving = pltpu.make_async_copy(held, pass_out, pass_sem.at[1])
-    leaving.start()
+    late.wait(0, 1, 2, 3)
 
     def prepare(tile, c):
         q0 = pl.multiple_of(tile * TQ, TQ)
@@ -257,31 +287,40 @@
             gt[tile, h, h % 2 * HEAD_DIM:(h % 2 + 1) * HEAD_DIM, :] = grads
             gt[tile, h, other:other + HEAD_DIM, :] = jnp.zeros((HEAD_DIM, TQ), BF)
             gt[tile, h, 128:256, :] = three_rows(delta).astype(BF)
+        lane = lax.broadcasted_iota(jnp.int32, (TQ, heads * HEAD_DIM), 1)
+        for held_rows, source in ((q_own, qt_ref), (g_own, gt_ref)):
+            rows = source[:, pl.ds(q0, TQ)].T
+            for h in range(heads):
+                own = (lane >= h * HEAD_DIM) & (lane < (h + 1) * HEAD_DIM)
+                held_rows[tile, h * TQ:(h + 1) * TQ, :] = jnp.where(own, rows, jnp.zeros_like(rows))
         return c
     lax.fori_loop(0, tiles, prepare, 0)
+    late.wait(*range(4, 9 if with_seen else 8))
+    entering.wait()
+    leaving = pltpu.make_async_copy(held, pass_out, pass_sem.at[1])
+    leaving.start()
 
     def one_step(s, c):
         out_tile, out_k = step_of(table, s)
         read_tile, read_k = real_step(table, s)
         in_tile, in_k = real_step(table, s + 2)
         keys = pl.ds(out_k, TK)
-        queries = pl.ds(pl.multiple_of(read_tile * TQ, TQ), TQ)
         own = [slice(h * HEAD_DIM, (h + 1) * HEAD_DIM) for h in range(heads)]
-        dk = [dk_sum[h, :, keys] + nt(qt_ref[own[h], queries], all_ds[h]) for h in range(heads)]
-        dv = [dv_sum[h, :, keys] + nt(gt_ref[own[h], queries], all_p[h]) for h in range(heads)]
-        dq = [dq_sum[out_tile, h] + nn(kt_ref[own[h], pl.ds(read_k, TK)], all_ds[h]) for h in range(heads)]
+        dk = dk_sum[keys, :] + nn(all_ds[...], q_own[read_tile])
+        dv = dv_sum[keys, :] + nn(all_p[...], g_own[read_tile])
+        dq = [dq_sum[out_tile, h] + nn(kt_ref[own[h], pl.ds(read_k, TK)], all_ds[:, h * TQ:(h + 1) * TQ]) for h in range(heads)]
         for h in range(heads):
             p = jnp.exp(sc[h])
-            all_ds[h] = (p * dps[h]).astype(BF)
-            all_p[h] = p.astype(BF)
+            all_ds[:, h * TQ:(h + 1) * TQ] = (p * dps[h]).astype(BF)
+            all_p[:, h * TQ:(h + 1) * TQ] = p.astype(BF)
         bias = seen_bias(rank_cols, counts, in_tile, in_k) if with_seen else None
         for h in range(heads):
             score = nn(pair_rows(k_ref, side_ref, h, in_k), qt[in_tile, h])
             sc[h] = score + bias if with_seen else score
             dps[h] = nn(pair_rows(v_ref, side_ref, h, in_k), gt[in_tile, h])
+        dk_sum[keys, :] = dk
+        dv_sum[keys, :] = dv
         for h in range(heads):
-            dk_sum[h, :, keys] = dk[h]
-            dv_sum[h, :, keys] = dv[h]
             dq_sum[out_tile, h] = dq[h]
         return c
     lax.fori_loop(0, table[0, STEPS - 1], one_step, 0)
@@ -290,12 +329,13 @@
         q0 = pl.multiple_of(tile * TQ, TQ)
         rows = pl.ds(q0, TQ)
         dq = jnp.concatenate([dq_sum[tile, h] for h in range(heads)], 0) * HEAD_DIM ** -0.5
-        dk = jnp.concatenate([dk_sum[h, :, rows] for h in range(heads)], 0) * HEAD_DIM ** -0.5
-        dv = jnp.concatenate([dv_sum[h, :, rows] for h in range(heads)], 0)
-        for ref, value in ((dq_ref, dq), (dk_ref, dk), (dv_ref, dv)):
-            ref[rows, :] = value.astype(BF).T
+        dk = dk_sum[rows, :] * HEAD_DIM ** -0.5
+        for i, (ref, value) in enumerate(((dq_ref, dq.astype(BF).T), (dk_ref, dk.astype(BF)), (dv_ref, dv_sum[rows, :].astype(BF)))):
+            ref[rows, :] = value
+            out.start(i, tile)
         return c
     lax.fori_loop(0, tiles, finish, 0)
+    out.drain(ROW)
     leaving.wait()
 
 
@@ -303,16 +343,21 @@
     rows, cols = v.shape
     heads = cols // HEAD_DIM
     side, hot, rank_cols = tables
-    args = [steps, qt, k, kt, v, gt, ot, lse, side, hot] + ([rank_cols, count] if with_seen else []) + [passed]
-    like = ((rows, cols), BF, "V")
+    args = [steps, count, lse, qt, hot, gt, ot, k, kt, v, side, rank_cols, passed]
     tiles = ROW // TQ
-    summed = pltpu.VMEM((heads, HEAD_DIM, rows + TK), F32)
+    like = ((rows, cols), BF, "A")
+    summed, own = pltpu.VMEM((rows + TK, cols), F32), pltpu.VMEM((tiles, heads * TQ, cols), BF)
     columns, square = pltpu.VMEM((tiles, heads, 256, TQ), BF), pltpu.VMEM((heads, TK, TQ), F32)
-    small = pltpu.VMEM((heads, TK, TQ), BF)
+    small = pltpu.VMEM((TK, heads * TQ), BF)
+    keys, keys_t = pltpu.VMEM((rows + TK, cols), BF), pltpu.VMEM((cols, rows + TK), BF)
+    held = [pltpu.VMEM(arg.shape, BF) for arg in (qt, hot, gt, ot)] + [
+        keys, keys_t, keys, pltpu.VMEM((rows + TK, 128), BF), pltpu.VMEM((rows + TK, 128), F32),
+        pltpu.VMEM(passed.shape, passed.dtype)]
     return call(partial(attn_bwd_kernel, with_seen, heads), "attend_self_backward" if with_seen else "attend_cross_backward",
-                args, "S" + "V" * (len(args) - 2) + "A", [like, like, like, (passed.shape, passed.dtype, "A")],
-                [summed, summed, pltpu.VMEM((tiles + 1, heads, HEAD_DIM, TQ), F32), columns, columns, square, square,
-                 small, small, pltpu.VMEM(passed.shape, passed.dtype), pltpu.SemaphoreType.DMA((2,))] + [pltpu.VMEM((ROW // TQ, 8, TQ), F32)])
+                args, "SVV" + "A" * 10, [like, like, like, (passed.shape, passed.dtype, "A")],
+                [summed, summed, pltpu.VMEM((tiles + 1, heads, HEAD_DIM, TQ), F32), columns, columns, own, own, square, square,
+                 small, small, pltpu.VMEM((ROW // TQ, 8, TQ), F32)] + held + [pltpu.VMEM((rows, cols), BF)] * 3
+                + [pltpu.SemaphoreType.DMA((9,)), out_semaphores(3, rows), pltpu.SemaphoreType.DMA((2,))])
 
 
 def send(src, dst, send_sem, recv_sem, **where):
@@ -374,89 +419,51 @@
     recv[d][1].wait_recv()
     diag.append(go(base + 2 - 4 * y, (half, rows - half), gx, d, xpeer))
 
-def part_sizes(rows):
-    first = rows // 2 // UNIT * UNIT
-    return [(part, pl.ds(start, size), size) for part, start, size in ((0, 0, first), (1, first, rows - first)) if size]
-
-
-class BlockSum:
-    def __init__(self, count, places, source, out, keep, r1, r2, r3, s1, s2, s3):
-        self.count, self.places, self.source, self.out = count, places, source, out
-        self.keep, self.r1, self.r2, self.r3, self.s1, self.s2, self.s3 = keep, r1, r2, r3, s1, s2, s3
-        self.parts = part_sizes(source.shape[1])
-        self.first, self.second, self.third = {}, {}, {}
-
-    def at(self, d, first, second, part):
-        z, across = self.places[3], self.count // 4
-        return lax.rem(z + d, across) * 4 + (first + 2 * second if part == 0 else 2 * first + second)
+class Spread:
+    def __init__(self, places, out, zs, xs, ys, gx, gy):
+        self.places, self.out, self.sems = places, out, dict(z=zs, x=xs, y=ys, gx=gx, gy=gy)
+        self.rows = out.shape[2]
+        self.half = self.rows // 2 // UNIT * UNIT
+        self.copies = {}
+
+    def go(self, name, d, f_from, d_from, f_to, d_to, to, start, size):
+        part, sems = pl.ds(start, size), self.sems[name]
+        self.copies[name, d] = send(self.out.at[f_from, d_from, part], self.out.at[f_to, d_to, part],
+                                    sems.at[0, d], sems.at[1, d], dp=to)
+
+    def over_plane(self, d):
+        xpeer, ypeer = self.places[4], self.places[5]
+        self.go("x", d, 0, d, 1, d, xpeer, 0, self.rows)
+        self.go("y", d, 0, d, 2, d, ypeer, 0, self.rows)
 
     def start(self):
-        me, x, y, z, xpeer, ypeer, order, ahead, behind = self.places
-        self.steps = order + [0]
-        self.mine = [(x, y), (y, x)]
-        self.peers = [(xpeer, ypeer), (ypeer, xpeer)]
-        for d in self.steps:
-            for part, rows, size in self.parts:
-                f, s = self.mine[part]
-                for t in (0, 1):
-                    second = s if t else 1 - s
-                    self.first[d, part, t] = send(
-                        self.source.at[self.at(d, 1 - f, second, part), rows], self.r1.at[part, d, t, pl.ds(0, size)],
-                        self.s1.at[0, part, d, t], self.s1.at[1, part, d, t], dp=self.peers[part][0])
-
-    def second_stage(self, d):
-        for part, rows, size in self.parts:
-            f, s = self.mine[part]
-            into = pl.ds(0, size)
-            for t in (0, 1):
-                second = s if t else 1 - s
-                self.first[d, part, t].wait_recv()
-                self.keep[part, d, t, into, :] = (self.source[self.at(d, f, second, part), rows, :].astype(F32)
-                                                  + self.r1[part, d, t, into, :].astype(F32)).astype(BF)
-                if t == 0:
-                    self.second[d, part] = send(self.keep.at[part, d, 0, into], self.r2.at[part, d, into],
-                                                self.s2.at[0, part, d], self.s2.at[1, part, d], dp=self.peers[part][1])
-
-    def third_stage(self, d):
-        ahead = self.places[7]
-        for part, rows, size in self.parts:
-            into = pl.ds(0, size)
-            self.second[d, part].wait_recv()
-            self.keep[part, d, 1, into, :] = (self.keep[part, d, 1, into, :].astype(F32)
-                                              + self.r2[part, d, into, :].astype(F32)).astype(BF)
-            if d:
-                self.third[d, part] = send(self.keep.at[part, d, 1, into], self.r3.at[part, d, into],
-                                           self.s3.at[0, part, d], self.s3.at[1, part, d], dp=ahead(d))
+        order, ahead = self.places[6], self.places[7]
+        for d in order:
+            self.go("z", d, 0, 0, 0, d, ahead(d), 0, self.rows)
+        self.over_plane(0)
+
+    def relay(self):
+        for d in self.places[6]:
+            self.copies["z", d].wait_recv()
+            self.over_plane(d)
+
+    def diagonal(self):
+        xpeer, ypeer, order = self.places[4:7]
+        for d in [0] + order:
+            self.copies["x", d].wait_recv()
+            if self.half:
+                self.go("gy", d, 1, d, 3, d, ypeer, 0, self.half)
+            self.copies["y", d].wait_recv()
+            self.go("gx", d, 2, d, 3, d, xpeer, self.half, self.rows - self.half)
 
     def finish(self):
-        me, order = self.places[0], self.places[6]
-        for k, d in enumerate(self.steps):
-            self.second_stage(d)
-            if k:
-                self.third_stage(self.steps[k - 1])
-        self.third_stage(0)
-        for part, rows, size in self.parts:
-            into = pl.ds(0, size)
-            total = self.keep[part, 0, 1, into, :].astype(F32)
-            for d in order:
-                self.third[d, part].wait_recv()
-                total = total + self.r3[part, d, into, :].astype(F32)
-            self.out[me, rows, :] = total.astype(BF)
+        for (name, d), copy in self.copies.items():
+            if name in ("gx", "gy"):
+                copy.wait_recv()
 
     def drain(self):
-        for copies in (self.first, self.second, self.third):
-            for copy in copies.values():
-                copy.wait_send()
-
-
-def block_sum_scratch(count, rows, cols):
-    across = count // 4
-    size = max(size for _, _, size in part_sizes(rows))
-    D = pltpu.SemaphoreType.DMA
-    return [
-        pltpu.VMEM((2, across, 2, size, cols), BF), pltpu.VMEM((2, across, 2, size, cols), BF),
-        pltpu.VMEM((2, across, size, cols), BF), pltpu.VMEM((2, across, size, cols), BF),
-        D((2, 2, across, 2)), D((2, 2, across)), D((2, 2, across))]
+        for copy in self.copies.values():
+            copy.wait_send()
 
 
 def plane_swap(value, count, f):
@@ -533,11 +540,11 @@
     greet([{"head": 1 - lax.axis_index("head")}])
 
 
-def chunks(total, body):
+def chunks(total, body, begin=0):
     def one(step, carry):
         body(step, pl.ds(pl.multiple_of(step * CHUNK, CHUNK), CHUNK))
         return carry
-    lax.fori_loop(0, total // CHUNK, one, 0)
+    lax.fori_loop(begin // CHUNK, total // CHUNK, one, 0)
 
 
 def drain(total, mine, theirs, sems):
@@ -763,7 +770,7 @@
 
 
 def feed_forward_kernel(devices, mixed, wo, res_hbm, w1, w2, out_grad_hbm, norms,
-                        out_out, gres_out, gmix_out, part0, part1, part2, part3, gwo_ref, sums_ref,
+                        out_out, gres_out, gmix_out, part0, part1, part2, part3, sums_ref,
                         res, out_grad, out_ref, gres_ref, gmix_ref, flat,
                         mine, theirs, nf_all, hid_all, pre_all, low_all, mine_o, theirs_o, mine_g, theirs_g,
                         sems, sems_o, sems_g, late_sems, out_sems):
@@ -805,15 +812,14 @@
     chunks(tokens, middle)
 
     order = interleave(features)
-    half = features // 2
+    half, cols = features // 2, mixed.shape[1]
     for block in range(hidden // 256):
         at = slice(block * 256, (block + 1) * 256)
-        flat[hidden + block * 256:hidden + (block + 1) * 256, :] = tn(hid_all[:, at], out_grad[...]).astype(BF)
+        flat[cols + hidden + block * 256:cols + hidden + (block + 1) * 256, :] = tn(hid_all[:, at], out_grad[...]).astype(BF)
     for block in range(hidden // features):
         gradient = tn(nf_all[:, block * half:(block + 1) * half], pre_all[...]).astype(BF)
         stacked = jnp.concatenate([gradient[:, :features], gradient[:, features:]], 0)
-        flat[block * features:(block + 1) * features, :] = nn(order, stacked).astype(BF)
-    spread_flat(devices, places, flat, (part0, part1, part2, part3))
+        flat[cols + block * features:cols + (block + 1) * features, :] = nn(order, stacked).astype(BF)
     sums_ref[...] = jnp.zeros_like(sums_ref)
 
     def close(step, rows):
@@ -834,24 +840,31 @@
         gmix_ref[:, rows] = nt(low, wo[...]).astype(BF).T
         out.start(2, step)
     chunks(tokens, close)
-    gwo_ref[...] = tn(mixed[...], low_all[...]).astype(BF)
+    flat[0:cols, :] = tn(mixed[...], low_all[...]).astype(BF)
+    if flat.shape[0] > cols + 2 * hidden:
+        flat[cols + 2 * hidden:, :] = jnp.zeros((flat.shape[0] - cols - 2 * hidden, features), BF)
+    spread_flat(devices, places, flat, (part0, part1, part2, part3))
     out.drain(tokens)
     drain(tokens, mine, theirs, sems)
     drain(tokens, mine_o, theirs_o, sems_o)
     drain(tokens, mine_g, theirs_g, sems_g)
 
 
+def whole_blocks(rows, devices):
+    return -(-rows // (devices * UNIT)) * devices * UNIT
+
+
 def feed_forward(devices, mixed, wo, res, w1, w2, out_grad, norms):
     tokens, features = out_grad.shape
     hidden = w2.shape[0]
-    part = ((devices // 4, 2 * hidden // devices, features), BF, "V")
+    flat_rows = whole_blocks(wo.shape[0] + 2 * hidden, devices)
+    part = ((devices // 4, flat_rows // devices, features), BF, "V")
     wide = (tokens, features)
     across = (mixed.shape[1], tokens)
-    outs = [(wide, BF, "A"), (wide, F32, "A"), (across, BF, "A")] + [part] * 4 + [
-        (wo.shape, BF, "V"), ((16, features), F32, "V")]
+    outs = [(wide, BF, "A"), (wide, F32, "A"), (across, BF, "A")] + [part] * 4 + [((16, features), F32, "V")]
     deep, narrow = pltpu.VMEM((tokens, hidden), BF), pltpu.VMEM(wide, BF)
     scratch = [pltpu.VMEM(wide, F32), narrow, narrow, pltpu.VMEM(wide, F32), pltpu.VMEM(across, BF),
-               pltpu.VMEM((2 * hidden, features), BF), narrow, narrow, narrow, deep, deep, narrow] + [narrow] * 4
+               pltpu.VMEM((flat_rows, features), BF), narrow, narrow, narrow, deep, deep, narrow] + [narrow] * 4
     scratch += [pair_sems(tokens)] * 3 + [pltpu.SemaphoreType.DMA((2,)), out_semaphores(3, tokens)]
     return call(partial(feed_forward_kernel, devices), "feed_forward", [mixed, wo, res, w1, w2, out_grad, norms], "VVAVVAV",
                 outs, scratch, 3)
@@ -891,7 +904,7 @@
     return (parts[0][at].astype(F32) + parts[1][at].astype(F32) + parts[2][at].astype(F32) + parts[3][at].astype(F32)).astype(BF)
 
 
-def cross_back_kernel(devices, dq, dk, dv, wc, nc_hbm, memory_hbm, res_hbm, gres_hbm, mixed, wo, norms, gwo_cross,
+def cross_back_kernel(devices, dq, dk, dv, wc, nc_hbm, memory_hbm, res_hbm, gres_hbm, mixed, wo, norms,
                       part0, part1, part2, part3,
                       gmem_out, gnew_out, gmix_out, give0, give1, give2, give3, sums_ref,
                       nc, memory, res, gres, gmem_ref, gnew_ref, gmix_ref, flat, pieces, landed, blocks,
@@ -933,9 +946,8 @@
         out.start(0, step)
     chunks(tokens, close)
     flat[3 * cols:4 * cols, :] = tn(mixed[...], low_all[...]).astype(BF)
-    flat[4 * cols:5 * cols, :] = gwo_cross[...]
-    if flat.shape[0] > 5 * cols:
-        flat[5 * cols:, :] = jnp.zeros((flat.shape[0] - 5 * cols, features), BF)
+    if flat.shape[0] > 4 * cols:
+        flat[4 * cols:, :] = jnp.zeros((flat.shape[0] - 4 * cols, features), BF)
     gives = (give0, give1, give2, give3)
     spread_flat(devices, places, flat, gives)
     for copy in zz_copies:
@@ -951,11 +963,11 @@
     drain(tokens, mine_b, theirs_b, sems_b)
 
 
-def cross_back(devices, dq, dk, dv, wc, nc, memory, res, gres, mixed, wo, norms, gwo_cross, parts):
+def cross_back(devices, dq, dk, dv, wc, nc, memory, res, gres, mixed, wo, norms, parts):
     tokens, features = nc.shape
     cols = dq.shape[1]
     across, ready_rows = devices // 4, parts[0].shape[1]
-    flat_rows = -(-5 * cols // (devices * UNIT)) * devices * UNIT
+    flat_rows = whole_blocks(4 * cols, devices)
     give = ((across, ready_rows + flat_rows // devices, features), BF, "V")
     wide = (tokens, features)
     outs = [(wide, BF, "A"), (wide, F32, "A"), ((cols, tokens), BF, "A")] + [give] * 4 + [((16, features), F32, "V")]
@@ -965,37 +977,38 @@
     scratch = [low, low, high, high, low, high, pltpu.VMEM((cols, tokens), BF), pltpu.VMEM((flat_rows, features), BF), small, small, small]
     scratch += [low] * 5 + [pair_sems(tokens)] * 2 + [pltpu.SemaphoreType.DMA((4,)), out_semaphores(3, tokens), z_sems, z_sems]
     return call(partial(cross_back_kernel, devices), "cross_back",
-                [dq, dk, dv, wc, nc, memory, res, gres, mixed, wo, norms, gwo_cross] + parts, "VVVVAAAAVVVVVVVV", outs, scratch, 4)
+                [dq, dk, dv, wc, nc, memory, res, gres, mixed, wo, norms] + parts, "VVVVAAAAVVVVVVV", outs, scratch, 4)
 
 
 def self_back_kernel(devices, ready_rows, dq, dk, dv, ws, nq_hbm, nkv_hbm, query_hbm, kv_hbm, gres_hbm, norms, sums_c, sums_f,
                      part0, part1, part2, part3,
-                     gquery_out, gkv_out, summed, gnorm_ref,
-                     nq, nkv, query, kv, gres, gquery_ref, gkv_ref, flat, source, pieces, landed, norm_mine, norm_all,
-                     mine_a, theirs_a, mine_b, theirs_b, sums, sems_a, sems_b, late_sems, out_sems, z_sems, n_sems, *block_refs):
+                     gquery_out, gkv_out, last_ref, more_ref, gnorm_ref,
+                     nq, nkv, query, kv, gres, gquery_ref, gkv_ref, flat, source, landing, pieces, landed, more_pieces, more_landed,
+                     norm_mine, norm_all, mine_a, theirs_a, mine_b, theirs_b, sums, sems_a, sems_b, late_sems, out_sems,
+                     z_sems, more_z_sems, plane_sems, n_sems, *spread_sems):
     tokens, features = nq.shape
     across = devices // 4
     places = places_of(devices)
     me, x, y, z, xpeer, ypeer, order, ahead, behind = places
     late = Late([(nq_hbm, nq), (nkv_hbm, nkv), (query_hbm, query), (kv_hbm, kv), (gres_hbm, gres)], late_sems)
     out = Out([(gquery_ref, gquery_out), (gkv_ref, gkv_out)], out_sems)
-    more_rows = part0.shape[1] - ready_rows
+    more_rows = more_ref.shape[2]
     for level in range(across):
-        pieces[level] = four_sum((part0, part1, part2, part3), (level, pl.ds(ready_rows, more_rows)))
+        more_pieces[level] = four_sum((part0, part1, part2, part3), (level, pl.ds(ready_rows, more_rows)))
     others = [lax.rem(me + d, devices) for d in range(1, devices)]
     greet([{"head": 1 - lax.axis_index("head")}] + [{"dp": other} for other in others])
-    z_copies = z_sum_start(devices, places, pieces, landed, z_sems)
+    more_copies = z_sum_start(devices, places, more_pieces, more_landed, more_z_sems)
     branch_give(dq, dk, dv, ws, mine_a, theirs_a, mine_b, theirs_b, sems_a, sems_b)
     late.wait(0, 1)
     branch_weights(nq, nkv, dq, dk, dv, flat)
-    rows = source.shape[1]
     if flat.shape[0] > 3 * dq.shape[1]:
         flat[3 * dq.shape[1]:, :] = jnp.zeros((flat.shape[0] - 3 * dq.shape[1], features), BF)
-    for block in range(devices):
-        source[block] = flat[block * rows:(block + 1) * rows, :]
-    block_sum = BlockSum(devices, places, source, summed, *block_refs[:7])
-    block_sum.start()
-    summed[me, pl.ds(rows, more_rows), :] = z_sum_end(places, pieces, landed, z_copies)
+    spread_flat(devices, places, flat, [source.at[f] for f in range(4)])
+    plane_copies = [send(source.at[f], landing.at[f], plane_sems.at[0, f], plane_sems.at[1, f], dp=peer)
+                    for f, peer in ((3, me + 3 - 2 * x - 4 * y), (1, xpeer), (2, ypeer))]
+    more_ref[0, 0] = z_sum_end(places, more_pieces, more_landed, more_copies)
+    more = Spread(places, more_ref, *spread_sems[:5])
+    more.start()
     sums[...] = jnp.zeros_like(sums)
     late.wait(2, 3, 4)
 
@@ -1014,23 +1027,36 @@
         out.start(1, step)
         sums[16:24, :] += fold_rows(grad * unit)
         sums[24:32, :] += fold_rows(grad)
-    chunks(tokens, close)
+    middle = tokens // 2
+    chunks(middle, close)
+    more.relay()
+    chunks(tokens, close, middle)
     parts = [sums[8 * i:8 * i + 8, :] for i in range(4)]
     parts += [sums_c[0:8, :], sums_c[8:16, :], sums_f[0:8, :], sums_f[8:16, :]]
     norm_mine[...] = jnp.concatenate([jnp.sum(part, 0, keepdims=True) for part in parts], 0)
+    for copy in plane_copies:
+        copy.wait_recv()
+    for level in range(across):
+        pieces[level] = four_sum((source.at[0], landing.at[1], landing.at[2], landing.at[3]), level)
+    z_copies = z_sum_start(devices, places, pieces, landed, z_sems)
     n_copies = [send(norm_mine, norm_all.at[d], n_sems.at[0, d], n_sems.at[1, d], dp=other)
                 for d, other in zip(range(1, devices), others)]
-    block_sum.finish()
-    out_rows = summed.shape[1]
-    spread_blocks(devices, lambda block, start, size: summed.at[block, pl.ds(start, size)], out_rows, out_rows // 2 // UNIT * UNIT,
-                  places, *block_refs[7:])
+    more.diagonal()
+    last_ref[0, 0] = z_sum_end(places, pieces, landed, z_copies)
+    last = Spread(places, last_ref, *spread_sems[5:])
+    last.start()
+    last.relay()
+    last.diagonal()
     total = norm_mine[...]
     for d, copy in zip(range(1, devices), n_copies):
         copy.wait_recv()
         total = total + norm_all[d]
     gnorm_ref[...] = total
-    block_sum.drain()
-    for copy in z_copies + n_copies:
+    more.finish()
+    last.finish()
+    more.drain()
+    last.drain()
+    for copy in more_copies + plane_copies + z_copies + n_copies:
         copy.wait_send()
     out.drain(tokens)
     drain(tokens, mine_a, theirs_a, sems_a)
@@ -1041,32 +1067,33 @@
     tokens, features = nq.shape
     cols = dq.shape[1]
     across, more_rows = devices // 4, parts[0].shape[1] - ready_rows
-    flat_rows = -(-3 * cols // (devices * UNIT)) * devices * UNIT
+    flat_rows = whole_blocks(3 * cols, devices)
     rows = flat_rows // devices
     wide = (tokens, features)
-    outs = [(wide, BF, "A"), (wide, BF, "A"), ((devices, rows + more_rows, features), BF, "V"), ((8, features), F32, "V")]
+    outs = [(wide, BF, "A"), (wide, BF, "A"), ((4, across, rows, features), BF, "V"), ((4, across, more_rows, features), BF, "V"),
+            ((8, features), F32, "V")]
     low, high = pltpu.VMEM(wide, BF), pltpu.VMEM(wide, F32)
-    small = pltpu.VMEM((across, more_rows, features), BF)
+    small, tiny = pltpu.VMEM((across, more_rows, features), BF), pltpu.VMEM((across, rows, features), BF)
+    four = pltpu.VMEM((4, across, rows, features), BF)
     D = pltpu.SemaphoreType.DMA
-    scratch = [low, low, low, low, high, low, low, pltpu.VMEM((flat_rows, features), BF), pltpu.VMEM((devices, rows, features), BF),
-               small, small, pltpu.VMEM((8, features), F32), pltpu.VMEM((devices, 8, features), F32)]
+    scratch = [low, low, low, low, high, low, low, pltpu.VMEM((flat_rows, features), BF), four, four, tiny, tiny, small, small,
+               pltpu.VMEM((8, features), F32), pltpu.VMEM((devices, 8, features), F32)]
     scratch += [low] * 4 + [pltpu.VMEM((32, features), F32)] + [pair_sems(tokens)] * 2
-    scratch += [D((5,)), out_semaphores(2, tokens), D((2, across)), D((2, devices))]
-    scratch += block_sum_scratch(devices, rows, features) + [D((2, across))] * 5
+    scratch += [D((5,)), out_semaphores(2, tokens), D((2, across)), D((2, across)), D((2, 4)), D((2, devices))]
+    scratch += [D((2, across))] * 10
     return call(partial(self_back_kernel, devices, ready_rows), "self_back",
                 [dq, dk, dv, ws, nq, nkv, query, kv, gres, norms, sums_c, sums_f] + parts, "VVVVAAAAAVVVVVVV", outs, scratch, 5)
 
 
-def update_kernel(devices, early_unit, late_unit, own_rows, last_rows, owner_ref, me_ref, summed, part0, part1, part2, part3,
+def update_kernel(devices, early_unit, late_unit, late_rows, owner_ref, me_ref, last, more, part0, part1, part2, part3,
                   master, first, second, gquery_in, gkv_in, grad_ref, first_ref, second_ref, new_ref, gquery_out, gkv_out,
                   held, taken, held_q, held_kv, sems):
     units = owner_ref.shape[0]
     slots = master.shape[0]
     across = devices // 4
-    more_rows = summed.shape[1] - own_rows
     me = me_ref[0]
+    here, level = lax.rem(me, 4), lax.div(me, 4)
     entering = Late([(gquery_in, held_q), (gkv_in, held_kv)], sems.at[0])
-    here, level = lax.rem(me, 4), lax.div(me, 4)
 
     def find(u, count):
         held[count] = u
@@ -1075,8 +1102,10 @@
     entering.wait(0, 1)
     leaving = Late([(held_q, gquery_out), (held_kv, gkv_out)], sems.at[1])
 
-    def rows_of(row, size, start):
-        return pl.ds(pl.multiple_of(lax.rem(row, size) + start, UNIT), UNIT)
+    def lookup(row, size):
+        block = lax.div(row, size)
+        behind = lax.rem(level - lax.div(block, 4) + across, across)
+        return lax.rem(block, 4) ^ here, behind, pl.ds(pl.multiple_of(lax.rem(row, size), UNIT), UNIT)
 
     def one(slot, carry):
         @pl.when(slot < count)
@@ -1085,23 +1114,19 @@
 
             @pl.when(unit < early_unit)
             def _():
-                row = unit * UNIT
-                taken[...] = summed[lax.div(row, own_rows), rows_of(row, own_rows, 0), :]
+                taken[...] = last[lookup(unit * UNIT, last.shape[2])]
 
             @pl.when((unit >= early_unit) & (unit < late_unit))
             def _():
-                row = (unit - early_unit) * UNIT
-                taken[...] = summed[lax.div(row, more_rows), rows_of(row, more_rows, own_rows), :]
+                taken[...] = more[lookup((unit - early_unit) * UNIT, more.shape[2])]
 
             @pl.when(unit >= late_unit)
             def _():
-                row = (unit - late_unit) * UNIT
-                block = lax.div(row, last_rows)
-                behind = lax.rem(level - lax.div(block, 4) + across, across)
+                offset, behind, rows = lookup((unit - late_unit) * UNIT, late_rows)
                 for f, part in enumerate((part0, part1, part2, part3)):
-                    @pl.when(lax.rem(block, 4) == here ^ f)
+                    @pl.when(offset == f)
                     def _():
-                        taken[...] = part[behind, rows_of(row, last_rows, 0), :]
+                        taken[...] = part[behind, rows]
             gradient = taken[...].astype(F32)
             first_new, second_new, weight = adamw_step(gradient, first[slot], second[slot], master[slot], RATE_MATRIX, WEIGHT_DECAY)
             grad_ref[slot] = gradient
@@ -1118,10 +1143,10 @@
     leaving.wait(0, 1)
 
 
-def update(devices, early_unit, late_unit, own_rows, last_rows, unit_owner, me, summed, parts, master, first, second, gquery, gkv):
+def update(devices, early_unit, late_unit, late_rows, unit_owner, me, last, more, parts, master, first, second, gquery, gkv):
     outs = [(master.shape, F32, "V")] * 4 + [(gquery.shape, BF, "A")] * 2
-    kernel = partial(update_kernel, devices, early_unit, late_unit, own_rows, last_rows)
-    return call(kernel, "update", [unit_owner, me, summed] + parts + [master, first, second, gquery, gkv], "SSVVVVVVVVAA", outs,
+    kernel = partial(update_kernel, devices, early_unit, late_unit, late_rows)
+    return call(kernel, "update", [unit_owner, me, last, more] + parts + [master, first, second, gquery, gkv], "SSVVVVVVVVVAA", outs,
                 [pltpu.SMEM((unit_owner.shape[0] + 8,), jnp.int32), pltpu.VMEM((UNIT, master.shape[2]), BF),
                  pltpu.VMEM(gquery.shape, BF), pltpu.VMEM(gkv.shape, BF), pltpu.SemaphoreType.DMA((2, 2))])
 
@@ -1159,7 +1184,7 @@
     mixed_self, mixed_self_t, total_self = attend_forward(steps, qt, k, vt, tables, count_row, True)
     residual, nc, qct = self_out(mixed_self, wo_self, query_stream, wc, norms)
     mixed_cross, mixed_cross_t, total_cross = attend_forward(steps, qct, kc, vct, tables, count_row, False)
-    output, grad_cross_res, grad_mixed, *parts, gwo_cross, sums_f = feed_forward(
+    output, grad_cross_res, grad_mixed, *parts, sums_f = feed_forward(
         devices, mixed_cross, wo_cross, residual, w1, w2, out_grad, norms)
     tie = lax.optimization_barrier
     ready_rows = parts[0].shape[1]
@@ -1168,18 +1193,17 @@
         steps, qct, kc, kct, vc, grad_mixed, mixed_cross_t, total_cross, tables, count_row, output, False)
     parts, dq = tie((parts, dq))
     grad_memory, grad_residual, grad_mixed, *parts, sums_c = cross_back(
-        devices, dq, dk, dv, wc, nc, memory, residual, grad_cross_res, mixed_self, wo_self, norms, gwo_cross, parts)
+        devices, dq, dk, dv, wc, nc, memory, residual, grad_cross_res, mixed_self, wo_self, norms, parts)
     parts = [parts[0]] + [plane_swap(parts[f], devices, f) for f in (1, 2, 3)]
     dq, dk, dv, grad_memory = attend_backward(
         steps, qt, k, kt, v, grad_mixed, mixed_self_t, total_self, tables, count_row, grad_memory, True)
     parts, dq = tie((parts, dq))
-    grad_query, grad_kv, summed, norm_grads = self_back(
+    grad_query, grad_kv, last, more, norm_grads = self_back(
         devices, ready_rows, dq, dk, dv, ws, nq, nkv, query_stream, kv_stream, grad_residual, norms, sums_c, sums_f, parts)
 
-    early, late = 3 * cols // unit_rows, 8 * cols // unit_rows
-    own_rows = -(-3 * cols // (devices * UNIT)) * UNIT
+    early, late = 3 * cols // unit_rows, 7 * cols // unit_rows
     weight_grad, weight_first, weight_second, weight_new, grad_query, grad_kv = update(
-        devices, early, late, own_rows, ready_rows, unit_owner, me.reshape(1), summed, parts, master.reshape(shape),
+        devices, early, late, ready_rows, unit_owner, me.reshape(1), last, more, parts, master.reshape(shape),
         first_moment.reshape(shape), second_moment.reshape(shape), grad_query, grad_kv)
     weight_grad, weight_first, weight_second, weight_new = [
         part.reshape(master.shape) for part in (weight_grad, weight_first, weight_second, weight_new)]

time: 377 us -> 367 us (0.973)
  Pallas kernels: 363 us -> 352 us
    pallas_call x11, Pallas kernels: 363 us -> 352 us  [call(): pl.pallas_call(kernel, out_shape=tuple((jax.ShapeDtypeStruct(shape, dtype...]
  transfers between devices with their start and end apart: 6 -> 6, of which waited for: 0 -> 1; matrix products, arithmetic and copies ran while one was open for 0% -> 0% of each run, Pallas kernels for 21% -> 19%
where the time goes in v5:
time: 367 us; the launch traced here: 369 us
  Pallas kernels  352 us (96%)
  starting transfers between devices  10.6 us (3%)
    pallas_call x11, Pallas kernels, call(): pl.pallas_call(kernel, out_shape=tuple((jax.ShapeDtypeStruct(shape, dtype...  352 us
    ppermute x6, starting transfers between devices, plane_swap(): lax.ppermute(value, 'dp', [(i, i // 4 * 4 + (i % 4 ^ f)) for i in range(c...  10.6 us
  transfers between devices with their start and end apart: 6, of which 1 were waited for; matrix products, arithmetic and copies ran while one was open for 0% of the time, Pallas kernels for 19%

profile of v5, /device:TPU:0, one launch (start us, length us, event | category | flops | bytes accessed | tf_op | source)
XLA Modules:
  0.0 368.8 jit_solution(14359560940000389244)
XLA Ops:
  0.7 0.0 copy-start
  0.7 3.5 plan.1
  4.2 0.0 copy-done
  4.2 0.0 copy-start.2
  4.2 0.6 copy-done.2
  4.8 92.0 %project.1 = (bf16[2048,512]{1,0:T(8,128)(2,1)}, bf16[2048,512]{1,0:T(8,128)(2,1)}, bf16[256,2048]{1,0:T(8,128)(2,1)}, bf16[2048,256]{1,0:T(8,128)(2,1)}, bf16[2...) custom-call(s32[256]{0:T(256)} %get-tuple-element.90.place_ref, ...), custom_call_target="tpu_custom_call" | custom-call | flops 40000000000 | bytes 16777216 | tf_op jit(solution)/shard_map/project/pallas_call | solution.py:481
  96.7 22.2 %attend_self_forward.1 = (bf16[2048,256]{1,0:T(8,128)(2,1)}, bf16[256,2048]{1,0:T(8,128)(2,1)}, f32[8,2048]{1,0:T(8,128)}) custom-call(s32[2,56]{1,0:T(2,128)} %get-tuple-element.89.table, s32[1,2048]{1,0:T(1,128)} %bitcast.29, bf16[256,2048]{1,0:T(8,128)(2,1)} %get-tuple-element.91.qt_hbm, bf16[128,2048]{1,0:T(8,128)(2,1)} %get-tuple-element.92.hot_hbm, ...), custom_call_target="tpu_custom_call" | custom-call | flops 40000000000 | bytes 16777216 | tf_op jit(solution)/shard_map/attend_self_forward/pallas_call | solution.py:481
  118.9 8.4 %self_out.1 = (f32[2048,512]{1,0:T(8,128)}, bf16[2048,512]{1,0:T(8,128)(2,1)}, bf16[256,2048]{1,0:T(8,128)(2,1)}) custom-call(bf16[2048,256]{1,0:T(8,128)(2,1)} %get-tuple-element.97.mixed, bf16[256,512]{1,0:T(8,128)(2,1)} %get-tuple-element.98.wo, bf16[2048,512]{1,0:T(8,128)(2,1)} %query_hbm.5, bf16[3,512,256]{2,1,0:T(8,128)(2,1)} %get-tuple-element.99.wc, ...), custom_call_target="tpu_custom_call" | custom-call | flops 40000000000 | bytes 16777216 | tf_op jit(solution)/shard_map/self_out/pallas_call | solution.py:481
  127.3 20.6 %attend_cross_forward.1 = (bf16[2048,256]{1,0:T(8,128)(2,1)}, bf16[256,2048]{1,0:T(8,128)(2,1)}, f32[8,2048]{1,0:T(8,128)}) custom-call(s32[2,56]{1,0:T(2,128)} %get-tuple-element.89.table, s32[1,2048]{1,0:T(1,128)} %bitcast.30, bf16[256,2048]{1,0:T(8,128)(2,1)} %get-tuple-element.101.qt_hbm, bf16[128,2048]{1,0:T(8,128)(2,1)} %get-tuple-element.92.hot_hbm, ...), custom_call_target="tpu_custom_call" | custom-call | flops 40000000000 | bytes 16777216 | tf_op jit(solution)/shard_map/attend_cross_forward/pallas_call | solution.py:481
  147.9 37.0 %feed_forward.1 = (bf16[2048,512]{1,0:T(8,128)(2,1)}, f32[2048,512]{1,0:T(8,128)}, bf16[256,2048]{1,0:T(8,128)(2,1)}, bf16[4,144,512]{2,1,0:T(8,128)(2,1)}, bf16...) custom-call(bf16[2048,256]{1,0:T(8,128)(2,1)} %get-tuple-element.105., ...), custom_call_target="tpu_custom_call" | custom-call | flops 40000000000 | bytes 16777216 | tf_op jit(solution)/shard_map/feed_forward/pallas_call | solution.py:481
  184.9 0.6 collective-permute-start
  185.5 0.5 collective-permute-start.1
  186.1 2.4 collective-permute-start.2
  188.5 34.8 %attend_cross_backward.1 = (bf16[2048,256]{1,0:T(8,128)(2,1)}, bf16[2048,256]{1,0:T(8,128)(2,1)}, bf16[2048,256]{1,0:T(8,128)(2,1)}, bf16[2048,512]{1,0:T(8,128)(2,1)}) custom-call(s32[2,56]{1,0:T(2,128)} %get-tuple-element.89.table, s32[1,2048]{1,0:T(1,128)} %bitcast.31, f32[8,2048]{1,0:T(8,128)} %get-tuple-element.104.lse_ref, ...), custom_call_target="tpu_custom_call" | custom-call | flops 40000000000 | bytes 16777216 | tf_op jit(solution)/shard_map/attend_cross_backward/pallas_call | solution.py:481
  223.3 0.0 collective-permute-done.part1
  223.3 0.0 copy-start.8
  223.3 0.0 collective-permute-done.1.part2
  223.3 0.0 copy-start.9
  223.4 0.0 collective-permute-done.2.part3
  223.4 0.0 copy-start.10
  223.4 0.8 copy-done.8
  224.1 0.2 copy-done.9
  224.3 0.2 copy-done.10
  224.6 38.5 %cross_back.1 = (bf16[2048,512]{1,0:T(8,128)(2,1)}, f32[2048,512]{1,0:T(8,128)}, bf16[256,2048]{1,0:T(8,128)(2,1)}, bf16[4,208,512]{2,1,0:T(8,128)(2,1)}, bf16[4...) custom-call(bf16[2048,256]{1,0:T(8,128)(2,1)} %get-tuple-element.121.dq, ...), custom_call_target="tpu_custom_call" | custom-call | flops 40000000000 | bytes 16777216 | tf_op jit(solution)/shard_map/cross_back/pallas_call | solution.py:481
  263.1 2.9 collective-permute-start.3
  265.9 2.8 collective-permute-start.4
  268.7 1.4 collective-permute-start.5
  270.1 35.8 %attend_self_backward.1 = (bf16[2048,256]{1,0:T(8,128)(2,1)}, bf16[2048,256]{1,0:T(8,128)(2,1)}, bf16[2048,256]{1,0:T(8,128)(2,1)}, bf16[2048,512]{1,0:T(8,128)(2,1)}) custom-call(s32[2,56]{1,0:T(2,128)} %get-tuple-element.89.table, s32[1,2048]{1,0:T(1,128)} %bitcast.32, f32[8,2048]{1,0:T(8,128)} %get-tuple-element.134.lse_ref, ...), custom_call_target="tpu_custom_call" | custom-call | flops 40000000000 | bytes 16777216 | tf_op jit(solution)/shard_map/attend_self_backward/pallas_call | solution.py:481
  305.9 0.0 collective-permute-done.3.part1
  305.9 0.0 copy-start.5
  306.0 0.0 collective-permute-done.4.part2
  306.0 0.0 copy-start.6
  306.0 0.8 collective-permute-done.5.part3
  306.8 0.0 copy-start.7
  306.8 0.1 copy-done.5
  306.9 0.3 copy-done.6
  307.2 0.5 copy-done.7
  307.7 0.0 copy-start.1
  307.7 0.0 copy-start.3
  307.7 0.0 copy-start.4
  307.7 49.7 %self_back.1 = (bf16[2048,512]{1,0:T(8,128)(2,1)}, bf16[2048,512]{1,0:T(8,128)(2,1)}, bf16[4,4,48,512]{3,2,1,0:T(8,128)(2,1)}, bf16[4,4,64,512]{3,2,1,0:T(8,128)(2,1)}, f32[8,512]{1,0:T(8,128)}) custom-call(bf16[2048,256]{1,0:T(8,128)(2,1)} %get-tuple-element.141.dq, bf16[2048,256]{1,0:T(8,128)(2,1)} %get-tuple-element.142.dk, ...), custom_call_target="tpu_custom_call" | custom-call | flops 40000000000 | bytes 16777216 | tf_op jit(solution)/shard_map/self_back/pallas_call | solution.py:481
  357.5 0.7 copy.30
  358.2 0.0 copy-done.1
  358.2 0.0 copy-done.3
  358.2 0.0 copy-done.4
  358.2 0.7 multiply_subtract_fusion
  358.9 9.7 %update.1 = (f32[32,16,512]{2,1,0:T(8,128)}, f32[32,16,512]{2,1,0:T(8,128)}, f32[32,16,512]{2,1,0:T(8,128)}, f32[32,16,512]{2,1,0:T(8,128)}, bf16[2048,512]{1,0:T(8,128)(2,1)}, /*index=5*/bf16[2048,512]{1,0:T(8,128)(2,1)}) custom-call(s32[256]{0:T(256)} %owner_ref.3, s32[1]{0:T(128)} %bitcast.4.me_ref, bf16[4,4,48,512]{3,2,1,0:T(8,128)(2,1)} %get-tuple-element.154.last, ...), custom_call_target="tpu_custom_call" | custom-call | flops 40000000000 | bytes 16777216 | tf_op jit(solution)/shard_map/update/pallas_call | solution.py:481
  (2 shorter events, 0.0 us)
Async XLA Ops:
  0.7 3.5 copy-start
  4.2 0.6 copy-start.2
  184.9 38.4 %collective-permute-start = (bf16[4,144,512]{2,1,0:T(8,128)(2,1)}, bf16[4,144,512]{2,1,0:T(8,128)(2,1)S(1)}, u32[]{:S(2)}, u32[]{:S(2)}) collective-permute-start(bf16[4,144,512]{2,1,0:T(8,128)(2,1)} %get-tuple-element.117), channel_id=1, source_target_pairs={{0,2},{2,0},{4,6},{6,4},{8,10},{10,8},{12,14},{14,12},{16,18},{18,... | collective-permute-start | bytes 1769480 | tf_op jit(solution)/shard_map/ppermute | solution.py:470
  185.5 37.8 %collective-permute-start.1 = (bf16[4,144,512]{2,1,0:T(8,128)(2,1)}, bf16[4,144,512]{2,1,0:T(8,128)(2,1)S(1)}, u32[]{:S(2)}, u32[]{:S(2)}) collective-permute-start(bf16[4,144,512]{2,1,0:T(8,128)(2,1)} %get-tuple-element.118), channel_id=1, source_target_pairs={{0,4},{2,6},{4,0},{6,2},{8,12},{10,14},{12,8},{14,10},{16,20},{18,... | collective-permute-start | bytes 1769480 | tf_op jit(solution)/shard_map/ppermute | solution.py:470
  186.1 37.3 %collective-permute-start.2 = (bf16[4,144,512]{2,1,0:T(8,128)(2,1)}, bf16[4,144,512]{2,1,0:T(8,128)(2,1)S(1)}, u32[]{:S(2)}, u32[]{:S(2)}) collective-permute-start(bf16[4,144,512]{2,1,0:T(8,128)(2,1)} %get-tuple-element.119), channel_id=1, source_target_pairs={{0,6},{2,4},{4,2},{6,0},{8,14},{10,12},{12,10},{14,8},{16,22},{18,... | collective-permute-start | bytes 1769480 | tf_op jit(solution)/shard_map/ppermute | solution.py:470
  223.3 0.8 copy-start.8
  223.3 1.0 copy-start.9
  223.4 1.2 copy-start.10
  263.1 42.9 %collective-permute-start.3 = (bf16[4,208,512]{2,1,0:T(8,128)(2,1)}, bf16[4,208,512]{2,1,0:T(8,128)(2,1)S(1)}, u32[]{:S(2)}, u32[]{:S(2)}) collective-permute-start(bf16[4,208,512]{2,1,0:T(8,128)(2,1)} %get-tuple-element.131), channel_id=1, source_target_pairs={{0,2},{2,0},{4,6},{6,4},{8,10},{10,8},{12,14},{14,12},{16,18},{18,... | collective-permute-start | bytes 2555912 | tf_op jit(solution)/shard_map/ppermute | solution.py:470
  265.9 40.0 %collective-permute-start.4 = (bf16[4,208,512]{2,1,0:T(8,128)(2,1)}, bf16[4,208,512]{2,1,0:T(8,128)(2,1)S(1)}, u32[]{:S(2)}, u32[]{:S(2)}) collective-permute-start(bf16[4,208,512]{2,1,0:T(8,128)(2,1)} %get-tuple-element.132), channel_id=1, source_target_pairs={{0,4},{2,6},{4,0},{6,2},{8,12},{10,14},{12,8},{14,10},{16,20},{18,... | collective-permute-start | bytes 2555912 | tf_op jit(solution)/shard_map/ppermute | solution.py:470
  268.7 38.1 %collective-permute-start.5 = (bf16[4,208,512]{2,1,0:T(8,128)(2,1)}, bf16[4,208,512]{2,1,0:T(8,128)(2,1)S(1)}, u32[]{:S(2)}, u32[]{:S(2)}) collective-permute-start(bf16[4,208,512]{2,1,0:T(8,128)(2,1)} %get-tuple-element.133), channel_id=1, source_target_pairs={{0,6},{2,4},{4,2},{6,0},{8,14},{10,12},{12,10},{14,8},{16,22},{18,... | collective-permute-start | bytes 2555912 | tf_op jit(solution)/shard_map/ppermute | solution.py:470
  305.9 1.0 copy-start.5
  306.0 1.2 copy-start.6
  306.8 0.9 copy-start.7
  307.7 50.5 %copy-start.1 = (f32[256]{0:T(256)S(1)}, f32[256]{0:T(256)}, u32[]{:S(2)}) copy-start(f32[256]{0:T(256)} %param.25) | copy-start | bytes 3076
  307.7 50.5 %copy-start.3 = (f32[256]{0:T(256)S(1)}, f32[256]{0:T(256)}, u32[]{:S(2)}) copy-start(f32[256]{0:T(256)} %param.27) | copy-start | bytes 3076
  307.7 50.5 %copy-start.4 = (f32[256]{0:T(256)S(1)}, f32[256]{0:T(256)}, u32[]{:S(2)}) copy-start(f32[256]{0:T(256)} %param.26) | copy-start | bytes 3076

commit v6 on v5

--- a/solution.py
+++ b/solution.py
@@ -382,42 +382,106 @@
     behind = lambda d: lax.rem(z + across - d, across) * 4 + y * 2 + x
     return me, x, y, z, xpeer, ypeer, order, ahead, behind
 
-def spread_blocks(count, piece, rows, half, places, zs, xs, ys, gx, gy, meanwhile=None):
-    me, x, y, z, xpeer, ypeer, order, ahead, behind = places
-    whole = (0, rows)
-    sent, recv = [], {}
-    def go(src_block, at, sem, d, to):
-        copy = send(piece(src_block, *at), piece(src_block, *at), sem.at[0, d], sem.at[1, d], dp=to)
-        sent.append(copy)
-        return copy
-    near = go(me, whole, xs, 0, xpeer), go(me, whole, ys, 0, ypeer)
-    recv[0] = near
-    zcopies = {}
-    for d in order:
-        zcopies[d] = go(me, whole, zs, d, ahead(d))
-    if meanwhile is not None:
+class LineGather:
+    def __init__(self, count, piece, units, cut, places, zs, ds, xs, ys, gx, gy):
+        self.across, self.piece, self.units, self.cut = count // 4, piece, units, cut
+        self.places = places
+        self.sems = dict(z=zs, d=ds, x=xs, y=ys, gx=gx, gy=gy)
+
+    def copy(self, name, side, k, arriving=False):
+        me, x, y, z, xpeer, ypeer = self.places[:6]
+        place = x + 2 * y
+        place = dict(z=place, x=place, y=place, d=3 - place, gy=place + 1 - 2 * x, gx=place + 2 - 4 * y)[name]
+        if arriving:
+            place = {"x": x + 2 * y + 1 - 2 * x, "y": x + 2 * y + 2 - 4 * y, "gx": 3 - x - 2 * y, "gy": 3 - x - 2 * y}.get(name, place)
+        level = z + k * (2 * side - 1)
+        whole = isinstance(k, int) and k == 0
+        half = self.units // 2 if whole else (self.units - self.cut) // 2
+        first = 0 if whole else self.cut
+        start, size = dict(d=(0, self.cut), gy=(first, half), gx=(first + half, self.units - first - half)).get(name, (0, self.units))
+        to = dict(x=xpeer, gx=xpeer, y=ypeer, gy=ypeer).get(name, me + 4 * (1 - 2 * side))
+        hop = 1 if name in ("z", "d") and not arriving else 0
+        if arriving:
+            to = xpeer
+        part, sems = self.piece(level * 4 + place, start, size), self.sems[name]
+        return pltpu.make_async_remote_copy(
+            src_ref=part, dst_ref=part, send_sem=sems.at[0, side, k], recv_sem=sems.at[1, side, k + hop],
+            device_id={"dp": to}, device_id_type=pl.DeviceIdType.MESH)
+
+    def here(self, side, k):
+        z = self.places[3]
+        return z >= k if side == 0 else z + k < self.across
+
+    def onward(self, side):
+        z = self.places[3]
+        return z + 1 < self.across if side == 0 else z > 0
+
+    def along(self, name, side, k, act):
+        pl.when(self.here(side, k) & self.onward(side))(lambda: act(self.copy(name, side, k)))
+
+    def run(self, meanwhile):
+        start, wait_send = (lambda copy: copy.start()), (lambda copy: copy.wait_send())
+
+        def diagonal(side, k):
+            self.copy("x", side, k, True).wait_recv()
+            self.copy("gy", side, k).start()
+            self.copy("y", side, k, True).wait_recv()
+            self.copy("gx", side, k).start()
+
+        def later(side, k):
+            diagonal(side, k)
+            self.copy("d", side, k, True).wait_recv()
+            pl.when(self.onward(side))(lambda: self.copy("d", side, k).start())
+        for side in (0, 1):
+            self.along("z", side, 0, start)
+        self.copy("x", 0, 0).start()
+        self.copy("y", 0, 0).start()
         meanwhile()
-    steps = [0] + order
-    diag = []
-    for k, d in enumerate(steps):
-        if d:
-            zcopies[d].wait_recv()
-            recv[d] = go(behind(d), whole, xs, d, xpeer), go(behind(d), whole, ys, d, ypeer)
-        if k:
-            forward(go, diag, recv, steps[k - 1], behind, places, half, rows, gx, gy)
-    forward(go, diag, recv, steps[-1], behind, places, half, rows, gx, gy)
-    for copy in diag:
-        copy.wait_recv()
-    for copy in sent:
-        copy.wait_send()
-
-def forward(go, diag, recv, d, behind, places, half, rows, gx, gy):
-    me, x, y, z, xpeer, ypeer, order, ahead, _ = places
-    base = behind(d) if d else me
-    recv[d][0].wait_recv()
-    diag.append(go(base + 1 - 2 * x, (0, half), gy, d, ypeer))
-    recv[d][1].wait_recv()
-    diag.append(go(base + 2 - 4 * y, (half, rows - half), gx, d, xpeer))
+        diagonal(0, 0)
+
+        def level(k, carry):
+            for side in (0, 1):
+                @pl.when(self.here(side, k))
+                def _():
+                    self.copy("z", side, k, True).wait_recv()
+                    pl.when(self.onward(side))(lambda: self.copy("z", side, k).start())
+                    self.copy("x", side, k).start()
+                    self.copy("y", side, k).start()
+
+            @pl.when(k == 1)
+            def _():
+                self.copy("gy", 0, 0, True).wait_recv()
+                self.copy("gx", 0, 0, True).wait_recv()
+                for side in (0, 1):
+                    self.along("d", side, 0, start)
+
+            @pl.when(k > 1)
+            def _():
+                for side in (0, 1):
+                    pl.when(self.here(side, k - 1))(lambda: later(side, k - 1))
+            return carry
+        lax.fori_loop(1, self.across, level, 0)
+        for side in (0, 1):
+            pl.when(self.here(side, self.across - 1))(lambda: later(side, self.across - 1))
+
+        def settle(k, carry):
+            for side in (0, 1):
+                @pl.when(self.here(side, k))
+                def _():
+                    for name in ("gy", "gx"):
+                        self.copy(name, side, k, True).wait_recv()
+                    for name in ("x", "y", "gy", "gx"):
+                        self.copy(name, side, k).wait_send()
+                for name in ("z", "d"):
+                    self.along(name, side, k, wait_send)
+            return carry
+        lax.fori_loop(1, self.across, settle, 0)
+        for name in ("x", "y", "gy", "gx"):
+            self.copy(name, 0, 0).wait_send()
+        for side in (0, 1):
+            for name in ("z", "d"):
+                self.along(name, side, 0, wait_send)
+
 
 class Spread:
     def __init__(self, places, out, zs, xs, ys, gx, gy):
@@ -611,7 +675,7 @@
                    ws_ref, wc_ref, wos_ref, woc_ref, w1_ref, w2_ref, norms, side_ref, hot_ref, rank_cols,
                    gathered, flat, query_ref, kv_ref, memory_ref, unit_q, unit_kv,
                    nq_ref, nkv_ref, qt_ref, k_ref, kt_ref, v_ref, vt_ref, kc_ref, kct_ref, vc_ref, vct_ref,
-                   late_sems, out_sems, zs, xs, ys, gx, gy):
+                   late_sems, out_sems, *line_sems):
     tokens, features = query_ref.shape
     units = place_ref.shape[0]
     late = Late([(query_hbm, query_ref), (kv_hbm, kv_ref), (memory_hbm, memory_ref)], late_sems)
@@ -633,8 +697,8 @@
             unit_q[rows, :] = normalise(query_ref[rows, :].astype(F32))[0]
             unit_kv[rows, :] = normalise(kv_ref[rows, :].astype(F32))[0]
         chunks(tokens, units_of)
-    spread_blocks(devices, lambda number, start, size: gathered.at[pl.ds(number * block + start, size)], block, block // 2,
-                  places, zs, xs, ys, gx, gy, meanwhile)
+    LineGather(devices, lambda number, start, size: gathered.at[pl.ds(number * block + start, size)], block, block * 3 // 5,
+               places, *line_sems).run(meanwhile)
 
     share = devices // 8
     vectors = []
@@ -706,7 +770,7 @@
     D = pltpu.SemaphoreType.DMA
     scratch = [pltpu.VMEM((devices * (master.shape[0] + 1), UNIT, features), BF), pltpu.VMEM((8 * cols + 2 * hidden, features), BF)]
     scratch += [pltpu.VMEM(wide, BF)] * 3 + [pltpu.VMEM(wide, F32)] * 2 + [pltpu.VMEM(shape, BF) for shape in shapes]
-    scratch += [D((3,)), out_semaphores(len(shapes), tokens)] + [D((2, devices // 4))] * 5
+    scratch += [D((3,)), out_semaphores(len(shapes), tokens)] + [D((2, 2, devices // 4 + 1))] * 6
     return call(partial(project_kernel, devices), "project",
                 [place_of, lengths, master, norm_row, rank_row, query_stream, kv_stream, memory], "SSVVVAAA",
                 outs, scratch, 0)

time: 367 us -> 352 us (0.959)
  Pallas kernels: 352 us -> 335 us
    pallas_call x11, Pallas kernels: 352 us -> 335 us  [call(): pl.pallas_call(kernel, out_shape=tuple((jax.ShapeDtypeStruct(shape, dtype...]
where the time goes in v6:
time: 352 us; the launch traced here: 350 us
  Pallas kernels  335 us (95%)
  starting transfers between devices  8.08 us (2%)
  local copies, waits for them, and re-layouts  3.72 us (1%)
    pallas_call x11, Pallas kernels, call(): pl.pallas_call(kernel, out_shape=tuple((jax.ShapeDtypeStruct(shape, dtype...  335 us
    ppermute x6, starting transfers between devices, plane_swap(): lax.ppermute(value, 'dp', [(i, i // 4 * 4 + (i % 4 ^ f)) for i in range(c...  8.08 us
  transfers between devices with their start and end apart: 6, of which 1 were waited for; matrix products, arithmetic and copies ran while one was open for 0% of the time, Pallas kernels for 19%

profile of v6, /device:TPU:0, one launch (start us, length us, event | category | flops | bytes accessed | tf_op | source)
XLA Modules:
  0.0 350.2 jit_solution(62509397479260020)
XLA Ops:
  0.7 0.0 copy-start
  0.7 3.5 plan.1
  4.2 0.0 copy-done
  4.2 0.0 copy-start.2
  4.2 0.6 copy-done.2
  4.8 82.2 %project.1 = (bf16[2048,512]{1,0:T(8,128)(2,1)}, bf16[2048,512]{1,0:T(8,128)(2,1)}, bf16[256,2048]{1,0:T(8,128)(2,1)}, bf16[2048,256]{1,0:T(8,128)(2,1)}, bf16[2...) custom-call(s32[256]{0:T(256)} %get-tuple-element.90.place_ref, ...), custom_call_target="tpu_custom_call" | custom-call | flops 40000000000 | bytes 16777216 | tf_op jit(solution)/shard_map/project/pallas_call | solution.py:545
  86.9 21.4 %attend_self_forward.1 = (bf16[2048,256]{1,0:T(8,128)(2,1)}, bf16[256,2048]{1,0:T(8,128)(2,1)}, f32[8,2048]{1,0:T(8,128)}) custom-call(s32[2,56]{1,0:T(2,128)} %get-tuple-element.89.table, s32[1,2048]{1,0:T(1,128)} %bitcast.29, bf16[256,2048]{1,0:T(8,128)(2,1)} %get-tuple-element.91.qt_hbm, bf16[128,2048]{1,0:T(8,128)(2,1)} %get-tuple-element.92.hot_hbm, ...), custom_call_target="tpu_custom_call" | custom-call | flops 40000000000 | bytes 16777216 | tf_op jit(solution)/shard_map/attend_self_forward/pallas_call | solution.py:545
  108.3 8.4 %self_out.1 = (f32[2048,512]{1,0:T(8,128)}, bf16[2048,512]{1,0:T(8,128)(2,1)}, bf16[256,2048]{1,0:T(8,128)(2,1)}) custom-call(bf16[2048,256]{1,0:T(8,128)(2,1)} %get-tuple-element.97.mixed, bf16[256,512]{1,0:T(8,128)(2,1)} %get-tuple-element.98.wo, bf16[2048,512]{1,0:T(8,128)(2,1)} %query_hbm.5, bf16[3,512,256]{2,1,0:T(8,128)(2,1)} %get-tuple-element.99.wc, ...), custom_call_target="tpu_custom_call" | custom-call | flops 40000000000 | bytes 16777216 | tf_op jit(solution)/shard_map/self_out/pallas_call | solution.py:545
  116.7 19.9 %attend_cross_forward.1 = (bf16[2048,256]{1,0:T(8,128)(2,1)}, bf16[256,2048]{1,0:T(8,128)(2,1)}, f32[8,2048]{1,0:T(8,128)}) custom-call(s32[2,56]{1,0:T(2,128)} %get-tuple-element.89.table, s32[1,2048]{1,0:T(1,128)} %bitcast.30, bf16[256,2048]{1,0:T(8,128)(2,1)} %get-tuple-element.101.qt_hbm, bf16[128,2048]{1,0:T(8,128)(2,1)} %get-tuple-element.92.hot_hbm, ...), custom_call_target="tpu_custom_call" | custom-call | flops 40000000000 | bytes 16777216 | tf_op jit(solution)/shard_map/attend_cross_forward/pallas_call | solution.py:545
  136.6 37.0 %feed_forward.1 = (bf16[2048,512]{1,0:T(8,128)(2,1)}, f32[2048,512]{1,0:T(8,128)}, bf16[256,2048]{1,0:T(8,128)(2,1)}, bf16[4,144,512]{2,1,0:T(8,128)(2,1)}, bf16...) custom-call(bf16[2048,256]{1,0:T(8,128)(2,1)} %get-tuple-element.105., ...), custom_call_target="tpu_custom_call" | custom-call | flops 40000000000 | bytes 16777216 | tf_op jit(solution)/shard_map/feed_forward/pallas_call | solution.py:545
  173.6 3.0 collective-permute-start
  176.6 0.0 collective-permute-start.1
  176.6 1.5 collective-permute-start.2
  178.1 33.6 %attend_cross_backward.1 = (bf16[2048,256]{1,0:T(8,128)(2,1)}, bf16[2048,256]{1,0:T(8,128)(2,1)}, bf16[2048,256]{1,0:T(8,128)(2,1)}, bf16[2048,512]{1,0:T(8,128)(2,1)}) custom-call(s32[2,56]{1,0:T(2,128)} %get-tuple-element.89.table, s32[1,2048]{1,0:T(1,128)} %bitcast.31, f32[8,2048]{1,0:T(8,128)} %get-tuple-element.104.lse_ref, ...), custom_call_target="tpu_custom_call" | custom-call | flops 40000000000 | bytes 16777216 | tf_op jit(solution)/shard_map/attend_cross_backward/pallas_call | solution.py:545
  211.8 0.0 collective-permute-done.part1
  211.8 0.0 copy-start.8
  211.8 0.0 collective-permute-done.1.part2
  211.8 0.0 copy-start.9
  211.8 0.0 collective-permute-done.2.part3
  211.8 0.0 copy-start.10
  211.9 0.8 copy-done.8
  212.6 0.2 copy-done.9
  212.8 0.2 copy-done.10
  213.0 36.3 %cross_back.1 = (bf16[2048,512]{1,0:T(8,128)(2,1)}, f32[2048,512]{1,0:T(8,128)}, bf16[256,2048]{1,0:T(8,128)(2,1)}, bf16[4,208,512]{2,1,0:T(8,128)(2,1)}, bf16[4...) custom-call(bf16[2048,256]{1,0:T(8,128)(2,1)} %get-tuple-element.121.dq, ...), custom_call_target="tpu_custom_call" | custom-call | flops 40000000000 | bytes 16777216 | tf_op jit(solution)/shard_map/cross_back/pallas_call | solution.py:545
  249.4 1.7 collective-permute-start.3
  251.0 0.5 collective-permute-start.4
  251.5 1.4 collective-permute-start.5
  252.9 34.6 %attend_self_backward.1 = (bf16[2048,256]{1,0:T(8,128)(2,1)}, bf16[2048,256]{1,0:T(8,128)(2,1)}, bf16[2048,256]{1,0:T(8,128)(2,1)}, bf16[2048,512]{1,0:T(8,128)(2,1)}) custom-call(s32[2,56]{1,0:T(2,128)} %get-tuple-element.89.table, s32[1,2048]{1,0:T(1,128)} %bitcast.32, f32[8,2048]{1,0:T(8,128)} %get-tuple-element.134.lse_ref, ...), custom_call_target="tpu_custom_call" | custom-call | flops 40000000000 | bytes 16777216 | tf_op jit(solution)/shard_map/attend_self_backward/pallas_call | solution.py:545
  287.5 0.0 collective-permute-done.3.part1
  287.5 0.0 copy-start.5
  287.5 1.6 collective-permute-done.4.part2
  289.1 0.0 copy-start.6
  289.1 0.0 collective-permute-done.5.part3
  289.1 0.0 copy-start.7
  289.1 0.0 copy-done.5
  289.1 1.0 copy-done.6
  290.1 0.2 copy-done.7
  290.3 0.0 copy-start.1
  290.3 0.0 copy-start.3
  290.4 0.0 copy-start.4
  290.4 48.6 %self_back.1 = (bf16[2048,512]{1,0:T(8,128)(2,1)}, bf16[2048,512]{1,0:T(8,128)(2,1)}, bf16[4,4,48,512]{3,2,1,0:T(8,128)(2,1)}, bf16[4,4,64,512]{3,2,1,0:T(8,128)(2,1)}, f32[8,512]{1,0:T(8,128)}) custom-call(bf16[2048,256]{1,0:T(8,128)(2,1)} %get-tuple-element.141.dq, bf16[2048,256]{1,0:T(8,128)(2,1)} %get-tuple-element.142.dk, ...), custom_call_target="tpu_custom_call" | custom-call | flops 40000000000 | bytes 16777216 | tf_op jit(solution)/shard_map/self_back/pallas_call | solution.py:545
  338.9 0.7 copy.30
  339.7 0.0 copy-done.1
  339.7 0.0 copy-done.3
  339.7 0.0 copy-done.4
  339.7 0.7 multiply_subtract_fusion
  340.3 9.7 %update.1 = (f32[32,16,512]{2,1,0:T(8,128)}, f32[32,16,512]{2,1,0:T(8,128)}, f32[32,16,512]{2,1,0:T(8,128)}, f32[32,16,512]{2,1,0:T(8,128)}, bf16[2048,512]{1,0:T(8,128)(2,1)}, /*index=5*/bf16[2048,512]{1,0:T(8,128)(2,1)}) custom-call(s32[256]{0:T(256)} %owner_ref.3, s32[1]{0:T(128)} %bitcast.4.me_ref, bf16[4,4,48,512]{3,2,1,0:T(8,128)(2,1)} %get-tuple-element.154.last, ...), custom_call_target="tpu_custom_call" | custom-call | flops 40000000000 | bytes 16777216 | tf_op jit(solution)/shard_map/update/pallas_call | solution.py:545
  (2 shorter events, 0.0 us)
Async XLA Ops:
  0.7 3.5 %copy-start = (f32[256]{0:T(256)S(1)}, f32[256]{0:T(256)}, u32[]{:S(2)}) copy-start(f32[256]{0:T(256)} %param.25) | copy-start | bytes 3076
  4.2 0.6 copy-start.2
  173.6 38.2 %collective-permute-start = (bf16[4,144,512]{2,1,0:T(8,128)(2,1)}, bf16[4,144,512]{2,1,0:T(8,128)(2,1)S(1)}, u32[]{:S(2)}, u32[]{:S(2)}) collective-permute-start(bf16[4,144,512]{2,1,0:T(8,128)(2,1)} %get-tuple-element.117), channel_id=1, source_target_pairs={{0,2},{2,0},{4,6},{6,4},{8,10},{10,8},{12,14},{14,12},{16,18},{18,... | collective-permute-start | bytes 1769480 | tf_op jit(solution)/shard_map/ppermute | solution.py:534
  176.6 35.2 %collective-permute-start.1 = (bf16[4,144,512]{2,1,0:T(8,128)(2,1)}, bf16[4,144,512]{2,1,0:T(8,128)(2,1)S(1)}, u32[]{:S(2)}, u32[]{:S(2)}) collective-permute-start(bf16[4,144,512]{2,1,0:T(8,128)(2,1)} %get-tuple-element.118), channel_id=1, source_target_pairs={{0,4},{2,6},{4,0},{6,2},{8,12},{10,14},{12,8},{14,10},{16,20},{18,... | collective-permute-start | bytes 1769480 | tf_op jit(solution)/shard_map/ppermute | solution.py:534
  176.6 35.2 %collective-permute-start.2 = (bf16[4,144,512]{2,1,0:T(8,128)(2,1)}, bf16[4,144,512]{2,1,0:T(8,128)(2,1)S(1)}, u32[]{:S(2)}, u32[]{:S(2)}) collective-permute-start(bf16[4,144,512]{2,1,0:T(8,128)(2,1)} %get-tuple-element.119), channel_id=1, source_target_pairs={{0,6},{2,4},{4,2},{6,0},{8,14},{10,12},{12,10},{14,8},{16,22},{18,... | collective-permute-start | bytes 1769480 | tf_op jit(solution)/shard_map/ppermute | solution.py:534
  211.8 0.8 copy-start.8
  211.8 1.0 copy-start.9
  211.8 1.2 copy-start.10
  249.4 38.2 %collective-permute-start.3 = (bf16[4,208,512]{2,1,0:T(8,128)(2,1)}, bf16[4,208,512]{2,1,0:T(8,128)(2,1)S(1)}, u32[]{:S(2)}, u32[]{:S(2)}) collective-permute-start(bf16[4,208,512]{2,1,0:T(8,128)(2,1)} %get-tuple-element.131), channel_id=1, source_target_pairs={{0,2},{2,0},{4,6},{6,4},{8,10},{10,8},{12,14},{14,12},{16,18},{18,... | collective-permute-start | bytes 2555912 | tf_op jit(solution)/shard_map/ppermute | solution.py:534
  251.0 38.1 %collective-permute-start.4 = (bf16[4,208,512]{2,1,0:T(8,128)(2,1)}, bf16[4,208,512]{2,1,0:T(8,128)(2,1)S(1)}, u32[]{:S(2)}, u32[]{:S(2)}) collective-permute-start(bf16[4,208,512]{2,1,0:T(8,128)(2,1)} %get-tuple-element.132), channel_id=1, source_target_pairs={{0,4},{2,6},{4,0},{6,2},{8,12},{10,14},{12,8},{14,10},{16,20},{18,... | collective-permute-start | bytes 2555912 | tf_op jit(solution)/shard_map/ppermute | solution.py:534
  251.5 37.7 %collective-permute-start.5 = (bf16[4,208,512]{2,1,0:T(8,128)(2,1)}, bf16[4,208,512]{2,1,0:T(8,128)(2,1)S(1)}, u32[]{:S(2)}, u32[]{:S(2)}) collective-permute-start(bf16[4,208,512]{2,1,0:T(8,128)(2,1)} %get-tuple-element.133), channel_id=1, source_target_pairs={{0,6},{2,4},{4,2},{6,0},{8,14},{10,12},{12,10},{14,8},{16,22},{18,... | collective-permute-start | bytes 2555912 | tf_op jit(solution)/shard_map/ppermute | solution.py:534
  287.5 1.6 copy-start.5
  289.1 1.0 copy-start.6
  289.1 1.2 copy-start.7
  290.3 49.3 %copy-start.1 = (f32[256]{0:T(256)S(1)}, f32[256]{0:T(256)}, u32[]{:S(2)}) copy-start(f32[256]{0:T(256)} %param.25) | copy-start | bytes 3076
  290.3 49.3 %copy-start.3 = (f32[256]{0:T(256)S(1)}, f32[256]{0:T(256)}, u32[]{:S(2)}) copy-start(f32[256]{0:T(256)} %param.27) | copy-start | bytes 3076
  290.4 49.3 %copy-start.4 = (f32[256]{0:T(256)S(1)}, f32[256]{0:T(256)}, u32[]{:S(2)}) copy-start(f32[256]{0:T(256)} %param.26) | copy-start | bytes 3076

commit v7 on v6

--- a/solution.py
+++ b/solution.py
@@ -24,7 +24,7 @@
 F32 = jnp.float32
 BF = jnp.bfloat16
 TQ = 256
-TK = 384
+TK = 512
 FAR = 32768.0
 LANES = (64, 72, 80)
 
@@ -255,16 +255,17 @@
 
 
 def attn_bwd_kernel(with_seen, heads, table, count_ref, lse_ref, qt_hbm, hot_hbm, gt_hbm, ot_hbm, k_hbm, kt_hbm, v_hbm, side_hbm,
-                    rank_hbm, pass_in,
-                    dq_out, dk_out, dv_out, pass_out, dk_sum, dv_sum, dq_sum, qt, gt, q_own, g_own, sc, dps, all_ds, all_p, counts,
-                    qt_ref, hot_ref, gt_ref, ot_ref, k_ref, kt_ref, v_ref, side_ref, rank_cols, held, dq_ref, dk_ref, dv_ref,
-                    late_sems, out_sems, pass_sem):
+                    rank_hbm, *refs):
+    passed = (len(refs) - 30) // 3
+    pass_in, (dq_out, dk_out, dv_out), pass_out, refs = refs[:passed], refs[passed:passed + 3], refs[passed + 3:2 * passed + 3], refs[2 * passed + 3:]
+    (dk_sum, dv_sum, dq_sum, qt, gt, q_own, g_own, sc, dps, all_ds, all_p, counts,
+     qt_ref, hot_ref, gt_ref, ot_ref, k_ref, kt_ref, v_ref, side_ref, rank_cols, *held, dq_ref, dk_ref, dv_ref,
+     late_sems, out_sems, pass_sem) = refs
     pairs = [(qt_hbm, qt_ref), (hot_hbm, hot_ref), (gt_hbm, gt_ref), (ot_hbm, ot_ref), (k_hbm, padded(k_ref)),
              (kt_hbm, padded(kt_ref)), (v_hbm, padded(v_ref)), (side_hbm, padded(side_ref))]
     late = Late(pairs + ([(rank_hbm, padded(rank_cols))] if with_seen else []), late_sems)
     fill_padding((k_ref, kt_ref, v_ref, rank_cols), side_ref)
-    entering = pltpu.make_async_copy(pass_in, held, pass_sem.at[0])
-    entering.start()
+    entering = Late(list(zip(pass_in, held)), pass_sem.at[0])
     out = Out([(dq_ref, dq_out), (dk_ref, dk_out), (dv_ref, dv_out)], out_sems)
     tiles = ROW // TQ
     dk_sum[...] = jnp.zeros_like(dk_sum)
@@ -296,9 +297,8 @@
         return c
     lax.fori_loop(0, tiles, prepare, 0)
     late.wait(*range(4, 9 if with_seen else 8))
-    entering.wait()
-    leaving = pltpu.make_async_copy(held, pass_out, pass_sem.at[1])
-    leaving.start()
+    entering.wait(*range(passed))
+    leaving = Late(list(zip(held, pass_out)), pass_sem.at[1])
 
     def one_step(s, c):
         out_tile, out_k = step_of(table, s)
@@ -336,14 +336,14 @@
         return c
     lax.fori_loop(0, tiles, finish, 0)
     out.drain(ROW)
-    leaving.wait()
+    leaving.wait(*range(passed))
 
 
 def attend_backward(steps, qt, k, kt, v, gt, ot, lse, tables, count, passed, with_seen):
     rows, cols = v.shape
     heads = cols // HEAD_DIM
     side, hot, rank_cols = tables
-    args = [steps, count, lse, qt, hot, gt, ot, k, kt, v, side, rank_cols, passed]
+    args = [steps, count, lse, qt, hot, gt, ot, k, kt, v, side, rank_cols] + passed
     tiles = ROW // TQ
     like = ((rows, cols), BF, "A")
     summed, own = pltpu.VMEM((rows + TK, cols), F32), pltpu.VMEM((tiles, heads * TQ, cols), BF)
@@ -351,13 +351,13 @@
     small = pltpu.VMEM((TK, heads * TQ), BF)
     keys, keys_t = pltpu.VMEM((rows + TK, cols), BF), pltpu.VMEM((cols, rows + TK), BF)
     held = [pltpu.VMEM(arg.shape, BF) for arg in (qt, hot, gt, ot)] + [
-        keys, keys_t, keys, pltpu.VMEM((rows + TK, 128), BF), pltpu.VMEM((rows + TK, 128), F32),
-        pltpu.VMEM(passed.shape, passed.dtype)]
+        keys, keys_t, keys, pltpu.VMEM((rows + TK, 128), BF), pltpu.VMEM((rows + TK, 128), F32)] + [
+        pltpu.VMEM(value.shape, value.dtype) for value in passed]
     return call(partial(attn_bwd_kernel, with_seen, heads), "attend_self_backward" if with_seen else "attend_cross_backward",
-                args, "SVV" + "A" * 10, [like, like, like, (passed.shape, passed.dtype, "A")],
+                args, "SVV" + "A" * (9 + len(passed)), [like, like, like] + [(value.shape, value.dtype, "A") for value in passed],
                 [summed, summed, pltpu.VMEM((tiles + 1, heads, HEAD_DIM, TQ), F32), columns, columns, own, own, square, square,
                  small, small, pltpu.VMEM((ROW // TQ, 8, TQ), F32)] + held + [pltpu.VMEM((rows, cols), BF)] * 3
-                + [pltpu.SemaphoreType.DMA((9,)), out_semaphores(3, rows), pltpu.SemaphoreType.DMA((2,))])
+                + [pltpu.SemaphoreType.DMA((9,)), out_semaphores(3, rows), pltpu.SemaphoreType.DMA((2, 2))])
 
 
 def send(src, dst, send_sem, recv_sem, **where):
@@ -419,7 +419,7 @@
     def along(self, name, side, k, act):
         pl.when(self.here(side, k) & self.onward(side))(lambda: act(self.copy(name, side, k)))
 
-    def run(self, meanwhile):
+    def run(self, at_start, at_first, at_second):
         start, wait_send = (lambda copy: copy.start()), (lambda copy: copy.wait_send())
 
         def diagonal(side, k):
@@ -436,7 +436,7 @@
             self.along("z", side, 0, start)
         self.copy("x", 0, 0).start()
         self.copy("y", 0, 0).start()
-        meanwhile()
+        at_start()
         diagonal(0, 0)
 
         def level(k, carry):
@@ -454,11 +454,13 @@
                 self.copy("gx", 0, 0, True).wait_recv()
                 for side in (0, 1):
                     self.along("d", side, 0, start)
+                at_first()
 
             @pl.when(k > 1)
             def _():
                 for side in (0, 1):
                     pl.when(self.here(side, k - 1))(lambda: later(side, k - 1))
+            pl.when(k == 2)(at_second)
             return carry
         lax.fori_loop(1, self.across, level, 0)
         for side in (0, 1):
@@ -651,34 +653,66 @@
         chunks(tokens, body)
 
 
-def plan_kernel(block, owner_ref, len_ref, place_ref, table, used):
-    for d in range(used.shape[0]):
-        used[d] = 0
-
-    def one_unit(u, carry):
-        owner = owner_ref[u]
-        slot = used[owner]
-        place_ref[u] = owner * block + slot
-        used[owner] = slot + 1
+def plan_kernel(block, owner_ref, len_ref, rank_ref, count_ref, place_ref, rank_out, count_out, table, info):
+    units = owner_ref.shape[1]
+    owner = owner_ref[...].astype(F32)
+    owner_cols = jnp.broadcast_to(owner, (128, units)).T
+    owner_cols = jnp.concatenate([owner_cols] * (units // 128), 1)
+    before = lax.broadcasted_iota(jnp.int32, (units, units), 0) < lax.broadcasted_iota(jnp.int32, (units, units), 1)
+    slots = jnp.sum(jnp.where(before & (owner_cols == owner), 1.0, 0.0), 0, keepdims=True)
+    place_ref[...] = (owner * block + slots).astype(jnp.int32)
+    longest, first, at, start = jnp.int32(0), jnp.int32(0), jnp.int32(0), jnp.int32(0)
+    for d in range(DOCS):
+        length = len_ref[0, d]
+        longer = length > longest
+        first = jnp.where(longer, d, first)
+        start = jnp.where(longer, at, start)
+        longest = jnp.where(longer, length, longest)
+        at = at + length
+    for d in range(DOCS):
+        info[0, d] = len_ref[0, lax.rem(first + d, DOCS)]
+    info[0, DOCS] = start
+    info[0, DOCS + 1] = lax.rem(ROW - start, ROW)
+    turn = lax.rem(ROW - start, ROW)
+    rank_out[...] = pltpu.roll(rank_ref[...], turn, 1)
+    count_out[...] = pltpu.roll(count_ref[...], turn, 1)
+    step_table(info, table)
+
+
+def plan(unit_owner, lengths, rank_row, count_row, block):
+    row = ((1, ROW), jnp.int32, "V")
+    return call(partial(plan_kernel, block), "plan", [unit_owner.reshape(1, -1), lengths, rank_row, count_row], "VSVV",
+                [((1, unit_owner.shape[0]), jnp.int32, "V"), row, row, ((2, STEPS), jnp.int32, "S"),
+                 ((1, DOCS + 2), jnp.int32, "S")], [])
+
+
+def turn_rows(source, target, shift):
+    tiles = source.shape[0]
+    whole, rest = lax.div(shift, UNIT), lax.rem(shift, UNIT)
+
+    def one(i, carry):
+        at = lax.rem(i + whole, tiles)
+        both = jnp.concatenate([source[at].astype(F32), source[lax.rem(at + 1, tiles)].astype(F32)], 0)
+        rows = pltpu.roll(both, lax.rem(2 * UNIT - rest, 2 * UNIT), 0)[:UNIT]
+        target[pl.ds(pl.multiple_of(i * UNIT, UNIT), UNIT), :] = rows.astype(target.dtype)
         return carry
-    lax.fori_loop(0, owner_ref.shape[0], one_unit, 0, unroll=4)
-    step_table(len_ref, table)
-
-
-def plan(unit_owner, lengths, devices, block):
-    return call(partial(plan_kernel, block), "plan", [unit_owner, lengths], "SS",
-                [(unit_owner.shape, jnp.int32, "S"), ((2, STEPS), jnp.int32, "S")], [pltpu.SMEM((devices,), jnp.int32)])
-
-
-def project_kernel(devices, place_ref, len_ref, master, norm_row, rank_ref, query_hbm, kv_hbm, memory_hbm,
+    lax.fori_loop(0, tiles, one, 0, unroll=4)
+
+
+def in_tiles(value):
+    return value.reshape(-1, UNIT, value.shape[1])
+
+
+def project_kernel(devices, place_ref, info, master, norm_row, rank_ref, query_hbm, kv_hbm, memory_hbm, grad_hbm,
                    nq_out, nkv_out, qt_out, k_out, kt_out, v_out, vt_out, kc_out, kct_out, vc_out, vct_out,
+                   query_out, kv_out, memory_out, grad_out,
                    ws_ref, wc_ref, wos_ref, woc_ref, w1_ref, w2_ref, norms, side_ref, hot_ref, rank_cols,
-                   gathered, flat, query_ref, kv_ref, memory_ref, unit_q, unit_kv,
+                   gathered, flat, stage_a, stage_b, query_ref, kv_ref, memory_ref, grad_ref, unit_q, unit_kv,
                    nq_ref, nkv_ref, qt_ref, k_ref, kt_ref, v_ref, vt_ref, kc_ref, kct_ref, vc_ref, vct_ref,
-                   late_sems, out_sems, *line_sems):
+                   late_sems, turned_sems, out_sems, *line_sems):
     tokens, features = query_ref.shape
-    units = place_ref.shape[0]
-    late = Late([(query_hbm, query_ref), (kv_hbm, kv_ref), (memory_hbm, memory_ref)], late_sems)
+    units = place_ref.shape[1]
+    late = Late([(query_hbm, stage_a), (kv_hbm, stage_b)], late_sems.at[0])
     held = (nq_ref, nkv_ref, qt_ref, k_ref, kt_ref, v_ref, vt_ref, kc_ref, kct_ref, vc_ref, vct_ref)
     out = Out(list(zip(held, (nq_out, nkv_out, qt_out, k_out, kt_out, v_out, vt_out, kc_out, kct_out, vc_out, vct_out))), out_sems)
     places = places_of(devices)
@@ -689,16 +723,34 @@
     gathered[me * block + slots] = jnp.broadcast_to(norm_row[...], (UNIT, features)).astype(BF)
     greet([{"dp": xpeer}, {"dp": ypeer}] + [{"dp": ahead(d)} for d in order])
 
-    def meanwhile():
-        mask_tables(len_ref, rank_ref, side_ref, hot_ref, rank_cols)
-        late.wait(0, 1, 2)
-
+    leaving = [(query_ref, query_out), (kv_ref, kv_out), (memory_ref, memory_out), (grad_ref, grad_out)]
+
+    def leave(number):
+        return pltpu.make_async_copy(*leaving[number], turned_sems.at[number])
+
+    def turn(stage, number):
+        turn_rows(stage, leaving[number][0], info[0, DOCS])
+        leave(number).start()
+
+    def first_turns():
+        mask_tables(info, rank_ref, side_ref, hot_ref, rank_cols)
+        late.wait(0, 1)
+        turn(stage_a, 0)
+        turn(stage_b, 1)
+
+    def norms_of_streams():
         def units_of(step, rows):
             unit_q[rows, :] = normalise(query_ref[rows, :].astype(F32))[0]
             unit_kv[rows, :] = normalise(kv_ref[rows, :].astype(F32))[0]
         chunks(tokens, units_of)
+
+    def last_turns():
+        more = Late([(memory_hbm, stage_a), (grad_hbm, stage_b)], late_sems.at[1])
+        more.wait(0, 1)
+        turn(stage_a, 2)
+        turn(stage_b, 3)
     LineGather(devices, lambda number, start, size: gathered.at[pl.ds(number * block + start, size)], block, block * 3 // 5,
-               places, *line_sems).run(meanwhile)
+               places, *line_sems).run(first_turns, norms_of_streams, last_turns)
 
     share = devices // 8
     vectors = []
@@ -711,7 +763,7 @@
     norms[...] = jnp.concatenate(vectors, 0)
 
     def one_unit(u, carry):
-        flat[pl.ds(pl.multiple_of(u * UNIT, UNIT), UNIT), :] = gathered[place_ref[u]]
+        flat[pl.ds(pl.multiple_of(u * UNIT, UNIT), UNIT), :] = gathered[place_ref[0, u]]
         return carry
     lax.fori_loop(0, units, one_unit, 0, unroll=4)
     order = interleave(features)
@@ -749,6 +801,8 @@
             out.start(i, step)
     chunks(tokens, body)
     out.drain(tokens)
+    for number in range(4):
+        leave(number).wait()
 
 
 def pair_sems(tokens):
@@ -759,21 +813,22 @@
     return pltpu.SemaphoreType.DMA((count, tokens // CHUNK))
 
 
-def project(devices, place_of, lengths, master, norm_row, rank_row, query_stream, kv_stream, memory, cols, hidden):
+def project(devices, place_of, info, master, norm_row, rank_row, query_stream, kv_stream, memory, out_grad, cols, hidden):
     tokens, features = query_stream.shape
     wide, narrow, across = (tokens, features), (tokens, cols), (cols, tokens)
     shapes = [wide, wide, across] + [narrow, across] * 4
-    outs = [(shape, BF, "A") for shape in shapes] + [
+    outs = [(shape, BF, "A") for shape in shapes] + [(wide, BF, "A")] * 4 + [
         ((3, features, cols), BF, "V"), ((3, features, cols), BF, "V"), ((cols, features), BF, "V"), ((cols, features), BF, "V"),
         ((features, hidden), BF, "V"), ((hidden, features), BF, "V"), ((8, features), F32, "V"),
         ((ROW, 128), BF, "V"), ((128, ROW), BF, "V"), ((ROW, 128), F32, "V")]
     D = pltpu.SemaphoreType.DMA
+    streams = [in_tiles(stream) for stream in (query_stream, kv_stream, memory, out_grad)]
     scratch = [pltpu.VMEM((devices * (master.shape[0] + 1), UNIT, features), BF), pltpu.VMEM((8 * cols + 2 * hidden, features), BF)]
-    scratch += [pltpu.VMEM(wide, BF)] * 3 + [pltpu.VMEM(wide, F32)] * 2 + [pltpu.VMEM(shape, BF) for shape in shapes]
-    scratch += [D((3,)), out_semaphores(len(shapes), tokens)] + [D((2, 2, devices // 4 + 1))] * 6
+    scratch += [pltpu.VMEM(streams[0].shape, BF)] * 2 + [pltpu.VMEM(wide, BF)] * 4 + [pltpu.VMEM(wide, F32)] * 2
+    scratch += [pltpu.VMEM(shape, BF) for shape in shapes]
+    scratch += [D((2, 2)), D((4,)), out_semaphores(len(shapes), tokens)] + [D((2, 2, devices // 4 + 1))] * 6
     return call(partial(project_kernel, devices), "project",
-                [place_of, lengths, master, norm_row, rank_row, query_stream, kv_stream, memory], "SSVVVAAA",
-                outs, scratch, 0)
+                [place_of, info, master, norm_row, rank_row] + streams, "SSVVVAAAA", outs, scratch, 0)
 
 
 def self_out_kernel(mixed, wo, query_hbm, wc, norms, res_out, nc_out, q_out,
@@ -816,11 +871,12 @@
 
 
 def gelu_parts(value):
-    size = jnp.abs(value)
-    bell = jnp.exp(-0.5 * value * value)
-    t = 1.0 / (1.0 + (0.3275911 * 0.7071067811865476) * size)
-    poly = ((((1.061405429 * t - 1.453152027) * t + 1.421413741) * t - 0.284496736) * t + 0.254829592) * t
-    tail = 0.5 * poly * bell
+    bell = jnp.exp2(value * value * (-0.5 * 1.4426950408889634))
+    base = 1.0 + (0.3275911 * 0.7071067811865476) * jnp.abs(value)
+    t = pl.reciprocal(base, approx=True)
+    t = t * (2.0 - base * t)
+    poly = ((((0.5307027145 * t - 0.7265760135) * t + 0.7107068705) * t - 0.142248368) * t + 0.127414796) * t
+    tail = poly * bell
     below = jnp.where(value < 0.0, tail, 1.0 - tail)
     return value * below, below + value * (bell * 0.3989422804014327)
 
@@ -968,18 +1024,18 @@
     return (parts[0][at].astype(F32) + parts[1][at].astype(F32) + parts[2][at].astype(F32) + parts[3][at].astype(F32)).astype(BF)
 
 
-def cross_back_kernel(devices, dq, dk, dv, wc, nc_hbm, memory_hbm, res_hbm, gres_hbm, mixed, wo, norms,
+def cross_back_kernel(devices, info, dq, dk, dv, wc, nc_hbm, memory_hbm, res_hbm, gres_hbm, output_hbm, mixed, wo, norms,
                       part0, part1, part2, part3,
-                      gmem_out, gnew_out, gmix_out, give0, give1, give2, give3, sums_ref,
-                      nc, memory, res, gres, gmem_ref, gnew_ref, gmix_ref, flat, pieces, landed, blocks,
-                      mine_a, theirs_a, mine_b, theirs_b, low_all, sems_a, sems_b, late_sems, out_sems, z_sems, zz_sems):
+                      gmem_out, output_out, gnew_out, gmix_out, give0, give1, give2, give3, sums_ref,
+                      nc, memory, res, gres, output_ref, gmem_ref, turned_a, turned_b, gnew_ref, gmix_ref, flat, pieces, landed, blocks,
+                      mine_a, theirs_a, mine_b, theirs_b, low_all, sems_a, sems_b, late_sems, out_sems, turned_sems, z_sems, zz_sems):
     tokens, features = nc.shape
     cols = dq.shape[1]
     across = devices // 4
     places = places_of(devices)
     me, x, y, z, xpeer, ypeer, order, ahead, behind = places
-    late = Late([(nc_hbm, nc), (memory_hbm, memory), (res_hbm, res), (gres_hbm, gres)], late_sems)
-    out = Out([(gmem_ref, gmem_out), (gnew_ref, gnew_out), (gmix_ref, gmix_out)], out_sems)
+    late = Late([(nc_hbm, nc), (memory_hbm, memory), (res_hbm, res), (gres_hbm, gres), (output_hbm, output_ref)], late_sems)
+    out = Out([(gnew_ref, gnew_out), (gmix_ref, gmix_out)], out_sems)
     for level in range(across):
         pieces[level] = four_sum((part0, part1, part2, part3), level)
     greet([{"head": 1 - lax.axis_index("head")}] + [{"dp": ahead(d)} for d in order])
@@ -998,22 +1054,26 @@
         unit, scale = normalise(res[rows, :])
         gnew = norm_back(unit, scale, norms[4:5, :], grad) + gres[rows, :]
         gnew_ref[rows, :] = gnew
-        out.start(1, step)
+        out.start(0, step)
         sums_ref[0:8, :] += fold_rows(grad * unit)
         sums_ref[8:16, :] += fold_rows(grad)
         low = gnew.astype(BF)
         low_all[rows, :] = low
         gmix_ref[:, rows] = nt(low, wo[...]).astype(BF).T
-        out.start(2, step)
+        out.start(1, step)
         other_core(mine_b, theirs_b, sems_b, step).wait_recv()
-        gmem_ref[rows, :] = (mine_b[rows, :].astype(F32) + theirs_b[rows, :].astype(F32)).astype(BF)
-        out.start(0, step)
+        total = (mine_b[rows, :].astype(F32) + theirs_b[rows, :].astype(F32)).astype(BF)
+        gmem_ref[pl.ds(step * (CHUNK // UNIT), CHUNK // UNIT)] = in_tiles(total)
     chunks(tokens, close)
     flat[3 * cols:4 * cols, :] = tn(mixed[...], low_all[...]).astype(BF)
     if flat.shape[0] > 4 * cols:
         flat[4 * cols:, :] = jnp.zeros((flat.shape[0] - 4 * cols, features), BF)
     gives = (give0, give1, give2, give3)
     spread_flat(devices, places, flat, gives)
+    late.wait(4)
+    turn_rows(gmem_ref, turned_a, info[0, DOCS + 1])
+    turn_rows(output_ref, turned_b, info[0, DOCS + 1])
+    turned = Late([(turned_a, gmem_out), (turned_b, output_out)], turned_sems)
     for copy in zz_copies:
         copy.wait_recv()
     ready_rows = blocks.shape[1]
@@ -1022,32 +1082,34 @@
             ref[d, 0:ready_rows, :] = blocks[d]
     for copy in z_copies + zz_copies:
         copy.wait_send()
+    turned.wait(0, 1)
     out.drain(tokens)
     drain(tokens, mine_a, theirs_a, sems_a)
     drain(tokens, mine_b, theirs_b, sems_b)
 
 
-def cross_back(devices, dq, dk, dv, wc, nc, memory, res, gres, mixed, wo, norms, parts):
+def cross_back(devices, info, dq, dk, dv, wc, nc, memory, res, gres, output, mixed, wo, norms, parts):
     tokens, features = nc.shape
     cols = dq.shape[1]
     across, ready_rows = devices // 4, parts[0].shape[1]
     flat_rows = whole_blocks(4 * cols, devices)
     give = ((across, ready_rows + flat_rows // devices, features), BF, "V")
     wide = (tokens, features)
-    outs = [(wide, BF, "A"), (wide, F32, "A"), ((cols, tokens), BF, "A")] + [give] * 4 + [((16, features), F32, "V")]
+    outs = [(wide, BF, "A"), (wide, BF, "A"), (wide, F32, "A"), ((cols, tokens), BF, "A")] + [give] * 4 + [((16, features), F32, "V")]
     low, high = pltpu.VMEM(wide, BF), pltpu.VMEM(wide, F32)
     small = pltpu.VMEM((across, ready_rows, features), BF)
     z_sems = pltpu.SemaphoreType.DMA((2, across))
-    scratch = [low, low, high, high, low, high, pltpu.VMEM((cols, tokens), BF), pltpu.VMEM((flat_rows, features), BF), small, small, small]
-    scratch += [low] * 5 + [pair_sems(tokens)] * 2 + [pltpu.SemaphoreType.DMA((4,)), out_semaphores(3, tokens), z_sems, z_sems]
+    tiles = pltpu.VMEM((tokens // UNIT, UNIT, features), BF)
+    scratch = [low, low, high, high, tiles, tiles, low, low, high, pltpu.VMEM((cols, tokens), BF), pltpu.VMEM((flat_rows, features), BF), small, small, small]
+    scratch += [low] * 5 + [pair_sems(tokens)] * 2 + [pltpu.SemaphoreType.DMA((5,)), out_semaphores(2, tokens), pltpu.SemaphoreType.DMA((2,)), z_sems, z_sems]
     return call(partial(cross_back_kernel, devices), "cross_back",
-                [dq, dk, dv, wc, nc, memory, res, gres, mixed, wo, norms] + parts, "VVVVAAAAVVVVVVV", outs, scratch, 4)
-
-
-def self_back_kernel(devices, ready_rows, dq, dk, dv, ws, nq_hbm, nkv_hbm, query_hbm, kv_hbm, gres_hbm, norms, sums_c, sums_f,
+                [info, dq, dk, dv, wc, nc, memory, res, gres, in_tiles(output), mixed, wo, norms] + parts, "SVVVVAAAAAVVVVVVV", outs, scratch, 4)
+
+
+def self_back_kernel(devices, ready_rows, info, dq, dk, dv, ws, nq_hbm, nkv_hbm, query_hbm, kv_hbm, gres_hbm, norms, sums_c, sums_f,
                      part0, part1, part2, part3,
                      gquery_out, gkv_out, last_ref, more_ref, gnorm_ref,
-                     nq, nkv, query, kv, gres, gquery_ref, gkv_ref, flat, source, landing, pieces, landed, more_pieces, more_landed,
+                     nq, nkv, query, kv, gres, gquery_ref, gkv_ref, turned_a, turned_b, flat, source, landing, pieces, landed, more_pieces, more_landed,
                      norm_mine, norm_all, mine_a, theirs_a, mine_b, theirs_b, sums, sems_a, sems_b, late_sems, out_sems,
                      z_sems, more_z_sems, plane_sems, n_sems, *spread_sems):
     tokens, features = nq.shape
@@ -1055,7 +1117,6 @@
     places = places_of(devices)
     me, x, y, z, xpeer, ypeer, order, ahead, behind = places
     late = Late([(nq_hbm, nq), (nkv_hbm, nkv), (query_hbm, query), (kv_hbm, kv), (gres_hbm, gres)], late_sems)
-    out = Out([(gquery_ref, gquery_out), (gkv_ref, gkv_out)], out_sems)
     more_rows = more_ref.shape[2]
     for level in range(across):
         more_pieces[level] = four_sum((part0, part1, part2, part3), (level, pl.ds(ready_rows, more_rows)))
@@ -1080,15 +1141,14 @@
         other_core(mine_a, theirs_a, sems_a, step).wait_recv()
         grad = mine_a[rows, :].astype(F32) + theirs_a[rows, :].astype(F32)
         unit, scale = normalise(query[rows, :].astype(F32))
-        gquery_ref[rows, :] = (norm_back(unit, scale, norms[0:1, :], grad) + gres[rows, :]).astype(BF)
-        out.start(0, step)
+        tiles = pl.ds(step * (CHUNK // UNIT), CHUNK // UNIT)
+        gquery_ref[tiles] = in_tiles((norm_back(unit, scale, norms[0:1, :], grad) + gres[rows, :]).astype(BF))
         sums[0:8, :] += fold_rows(grad * unit)
         sums[8:16, :] += fold_rows(grad)
         other_core(mine_b, theirs_b, sems_b, step).wait_recv()
         grad = mine_b[rows, :].astype(F32) + theirs_b[rows, :].astype(F32)
         unit, scale = normalise(kv[rows, :].astype(F32))
-        gkv_ref[rows, :] = norm_back(unit, scale, norms[2:3, :], grad).astype(BF)
-        out.start(1, step)
+        gkv_ref[tiles] = in_tiles(norm_back(unit, scale, norms[2:3, :], grad).astype(BF))
         sums[16:24, :] += fold_rows(grad * unit)
         sums[24:32, :] += fold_rows(grad)
     middle = tokens // 2
@@ -1105,10 +1165,13 @@
     z_copies = z_sum_start(devices, places, pieces, landed, z_sems)
     n_copies = [send(norm_mine, norm_all.at[d], n_sems.at[0, d], n_sems.at[1, d], dp=other)
                 for d, other in zip(range(1, devices), others)]
+    turn_rows(gquery_ref, turned_a, info[0, DOCS + 1])
     more.diagonal()
     last_ref[0, 0] = z_sum_end(places, pieces, landed, z_copies)
     last = Spread(places, last_ref, *spread_sems[5:])
     last.start()
+    turn_rows(gkv_ref, turned_b, info[0, DOCS + 1])
+    turned = Late([(turned_a, gquery_out), (turned_b, gkv_out)], out_sems)
     last.relay()
     last.diagonal()
     total = norm_mine[...]
@@ -1122,12 +1185,12 @@
     last.drain()
     for copy in more_copies + plane_copies + z_copies + n_copies:
         copy.wait_send()
-    out.drain(tokens)
+    turned.wait(0, 1)
     drain(tokens, mine_a, theirs_a, sems_a)
     drain(tokens, mine_b, theirs_b, sems_b)
 
 
-def self_back(devices, ready_rows, dq, dk, dv, ws, nq, nkv, query, kv, gres, norms, sums_c, sums_f, parts):
+def self_back(devices, ready_rows, info, dq, dk, dv, ws, nq, nkv, query, kv, gres, norms, sums_c, sums_f, parts):
     tokens, features = nq.shape
     cols = dq.shape[1]
     across, more_rows = devices // 4, parts[0].shape[1] - ready_rows
@@ -1140,31 +1203,35 @@
     small, tiny = pltpu.VMEM((across, more_rows, features), BF), pltpu.VMEM((across, rows, features), BF)
     four = pltpu.VMEM((4, across, rows, features), BF)
     D = pltpu.SemaphoreType.DMA
-    scratch = [low, low, low, low, high, low, low, pltpu.VMEM((flat_rows, features), BF), four, four, tiny, tiny, small, small,
+    tiles = pltpu.VMEM((tokens // UNIT, UNIT, features), BF)
+    scratch = [low, low, low, low, high, tiles, tiles, low, low, pltpu.VMEM((flat_rows, features), BF), four, four, tiny, tiny, small, small,
                pltpu.VMEM((8, features), F32), pltpu.VMEM((devices, 8, features), F32)]
     scratch += [low] * 4 + [pltpu.VMEM((32, features), F32)] + [pair_sems(tokens)] * 2
-    scratch += [D((5,)), out_semaphores(2, tokens), D((2, across)), D((2, across)), D((2, 4)), D((2, devices))]
+    scratch += [D((5,)), D((2,)), D((2, across)), D((2, across)), D((2, 4)), D((2, devices))]
     scratch += [D((2, across))] * 10
     return call(partial(self_back_kernel, devices, ready_rows), "self_back",
-                [dq, dk, dv, ws, nq, nkv, query, kv, gres, norms, sums_c, sums_f] + parts, "VVVVAAAAAVVVVVVV", outs, scratch, 5)
+                [info, dq, dk, dv, ws, nq, nkv, query, kv, gres, norms, sums_c, sums_f] + parts, "SVVVVAAAAAVVVVVVV", outs, scratch, 5)
 
 
 def update_kernel(devices, early_unit, late_unit, late_rows, owner_ref, me_ref, last, more, part0, part1, part2, part3,
-                  master, first, second, gquery_in, gkv_in, grad_ref, first_ref, second_ref, new_ref, gquery_out, gkv_out,
-                  held, taken, held_q, held_kv, sems):
+                  master_hbm, first_hbm, second_hbm, gquery_in, gkv_in,
+                  grad_out, first_out, second_out, new_out, gquery_out, gkv_out,
+                  held, taken, master, first, second, held_q, held_kv, grad_ref, first_ref, second_ref, new_ref, sems, out_sems):
     units = owner_ref.shape[0]
     slots = master.shape[0]
     across = devices // 4
     me = me_ref[0]
     here, level = lax.rem(me, 4), lax.div(me, 4)
-    entering = Late([(gquery_in, held_q), (gkv_in, held_kv)], sems.at[0])
+    entering = Late([(master_hbm, master), (first_hbm, first), (second_hbm, second), (gquery_in, held_q), (gkv_in, held_kv)], sems)
+    results = list(zip((grad_ref, first_ref, second_ref, new_ref), (grad_out, first_out, second_out, new_out)))
 
     def find(u, count):
         held[count] = u
         return count + (owner_ref[u] == me).astype(jnp.int32)
     count = lax.fori_loop(0, units, find, jnp.int32(0), unroll=4)
-    entering.wait(0, 1)
-    leaving = Late([(held_q, gquery_out), (held_kv, gkv_out)], sems.at[1])
+    entering.wait(3, 4)
+    leaving = Late([(held_q, gquery_out), (held_kv, gkv_out)], out_sems.at[0])
+    entering.wait(0, 1, 2)
 
     def lookup(row, size):
         block = lax.div(row, size)
@@ -1203,16 +1270,24 @@
             for ref in (grad_ref, first_ref, second_ref, new_ref):
                 ref[slot] = jnp.zeros(ref.shape[1:], F32)
         return carry
-    lax.fori_loop(0, slots, one, 0)
+    half = slots // 2
+    lax.fori_loop(0, half, one, 0)
+    early = Late([(ref.at[pl.ds(0, half)], out.at[pl.ds(0, half)]) for ref, out in results], out_sems.at[1])
+    lax.fori_loop(half, slots, one, 0)
+    rest = Late([(ref.at[pl.ds(half, half)], out.at[pl.ds(half, half)]) for ref, out in results], out_sems.at[2])
+    for copies in (early, rest):
+        copies.wait(*range(4))
     leaving.wait(0, 1)
 
 
 def update(devices, early_unit, late_unit, late_rows, unit_owner, me, last, more, parts, master, first, second, gquery, gkv):
-    outs = [(master.shape, F32, "V")] * 4 + [(gquery.shape, BF, "A")] * 2
+    outs = [(master.shape, F32, "A")] * 4 + [(gquery.shape, BF, "A")] * 2
     kernel = partial(update_kernel, devices, early_unit, late_unit, late_rows)
-    return call(kernel, "update", [unit_owner, me, last, more] + parts + [master, first, second, gquery, gkv], "SSVVVVVVVVVAA", outs,
-                [pltpu.SMEM((unit_owner.shape[0] + 8,), jnp.int32), pltpu.VMEM((UNIT, master.shape[2]), BF),
-                 pltpu.VMEM(gquery.shape, BF), pltpu.VMEM(gkv.shape, BF), pltpu.SemaphoreType.DMA((2, 2))])
+    owned = pltpu.VMEM(master.shape, F32)
+    return call(kernel, "update", [unit_owner, me, last, more] + parts + [master, first, second, gquery, gkv], "SSVVVVVVAAAAA", outs,
+                [pltpu.SMEM((unit_owner.shape[0] + 8,), jnp.int32), pltpu.VMEM((UNIT, master.shape[2]), BF), owned, owned, owned,
+                 pltpu.VMEM(gquery.shape, BF), pltpu.VMEM(gkv.shape, BF), owned, owned, owned, owned,
+                 pltpu.SemaphoreType.DMA((5,)), pltpu.SemaphoreType.DMA((3, 4))])
 
 
 def adamw_step(gradient, first, second, weight, rate, decay):
@@ -1241,29 +1316,27 @@
     norm_row = lax.dynamic_update_slice(
         jnp.zeros((1, features), F32), norm_master.reshape(1, norm_share), (0, lax.rem(me * norm_share, features)))
     rank_row, count_row = obs_rank.reshape(1, ROW), obs_count.reshape(1, ROW)
-    place_of, steps = plan(unit_owner, lengths, devices, slots + 1)
-    nq, nkv, qt, k, kt, v, vt, kc, kct, vc, vct, ws, wc, wo_self, wo_cross, w1, w2, norms, *tables = project(
-        devices, place_of, lengths, master.reshape(shape), norm_row, rank_row,
-        query_stream, kv_stream, memory, cols, hidden)
+    place_of, rank_row, count_row, steps, info = plan(unit_owner, lengths, rank_row, count_row, slots + 1)
+    nq, nkv, qt, k, kt, v, vt, kc, kct, vc, vct, query, kv, source, cotangent, ws, wc, wo_self, wo_cross, w1, w2, norms, *tables = project(
+        devices, place_of, info, master.reshape(shape), norm_row, rank_row, query_stream, kv_stream, memory, out_grad, cols, hidden)
     mixed_self, mixed_self_t, total_self = attend_forward(steps, qt, k, vt, tables, count_row, True)
-    residual, nc, qct = self_out(mixed_self, wo_self, query_stream, wc, norms)
+    residual, nc, qct = self_out(mixed_self, wo_self, query, wc, norms)
     mixed_cross, mixed_cross_t, total_cross = attend_forward(steps, qct, kc, vct, tables, count_row, False)
     output, grad_cross_res, grad_mixed, *parts, sums_f = feed_forward(
-        devices, mixed_cross, wo_cross, residual, w1, w2, out_grad, norms)
+        devices, mixed_cross, wo_cross, residual, w1, w2, cotangent, norms)
     tie = lax.optimization_barrier
     ready_rows = parts[0].shape[1]
     parts = [parts[0]] + [plane_swap(parts[f], devices, f) for f in (1, 2, 3)]
-    dq, dk, dv, output = attend_backward(
-        steps, qct, kc, kct, vc, grad_mixed, mixed_cross_t, total_cross, tables, count_row, output, False)
+    dq, dk, dv = attend_backward(steps, qct, kc, kct, vc, grad_mixed, mixed_cross_t, total_cross, tables, count_row, [], False)
     parts, dq = tie((parts, dq))
-    grad_memory, grad_residual, grad_mixed, *parts, sums_c = cross_back(
-        devices, dq, dk, dv, wc, nc, memory, residual, grad_cross_res, mixed_self, wo_self, norms, parts)
+    grad_memory, output, grad_residual, grad_mixed, *parts, sums_c = cross_back(
+        devices, info, dq, dk, dv, wc, nc, source, residual, grad_cross_res, output, mixed_self, wo_self, norms, parts)
     parts = [parts[0]] + [plane_swap(parts[f], devices, f) for f in (1, 2, 3)]
-    dq, dk, dv, grad_memory = attend_backward(
-        steps, qt, k, kt, v, grad_mixed, mixed_self_t, total_self, tables, count_row, grad_memory, True)
+    dq, dk, dv, grad_memory, output = attend_backward(
+        steps, qt, k, kt, v, grad_mixed, mixed_self_t, total_self, tables, count_row, [grad_memory, output], True)
     parts, dq = tie((parts, dq))
     grad_query, grad_kv, last, more, norm_grads = self_back(
-        devices, ready_rows, dq, dk, dv, ws, nq, nkv, query_stream, kv_stream, grad_residual, norms, sums_c, sums_f, parts)
+        devices, ready_rows, info, dq, dk, dv, ws, nq, nkv, query, kv, grad_residual, norms, sums_c, sums_f, parts)
 
     early, late = 3 * cols // unit_rows, 7 * cols // unit_rows
     weight_grad, weight_first, weight_second, weight_new, grad_query, grad_kv = update(

time: 352 us -> 336 us (0.955)
  Pallas kernels: 335 us -> 316 us
  waiting for transfers between devices: 1.6 us -> 6.71 us
    pallas_call x11, Pallas kernels: 335 us -> 316 us  [call(): pl.pallas_call(kernel, out_shape=tuple((jax.ShapeDtypeStruct(shape, dtype...]
    ppermute x6, waiting for transfers between devices: 1.6 us -> 6.71 us  [plane_swap(): lax.ppermute(value, 'dp', [(i, i // 4 * 4 + (i % 4 ^ f)) for i in range(c...]
  transfers between devices with their start and end apart: 6 -> 6, of which waited for: 1 -> 1; matrix products, arithmetic and copies ran while one was open for 0% -> 0% of each run, Pallas kernels for 19% -> 17%
where the time goes in v7:
time: 336 us
  Pallas kernels  316 us (94%)
  starting transfers between devices  7.3 us (2%)
  waiting for transfers between devices  6.71 us (2%)
  local copies, waits for them, and re-layouts  3.77 us (1%)
    pallas_call x11, Pallas kernels, call(): pl.pallas_call(kernel, out_shape=tuple((jax.ShapeDtypeStruct(shape, dtype...  316 us
    ppermute x6, starting transfers between devices, plane_swap(): lax.ppermute(value, 'dp', [(i, i // 4 * 4 + (i % 4 ^ f)) for i in range(c...  7.3 us
  transfers between devices with their start and end apart: 6, of which 1 were waited for; matrix products, arithmetic and copies ran while one was open for 0% of the time, Pallas kernels for 17%

profile of v7, /device:TPU:0, one launch (start us, length us, event | category | flops | bytes accessed | tf_op | source)
XLA Modules:
  0.0 335.5 jit_solution(17591719754375580613)
XLA Ops:
  0.7 0.7 constant_dynamic-update-slice_fusion.norm_row
  1.4 0.0 copy-start.1
  1.4 2.1 plan.1
  3.5 0.0 copy-done.1
  3.5 82.5 %project.1 = (bf16[2048,512]{1,0:T(8,128)(2,1)}, bf16[2048,512]{1,0:T(8,128)(2,1)}, bf16[256,2048]{1,0:T(8,128)(2,1)}, bf16[2048,256]{1,0:T(8,128)(2,1)}, bf16[2...) custom-call(s32[1,256]{1,0:T(1,128)} %get-tuple-element.99.place_ref, ...), custom_call_target="tpu_custom_call" | custom-call | flops 40000000000 | bytes 16777216 | tf_op jit(solution)/shard_map/project/pallas_call | solution.py:547
  86.1 17.3 %attend_self_forward.1 = (bf16[2048,256]{1,0:T(8,128)(2,1)}, bf16[256,2048]{1,0:T(8,128)(2,1)}, f32[8,2048]{1,0:T(8,128)}) custom-call(s32[2,40]{1,0:T(2,128)} %get-tuple-element.97.table, s32[1,2048]{1,0:T(1,128)} %get-tuple-element.98.count_ref, bf16[256,2048]{1,0:T(8,128)(2,1)} %get-tuple-element.102.qt_hbm, ...), custom_call_target="tpu_custom_call" | custom-call | flops 40000000000 | bytes 16777216 | tf_op jit(solution)/shard_map/attend_self_forward/pallas_call | solution.py:547
  103.4 8.4 %self_out.1 = (f32[2048,512]{1,0:T(8,128)}, bf16[2048,512]{1,0:T(8,128)(2,1)}, bf16[256,2048]{1,0:T(8,128)(2,1)}) custom-call(bf16[2048,256]{1,0:T(8,128)(2,1)} %get-tuple-element.109.mixed, bf16[256,512]{1,0:T(8,128)(2,1)} %get-tuple-element.110.wo, bf16[2048,512]{1,0:T(8,128)(2,1)} %get-tuple-element.111.query_hbm, ...), custom_call_target="tpu_custom_call" | custom-call | flops 40000000000 | bytes 16777216 | tf_op jit(solution)/shard_map/self_out/pallas_call | solution.py:547
  111.8 16.9 %attend_cross_forward.1 = (bf16[2048,256]{1,0:T(8,128)(2,1)}, bf16[256,2048]{1,0:T(8,128)(2,1)}, f32[8,2048]{1,0:T(8,128)}) custom-call(s32[2,40]{1,0:T(2,128)} %get-tuple-element.97.table, s32[1,2048]{1,0:T(1,128)} %get-tuple-element.98.count_ref, bf16[256,2048]{1,0:T(8,128)(2,1)} %get-tuple-element.114.qt_hbm, ...), custom_call_target="tpu_custom_call" | custom-call | flops 40000000000 | bytes 16777216 | tf_op jit(solution)/shard_map/attend_cross_forward/pallas_call | solution.py:547
  128.8 37.3 %feed_forward.1 = (bf16[2048,512]{1,0:T(8,128)(2,1)}, f32[2048,512]{1,0:T(8,128)}, bf16[256,2048]{1,0:T(8,128)(2,1)}, bf16[4,144,512]{2,1,0:T(8,128)(2,1)}, bf16...) custom-call(bf16[2048,256]{1,0:T(8,128)(2,1)} %get-tuple-element.117., ...), custom_call_target="tpu_custom_call" | custom-call | flops 40000000000 | bytes 16777216 | tf_op jit(solution)/shard_map/feed_forward/pallas_call | solution.py:547
  166.1 1.6 collective-permute-start
  167.6 2.2 collective-permute-start.1
  169.8 0.0 collective-permute-start.2
  169.8 27.7 %attend_cross_backward.1 = (bf16[2048,256]{1,0:T(8,128)(2,1)}, bf16[2048,256]{1,0:T(8,128)(2,1)}, bf16[2048,256]{1,0:T(8,128)(2,1)}) custom-call(s32[2,40]{1,0:T(2,128)} %get-tuple-element.97.table, s32[1,2048]{1,0:T(1,128)} %get-tuple-element.98.count_ref, f32[8,2048]{1,0:T(8,128)} %get-tuple-element.127.lse_ref, ...), custom_call_target="tpu_custom_call" | custom-call | flops 40000000000 | bytes 16777216 | tf_op jit(solution)/shard_map/attend_cross_backward/pallas_call | solution.py:547
  197.5 0.0 collective-permute-done.part1
  197.5 0.0 copy-start.7
  197.6 0.0 collective-permute-done.1.part2
  197.6 0.0 copy-start.8
  197.6 0.0 collective-permute-done.2.part3
  197.6 0.0 copy-start.9
  197.6 0.8 copy-done.7
  198.4 0.2 copy-done.8
  198.6 0.2 copy-done.9
  198.7 36.5 %cross_back.1 = (bf16[2048,512]{1,0:T(8,128)(2,1)}, bf16[2048,512]{1,0:T(8,128)(2,1)}, f32[2048,512]{1,0:T(8,128)}, bf16[256,2048]{1,0:T(8,128)(2,1)}, bf16[4,20...) custom-call(s32[1,34]{1,0:T(1,128)} %get-tuple-element.100.info, ...), custom_call_target="tpu_custom_call" | custom-call | flops 40000000000 | bytes 16777216 | tf_op jit(solution)/shard_map/cross_back/pallas_call | solution.py:547
  235.3 0.3 collective-permute-start.3
  235.5 2.9 collective-permute-start.4
  238.4 0.4 collective-permute-start.5
  238.8 29.3 %attend_self_backward.1 = (bf16[2048,256]{1,0:T(8,128)(2,1)}, bf16[2048,256]{1,0:T(8,128)(2,1)}, bf16[2048,256]{1,0:T(8,128)(2,1)}, bf16[2048,512]{1,0:T(8,128)(2,1)}, bf16[2048,512]{1,0:T(8,128)(2,1)}) custom-call(s32[2,40]{1,0:T(2,128)} %get-tuple-element.97.table, s32[1,2048]{1,0:T(1,128)} %get-tuple-element.98.count_ref, ...), custom_call_target="tpu_custom_call" | custom-call | flops 40000000000 | bytes 16777216 | tf_op jit(solution)/shard_map/attend_self_backward/pallas_call | solution.py:547
  268.1 0.0 collective-permute-done.3.part1
  268.1 0.0 copy-start.4
  268.1 6.7 %collective-permute-done.4.part2 = bf16[4,208,512]{2,1,0:T(8,128)(2,1)S(1)} collective-permute-done((bf16[4,208,512]{2,1,0:T(8,128)(2,1)}, bf16[4,208,512]{2,1,0:T(8,128)(2,1)S(1)}, u32[]{:S(2)}, u32[]{:S(2)}) %collective-permute-start.4) | collective-permute-done | bytes 852000 | tf_op jit(solution)/shard_map/ppermute | solution.py:536
  274.8 0.0 copy-start.5
  274.8 0.0 collective-permute-done.5.part3
  274.8 0.0 copy-start.6
  274.8 0.0 copy-done.4
  274.8 0.9 copy-done.5
  275.7 0.3 copy-done.6
  276.0 0.0 copy-start
  276.0 0.0 copy-start.2
  276.0 0.0 copy-start.3
  276.0 48.7 %self_back.1 = (bf16[2048,512]{1,0:T(8,128)(2,1)}, bf16[2048,512]{1,0:T(8,128)(2,1)}, bf16[4,4,48,512]{3,2,1,0:T(8,128)(2,1)}, bf16[4,4,64,512]{3,2,1,0:T(8,128)(2,1)}, f32[8,512]{1,0:T(8,128)}) custom-call(s32[1,34]{1,0:T(1,128)} %get-tuple-element.100.info, bf16[2048,256]{1,0:T(8,128)(2,1)} %get-tuple-element.156.dq, ...), custom_call_target="tpu_custom_call" | custom-call | flops 40000000000 | bytes 16777216 | tf_op jit(solution)/shard_map/self_back/pallas_call | solution.py:547
  324.7 0.7 copy.30
  325.4 0.0 copy-done
  325.4 0.0 copy-done.2
  325.4 0.0 copy-done.3
  325.4 0.7 multiply_subtract_fusion
  326.1 9.3 %update.1 = (f32[32,16,512]{2,1,0:T(8,128)}, f32[32,16,512]{2,1,0:T(8,128)}, f32[32,16,512]{2,1,0:T(8,128)}, f32[32,16,512]{2,1,0:T(8,128)}, bf16[2048,512]{1,0:T(8,128)(2,1)}, /*index=5*/bf16[2048,512]{1,0:T(8,128)(2,1)}) custom-call(s32[256]{0:T(256)} %owner_ref.1, s32[1]{0:T(128)} %bitcast.10.me_ref, bf16[4,4,48,512]{3,2,1,0:T(8,128)(2,1)} %get-tuple-element.170.last, ...), custom_call_target="tpu_custom_call" | custom-call | flops 40000000000 | bytes 16777216 | tf_op jit(solution)/shard_map/update/pallas_call | solution.py:547
  (1 shorter events, 0.0 us)
Async XLA Ops:
  1.4 2.2 copy-start.1
  166.1 31.5 %collective-permute-start = (bf16[4,144,512]{2,1,0:T(8,128)(2,1)}, bf16[4,144,512]{2,1,0:T(8,128)(2,1)S(1)}, u32[]{:S(2)}, u32[]{:S(2)}) collective-permute-start(bf16[4,144,512]{2,1,0:T(8,128)(2,1)} %get-tuple-element.124), channel_id=1, source_target_pairs={{0,2},{2,0},{4,6},{6,4},{8,10},{10,8},{12,14},{14,12},{16,18},{18,... | collective-permute-start | bytes 1769480 | tf_op jit(solution)/shard_map/ppermute | solution.py:536
  167.6 29.9 %collective-permute-start.1 = (bf16[4,144,512]{2,1,0:T(8,128)(2,1)}, bf16[4,144,512]{2,1,0:T(8,128)(2,1)S(1)}, u32[]{:S(2)}, u32[]{:S(2)}) collective-permute-start(bf16[4,144,512]{2,1,0:T(8,128)(2,1)} %get-tuple-element.125), channel_id=1, source_target_pairs={{0,4},{2,6},{4,0},{6,2},{8,12},{10,14},{12,8},{14,10},{16,20},{18,... | collective-permute-start | bytes 1769480 | tf_op jit(solution)/shard_map/ppermute | solution.py:536
  169.8 27.8 %collective-permute-start.2 = (bf16[4,144,512]{2,1,0:T(8,128)(2,1)}, bf16[4,144,512]{2,1,0:T(8,128)(2,1)S(1)}, u32[]{:S(2)}, u32[]{:S(2)}) collective-permute-start(bf16[4,144,512]{2,1,0:T(8,128)(2,1)} %get-tuple-element.126), channel_id=1, source_target_pairs={{0,6},{2,4},{4,2},{6,0},{8,14},{10,12},{12,10},{14,8},{16,22},{18,... | collective-permute-start | bytes 1769480 | tf_op jit(solution)/shard_map/ppermute | solution.py:536
  197.5 0.8 copy-start.7
  197.6 1.0 copy-start.8
  197.6 1.2 copy-start.9
  235.3 32.8 %collective-permute-start.3 = (bf16[4,208,512]{2,1,0:T(8,128)(2,1)}, bf16[4,208,512]{2,1,0:T(8,128)(2,1)S(1)}, u32[]{:S(2)}, u32[]{:S(2)}) collective-permute-start(bf16[4,208,512]{2,1,0:T(8,128)(2,1)} %get-tuple-element.152), channel_id=1, source_target_pairs={{0,2},{2,0},{4,6},{6,4},{8,10},{10,8},{12,14},{14,12},{16,18},{18,... | collective-permute-start | bytes 2555912 | tf_op jit(solution)/shard_map/ppermute | solution.py:536
  235.5 39.3 %collective-permute-start.4 = (bf16[4,208,512]{2,1,0:T(8,128)(2,1)}, bf16[4,208,512]{2,1,0:T(8,128)(2,1)S(1)}, u32[]{:S(2)}, u32[]{:S(2)}) collective-permute-start(bf16[4,208,512]{2,1,0:T(8,128)(2,1)} %get-tuple-element.153), channel_id=1, source_target_pairs={{0,4},{2,6},{4,0},{6,2},{8,12},{10,14},{12,8},{14,10},{16,20},{18,... | collective-permute-start | bytes 2555912 | tf_op jit(solution)/shard_map/ppermute | solution.py:536
  238.4 36.4 %collective-permute-start.5 = (bf16[4,208,512]{2,1,0:T(8,128)(2,1)}, bf16[4,208,512]{2,1,0:T(8,128)(2,1)S(1)}, u32[]{:S(2)}, u32[]{:S(2)}) collective-permute-start(bf16[4,208,512]{2,1,0:T(8,128)(2,1)} %get-tuple-element.154), channel_id=1, source_target_pairs={{0,6},{2,4},{4,2},{6,0},{8,14},{10,12},{12,10},{14,8},{16,22},{18,... | collective-permute-start | bytes 2555912 | tf_op jit(solution)/shard_map/ppermute | solution.py:536
  268.1 6.7 %copy-start.4 = (bf16[4,208,512]{2,1,0:T(8,128)(2,1)}, bf16[4,208,512]{2,1,0:T(8,128)(2,1)S(1)}, u32[]{:S(2)}) copy-start(bf16[4,208,512]{2,1,0:T(8,128)(2,1)S(1)} %collective-permute-done.3.part1) | copy-start | bytes 2555908
  274.8 0.9 copy-start.5
  274.8 1.2 copy-start.6
  276.0 49.4 %copy-start = (f32[256]{0:T(256)S(1)}, f32[256]{0:T(256)}, u32[]{:S(2)}) copy-start(f32[256]{0:T(256)} %param.25) | copy-start | bytes 3076
  276.0 49.4 %copy-start.2 = (f32[256]{0:T(256)S(1)}, f32[256]{0:T(256)}, u32[]{:S(2)}) copy-start(f32[256]{0:T(256)} %param.27) | copy-start | bytes 3076
  276.0 49.4 %copy-start.3 = (f32[256]{0:T(256)S(1)}, f32[256]{0:T(256)}, u32[]{:S(2)}) copy-start(f32[256]{0:T(256)} %param.26) | copy-start | bytes 3076

commit v8 on v7

--- a/solution.py
+++ b/solution.py
@@ -653,14 +653,22 @@
         chunks(tokens, body)
 
 
-def plan_kernel(block, owner_ref, len_ref, rank_ref, count_ref, place_ref, rank_out, count_out, table, info):
+def plan_kernel(block, owner_ref, len_ref, me_ref, rank_ref, count_ref, place_ref, held_ref, rank_out, count_out, table, info):
     units = owner_ref.shape[1]
     owner = owner_ref[...].astype(F32)
     owner_cols = jnp.broadcast_to(owner, (128, units)).T
     owner_cols = jnp.concatenate([owner_cols] * (units // 128), 1)
     before = lax.broadcasted_iota(jnp.int32, (units, units), 0) < lax.broadcasted_iota(jnp.int32, (units, units), 1)
     slots = jnp.sum(jnp.where(before & (owner_cols == owner), 1.0, 0.0), 0, keepdims=True)
-    place_ref[...] = (owner * block + slots).astype(jnp.int32)
+    place = owner * block + slots
+    place_ref[...] = place.astype(jnp.int32)
+    me = me_ref[0].astype(F32)
+    place_cols = jnp.broadcast_to(place, (128, units)).T
+    lane = lax.broadcasted_iota(jnp.int32, (units, 128), 1)
+    unit = lax.broadcasted_iota(jnp.int32, (units, 128), 0).astype(F32)
+    mine = jnp.where(place_cols == me * block + lane.astype(F32), unit, 0.0)
+    mine = jnp.where(lane == 127, jnp.where(owner_cols[:, :128] == me, 1.0, 0.0), jnp.where(lane < block - 1, mine, 0.0))
+    held_ref[...] = jnp.sum(mine, 0, keepdims=True).astype(jnp.int32)
     longest, first, at, start = jnp.int32(0), jnp.int32(0), jnp.int32(0), jnp.int32(0)
     for d in range(DOCS):
         length = len_ref[0, d]
@@ -679,10 +687,10 @@
     step_table(info, table)
 
 
-def plan(unit_owner, lengths, rank_row, count_row, block):
+def plan(unit_owner, lengths, me, rank_row, count_row, block):
     row = ((1, ROW), jnp.int32, "V")
-    return call(partial(plan_kernel, block), "plan", [unit_owner.reshape(1, -1), lengths, rank_row, count_row], "VSVV",
-                [((1, unit_owner.shape[0]), jnp.int32, "V"), row, row, ((2, STEPS), jnp.int32, "S"),
+    return call(partial(plan_kernel, block), "plan", [unit_owner.reshape(1, -1), lengths, me, rank_row, count_row], "VSSVV",
+                [((1, unit_owner.shape[0]), jnp.int32, "V"), ((1, 128), jnp.int32, "V"), row, row, ((2, STEPS), jnp.int32, "S"),
                  ((1, DOCS + 2), jnp.int32, "S")], [])
 
 
@@ -1020,29 +1028,40 @@
     return total.astype(BF)
 
 
+def plane_sum_start(devices, places, flat, used, source, landing, sems):
+    me, x, y, z, xpeer, ypeer = places[:6]
+    if flat.shape[0] > used:
+        flat[used:, :] = jnp.zeros((flat.shape[0] - used, flat.shape[1]), BF)
+    spread_flat(devices, places, flat, [source.at[f] for f in range(4)])
+    return [send(source.at[f], landing.at[f], sems.at[0, f], sems.at[1, f], dp=peer)
+            for f, peer in ((3, me + 3 - 2 * x - 4 * y), (1, xpeer), (2, ypeer))]
+
+
 def four_sum(parts, at):
     return (parts[0][at].astype(F32) + parts[1][at].astype(F32) + parts[2][at].astype(F32) + parts[3][at].astype(F32)).astype(BF)
 
 
 def cross_back_kernel(devices, info, dq, dk, dv, wc, nc_hbm, memory_hbm, res_hbm, gres_hbm, output_hbm, mixed, wo, norms,
                       part0, part1, part2, part3,
-                      gmem_out, output_out, gnew_out, gmix_out, give0, give1, give2, give3, sums_ref,
-                      nc, memory, res, gres, output_ref, gmem_ref, turned_a, turned_b, gnew_ref, gmix_ref, flat, pieces, landed, blocks,
-                      mine_a, theirs_a, mine_b, theirs_b, low_all, sems_a, sems_b, late_sems, out_sems, turned_sems, z_sems, zz_sems):
+                      gmem_out, output_out, gnew_out, gmix_out, give0, give1, give2, give3, more_ref, sums_ref,
+                      nc, memory, res, gres, output_ref, gmem_ref, turned_a, turned_b, gmix_ref, flat, flat_o, source, landing, pieces, landed, blocks,
+                      mine_a, theirs_a, mine_b, theirs_b, low_all, sems_a, sems_b, late_sems, out_sems, turned_sems, z_sems, zz_sems, plane_sems):
     tokens, features = nc.shape
     cols = dq.shape[1]
     across = devices // 4
     places = places_of(devices)
     me, x, y, z, xpeer, ypeer, order, ahead, behind = places
     late = Late([(nc_hbm, nc), (memory_hbm, memory), (res_hbm, res), (gres_hbm, gres), (output_hbm, output_ref)], late_sems)
-    out = Out([(gnew_ref, gnew_out), (gmix_ref, gmix_out)], out_sems)
+    out = Out([(gres, gnew_out), (gmix_ref, gmix_out)], out_sems)
     for level in range(across):
         pieces[level] = four_sum((part0, part1, part2, part3), level)
-    greet([{"head": 1 - lax.axis_index("head")}] + [{"dp": ahead(d)} for d in order])
+    greet([{"head": 1 - lax.axis_index("head")}] + [{"dp": ahead(d)} for d in order]
+          + [{"dp": peer} for peer in (xpeer, ypeer, me + 3 - 2 * x - 4 * y)])
     z_copies = z_sum_start(devices, places, pieces, landed, z_sems)
     branch_give(dq, dk, dv, wc, mine_a, theirs_a, mine_b, theirs_b, sems_a, sems_b)
     late.wait(0, 1)
     branch_weights(nc, memory, dq, dk, dv, flat)
+    plane_copies = plane_sum_start(devices, places, flat, 3 * cols, source, landing, plane_sems)
     blocks[0] = z_sum_end(places, pieces, landed, z_copies)
     zz_copies = [send(blocks.at[0], blocks.at[d], zz_sems.at[0, d], zz_sems.at[1, d], dp=ahead(d)) for d in order]
     sums_ref[...] = jnp.zeros_like(sums_ref)
@@ -1053,7 +1072,7 @@
         grad = mine_a[rows, :].astype(F32) + theirs_a[rows, :].astype(F32)
         unit, scale = normalise(res[rows, :])
         gnew = norm_back(unit, scale, norms[4:5, :], grad) + gres[rows, :]
-        gnew_ref[rows, :] = gnew
+        gres[rows, :] = gnew
         out.start(0, step)
         sums_ref[0:8, :] += fold_rows(grad * unit)
         sums_ref[8:16, :] += fold_rows(grad)
@@ -1065,11 +1084,15 @@
         total = (mine_b[rows, :].astype(F32) + theirs_b[rows, :].astype(F32)).astype(BF)
         gmem_ref[pl.ds(step * (CHUNK // UNIT), CHUNK // UNIT)] = in_tiles(total)
     chunks(tokens, close)
-    flat[3 * cols:4 * cols, :] = tn(mixed[...], low_all[...]).astype(BF)
-    if flat.shape[0] > 4 * cols:
-        flat[4 * cols:, :] = jnp.zeros((flat.shape[0] - 4 * cols, features), BF)
+    flat_o[0:cols, :] = tn(mixed[...], low_all[...]).astype(BF)
+    if flat_o.shape[0] > cols:
+        flat_o[cols:, :] = jnp.zeros((flat_o.shape[0] - cols, features), BF)
     gives = (give0, give1, give2, give3)
-    spread_flat(devices, places, flat, gives)
+    spread_flat(devices, places, flat_o, gives)
+    for copy in plane_copies:
+        copy.wait_recv()
+    for d in range(across):
+        more_ref[d] = four_sum((source.at[0], landing.at[1], landing.at[2], landing.at[3]), d)
     late.wait(4)
     turn_rows(gmem_ref, turned_a, info[0, DOCS + 1])
     turn_rows(output_ref, turned_b, info[0, DOCS + 1])
@@ -1080,7 +1103,7 @@
     for ref in gives:
         for d in range(across):
             ref[d, 0:ready_rows, :] = blocks[d]
-    for copy in z_copies + zz_copies:
+    for copy in z_copies + zz_copies + plane_copies:
         copy.wait_send()
     turned.wait(0, 1)
     out.drain(tokens)
@@ -1092,45 +1115,49 @@
     tokens, features = nc.shape
     cols = dq.shape[1]
     across, ready_rows = devices // 4, parts[0].shape[1]
-    flat_rows = whole_blocks(4 * cols, devices)
-    give = ((across, ready_rows + flat_rows // devices, features), BF, "V")
+    flat_rows, o_rows = whole_blocks(3 * cols, devices), whole_blocks(cols, devices)
+    give = ((across, ready_rows + o_rows // devices, features), BF, "V")
+    part = (across, flat_rows // devices, features)
     wide = (tokens, features)
-    outs = [(wide, BF, "A"), (wide, BF, "A"), (wide, F32, "A"), ((cols, tokens), BF, "A")] + [give] * 4 + [((16, features), F32, "V")]
+    outs = [(wide, BF, "A"), (wide, BF, "A"), (wide, F32, "A"), ((cols, tokens), BF, "A")] + [give] * 4 + [
+        (part, BF, "V"), ((16, features), F32, "V")]
     low, high = pltpu.VMEM(wide, BF), pltpu.VMEM(wide, F32)
     small = pltpu.VMEM((across, ready_rows, features), BF)
     z_sems = pltpu.SemaphoreType.DMA((2, across))
     tiles = pltpu.VMEM((tokens // UNIT, UNIT, features), BF)
-    scratch = [low, low, high, high, tiles, tiles, low, low, high, pltpu.VMEM((cols, tokens), BF), pltpu.VMEM((flat_rows, features), BF), small, small, small]
-    scratch += [low] * 5 + [pair_sems(tokens)] * 2 + [pltpu.SemaphoreType.DMA((5,)), out_semaphores(2, tokens), pltpu.SemaphoreType.DMA((2,)), z_sems, z_sems]
+    scratch = [low, low, high, high, tiles, tiles, low, low, pltpu.VMEM((cols, tokens), BF), pltpu.VMEM((flat_rows, features), BF),
+               pltpu.VMEM((o_rows, features), BF), pltpu.VMEM((4,) + part, BF), pltpu.VMEM((4,) + part, BF), small, small, small]
+    scratch += [low] * 5 + [pair_sems(tokens)] * 2 + [pltpu.SemaphoreType.DMA((5,)), out_semaphores(2, tokens), pltpu.SemaphoreType.DMA((2,)), z_sems, z_sems,
+                                                 pltpu.SemaphoreType.DMA((2, 4))]
     return call(partial(cross_back_kernel, devices), "cross_back",
                 [info, dq, dk, dv, wc, nc, memory, res, gres, in_tiles(output), mixed, wo, norms] + parts, "SVVVVAAAAAVVVVVVV", outs, scratch, 4)
 
 
-def self_back_kernel(devices, ready_rows, info, dq, dk, dv, ws, nq_hbm, nkv_hbm, query_hbm, kv_hbm, gres_hbm, norms, sums_c, sums_f,
+def self_back_kernel(devices, ready_rows, info, dq, dk, dv, ws, nq_hbm, nkv_hbm, query_hbm, kv_hbm, gres_hbm, norms, sums_c, sums_f, more_in,
                      part0, part1, part2, part3,
                      gquery_out, gkv_out, last_ref, more_ref, gnorm_ref,
                      nq, nkv, query, kv, gres, gquery_ref, gkv_ref, turned_a, turned_b, flat, source, landing, pieces, landed, more_pieces, more_landed,
                      norm_mine, norm_all, mine_a, theirs_a, mine_b, theirs_b, sums, sems_a, sems_b, late_sems, out_sems,
-                     z_sems, more_z_sems, plane_sems, n_sems, *spread_sems):
+                     z_sems, more_z_sems, plane_sems, n_sems, part_rows, part_sems, *spread_sems):
     tokens, features = nq.shape
     across = devices // 4
     places = places_of(devices)
     me, x, y, z, xpeer, ypeer, order, ahead, behind = places
     late = Late([(nq_hbm, nq), (nkv_hbm, nkv), (query_hbm, query), (kv_hbm, kv), (gres_hbm, gres)], late_sems)
-    more_rows = more_ref.shape[2]
-    for level in range(across):
-        more_pieces[level] = four_sum((part0, part1, part2, part3), (level, pl.ds(ready_rows, more_rows)))
+    in_rows, more_rows = more_in.shape[1], more_ref.shape[2]
+    late_parts = Late([(part.at[:, pl.ds(ready_rows, more_rows - in_rows)], part_rows.at[f])
+                       for f, part in enumerate((part0, part1, part2, part3))], part_sems)
     others = [lax.rem(me + d, devices) for d in range(1, devices)]
     greet([{"head": 1 - lax.axis_index("head")}] + [{"dp": other} for other in others])
+    late.wait(0, 1)
+    branch_weights(nq, nkv, dq, dk, dv, flat)
+    plane_copies = plane_sum_start(devices, places, flat, 3 * dq.shape[1], source, landing, plane_sems)
+    late_parts.wait(0, 1, 2, 3)
+    for level in range(across):
+        more_pieces[level, 0:in_rows, :] = more_in[level]
+        more_pieces[level, in_rows:, :] = four_sum([part_rows.at[f] for f in range(4)], level)
     more_copies = z_sum_start(devices, places, more_pieces, more_landed, more_z_sems)
     branch_give(dq, dk, dv, ws, mine_a, theirs_a, mine_b, theirs_b, sems_a, sems_b)
-    late.wait(0, 1)
-    branch_weights(nq, nkv, dq, dk, dv, flat)
-    if flat.shape[0] > 3 * dq.shape[1]:
-        flat[3 * dq.shape[1]:, :] = jnp.zeros((flat.shape[0] - 3 * dq.shape[1], features), BF)
-    spread_flat(devices, places, flat, [source.at[f] for f in range(4)])
-    plane_copies = [send(source.at[f], landing.at[f], plane_sems.at[0, f], plane_sems.at[1, f], dp=peer)
-                    for f, peer in ((3, me + 3 - 2 * x - 4 * y), (1, xpeer), (2, ypeer))]
     more_ref[0, 0] = z_sum_end(places, more_pieces, more_landed, more_copies)
     more = Spread(places, more_ref, *spread_sems[:5])
     more.start()
@@ -1190,10 +1217,10 @@
     drain(tokens, mine_b, theirs_b, sems_b)
 
 
-def self_back(devices, ready_rows, info, dq, dk, dv, ws, nq, nkv, query, kv, gres, norms, sums_c, sums_f, parts):
+def self_back(devices, ready_rows, info, dq, dk, dv, ws, nq, nkv, query, kv, gres, norms, sums_c, sums_f, more_in, parts):
     tokens, features = nq.shape
     cols = dq.shape[1]
-    across, more_rows = devices // 4, parts[0].shape[1] - ready_rows
+    across, more_rows = devices // 4, more_in.shape[1] + parts[0].shape[1] - ready_rows
     flat_rows = whole_blocks(3 * cols, devices)
     rows = flat_rows // devices
     wide = (tokens, features)
@@ -1207,53 +1234,53 @@
     scratch = [low, low, low, low, high, tiles, tiles, low, low, pltpu.VMEM((flat_rows, features), BF), four, four, tiny, tiny, small, small,
                pltpu.VMEM((8, features), F32), pltpu.VMEM((devices, 8, features), F32)]
     scratch += [low] * 4 + [pltpu.VMEM((32, features), F32)] + [pair_sems(tokens)] * 2
-    scratch += [D((5,)), D((2,)), D((2, across)), D((2, across)), D((2, 4)), D((2, devices))]
+    scratch += [D((5,)), D((2,)), D((2, across)), D((2, across)), D((2, 4)), D((2, devices)),
+                pltpu.VMEM((4, across, more_rows - more_in.shape[1], features), BF), D((4,))]
     scratch += [D((2, across))] * 10
     return call(partial(self_back_kernel, devices, ready_rows), "self_back",
-                [info, dq, dk, dv, ws, nq, nkv, query, kv, gres, norms, sums_c, sums_f] + parts, "SVVVVAAAAAVVVVVVV", outs, scratch, 5)
-
-
-def update_kernel(devices, early_unit, late_unit, late_rows, owner_ref, me_ref, last, more, part0, part1, part2, part3,
-                  master_hbm, first_hbm, second_hbm, gquery_in, gkv_in,
-                  grad_out, first_out, second_out, new_out, gquery_out, gkv_out,
-                  held, taken, master, first, second, held_q, held_kv, grad_ref, first_ref, second_ref, new_ref, sems, out_sems):
-    units = owner_ref.shape[0]
+                [info, dq, dk, dv, ws, nq, nkv, query, kv, gres, norms, sums_c, sums_f, more_in] + parts, "SVVVVAAAAAVVVVAAAA", outs, scratch, 5)
+
+
+def update_kernel(devices, firsts, late_rows, more_first, held, me_ref, *refs):
+    hbm, (grad_out, first_out, second_out, new_out, gquery_out, gkv_out) = refs[:11], refs[11:17]
+    last, more, part0, part1, part2, part3, master, first, second, held_q, held_kv = refs[17:28]
+    taken, grad_ref, first_ref, second_ref, new_ref, sems, out_sems = refs[28:]
+    entering = Late(list(zip(hbm, refs[17:28])), sems)
     slots = master.shape[0]
     across = devices // 4
     me = me_ref[0]
     here, level = lax.rem(me, 4), lax.div(me, 4)
-    entering = Late([(master_hbm, master), (first_hbm, first), (second_hbm, second), (gquery_in, held_q), (gkv_in, held_kv)], sems)
+    count = held[0, 127]
     results = list(zip((grad_ref, first_ref, second_ref, new_ref), (grad_out, first_out, second_out, new_out)))
-
-    def find(u, count):
-        held[count] = u
-        return count + (owner_ref[u] == me).astype(jnp.int32)
-    count = lax.fori_loop(0, units, find, jnp.int32(0), unroll=4)
-    entering.wait(3, 4)
+    entering.wait(9, 10)
     leaving = Late([(held_q, gquery_out), (held_kv, gkv_out)], out_sems.at[0])
-    entering.wait(0, 1, 2)
-
-    def lookup(row, size):
+    entering.wait(*range(9))
+
+    def lookup(row, size, start=0):
         block = lax.div(row, size)
         behind = lax.rem(level - lax.div(block, 4) + across, across)
-        return lax.rem(block, 4) ^ here, behind, pl.ds(pl.multiple_of(lax.rem(row, size), UNIT), UNIT)
+        return lax.rem(block, 4) ^ here, behind, pl.ds(pl.multiple_of(lax.rem(row, size) + start, UNIT), UNIT)
 
     def one(slot, carry):
         @pl.when(slot < count)
         def _():
-            unit = held[slot]
-
-            @pl.when(unit < early_unit)
+            unit = held[0, slot]
+
+            @pl.when(unit < firsts[0])
             def _():
                 taken[...] = last[lookup(unit * UNIT, last.shape[2])]
 
-            @pl.when((unit >= early_unit) & (unit < late_unit))
+            @pl.when((unit >= firsts[0]) & (unit < firsts[1]))
             def _():
-                taken[...] = more[lookup((unit - early_unit) * UNIT, more.shape[2])]
-
-            @pl.when(unit >= late_unit)
+                taken[...] = more[lookup((unit - firsts[0]) * UNIT, more_first)]
+
+            @pl.when((unit >= firsts[1]) & (unit < firsts[2]))
             def _():
-                offset, behind, rows = lookup((unit - late_unit) * UNIT, late_rows)
+                taken[...] = more[lookup((unit - firsts[1]) * UNIT, more.shape[2] - more_first, more_first)]
+
+            @pl.when(unit >= firsts[2])
+            def _():
+                offset, behind, rows = lookup((unit - firsts[2]) * UNIT, late_rows)
                 for f, part in enumerate((part0, part1, part2, part3)):
                     @pl.when(offset == f)
                     def _():
@@ -1280,14 +1307,13 @@
     leaving.wait(0, 1)
 
 
-def update(devices, early_unit, late_unit, late_rows, unit_owner, me, last, more, parts, master, first, second, gquery, gkv):
+def update(devices, firsts, late_rows, more_first, held, me, last, more, parts, master, first, second, gquery, gkv):
     outs = [(master.shape, F32, "A")] * 4 + [(gquery.shape, BF, "A")] * 2
-    kernel = partial(update_kernel, devices, early_unit, late_unit, late_rows)
-    owned = pltpu.VMEM(master.shape, F32)
-    return call(kernel, "update", [unit_owner, me, last, more] + parts + [master, first, second, gquery, gkv], "SSVVVVVVAAAAA", outs,
-                [pltpu.SMEM((unit_owner.shape[0] + 8,), jnp.int32), pltpu.VMEM((UNIT, master.shape[2]), BF), owned, owned, owned,
-                 pltpu.VMEM(gquery.shape, BF), pltpu.VMEM(gkv.shape, BF), owned, owned, owned, owned,
-                 pltpu.SemaphoreType.DMA((5,)), pltpu.SemaphoreType.DMA((3, 4))])
+    args = [last, more] + parts + [master, first, second, gquery, gkv]
+    scratch = [pltpu.VMEM(arg.shape, arg.dtype) for arg in args] + [pltpu.VMEM((UNIT, master.shape[2]), BF)]
+    scratch += [pltpu.VMEM(master.shape, F32)] * 4 + [pltpu.SemaphoreType.DMA((11,)), pltpu.SemaphoreType.DMA((3, 4))]
+    return call(partial(update_kernel, devices, firsts, late_rows, more_first), "update", [held, me] + args, "SS" + "A" * 11,
+                outs, scratch)
 
 
 def adamw_step(gradient, first, second, weight, rate, decay):
@@ -1316,7 +1342,7 @@
     norm_row = lax.dynamic_update_slice(
         jnp.zeros((1, features), F32), norm_master.reshape(1, norm_share), (0, lax.rem(me * norm_share, features)))
     rank_row, count_row = obs_rank.reshape(1, ROW), obs_count.reshape(1, ROW)
-    place_of, rank_row, count_row, steps, info = plan(unit_owner, lengths, rank_row, count_row, slots + 1)
+    place_of, held, rank_row, count_row, steps, info = plan(unit_owner, lengths, me.reshape(1), rank_row, count_row, slots + 1)
     nq, nkv, qt, k, kt, v, vt, kc, kct, vc, vct, query, kv, source, cotangent, ws, wc, wo_self, wo_cross, w1, w2, norms, *tables = project(
         devices, place_of, info, master.reshape(shape), norm_row, rank_row, query_stream, kv_stream, memory, out_grad, cols, hidden)
     mixed_self, mixed_self_t, total_self = attend_forward(steps, qt, k, vt, tables, count_row, True)
@@ -1329,18 +1355,19 @@
     parts = [parts[0]] + [plane_swap(parts[f], devices, f) for f in (1, 2, 3)]
     dq, dk, dv = attend_backward(steps, qct, kc, kct, vc, grad_mixed, mixed_cross_t, total_cross, tables, count_row, [], False)
     parts, dq = tie((parts, dq))
-    grad_memory, output, grad_residual, grad_mixed, *parts, sums_c = cross_back(
+    grad_memory, output, grad_residual, grad_mixed, *parts, more, sums_c = cross_back(
         devices, info, dq, dk, dv, wc, nc, source, residual, grad_cross_res, output, mixed_self, wo_self, norms, parts)
     parts = [parts[0]] + [plane_swap(parts[f], devices, f) for f in (1, 2, 3)]
     dq, dk, dv, grad_memory, output = attend_backward(
         steps, qt, k, kt, v, grad_mixed, mixed_self_t, total_self, tables, count_row, [grad_memory, output], True)
     parts, dq = tie((parts, dq))
+    more_first = more.shape[1]
     grad_query, grad_kv, last, more, norm_grads = self_back(
-        devices, ready_rows, info, dq, dk, dv, ws, nq, nkv, query, kv, grad_residual, norms, sums_c, sums_f, parts)
-
-    early, late = 3 * cols // unit_rows, 7 * cols // unit_rows
+        devices, ready_rows, info, dq, dk, dv, ws, nq, nkv, query, kv, grad_residual, norms, sums_c, sums_f, more, parts)
+
+    firsts = [count * cols // unit_rows for count in (3, 6, 7)]
     weight_grad, weight_first, weight_second, weight_new, grad_query, grad_kv = update(
-        devices, early, late, ready_rows, unit_owner, me.reshape(1), last, more, parts, master.reshape(shape),
+        devices, firsts, ready_rows, more_first, held, me.reshape(1), last, more, parts, master.reshape(shape),
         first_moment.reshape(shape), second_moment.reshape(shape), grad_query, grad_kv)
     weight_grad, weight_first, weight_second, weight_new = [
         part.reshape(master.shape) for part in (weight_grad, weight_first, weight_second, weight_new)]

time: 336 us -> 330 us (0.982)
  waiting for transfers between devices: 6.71 us -> 0.02 us
    ppermute x6, waiting for transfers between devices: 6.71 us -> 0.02 us  [plane_swap(): lax.ppermute(value, 'dp', [(i, i // 4 * 4 + (i % 4 ^ f)) for i in range(c...]
  transfers between devices with their start and end apart: 6 -> 6, of which waited for: 1 -> 0; matrix products, arithmetic and copies ran while one was open for 0% -> 0% of each run, Pallas kernels for 17% -> 17%
where the time goes in v8:
time: 330 us
  Pallas kernels  316 us (96%)
  starting transfers between devices  8.29 us (3%)
  local copies, waits for them, and re-layouts  3.84 us (1%)
    pallas_call x11, Pallas kernels, call(): pl.pallas_call(kernel, out_shape=tuple((jax.ShapeDtypeStruct(shape, dtype...  316 us
    ppermute x6, starting transfers between devices, plane_swap(): lax.ppermute(value, 'dp', [(i, i // 4 * 4 + (i % 4 ^ f)) for i in range(c...  8.29 us
  transfers between devices with their start and end apart: 6, of which 0 were waited for; matrix products, arithmetic and copies ran while one was open for 0% of the time, Pallas kernels for 17%

profile of v8, /device:TPU:0, one launch (start us, length us, event | category | flops | bytes accessed | tf_op | source)
XLA Modules:
  0.0 330.0 jit_solution(18403122695644298664)
XLA Ops:
  0.7 0.7 constant_dynamic-update-slice_fusion.norm_row
  1.4 0.0 copy-start.1
  1.4 2.2 plan.1
  3.6 0.0 copy-done.1
  3.6 82.4 %project.1 = (bf16[2048,512]{1,0:T(8,128)(2,1)}, bf16[2048,512]{1,0:T(8,128)(2,1)}, bf16[256,2048]{1,0:T(8,128)(2,1)}, bf16[2048,256]{1,0:T(8,128)(2,1)}, bf16[2...) custom-call(s32[1,256]{1,0:T(1,128)} %get-tuple-element.101.place_re, ...), custom_call_target="tpu_custom_call" | custom-call | flops 40000000000 | bytes 16777216 | tf_op jit(solution)/shard_map/project/pallas_call | solution.py:547
  86.0 17.3 %attend_self_forward.1 = (bf16[2048,256]{1,0:T(8,128)(2,1)}, bf16[256,2048]{1,0:T(8,128)(2,1)}, f32[8,2048]{1,0:T(8,128)}) custom-call(s32[2,40]{1,0:T(2,128)} %get-tuple-element.99.table, s32[1,2048]{1,0:T(1,128)} %get-tuple-element.100.count_ref, bf16[256,2048]{1,0:T(8,128)(2,1)} %get-tuple-element.104.qt_hbm, ...), custom_call_target="tpu_custom_call" | custom-call | flops 40000000000 | bytes 16777216 | tf_op jit(solution)/shard_map/attend_self_forward/pallas_call | solution.py:547
  103.4 8.4 %self_out.1 = (f32[2048,512]{1,0:T(8,128)}, bf16[2048,512]{1,0:T(8,128)(2,1)}, bf16[256,2048]{1,0:T(8,128)(2,1)}) custom-call(bf16[2048,256]{1,0:T(8,128)(2,1)} %get-tuple-element.111.mixed, bf16[256,512]{1,0:T(8,128)(2,1)} %get-tuple-element.112.wo, bf16[2048,512]{1,0:T(8,128)(2,1)} %get-tuple-element.113.query_hbm, ...), custom_call_target="tpu_custom_call" | custom-call | flops 40000000000 | bytes 16777216 | tf_op jit(solution)/shard_map/self_out/pallas_call | solution.py:547
  111.8 16.9 %attend_cross_forward.1 = (bf16[2048,256]{1,0:T(8,128)(2,1)}, bf16[256,2048]{1,0:T(8,128)(2,1)}, f32[8,2048]{1,0:T(8,128)}) custom-call(s32[2,40]{1,0:T(2,128)} %get-tuple-element.99.table, s32[1,2048]{1,0:T(1,128)} %get-tuple-element.100.count_ref, bf16[256,2048]{1,0:T(8,128)(2,1)} %get-tuple-element.116.qt_hbm, ...), custom_call_target="tpu_custom_call" | custom-call | flops 40000000000 | bytes 16777216 | tf_op jit(solution)/shard_map/attend_cross_forward/pallas_call | solution.py:547
  128.7 37.2 %feed_forward.1 = (bf16[2048,512]{1,0:T(8,128)(2,1)}, f32[2048,512]{1,0:T(8,128)}, bf16[256,2048]{1,0:T(8,128)(2,1)}, bf16[4,144,512]{2,1,0:T(8,128)(2,1)}, bf16...) custom-call(bf16[2048,256]{1,0:T(8,128)(2,1)} %get-tuple-element.119., ...), custom_call_target="tpu_custom_call" | custom-call | flops 40000000000 | bytes 16777216 | tf_op jit(solution)/shard_map/feed_forward/pallas_call | solution.py:547
  166.0 1.6 collective-permute-start
  167.6 1.7 collective-permute-start.1
  169.3 1.4 collective-permute-start.2
  170.7 27.7 %attend_cross_backward.1 = (bf16[2048,256]{1,0:T(8,128)(2,1)}, bf16[2048,256]{1,0:T(8,128)(2,1)}, bf16[2048,256]{1,0:T(8,128)(2,1)}) custom-call(s32[2,40]{1,0:T(2,128)} %get-tuple-element.99.table, s32[1,2048]{1,0:T(1,128)} %get-tuple-element.100.count_ref, f32[8,2048]{1,0:T(8,128)} %get-tuple-element.129.lse_ref, ...), custom_call_target="tpu_custom_call" | custom-call | flops 40000000000 | bytes 16777216 | tf_op jit(solution)/shard_map/attend_cross_backward/pallas_call | solution.py:547
  198.4 0.0 collective-permute-done.part1
  198.4 0.0 copy-start.7
  198.4 0.0 collective-permute-done.1.part2
  198.4 0.0 copy-start.8
  198.5 0.0 collective-permute-done.2.part3
  198.5 0.0 copy-start.9
  198.5 0.8 copy-done.7
  199.2 0.2 copy-done.8
  199.4 0.2 copy-done.9
  199.6 36.4 %cross_back.1 = (bf16[2048,512]{1,0:T(8,128)(2,1)}, bf16[2048,512]{1,0:T(8,128)(2,1)}, f32[2048,512]{1,0:T(8,128)}, bf16[256,2048]{1,0:T(8,128)(2,1)}, bf16[4,16...) custom-call(s32[1,34]{1,0:T(1,128)} %get-tuple-element.102.info, ...), custom_call_target="tpu_custom_call" | custom-call | flops 40000000000 | bytes 16777216 | tf_op jit(solution)/shard_map/cross_back/pallas_call | solution.py:547
  236.0 0.1 collective-permute-start.3
  236.2 2.0 collective-permute-start.4
  238.1 1.4 collective-permute-start.5
  239.6 29.3 %attend_self_backward.1 = (bf16[2048,256]{1,0:T(8,128)(2,1)}, bf16[2048,256]{1,0:T(8,128)(2,1)}, bf16[2048,256]{1,0:T(8,128)(2,1)}, bf16[2048,512]{1,0:T(8,128)(2,1)}, bf16[2048,512]{1,0:T(8,128)(2,1)}) custom-call(s32[2,40]{1,0:T(2,128)} %get-tuple-element.99.table, s32[1,2048]{1,0:T(1,128)} %get-tuple-element.100.count_ref, ...), custom_call_target="tpu_custom_call" | custom-call | flops 40000000000 | bytes 16777216 | tf_op jit(solution)/shard_map/attend_self_backward/pallas_call | solution.py:547
  268.9 0.0 collective-permute-done.3.part1.refs_3_
  268.9 0.0 copy-start.4
  268.9 0.0 collective-permute-done.4.part2.refs_4_
  268.9 0.0 copy-start.5
  268.9 0.0 collective-permute-done.5.part3.refs_5_
  268.9 0.0 copy-start.6
  268.9 0.8 copy-done.4
  269.7 0.2 copy-done.5
  269.9 0.2 copy-done.6
  270.2 0.0 copy-start
  270.2 0.0 copy-start.2
  270.2 0.0 copy-start.3
  270.2 49.6 %self_back.1 = (bf16[2048,512]{1,0:T(8,128)(2,1)}, bf16[2048,512]{1,0:T(8,128)(2,1)}, bf16[4,4,48,512]{3,2,1,0:T(8,128)(2,1)}, bf16[4,4,64,512]{3,2,1,0:T(8,128)(2,1)}, f32[8,512]{1,0:T(8,128)}) custom-call(s32[1,34]{1,0:T(1,128)} %get-tuple-element.102.info, bf16[2048,256]{1,0:T(8,128)(2,1)} %get-tuple-element.159.dq, ...), custom_call_target="tpu_custom_call" | custom-call | flops 40000000000 | bytes 16777216 | tf_op jit(solution)/shard_map/self_back/pallas_call | solution.py:547
  319.8 0.7 copy.30
  320.5 0.0 copy-done
  320.5 0.0 copy-done.2
  320.5 0.0 copy-done.3
  320.5 0.7 multiply_subtract_fusion
  321.2 8.6 %update.1 = (f32[32,16,512]{2,1,0:T(8,128)}, f32[32,16,512]{2,1,0:T(8,128)}, f32[32,16,512]{2,1,0:T(8,128)}, f32[32,16,512]{2,1,0:T(8,128)}, bf16[2048,512]{1,0:T(8,128)(2,1)}, /*index=5*/bf16[2048,512]{1,0:T(8,128)(2,1)}) custom-call(s32[1,128]{1,0:T(1,128)} %get-tuple-element.153.held, s32[1]{0:T(128)} %bitcast.1.me_ref, ...), custom_call_target="tpu_custom_call" | custom-call | flops 40000000000 | bytes 16777216 | tf_op jit(solution)/shard_map/update/pallas_call | solution.py:547
  (1 shorter events, 0.0 us)
Async XLA Ops:
  1.4 2.2 copy-start.1
  166.0 32.5 %collective-permute-start = (bf16[4,144,512]{2,1,0:T(8,128)(2,1)}, bf16[4,144,512]{2,1,0:T(8,128)(2,1)S(1)}, u32[]{:S(2)}, u32[]{:S(2)}) collective-permute-start(bf16[4,144,512]{2,1,0:T(8,128)(2,1)} %get-tuple-element.126), channel_id=1, source_target_pairs={{0,2},{2,0},{4,6},{6,4},{8,10},{10,8},{12,14},{14,12},{16,18},{18,... | collective-permute-start | bytes 1769480 | tf_op jit(solution)/shard_map/ppermute | solution.py:536
  167.6 30.9 %collective-permute-start.1 = (bf16[4,144,512]{2,1,0:T(8,128)(2,1)}, bf16[4,144,512]{2,1,0:T(8,128)(2,1)S(1)}, u32[]{:S(2)}, u32[]{:S(2)}) collective-permute-start(bf16[4,144,512]{2,1,0:T(8,128)(2,1)} %get-tuple-element.127), channel_id=1, source_target_pairs={{0,4},{2,6},{4,0},{6,2},{8,12},{10,14},{12,8},{14,10},{16,20},{18,... | collective-permute-start | bytes 1769480 | tf_op jit(solution)/shard_map/ppermute | solution.py:536
  169.3 29.2 %collective-permute-start.2 = (bf16[4,144,512]{2,1,0:T(8,128)(2,1)}, bf16[4,144,512]{2,1,0:T(8,128)(2,1)S(1)}, u32[]{:S(2)}, u32[]{:S(2)}) collective-permute-start(bf16[4,144,512]{2,1,0:T(8,128)(2,1)} %get-tuple-element.128), channel_id=1, source_target_pairs={{0,6},{2,4},{4,2},{6,0},{8,14},{10,12},{12,10},{14,8},{16,22},{18,... | collective-permute-start | bytes 1769480 | tf_op jit(solution)/shard_map/ppermute | solution.py:536
  198.4 0.8 copy-start.7
  198.4 1.0 copy-start.8
  198.5 1.2 copy-start.9
  236.0 32.8 %collective-permute-start.3 = (bf16[4,160,512]{2,1,0:T(8,128)(2,1)}, bf16[4,160,512]{2,1,0:T(8,128)(2,1)S(1)}, u32[]{:S(2)}, u32[]{:S(2)}) collective-permute-start(bf16[4,160,512]{2,1,0:T(8,128)(2,1)} %get-tuple-element.155), channel_id=1, source_target_pairs={{0,2},{2,0},{4,6},{6,4},{8,10},{10,8},{12,14},{14,12},{16,18},{18,... | collective-permute-start | bytes 1966088 | tf_op jit(solution)/shard_map/ppermute | solution.py:536
  236.2 32.7 %collective-permute-start.4 = (bf16[4,160,512]{2,1,0:T(8,128)(2,1)}, bf16[4,160,512]{2,1,0:T(8,128)(2,1)S(1)}, u32[]{:S(2)}, u32[]{:S(2)}) collective-permute-start(bf16[4,160,512]{2,1,0:T(8,128)(2,1)} %get-tuple-element.156), channel_id=1, source_target_pairs={{0,4},{2,6},{4,0},{6,2},{8,12},{10,14},{12,8},{14,10},{16,20},{18,... | collective-permute-start | bytes 1966088 | tf_op jit(solution)/shard_map/ppermute | solution.py:536
  238.1 30.8 %collective-permute-start.5 = (bf16[4,160,512]{2,1,0:T(8,128)(2,1)}, bf16[4,160,512]{2,1,0:T(8,128)(2,1)S(1)}, u32[]{:S(2)}, u32[]{:S(2)}) collective-permute-start(bf16[4,160,512]{2,1,0:T(8,128)(2,1)} %get-tuple-element.157), channel_id=1, source_target_pairs={{0,6},{2,4},{4,2},{6,0},{8,14},{10,12},{12,10},{14,8},{16,22},{18,... | collective-permute-start | bytes 1966088 | tf_op jit(solution)/shard_map/ppermute | solution.py:536
  268.9 0.8 copy-start.4
  268.9 1.0 copy-start.5
  268.9 1.3 copy-start.6
  270.2 50.3 %copy-start = (f32[256]{0:T(256)S(1)}, f32[256]{0:T(256)}, u32[]{:S(2)}) copy-start(f32[256]{0:T(256)} %param.25) | copy-start | bytes 3076
  270.2 50.3 %copy-start.2 = (f32[256]{0:T(256)S(1)}, f32[256]{0:T(256)}, u32[]{:S(2)}) copy-start(f32[256]{0:T(256)} %param.27) | copy-start | bytes 3076
  270.2 50.3 %copy-start.3 = (f32[256]{0:T(256)S(1)}, f32[256]{0:T(256)}, u32[]{:S(2)}) copy-start(f32[256]{0:T(256)} %param.26) | copy-start | bytes 3076

commit v9 on v8

--- a/solution.py
+++ b/solution.py
@@ -486,8 +486,8 @@
 
 
 class Spread:
-    def __init__(self, places, out, zs, xs, ys, gx, gy):
-        self.places, self.out, self.sems = places, out, dict(z=zs, x=xs, y=ys, gx=gx, gy=gy)
+    def __init__(self, places, out, zs, xs, ys, gx, gy, direct=False):
+        self.places, self.out, self.sems, self.direct = places, out, dict(z=zs, x=xs, y=ys, gx=gx, gy=gy), direct
         self.rows = out.shape[2]
         self.half = self.rows // 2 // UNIT * UNIT
         self.copies = {}
@@ -501,6 +501,9 @@
         xpeer, ypeer = self.places[4], self.places[5]
         self.go("x", d, 0, d, 1, d, xpeer, 0, self.rows)
         self.go("y", d, 0, d, 2, d, ypeer, 0, self.rows)
+        if self.direct:
+            me, x, y = self.places[:3]
+            self.go("gx", d, 0, d, 3, d, me + 3 - 2 * x - 4 * y, 0, self.rows)
 
     def start(self):
         order, ahead = self.places[6], self.places[7]
@@ -517,10 +520,11 @@
         xpeer, ypeer, order = self.places[4:7]
         for d in [0] + order:
             self.copies["x", d].wait_recv()
-            if self.half:
+            if self.half and not self.direct:
                 self.go("gy", d, 1, d, 3, d, ypeer, 0, self.half)
             self.copies["y", d].wait_recv()
-            self.go("gx", d, 2, d, 3, d, xpeer, self.half, self.rows - self.half)
+            if not self.direct:
+                self.go("gx", d, 2, d, 3, d, xpeer, self.half, self.rows - self.half)
 
     def finish(self):
         for (name, d), copy in self.copies.items():
@@ -897,15 +901,15 @@
             ref[level, ref.shape[1] - rows:, :] = flat[pl.ds(pl.multiple_of((level * 4 + place) * rows, UNIT), rows), :]
 
 
-def feed_forward_kernel(devices, mixed, wo, res_hbm, w1, w2, out_grad_hbm, norms,
+def feed_forward_kernel(devices, mixed, wo, res_hbm, w1_hbm, w2_hbm, out_grad_hbm, norms,
                         out_out, gres_out, gmix_out, part0, part1, part2, part3, sums_ref,
-                        res, out_grad, out_ref, gres_ref, gmix_ref, flat,
+                        w1, w2, res, out_grad, out_ref, gres_ref, gmix_ref, flat,
                         mine, theirs, nf_all, hid_all, pre_all, low_all, mine_o, theirs_o, mine_g, theirs_g,
                         sems, sems_o, sems_g, late_sems, out_sems):
     tokens, features = out_grad.shape
     hidden = w2.shape[0]
     places = places_of(devices)
-    late = Late([(res_hbm, res), (out_grad_hbm, out_grad)], late_sems)
+    late = Late([(res_hbm, res), (out_grad_hbm, out_grad), (w1_hbm, w1), (w2_hbm, w2)], late_sems)
     out = Out([(out_ref, out_out), (gres_ref, gres_out), (gmix_ref, gmix_out)], out_sems)
     greet_core()
 
@@ -913,7 +917,7 @@
         mine[rows, :] = nn(mixed[rows, :], wo[...]).astype(BF)
         other_core(mine, theirs, sems, step).start()
     chunks(tokens, give)
-    late.wait(0, 1)
+    late.wait(0, 1, 2, 3)
 
     def middle(step, rows):
         other_core(mine, theirs, sems, step).wait_recv()
@@ -991,10 +995,10 @@
     across = (mixed.shape[1], tokens)
     outs = [(wide, BF, "A"), (wide, F32, "A"), (across, BF, "A")] + [part] * 4 + [((16, features), F32, "V")]
     deep, narrow = pltpu.VMEM((tokens, hidden), BF), pltpu.VMEM(wide, BF)
-    scratch = [pltpu.VMEM(wide, F32), narrow, narrow, pltpu.VMEM(wide, F32), pltpu.VMEM(across, BF),
+    scratch = [pltpu.VMEM(w1.shape, BF), pltpu.VMEM(w2.shape, BF), pltpu.VMEM(wide, F32), narrow, narrow, pltpu.VMEM(wide, F32), pltpu.VMEM(across, BF),
                pltpu.VMEM((flat_rows, features), BF), narrow, narrow, narrow, deep, deep, narrow] + [narrow] * 4
-    scratch += [pair_sems(tokens)] * 3 + [pltpu.SemaphoreType.DMA((2,)), out_semaphores(3, tokens)]
-    return call(partial(feed_forward_kernel, devices), "feed_forward", [mixed, wo, res, w1, w2, out_grad, norms], "VVAVVAV",
+    scratch += [pair_sems(tokens)] * 3 + [pltpu.SemaphoreType.DMA((4,)), out_semaphores(3, tokens)]
+    return call(partial(feed_forward_kernel, devices), "feed_forward", [mixed, wo, res, w1, w2, out_grad, norms], "VVAAAAV",
                 outs, scratch, 3)
 
 
@@ -1041,23 +1045,25 @@
     return (parts[0][at].astype(F32) + parts[1][at].astype(F32) + parts[2][at].astype(F32) + parts[3][at].astype(F32)).astype(BF)
 
 
-def cross_back_kernel(devices, info, dq, dk, dv, wc, nc_hbm, memory_hbm, res_hbm, gres_hbm, output_hbm, mixed, wo, norms,
+def cross_back_kernel(devices, info, dq_hbm, dk_hbm, dv_hbm, wc_hbm, nc_hbm, memory_hbm, res_hbm, gres_hbm, output_hbm, mixed_hbm, wo, norms,
                       part0, part1, part2, part3,
                       gmem_out, output_out, gnew_out, gmix_out, give0, give1, give2, give3, more_ref, sums_ref,
-                      nc, memory, res, gres, output_ref, gmem_ref, turned_a, turned_b, gmix_ref, flat, flat_o, source, landing, pieces, landed, blocks,
+                      dq, dk, dv, wc, mixed, nc, memory, res, gres, output_ref, gmem_ref, turned_a, turned_b, gmix_ref, flat, flat_o, source, landing, pieces, landed, blocks,
                       mine_a, theirs_a, mine_b, theirs_b, low_all, sems_a, sems_b, late_sems, out_sems, turned_sems, z_sems, zz_sems, plane_sems):
     tokens, features = nc.shape
     cols = dq.shape[1]
     across = devices // 4
     places = places_of(devices)
     me, x, y, z, xpeer, ypeer, order, ahead, behind = places
-    late = Late([(nc_hbm, nc), (memory_hbm, memory), (res_hbm, res), (gres_hbm, gres), (output_hbm, output_ref)], late_sems)
+    late = Late([(nc_hbm, nc), (memory_hbm, memory), (res_hbm, res), (gres_hbm, gres), (output_hbm, output_ref), (dq_hbm, dq),
+                 (wc_hbm, wc), (dk_hbm, dk), (dv_hbm, dv), (mixed_hbm, mixed)], late_sems)
     out = Out([(gres, gnew_out), (gmix_ref, gmix_out)], out_sems)
     for level in range(across):
         pieces[level] = four_sum((part0, part1, part2, part3), level)
     greet([{"head": 1 - lax.axis_index("head")}] + [{"dp": ahead(d)} for d in order]
           + [{"dp": peer} for peer in (xpeer, ypeer, me + 3 - 2 * x - 4 * y)])
     z_copies = z_sum_start(devices, places, pieces, landed, z_sems)
+    late.wait(5, 6, 7, 8)
     branch_give(dq, dk, dv, wc, mine_a, theirs_a, mine_b, theirs_b, sems_a, sems_b)
     late.wait(0, 1)
     branch_weights(nc, memory, dq, dk, dv, flat)
@@ -1084,6 +1090,7 @@
         total = (mine_b[rows, :].astype(F32) + theirs_b[rows, :].astype(F32)).astype(BF)
         gmem_ref[pl.ds(step * (CHUNK // UNIT), CHUNK // UNIT)] = in_tiles(total)
     chunks(tokens, close)
+    late.wait(9)
     flat_o[0:cols, :] = tn(mixed[...], low_all[...]).astype(BF)
     if flat_o.shape[0] > cols:
         flat_o[cols:, :] = jnp.zeros((flat_o.shape[0] - cols, features), BF)
@@ -1125,12 +1132,13 @@
     small = pltpu.VMEM((across, ready_rows, features), BF)
     z_sems = pltpu.SemaphoreType.DMA((2, across))
     tiles = pltpu.VMEM((tokens // UNIT, UNIT, features), BF)
-    scratch = [low, low, high, high, tiles, tiles, low, low, pltpu.VMEM((cols, tokens), BF), pltpu.VMEM((flat_rows, features), BF),
+    scratch = [pltpu.VMEM(arg.shape, BF) for arg in (dq, dk, dv, wc, mixed)]
+    scratch += [low, low, high, high, tiles, tiles, low, low, pltpu.VMEM((cols, tokens), BF), pltpu.VMEM((flat_rows, features), BF),
                pltpu.VMEM((o_rows, features), BF), pltpu.VMEM((4,) + part, BF), pltpu.VMEM((4,) + part, BF), small, small, small]
-    scratch += [low] * 5 + [pair_sems(tokens)] * 2 + [pltpu.SemaphoreType.DMA((5,)), out_semaphores(2, tokens), pltpu.SemaphoreType.DMA((2,)), z_sems, z_sems,
+    scratch += [low] * 5 + [pair_sems(tokens)] * 2 + [pltpu.SemaphoreType.DMA((10,)), out_semaphores(2, tokens), pltpu.SemaphoreType.DMA((2,)), z_sems, z_sems,
                                                  pltpu.SemaphoreType.DMA((2, 4))]
     return call(partial(cross_back_kernel, devices), "cross_back",
-                [info, dq, dk, dv, wc, nc, memory, res, gres, in_tiles(output), mixed, wo, norms] + parts, "SVVVVAAAAAVVVVVVV", outs, scratch, 4)
+                [info, dq, dk, dv, wc, nc, memory, res, gres, in_tiles(output), mixed, wo, norms] + parts, "SAAAAAAAAAAVVVVVV", outs, scratch, 4)
 
 
 def self_back_kernel(devices, ready_rows, info, dq, dk, dv, ws, nq_hbm, nkv_hbm, query_hbm, kv_hbm, gres_hbm, norms, sums_c, sums_f, more_in,
@@ -1195,7 +1203,7 @@
     turn_rows(gquery_ref, turned_a, info[0, DOCS + 1])
     more.diagonal()
     last_ref[0, 0] = z_sum_end(places, pieces, landed, z_copies)
-    last = Spread(places, last_ref, *spread_sems[5:])
+    last = Spread(places, last_ref, *spread_sems[5:], direct=True)
     last.start()
     turn_rows(gkv_ref, turned_b, info[0, DOCS + 1])
     turned = Late([(turned_a, gquery_out), (turned_b, gkv_out)], out_sems)
@@ -1242,10 +1250,23 @@
 
 
 def update_kernel(devices, firsts, late_rows, more_first, held, me_ref, *refs):
-    hbm, (grad_out, first_out, second_out, new_out, gquery_out, gkv_out) = refs[:11], refs[11:17]
-    last, more, part0, part1, part2, part3, master, first, second, held_q, held_kv = refs[17:28]
-    taken, grad_ref, first_ref, second_ref, new_ref, sems, out_sems = refs[28:]
-    entering = Late(list(zip(hbm, refs[17:28])), sems)
+    norm_grads, *norm_in = refs[:4]
+    hbm, (grad_out, first_out, second_out, new_out, gquery_out, gkv_out) = refs[4:15], refs[15:21]
+    norm_out, vmem = refs[21:25], refs[25:36]
+    last, more, part0, part1, part2, part3, master, first, second, held_q, held_kv = vmem
+    taken, grad_ref, first_ref, second_ref, new_ref, sems, out_sems = refs[36:]
+    entering = Late(list(zip(hbm, vmem)), sems)
+    share = norm_in[0].shape[1]
+    if share % 128 == 0:
+        at = me_ref[0] * share
+        features = norm_grads.shape[1]
+        norm_grad = norm_grads[pl.ds(lax.div(at, features), 1), pl.ds(pl.multiple_of(lax.rem(at, features), 128), share)]
+        norm_values = (norm_grad,) + adamw_step(norm_grad, *(ref[...] for ref in norm_in), RATE_NORM, 0.0)
+        for ref, value in zip(norm_out, norm_values):
+            ref[...] = value
+    else:
+        for ref in norm_out:
+            ref[...] = jnp.zeros_like(ref)
     slots = master.shape[0]
     across = devices // 4
     me = me_ref[0]
@@ -1307,12 +1328,12 @@
     leaving.wait(0, 1)
 
 
-def update(devices, firsts, late_rows, more_first, held, me, last, more, parts, master, first, second, gquery, gkv):
-    outs = [(master.shape, F32, "A")] * 4 + [(gquery.shape, BF, "A")] * 2
+def update(devices, firsts, late_rows, more_first, held, me, norm_args, last, more, parts, master, first, second, gquery, gkv):
+    outs = [(master.shape, F32, "A")] * 4 + [(gquery.shape, BF, "A")] * 2 + [(norm_args[1].shape, F32, "V")] * 4
     args = [last, more] + parts + [master, first, second, gquery, gkv]
     scratch = [pltpu.VMEM(arg.shape, arg.dtype) for arg in args] + [pltpu.VMEM((UNIT, master.shape[2]), BF)]
     scratch += [pltpu.VMEM(master.shape, F32)] * 4 + [pltpu.SemaphoreType.DMA((11,)), pltpu.SemaphoreType.DMA((3, 4))]
-    return call(partial(update_kernel, devices, firsts, late_rows, more_first), "update", [held, me] + args, "SS" + "A" * 11,
+    return call(partial(update_kernel, devices, firsts, late_rows, more_first), "update", [held, me] + norm_args + args, "SSVVVV" + "A" * 11,
                 outs, scratch)
 
 
@@ -1366,14 +1387,18 @@
         devices, ready_rows, info, dq, dk, dv, ws, nq, nkv, query, kv, grad_residual, norms, sums_c, sums_f, more, parts)
 
     firsts = [count * cols // unit_rows for count in (3, 6, 7)]
-    weight_grad, weight_first, weight_second, weight_new, grad_query, grad_kv = update(
-        devices, firsts, ready_rows, more_first, held, me.reshape(1), last, more, parts, master.reshape(shape),
+    norm_args = [norm_grads] + [value.reshape(1, norm_share) for value in (norm_first, norm_second, norm_master)]
+    weight_grad, weight_first, weight_second, weight_new, grad_query, grad_kv, *norm_results = update(
+        devices, firsts, ready_rows, more_first, held, me.reshape(1), norm_args, last, more, parts, master.reshape(shape),
         first_moment.reshape(shape), second_moment.reshape(shape), grad_query, grad_kv)
     weight_grad, weight_first, weight_second, weight_new = [
         part.reshape(master.shape) for part in (weight_grad, weight_first, weight_second, weight_new)]
-    norm_grad = lax.dynamic_slice_in_dim(norm_grads.reshape(-1), me * norm_share, norm_share)
-    norm_first_new, norm_second_new, norm_new = adamw_step(
-        norm_grad, norm_first, norm_second, norm_master, RATE_NORM, 0.0)
+    if norm_share % 128 == 0:
+        norm_grad, norm_first_new, norm_second_new, norm_new = [value.reshape(norm_share) for value in norm_results]
+    else:
+        norm_grad = lax.dynamic_slice_in_dim(norm_grads.reshape(-1), me * norm_share, norm_share)
+        norm_first_new, norm_second_new, norm_new = adamw_step(
+            norm_grad, norm_first, norm_second, norm_master, RATE_NORM, 0.0)
     return (
         output, grad_query, grad_kv, grad_memory, weight_grad, weight_first, weight_second, weight_new,
         norm_grad, norm_first_new, norm_second_new, norm_new,

time: 330 us -> 328 us (level)
  no operation moved by 1% of the time
where the time goes in v9:
time: 328 us
  Pallas kernels  315 us (96%)
  starting transfers between devices  8.35 us (3%)
    pallas_call x11, Pallas kernels, call(): pl.pallas_call(kernel, out_shape=tuple((jax.ShapeDtypeStruct(shape, dtype...  315 us
    ppermute x6, starting transfers between devices, plane_swap(): lax.ppermute(value, 'dp', [(i, i // 4 * 4 + (i % 4 ^ f)) for i in range(c...  8.35 us
  transfers between devices with their start and end apart: 6, of which 0 were waited for; matrix products, arithmetic and copies ran while one was open for 0% of the time, Pallas kernels for 17%

profile of v9, /device:TPU:0, one launch (start us, length us, event | category | flops | bytes accessed | tf_op | source)
XLA Modules:
  0.0 327.6 jit_solution(6638739814900722448)
XLA Ops:
  0.7 0.7 constant_dynamic-update-slice_fusion.norm_row
  1.4 0.0 copy-start
  1.4 2.2 plan.1
  3.6 0.0 copy-done
  3.6 82.4 %project.1 = (bf16[2048,512]{1,0:T(8,128)(2,1)}, bf16[2048,512]{1,0:T(8,128)(2,1)}, bf16[256,2048]{1,0:T(8,128)(2,1)}, bf16[2048,256]{1,0:T(8,128)(2,1)}, bf16[2...) custom-call(s32[1,256]{1,0:T(1,128)} %get-tuple-element.105.place_re, ...), custom_call_target="tpu_custom_call" | custom-call | flops 40000000000 | bytes 16777216 | tf_op jit(solution)/shard_map/project/pallas_call | solution.py:551
  86.0 17.3 %attend_self_forward.1 = (bf16[2048,256]{1,0:T(8,128)(2,1)}, bf16[256,2048]{1,0:T(8,128)(2,1)}, f32[8,2048]{1,0:T(8,128)}) custom-call(s32[2,40]{1,0:T(2,128)} %get-tuple-element.103.table, s32[1,2048]{1,0:T(1,128)} %get-tuple-element.104.count_ref, bf16[256,2048]{1,0:T(8,128)(2,1)} %get-tuple-element.108.qt_hbm, ...), custom_call_target="tpu_custom_call" | custom-call | flops 40000000000 | bytes 16777216 | tf_op jit(solution)/shard_map/attend_self_forward/pallas_call | solution.py:551
  103.4 8.4 %self_out.1 = (f32[2048,512]{1,0:T(8,128)}, bf16[2048,512]{1,0:T(8,128)(2,1)}, bf16[256,2048]{1,0:T(8,128)(2,1)}) custom-call(bf16[2048,256]{1,0:T(8,128)(2,1)} %get-tuple-element.115.mixed.mixed_hbm, bf16[256,512]{1,0:T(8,128)(2,1)} %get-tuple-element.116.wo, bf16[2048,512]{1,0:T(8,128)(2,1)} %get-tuple-element.117.query_hbm, ...), custom_call_target="tpu_custom_call" | custom-call | flops 40000000000 | bytes 16777216 | tf_op jit(solution)/shard_map/self_out/pallas_call | solution.py:551
  111.8 16.9 %attend_cross_forward.1 = (bf16[2048,256]{1,0:T(8,128)(2,1)}, bf16[256,2048]{1,0:T(8,128)(2,1)}, f32[8,2048]{1,0:T(8,128)}) custom-call(s32[2,40]{1,0:T(2,128)} %get-tuple-element.103.table, s32[1,2048]{1,0:T(1,128)} %get-tuple-element.104.count_ref, bf16[256,2048]{1,0:T(8,128)(2,1)} %get-tuple-element.120.qt_hbm, ...), custom_call_target="tpu_custom_call" | custom-call | flops 40000000000 | bytes 16777216 | tf_op jit(solution)/shard_map/attend_cross_forward/pallas_call | solution.py:551
  128.7 37.2 %feed_forward.1 = (bf16[2048,512]{1,0:T(8,128)(2,1)}, f32[2048,512]{1,0:T(8,128)}, bf16[256,2048]{1,0:T(8,128)(2,1)}, bf16[4,144,512]{2,1,0:T(8,128)(2,1)}, bf16...) custom-call(bf16[2048,256]{1,0:T(8,128)(2,1)} %get-tuple-element.123., ...), custom_call_target="tpu_custom_call" | custom-call | flops 40000000000 | bytes 16777216 | tf_op jit(solution)/shard_map/feed_forward/pallas_call | solution.py:551
  165.9 3.3 collective-permute-start
  169.1 0.0 collective-permute-start.1
  169.2 1.5 collective-permute-start.2
  170.7 27.7 %attend_cross_backward.1 = (bf16[2048,256]{1,0:T(8,128)(2,1)}, bf16[2048,256]{1,0:T(8,128)(2,1)}, bf16[2048,256]{1,0:T(8,128)(2,1)}) custom-call(s32[2,40]{1,0:T(2,128)} %get-tuple-element.103.table, s32[1,2048]{1,0:T(1,128)} %get-tuple-element.104.count_ref, f32[8,2048]{1,0:T(8,128)} %get-tuple-element.133.lse_ref, ...), custom_call_target="tpu_custom_call" | custom-call | flops 40000000000 | bytes 16777216 | tf_op jit(solution)/shard_map/attend_cross_backward/pallas_call | solution.py:551
  198.4 0.0 collective-permute-done.part1
  198.4 0.0 copy-start.4
  198.4 0.0 collective-permute-done.1.part2
  198.4 0.0 copy-start.5
  198.5 0.0 collective-permute-done.2.part3
  198.5 0.0 copy-start.6
  198.5 0.8 copy-done.4
  199.2 0.2 copy-done.5
  199.4 0.2 copy-done.6
  199.6 37.3 %cross_back.1 = (bf16[2048,512]{1,0:T(8,128)(2,1)}, bf16[2048,512]{1,0:T(8,128)(2,1)}, f32[2048,512]{1,0:T(8,128)}, bf16[256,2048]{1,0:T(8,128)(2,1)}, bf16[4,16...) custom-call(s32[1,34]{1,0:T(1,128)} %get-tuple-element.106.info, ...), custom_call_target="tpu_custom_call" | custom-call | flops 40000000000 | bytes 16777216 | tf_op jit(solution)/shard_map/cross_back/pallas_call | solution.py:551
  236.9 0.1 collective-permute-start.3
  237.0 0.3 collective-permute-start.4
  237.3 3.2 collective-permute-start.5
  240.4 29.3 %attend_self_backward.1 = (bf16[2048,256]{1,0:T(8,128)(2,1)}, bf16[2048,256]{1,0:T(8,128)(2,1)}, bf16[2048,256]{1,0:T(8,128)(2,1)}, bf16[2048,512]{1,0:T(8,128)(2,1)}, bf16[2048,512]{1,0:T(8,128)(2,1)}) custom-call(s32[2,40]{1,0:T(2,128)} %get-tuple-element.103.table, s32[1,2048]{1,0:T(1,128)} %get-tuple-element.104.count_ref, ...), custom_call_target="tpu_custom_call" | custom-call | flops 40000000000 | bytes 16777216 | tf_op jit(solution)/shard_map/attend_self_backward/pallas_call | solution.py:551
  269.7 0.0 collective-permute-done.3.part1.refs_7_
  269.7 0.0 copy-start.1
  269.7 0.0 collective-permute-done.4.part2.refs_8_
  269.8 0.0 copy-start.2
  269.8 0.0 collective-permute-done.5.part3.refs_9_
  269.8 0.0 copy-start.3
  269.8 0.8 copy-done.1
  270.6 0.2 copy-done.2
  270.8 0.2 copy-done.3
  271.0 47.0 %self_back.1 = (bf16[2048,512]{1,0:T(8,128)(2,1)}, bf16[2048,512]{1,0:T(8,128)(2,1)}, bf16[4,4,48,512]{3,2,1,0:T(8,128)(2,1)}, bf16[4,4,64,512]{3,2,1,0:T(8,128)(2,1)}, f32[8,512]{1,0:T(8,128)}) custom-call(s32[1,34]{1,0:T(1,128)} %get-tuple-element.106.info, bf16[2048,256]{1,0:T(8,128)(2,1)} %get-tuple-element.163.dq, ...), custom_call_target="tpu_custom_call" | custom-call | flops 40000000000 | bytes 16777216 | tf_op jit(solution)/shard_map/self_back/pallas_call | solution.py:551
  318.0 9.3 %update.1 = (f32[32,16,512]{2,1,0:T(8,128)}, f32[32,16,512]{2,1,0:T(8,128)}, f32[32,16,512]{2,1,0:T(8,128)}, f32[32,16,512]{2,1,0:T(8,128)}, bf16[2048,512]{1,0:...) custom-call(s32[1,128]{1,0:T(1,128)} %get-tuple-element.157.held, ...), custom_call_target="tpu_custom_call" | custom-call | flops 40000000000 | bytes 16777216 | tf_op jit(solution)/shard_map/update/pallas_call | solution.py:551
  (1 shorter events, 0.0 us)
Async XLA Ops:
  1.4 2.2 copy-start
  165.9 32.5 %collective-permute-start = (bf16[4,144,512]{2,1,0:T(8,128)(2,1)}, bf16[4,144,512]{2,1,0:T(8,128)(2,1)S(1)}, u32[]{:S(2)}, u32[]{:S(2)}) collective-permute-start(bf16[4,144,512]{2,1,0:T(8,128)(2,1)} %get-tuple-element.130), channel_id=1, source_target_pairs={{0,2},{2,0},{4,6},{6,4},{8,10},{10,8},{12,14},{14,12},{16,18},{18,... | collective-permute-start | bytes 1769480 | tf_op jit(solution)/shard_map/ppermute | solution.py:540
  169.1 29.3 %collective-permute-start.1 = (bf16[4,144,512]{2,1,0:T(8,128)(2,1)}, bf16[4,144,512]{2,1,0:T(8,128)(2,1)S(1)}, u32[]{:S(2)}, u32[]{:S(2)}) collective-permute-start(bf16[4,144,512]{2,1,0:T(8,128)(2,1)} %get-tuple-element.131), channel_id=1, source_target_pairs={{0,4},{2,6},{4,0},{6,2},{8,12},{10,14},{12,8},{14,10},{16,20},{18,... | collective-permute-start | bytes 1769480 | tf_op jit(solution)/shard_map/ppermute | solution.py:540
  169.2 29.3 %collective-permute-start.2 = (bf16[4,144,512]{2,1,0:T(8,128)(2,1)}, bf16[4,144,512]{2,1,0:T(8,128)(2,1)S(1)}, u32[]{:S(2)}, u32[]{:S(2)}) collective-permute-start(bf16[4,144,512]{2,1,0:T(8,128)(2,1)} %get-tuple-element.132), channel_id=1, source_target_pairs={{0,6},{2,4},{4,2},{6,0},{8,14},{10,12},{12,10},{14,8},{16,22},{18,... | collective-permute-start | bytes 1769480 | tf_op jit(solution)/shard_map/ppermute | solution.py:540
  198.4 0.8 copy-start.4
  198.4 1.0 copy-start.5
  198.5 1.2 copy-start.6
  236.9 32.8 %collective-permute-start.3 = (bf16[4,160,512]{2,1,0:T(8,128)(2,1)}, bf16[4,160,512]{2,1,0:T(8,128)(2,1)S(1)}, u32[]{:S(2)}, u32[]{:S(2)}) collective-permute-start(bf16[4,160,512]{2,1,0:T(8,128)(2,1)} %get-tuple-element.159), channel_id=1, source_target_pairs={{0,2},{2,0},{4,6},{6,4},{8,10},{10,8},{12,14},{14,12},{16,18},{18,... | collective-permute-start | bytes 1966088 | tf_op jit(solution)/shard_map/ppermute | solution.py:540
  237.0 32.8 %collective-permute-start.4 = (bf16[4,160,512]{2,1,0:T(8,128)(2,1)}, bf16[4,160,512]{2,1,0:T(8,128)(2,1)S(1)}, u32[]{:S(2)}, u32[]{:S(2)}) collective-permute-start(bf16[4,160,512]{2,1,0:T(8,128)(2,1)} %get-tuple-element.160), channel_id=1, source_target_pairs={{0,4},{2,6},{4,0},{6,2},{8,12},{10,14},{12,8},{14,10},{16,20},{18,... | collective-permute-start | bytes 1966088 | tf_op jit(solution)/shard_map/ppermute | solution.py:540
  237.3 32.5 %collective-permute-start.5 = (bf16[4,160,512]{2,1,0:T(8,128)(2,1)}, bf16[4,160,512]{2,1,0:T(8,128)(2,1)S(1)}, u32[]{:S(2)}, u32[]{:S(2)}) collective-permute-start(bf16[4,160,512]{2,1,0:T(8,128)(2,1)} %get-tuple-element.161), channel_id=1, source_target_pairs={{0,6},{2,4},{4,2},{6,0},{8,14},{10,12},{12,10},{14,8},{16,22},{18,... | collective-permute-start | bytes 1966088 | tf_op jit(solution)/shard_map/ppermute | solution.py:540
  269.7 0.8 copy-start.1
  269.8 1.0 copy-start.2
  269.8 1.2 copy-start.3

commit v10 on v9

--- a/solution.py
+++ b/solution.py
@@ -458,12 +458,12 @@
 
             @pl.when(k > 1)
             def _():
-                for side in (0, 1):
+                for side in (1, 0):
                     pl.when(self.here(side, k - 1))(lambda: later(side, k - 1))
             pl.when(k == 2)(at_second)
             return carry
         lax.fori_loop(1, self.across, level, 0)
-        for side in (0, 1):
+        for side in (1, 0):
             pl.when(self.here(side, self.across - 1))(lambda: later(side, self.across - 1))
 
         def settle(k, carry):
@@ -671,7 +671,7 @@
     lane = lax.broadcasted_iota(jnp.int32, (units, 128), 1)
     unit = lax.broadcasted_iota(jnp.int32, (units, 128), 0).astype(F32)
     mine = jnp.where(place_cols == me * block + lane.astype(F32), unit, 0.0)
-    mine = jnp.where(lane == 127, jnp.where(owner_cols[:, :128] == me, 1.0, 0.0), jnp.where(lane < block - 1, mine, 0.0))
+    mine = jnp.where(lane == 127, jnp.where(owner_cols[:, :128] == me, 1.0, 0.0), jnp.where(lane < block, mine, 0.0))
     held_ref[...] = jnp.sum(mine, 0, keepdims=True).astype(jnp.int32)
     longest, first, at, start = jnp.int32(0), jnp.int32(0), jnp.int32(0), jnp.int32(0)
     for d in range(DOCS):
@@ -719,9 +719,9 @@
                    nq_out, nkv_out, qt_out, k_out, kt_out, v_out, vt_out, kc_out, kct_out, vc_out, vct_out,
                    query_out, kv_out, memory_out, grad_out,
                    ws_ref, wc_ref, wos_ref, woc_ref, w1_ref, w2_ref, norms, side_ref, hot_ref, rank_cols,
-                   gathered, flat, stage_a, stage_b, query_ref, kv_ref, memory_ref, grad_ref, unit_q, unit_kv,
+                   gathered, norm_all, flat, stage_a, stage_b, query_ref, kv_ref, memory_ref, grad_ref, unit_q, unit_kv,
                    nq_ref, nkv_ref, qt_ref, k_ref, kt_ref, v_ref, vt_ref, kc_ref, kct_ref, vc_ref, vct_ref,
-                   late_sems, turned_sems, out_sems, *line_sems):
+                   late_sems, turned_sems, out_sems, norm_sems, *line_sems):
     tokens, features = query_ref.shape
     units = place_ref.shape[1]
     late = Late([(query_hbm, stage_a), (kv_hbm, stage_b)], late_sems.at[0])
@@ -729,11 +729,13 @@
     out = Out(list(zip(held, (nq_out, nkv_out, qt_out, k_out, kt_out, v_out, vt_out, kc_out, kct_out, vc_out, vct_out))), out_sems)
     places = places_of(devices)
     me, x, y, z, xpeer, ypeer, order, ahead, behind = places
-    slots = master.shape[0]
-    block = slots + 1
-    gathered[pl.ds(me * block, slots)] = master[...].astype(BF)
-    gathered[me * block + slots] = jnp.broadcast_to(norm_row[...], (UNIT, features)).astype(BF)
-    greet([{"dp": xpeer}, {"dp": ypeer}] + [{"dp": ahead(d)} for d in order])
+    block = master.shape[0]
+    gathered[pl.ds(me * block, block)] = master[...].astype(BF)
+    others = [lax.rem(me + d, devices) for d in range(1, devices)]
+    norm_all[me] = norm_row[...]
+    greet([{"dp": other} for other in others])
+    norm_copies = [send(norm_row, norm_all.at[me], norm_sems.at[0, d], norm_sems.at[1, d], dp=other)
+                   for d, other in zip(range(1, devices), others)]
 
     leaving = [(query_ref, query_out), (kv_ref, kv_out), (memory_ref, memory_out), (grad_ref, grad_out)]
 
@@ -764,15 +766,20 @@
     LineGather(devices, lambda number, start, size: gathered.at[pl.ds(number * block + start, size)], block, block * 3 // 5,
                places, *line_sems).run(first_turns, norms_of_streams, last_turns)
 
-    share = devices // 8
+    for copy in norm_copies:
+        copy.wait()
+    share, whole_lanes = devices // 8, norm_row.shape[1] < features
     vectors = []
     for number in range(8):
-        pieces = [gathered[(number * share + i) * block + slots].astype(F32) for i in range(share)]
-        total = pieces[0]
-        for piece in pieces[1:]:
-            total = total + piece
-        vectors.append(total[0:1, :])
-    norms[...] = jnp.concatenate(vectors, 0)
+        pieces = [norm_all[number * share + i] for i in range(share)]
+        if whole_lanes:
+            vectors.append(jnp.concatenate(pieces, 1))
+        else:
+            total = pieces[0]
+            for piece in pieces[1:]:
+                total = total + piece
+            vectors.append(total)
+    norms[...] = jnp.concatenate(vectors, 0).astype(BF).astype(F32)
 
     def one_unit(u, carry):
         flat[pl.ds(pl.multiple_of(u * UNIT, UNIT), UNIT), :] = gathered[place_ref[0, u]]
@@ -798,7 +805,8 @@
         w1_ref[block * half:(block + 1) * half, :] = jnp.concatenate([parted[:half], parted[half:]], 1)
     w2_ref[...] = flat[8 * cols + hidden:, :]
 
-    def body(step, rows):
+    def body(step, carry):
+        rows = pl.ds(pl.multiple_of(step * 2 * CHUNK, 2 * CHUNK), 2 * CHUNK)
         nq = (unit_q[rows, :] * norms[0:1, :] + norms[1:2, :]).astype(BF)
         nkv = (unit_kv[rows, :] * norms[2:3, :] + norms[3:4, :]).astype(BF)
         source = memory_ref[rows, :]
@@ -810,8 +818,10 @@
                 ref[:, rows] = result
             else:
                 ref[rows, :] = result
-            out.start(i, step)
-    chunks(tokens, body)
+            out.start(i, 2 * step)
+            out.start(i, 2 * step + 1)
+        return carry
+    lax.fori_loop(0, tokens // (2 * CHUNK), body, 0)
     out.drain(tokens)
     for number in range(4):
         leave(number).wait()
@@ -835,10 +845,11 @@
         ((ROW, 128), BF, "V"), ((128, ROW), BF, "V"), ((ROW, 128), F32, "V")]
     D = pltpu.SemaphoreType.DMA
     streams = [in_tiles(stream) for stream in (query_stream, kv_stream, memory, out_grad)]
-    scratch = [pltpu.VMEM((devices * (master.shape[0] + 1), UNIT, features), BF), pltpu.VMEM((8 * cols + 2 * hidden, features), BF)]
+    scratch = [pltpu.VMEM((devices * master.shape[0], UNIT, features), BF), pltpu.VMEM((devices,) + norm_row.shape, F32),
+               pltpu.VMEM((8 * cols + 2 * hidden, features), BF)]
     scratch += [pltpu.VMEM(streams[0].shape, BF)] * 2 + [pltpu.VMEM(wide, BF)] * 4 + [pltpu.VMEM(wide, F32)] * 2
     scratch += [pltpu.VMEM(shape, BF) for shape in shapes]
-    scratch += [D((2, 2)), D((4,)), out_semaphores(len(shapes), tokens)] + [D((2, 2, devices // 4 + 1))] * 6
+    scratch += [D((2, 2)), D((4,)), out_semaphores(len(shapes), tokens), D((2, devices))] + [D((2, 2, devices // 4 + 1))] * 6
     return call(partial(project_kernel, devices), "project",
                 [place_of, info, master, norm_row, rank_row] + streams, "SSVVVAAAA", outs, scratch, 0)
 
@@ -1011,10 +1022,12 @@
     chunks(dq.shape[0], give)
 
 
-def branch_weights(first_in, second_in, dq, dk, dv, flat):
+def branch_weights(first_in, second_in, dq, dk, dv, flat, between=lambda: None):
     cols = dq.shape[1]
     order = interleave(first_in.shape[1])
     for number, (entering, grad) in enumerate(((first_in, dq), (second_in, dk), (second_in, dv))):
+        if number == 1:
+            between()
         flat[number * cols:(number + 1) * cols, :] = as_units(tn(entering[...], grad[...]), order)
 
 
@@ -1157,8 +1170,8 @@
                        for f, part in enumerate((part0, part1, part2, part3))], part_sems)
     others = [lax.rem(me + d, devices) for d in range(1, devices)]
     greet([{"head": 1 - lax.axis_index("head")}] + [{"dp": other} for other in others])
-    late.wait(0, 1)
-    branch_weights(nq, nkv, dq, dk, dv, flat)
+    late.wait(0)
+    branch_weights(nq, nkv, dq, dk, dv, flat, lambda: late.wait(1))
     plane_copies = plane_sum_start(devices, places, flat, 3 * dq.shape[1], source, landing, plane_sems)
     late_parts.wait(0, 1, 2, 3)
     for level in range(across):
@@ -1186,7 +1199,7 @@
         gkv_ref[tiles] = in_tiles(norm_back(unit, scale, norms[2:3, :], grad).astype(BF))
         sums[16:24, :] += fold_rows(grad * unit)
         sums[24:32, :] += fold_rows(grad)
-    middle = tokens // 2
+    middle = tokens // 4 * 3
     chunks(middle, close)
     more.relay()
     chunks(tokens, close, middle)
@@ -1360,10 +1373,11 @@
     hidden = (units * unit_rows - 8 * cols) // 2
 
     shape = (slots, unit_rows, features)
-    norm_row = lax.dynamic_update_slice(
-        jnp.zeros((1, features), F32), norm_master.reshape(1, norm_share), (0, lax.rem(me * norm_share, features)))
+    norm_row = norm_master.reshape(1, norm_share)
+    if norm_share % 128:
+        norm_row = lax.dynamic_update_slice(jnp.zeros((1, features), F32), norm_row, (0, lax.rem(me * norm_share, features)))
     rank_row, count_row = obs_rank.reshape(1, ROW), obs_count.reshape(1, ROW)
-    place_of, held, rank_row, count_row, steps, info = plan(unit_owner, lengths, me.reshape(1), rank_row, count_row, slots + 1)
+    place_of, held, rank_row, count_row, steps, info = plan(unit_owner, lengths, me.reshape(1), rank_row, count_row, slots)
     nq, nkv, qt, k, kt, v, vt, kc, kct, vc, vct, query, kv, source, cotangent, ws, wc, wo_self, wo_cross, w1, w2, norms, *tables = project(
         devices, place_of, info, master.reshape(shape), norm_row, rank_row, query_stream, kv_stream, memory, out_grad, cols, hidden)
     mixed_self, mixed_self_t, total_self = attend_forward(steps, qt, k, vt, tables, count_row, True)

time: 328 us -> 325 us (level)
  transfers between devices with their start and end apart: 6 -> 6, of which waited for: 0 -> 0; matrix products, arithmetic and copies ran while one was open for 0% -> 0% of each run, Pallas kernels for 17% -> 18%
where the time goes in v10:
time: 325 us; the launch traced here: 324 us
  Pallas kernels  313 us (96%)
  starting transfers between devices  7.11 us (2%)
    pallas_call x11, Pallas kernels, call(): pl.pallas_call(kernel, out_shape=tuple((jax.ShapeDtypeStruct(shape, dtype...  313 us
    ppermute x6, starting transfers between devices, plane_swap(): lax.ppermute(value, 'dp', [(i, i // 4 * 4 + (i % 4 ^ f)) for i in range(c...  7.11 us
  transfers between devices with their start and end apart: 6, of which 0 were waited for; matrix products, arithmetic and copies ran while one was open for 0% of the time, Pallas kernels for 18%

profile of v10, /device:TPU:0, one launch (start us, length us, event | category | flops | bytes accessed | tf_op | source)
XLA Modules:
  0.0 323.8 jit_solution(10707726442783916722)
XLA Ops:
  0.6 2.2 plan.1
  2.9 82.2 %project.1 = (bf16[2048,512]{1,0:T(8,128)(2,1)}, bf16[2048,512]{1,0:T(8,128)(2,1)}, bf16[256,2048]{1,0:T(8,128)(2,1)}, bf16[2048,256]{1,0:T(8,128)(2,1)}, bf16[2...) custom-call(s32[1,256]{1,0:T(1,128)} %get-tuple-element.105.place_re, ...), custom_call_target="tpu_custom_call" | custom-call | flops 40000000000 | bytes 16777216 | tf_op jit(solution)/shard_map/project/pallas_call | solution.py:551
  85.1 17.4 %attend_self_forward.1 = (bf16[2048,256]{1,0:T(8,128)(2,1)}, bf16[256,2048]{1,0:T(8,128)(2,1)}, f32[8,2048]{1,0:T(8,128)}) custom-call(s32[2,40]{1,0:T(2,128)} %get-tuple-element.103.table, s32[1,2048]{1,0:T(1,128)} %get-tuple-element.104.count_ref, bf16[256,2048]{1,0:T(8,128)(2,1)} %get-tuple-element.108.qt_hbm, ...), custom_call_target="tpu_custom_call" | custom-call | flops 40000000000 | bytes 16777216 | tf_op jit(solution)/shard_map/attend_self_forward/pallas_call | solution.py:551
  102.5 8.4 %self_out.1 = (f32[2048,512]{1,0:T(8,128)}, bf16[2048,512]{1,0:T(8,128)(2,1)}, bf16[256,2048]{1,0:T(8,128)(2,1)}) custom-call(bf16[2048,256]{1,0:T(8,128)(2,1)} %get-tuple-element.115.mixed.mixed_hbm, bf16[256,512]{1,0:T(8,128)(2,1)} %get-tuple-element.116.wo, bf16[2048,512]{1,0:T(8,128)(2,1)} %get-tuple-element.117.query_hbm, ...), custom_call_target="tpu_custom_call" | custom-call | flops 40000000000 | bytes 16777216 | tf_op jit(solution)/shard_map/self_out/pallas_call | solution.py:551
  110.9 16.9 %attend_cross_forward.1 = (bf16[2048,256]{1,0:T(8,128)(2,1)}, bf16[256,2048]{1,0:T(8,128)(2,1)}, f32[8,2048]{1,0:T(8,128)}) custom-call(s32[2,40]{1,0:T(2,128)} %get-tuple-element.103.table, s32[1,2048]{1,0:T(1,128)} %get-tuple-element.104.count_ref, bf16[256,2048]{1,0:T(8,128)(2,1)} %get-tuple-element.120.qt_hbm, ...), custom_call_target="tpu_custom_call" | custom-call | flops 40000000000 | bytes 16777216 | tf_op jit(solution)/shard_map/attend_cross_forward/pallas_call | solution.py:551
  127.8 37.2 %feed_forward.1 = (bf16[2048,512]{1,0:T(8,128)(2,1)}, f32[2048,512]{1,0:T(8,128)}, bf16[256,2048]{1,0:T(8,128)(2,1)}, bf16[4,144,512]{2,1,0:T(8,128)(2,1)}, bf16...) custom-call(bf16[2048,256]{1,0:T(8,128)(2,1)} %get-tuple-element.123., ...), custom_call_target="tpu_custom_call" | custom-call | flops 40000000000 | bytes 16777216 | tf_op jit(solution)/shard_map/feed_forward/pallas_call | solution.py:551
  164.9 1.5 collective-permute-start
  166.5 0.4 collective-permute-start.1
  166.9 1.6 collective-permute-start.2
  168.5 27.7 %attend_cross_backward.1 = (bf16[2048,256]{1,0:T(8,128)(2,1)}, bf16[2048,256]{1,0:T(8,128)(2,1)}, bf16[2048,256]{1,0:T(8,128)(2,1)}) custom-call(s32[2,40]{1,0:T(2,128)} %get-tuple-element.103.table, s32[1,2048]{1,0:T(1,128)} %get-tuple-element.104.count_ref, f32[8,2048]{1,0:T(8,128)} %get-tuple-element.133.lse_ref, ...), custom_call_target="tpu_custom_call" | custom-call | flops 40000000000 | bytes 16777216 | tf_op jit(solution)/shard_map/attend_cross_backward/pallas_call | solution.py:551
  196.2 0.0 collective-permute-done.part1
  196.2 0.0 copy-start.3
  196.2 0.0 collective-permute-done.1.part2
  196.3 0.0 copy-start.4
  196.3 0.0 collective-permute-done.2.part3
  196.3 0.0 copy-start.5
  196.3 0.8 copy-done.3
  197.1 0.2 copy-done.4
  197.2 0.2 copy-done.5
  197.4 35.3 %cross_back.1 = (bf16[2048,512]{1,0:T(8,128)(2,1)}, bf16[2048,512]{1,0:T(8,128)(2,1)}, f32[2048,512]{1,0:T(8,128)}, bf16[256,2048]{1,0:T(8,128)(2,1)}, bf16[4,16...) custom-call(s32[1,34]{1,0:T(1,128)} %get-tuple-element.106.info, ...), custom_call_target="tpu_custom_call" | custom-call | flops 40000000000 | bytes 16777216 | tf_op jit(solution)/shard_map/cross_back/pallas_call | solution.py:551
  232.8 1.2 collective-permute-start.3
  234.0 1.9 collective-permute-start.4
  235.8 0.5 collective-permute-start.5
  236.3 29.3 %attend_self_backward.1 = (bf16[2048,256]{1,0:T(8,128)(2,1)}, bf16[2048,256]{1,0:T(8,128)(2,1)}, bf16[2048,256]{1,0:T(8,128)(2,1)}, bf16[2048,512]{1,0:T(8,128)(2,1)}, bf16[2048,512]{1,0:T(8,128)(2,1)}) custom-call(s32[2,40]{1,0:T(2,128)} %get-tuple-element.103.table, s32[1,2048]{1,0:T(1,128)} %get-tuple-element.104.count_ref, ...), custom_call_target="tpu_custom_call" | custom-call | flops 40000000000 | bytes 16777216 | tf_op jit(solution)/shard_map/attend_self_backward/pallas_call | solution.py:551
  265.6 0.0 collective-permute-done.3.part1.refs_7_
  265.6 0.0 copy-start
  265.6 0.0 collective-permute-done.4.part2.refs_8_
  265.6 0.0 copy-start.1
  265.6 0.0 collective-permute-done.5.part3.refs_9_
  265.6 0.0 copy-start.2
  265.7 0.8 copy-done
  266.5 0.2 copy-done.1
  266.7 0.2 copy-done.2
  266.9 47.4 %self_back.1 = (bf16[2048,512]{1,0:T(8,128)(2,1)}, bf16[2048,512]{1,0:T(8,128)(2,1)}, bf16[4,4,48,512]{3,2,1,0:T(8,128)(2,1)}, bf16[4,4,64,512]{3,2,1,0:T(8,128)(2,1)}, f32[8,512]{1,0:T(8,128)}) custom-call(s32[1,34]{1,0:T(1,128)} %get-tuple-element.106.info, bf16[2048,256]{1,0:T(8,128)(2,1)} %get-tuple-element.163.dq, ...), custom_call_target="tpu_custom_call" | custom-call | flops 40000000000 | bytes 16777216 | tf_op jit(solution)/shard_map/self_back/pallas_call | solution.py:551
  314.3 9.3 %update.1 = (f32[32,16,512]{2,1,0:T(8,128)}, f32[32,16,512]{2,1,0:T(8,128)}, f32[32,16,512]{2,1,0:T(8,128)}, f32[32,16,512]{2,1,0:T(8,128)}, bf16[2048,512]{1,0:...) custom-call(s32[1,128]{1,0:T(1,128)} %get-tuple-element.157.held, ...), custom_call_target="tpu_custom_call" | custom-call | flops 40000000000 | bytes 16777216 | tf_op jit(solution)/shard_map/update/pallas_call | solution.py:551
Async XLA Ops:
  164.9 31.3 %collective-permute-start = (bf16[4,144,512]{2,1,0:T(8,128)(2,1)}, bf16[4,144,512]{2,1,0:T(8,128)(2,1)S(1)}, u32[]{:S(2)}, u32[]{:S(2)}) collective-permute-start(bf16[4,144,512]{2,1,0:T(8,128)(2,1)} %get-tuple-element.130), channel_id=1, source_target_pairs={{0,2},{2,0},{4,6},{6,4},{8,10},{10,8},{12,14},{14,12},{16,18},{18,... | collective-permute-start | bytes 1769480 | tf_op jit(solution)/shard_map/ppermute | solution.py:540
  166.5 29.8 %collective-permute-start.1 = (bf16[4,144,512]{2,1,0:T(8,128)(2,1)}, bf16[4,144,512]{2,1,0:T(8,128)(2,1)S(1)}, u32[]{:S(2)}, u32[]{:S(2)}) collective-permute-start(bf16[4,144,512]{2,1,0:T(8,128)(2,1)} %get-tuple-element.131), channel_id=1, source_target_pairs={{0,4},{2,6},{4,0},{6,2},{8,12},{10,14},{12,8},{14,10},{16,20},{18,... | collective-permute-start | bytes 1769480 | tf_op jit(solution)/shard_map/ppermute | solution.py:540
  166.9 29.4 %collective-permute-start.2 = (bf16[4,144,512]{2,1,0:T(8,128)(2,1)}, bf16[4,144,512]{2,1,0:T(8,128)(2,1)S(1)}, u32[]{:S(2)}, u32[]{:S(2)}) collective-permute-start(bf16[4,144,512]{2,1,0:T(8,128)(2,1)} %get-tuple-element.132), channel_id=1, source_target_pairs={{0,6},{2,4},{4,2},{6,0},{8,14},{10,12},{12,10},{14,8},{16,22},{18,... | collective-permute-start | bytes 1769480 | tf_op jit(solution)/shard_map/ppermute | solution.py:540
  196.2 0.8 copy-start.3
  196.3 1.0 copy-start.4
  196.3 1.2 copy-start.5
  232.8 32.8 %collective-permute-start.3 = (bf16[4,160,512]{2,1,0:T(8,128)(2,1)}, bf16[4,160,512]{2,1,0:T(8,128)(2,1)S(1)}, u32[]{:S(2)}, u32[]{:S(2)}) collective-permute-start(bf16[4,160,512]{2,1,0:T(8,128)(2,1)} %get-tuple-element.159), channel_id=1, source_target_pairs={{0,2},{2,0},{4,6},{6,4},{8,10},{10,8},{12,14},{14,12},{16,18},{18,... | collective-permute-start | bytes 1966088 | tf_op jit(solution)/shard_map/ppermute | solution.py:540
  234.0 31.7 %collective-permute-start.4 = (bf16[4,160,512]{2,1,0:T(8,128)(2,1)}, bf16[4,160,512]{2,1,0:T(8,128)(2,1)S(1)}, u32[]{:S(2)}, u32[]{:S(2)}) collective-permute-start(bf16[4,160,512]{2,1,0:T(8,128)(2,1)} %get-tuple-element.160), channel_id=1, source_target_pairs={{0,4},{2,6},{4,0},{6,2},{8,12},{10,14},{12,8},{14,10},{16,20},{18,... | collective-permute-start | bytes 1966088 | tf_op jit(solution)/shard_map/ppermute | solution.py:540
  235.8 29.8 %collective-permute-start.5 = (bf16[4,160,512]{2,1,0:T(8,128)(2,1)}, bf16[4,160,512]{2,1,0:T(8,128)(2,1)S(1)}, u32[]{:S(2)}, u32[]{:S(2)}) collective-permute-start(bf16[4,160,512]{2,1,0:T(8,128)(2,1)} %get-tuple-element.161), channel_id=1, source_target_pairs={{0,6},{2,4},{4,2},{6,0},{8,14},{10,12},{12,10},{14,8},{16,22},{18,... | collective-permute-start | bytes 1966088 | tf_op jit(solution)/shard_map/ppermute | solution.py:540
  265.6 0.9 copy-start
  265.6 1.0 copy-start.1
  265.6 1.2 copy-start.2
